TPU v7x, 32 devices: a whole 2x2x4 slice. The times are simulated.
32 devices in a mesh: nbhd: 8 (over y, x, core), sub: 4 (over z).
Axes of the slice: x: 2, y: 2, z: 4, core: 2. Of those that a mesh axis runs over, the one named last changes fastest.
Arguments:
- snap_init: bfloat16 [8, 16, 16, 96, 128], P('nbhd', 'sub'), may hold values from -8 to 8
- channel_map: int32 [8, 16, 16, 96], P('nbhd', 'sub'), may hold values from 0 to 3
- yface_vals: bfloat16 [8, 96, 128], P('nbhd'), may hold values from -6 to 6
- zface_vals: bfloat16 [8, 16, 128], P('nbhd'), may hold values from -6 to 6
- face_of: int32 [8, 128], P('nbhd'), may hold values from 0 to 3
- start_block: float32 [8, 128, 32], P('nbhd'), may hold values from -6 to 6
- correlation: int32 [8, 8], replicated, may hold values 0 or 1
Outputs:
- owner_basis: bfloat16 [8, 4, 8, 32, 768], P('nbhd', 'sub')
All inputs are finite; a program needn't handle non-finite values.
Results may differ from a plain program's by a relative error of at most 0.0072.
Values may be sent and summed in bfloat16 or wider, within the bound.
No kernel may reach another device: no remote copies, remote signals or barrier semaphores. Data moves between devices by JAX's collectives and lax.ppermute only.
A program may use at most 128 MiB of HBM per device.

v0:
```python
import jax
import jax.numpy as jnp
from jax import lax
from jax.sharding import PartitionSpec as P

SWEEPS = 3
ITERS = 4


def with_halo(cells, sides, width):
    for axis, dim in sides:
        count = lax.axis_size(axis)
        ends = count - 1
        head = lax.slice_in_dim(cells, 0, width, axis=dim)
        tail = lax.slice_in_dim(cells, cells.shape[dim] - width, cells.shape[dim], axis=dim)
        cells = jnp.concatenate(
            [
                lax.ppermute(tail, axis, [(i, (i + 1) % count) for i in range(ends)]),
                cells,
                lax.ppermute(head, axis, [((i + 1) % count, i) for i in range(ends)]),
            ],
            axis=dim,
        )
    return cells


def harmonic(left_k, right_k):
    return 2.0 * left_k * right_k / (left_k + right_k)


def face_terms(field_ext, kappa_ext, first_plane, plane_count, ghosts):
    length = field_ext.shape[0]
    plane_ids = first_plane + jnp.arange(length, dtype=jnp.int32)
    inside = (plane_ids >= 0) & (plane_ids < plane_count)
    kappa = jnp.where(inside[:, None, None], kappa_ext, jnp.float32(1.0))
    centre = kappa[1:-1]
    x_lower = jnp.where(inside[:-2, None, None], harmonic(centre, kappa[:-2]), centre)
    x_upper = jnp.where(inside[2:, None, None], harmonic(centre, kappa[2:]), centre)
    y_inner = harmonic(centre[:, 1:], centre[:, :-1])
    y_lower = jnp.concatenate([centre[:, :1], y_inner], axis=1)
    y_upper = jnp.concatenate([y_inner, centre[:, -1:]], axis=1)
    z_inner = harmonic(centre[:, :, 1:], centre[:, :, :-1])
    z_lower = jnp.concatenate([centre[:, :, :1], z_inner], axis=2)
    z_upper = jnp.concatenate([z_inner, centre[:, :, -1:]], axis=2)
    middle = field_ext[1:-1].astype(jnp.float32)
    count, rows_y, rows_z, width = middle.shape
    ghost_ylo, ghost_yhi, ghost_zlo, ghost_zhi = ghosts
    below_y = jnp.concatenate(
        [jnp.broadcast_to(ghost_ylo, (count, 1, rows_z, width)), middle[:, :-1]], axis=1
    )
    above_y = jnp.concatenate(
        [middle[:, 1:], jnp.broadcast_to(ghost_yhi, (count, 1, rows_z, width))], axis=1
    )
    below_z = jnp.concatenate(
        [jnp.broadcast_to(ghost_zlo[:, None, :], (count, rows_y, 1, width)), middle[:, :, :-1]],
        axis=2,
    )
    above_z = jnp.concatenate(
        [middle[:, :, 1:], jnp.broadcast_to(ghost_zhi[:, None, :], (count, rows_y, 1, width))],
        axis=2,
    )
    numer = (
        x_lower[..., None] * field_ext[:-2].astype(jnp.float32)
        + x_upper[..., None] * field_ext[2:].astype(jnp.float32)
        + y_lower[..., None] * below_y
        + y_upper[..., None] * above_y
        + z_lower[..., None] * below_z
        + z_upper[..., None] * above_z
    )
    denom = x_lower + x_upper + y_lower + y_upper + z_lower + z_upper
    return (numer, denom, middle, inside[1:-1])


def relax(field_ext, kappa_ext, first_plane, plane_count, ghosts):
    numer, denom, middle, inside = face_terms(
        field_ext, kappa_ext, first_plane, plane_count, ghosts
    )
    updated = numer / denom[..., None]
    return jnp.where(inside[:, None, None, None], updated, jnp.float32(0.0)).astype(jnp.bfloat16)


def stiffness(field_ext, kappa_ext, first_plane, plane_count):
    rows_y, rows_z, width = (field_ext.shape[1], field_ext.shape[2], field_ext.shape[3])
    zero_y = jnp.zeros((rows_z, width), jnp.float32)
    zero_z = jnp.zeros((rows_y, width), jnp.float32)
    numer, denom, middle, inside = face_terms(
        field_ext, kappa_ext, first_plane, plane_count, (zero_y, zero_y, zero_z, zero_z)
    )
    return (denom[..., None] * middle - numer).astype(jnp.bfloat16)


def make_ghosts(y_values, z_values, face_ids):
    y_float = y_values.astype(jnp.float32)
    z_float = z_values.astype(jnp.float32)
    picks = [(face_ids == side).astype(jnp.float32)[None, :] for side in range(4)]
    return (y_float * picks[0], y_float * picks[1], z_float * picks[2], z_float * picks[3])


def gram_terms(snapshots, kappa, stiff_apply):
    width = snapshots.shape[-1]
    flat = snapshots.reshape(-1, width)
    weighted = (flat * (kappa.reshape(-1, 1) / 16.0)).astype(jnp.bfloat16)
    stiff_flat = stiff_apply.reshape(-1, width)
    dims = (((0,), (0,)), ((), ()))
    mass_part = lax.dot_general(flat, weighted, dims, preferred_element_type=jnp.float32)
    stiff_part = lax.dot_general(flat, stiff_flat, dims, preferred_element_type=jnp.float32)
    return (mass_part, stiff_part)


def subspace(mass_sum, stiff_sum, start, cell_count):
    highest = lax.Precision.HIGHEST
    mass_gram = mass_sum / cell_count
    stiff_gram = (stiff_sum + stiff_sum.T) * (0.5 / cell_count)
    factor = jnp.linalg.cholesky(stiff_gram)
    mode_block = start
    for step in range(ITERS):
        right_side = jnp.dot(mass_gram, mode_block, precision=highest)
        solved = jax.scipy.linalg.cho_solve((factor, True), right_side)
        inner = jnp.dot(solved.T, jnp.dot(mass_gram, solved, precision=highest), precision=highest)
        inner = 0.5 * (inner + inner.T)
        lower = jnp.linalg.cholesky(inner)
        mode_block = jax.scipy.linalg.solve_triangular(lower, solved.T, lower=True).T
    return mode_block


def on_device(snap_init, channel_map, yface_vals, zface_vals, face_of, start_block, correlation):
    initial = snap_init[0]
    class_map = channel_map[0]
    planes = initial.shape[0]
    plane_count = planes * lax.axis_size("sub")
    base_plane = lax.axis_index("sub") * planes
    ghosts = make_ghosts(yface_vals[0], zface_vals[0], face_of[0])
    class_ext = with_halo(class_map, (("sub", 0),), 1)
    kappa_edge = jnp.exp2(2.0 * class_ext.astype(jnp.float32))
    state = initial
    for sweep_no in range(SWEEPS):
        padded = with_halo(state, (("sub", 0),), 1)
        state = relax(padded, kappa_edge, base_plane - 1, plane_count, ghosts)
    field_edge = with_halo(state, (("sub", 0),), 1)
    snapshots = field_edge[1:-1]
    kappa_local = kappa_edge[1:-1]
    stiff_apply = stiffness(field_edge, kappa_edge, base_plane - 1, plane_count)
    mass_part, stiff_part = gram_terms(snapshots, kappa_local, stiff_apply)
    mass_sum, stiff_sum = lax.psum((mass_part, stiff_part), "sub")
    cell_count = float(plane_count * snapshots.shape[1] * snapshots.shape[2])
    mode_block = subspace(mass_sum, stiff_sum, start_block[0], cell_count)
    owner_count = lax.axis_size("nbhd")
    width = snapshots.shape[-1]
    piece_cells = snapshots.size // width // owner_count
    blocks = snapshots.reshape(owner_count, piece_cells, width)
    pieces = jnp.einsum(
        "pcs,sm->pmc", blocks, mode_block.astype(jnp.bfloat16), preferred_element_type=jnp.float32
    ).astype(jnp.bfloat16)
    received = lax.all_to_all(pieces, "nbhd", split_axis=0, concat_axis=0, tiled=True)
    column = lax.dynamic_slice_in_dim(correlation, lax.axis_index("nbhd"), 1, axis=1)[:, 0]
    result = received * column.astype(jnp.bfloat16)[:, None, None]
    return result[None, None]


def solution(mesh):
    return jax.shard_map(
        on_device,
        mesh=mesh,
        in_specs=(
            P("nbhd", "sub", None, None, None),
            P("nbhd", "sub", None, None),
            P("nbhd", None, None),
            P("nbhd", None, None),
            P("nbhd", None),
            P("nbhd", None, None),
            P(),
        ),
        out_specs=P("nbhd", "sub", None, None, None),
        check_vma=False,
    )
```

profile of v0, /device:TPU:0, one launch (start us, length us, event | category | flops | bytes accessed | tf_op | source)
XLA Modules:
  0.0 230.0 jit_solution(14710982466676849986)
XLA Ops:
  7.9 5.5 %collective-permute-start = (s32[1,16,96]{2,1,0:T(8,128)}, s32[1,16,96]{2,1,0:T(8,128)}, u32[]{:S(2)}, u32[]{:S(2)}) collective-permute-start(s32[1,16,96]{2,1,0:T(8,128)} %get-tuple-element.47), channel_id=1, source_target_pairs={{0,1},{1,2},{2,3},{4,5},{5,6},{6,7},{8,9},{9,10},{10,11},{12,13},{... | collective-permute-start | bytes 18440 | tf_op jit(solution)/shard_map/ppermute | solution.py:18
  16.6 5.3 %collective-permute-start.2 = (bf16[1,16,96,128]{3,2,1,0:T(8,128)(2,1)}, bf16[1,16,96,128]{3,2,1,0:T(8,128)(2,1)}, u32[]{:S(2)}, u32[]{:S(2)}) collective-permute-start(bf16[1,16,96,128]{3,2,1,0:T(8,128)(2,1)} %get-tuple-element.39), channel_id=1, source_target_pairs={{0,1},{1,2},{2,3},{4,5},{5,6},{6,7},{8,9},{9,10},{10,11},{12,13},{... | collective-permute-start | bytes 1179656 | tf_op jit(solution)/shard_map/ppermute | solution.py:18
  25.0 3.3 %fusion.140 = (f32[4,15,96,128]{3,2,1,0:T(8,128)}, f32[4,15,96,128]{3,2,1,0:T(8,128)}) fusion(f32[4,16,96,128]{3,2,1,0:T(8,128)S(1)} %bitcast_convert_fusion), kind=kLoop, calls=%fused_computation.218 | loop fusion | bytes 11796480 | tf_op jit(solution)/shard_map/slice | solution.py:49
  34.1 9.9 %fusion.32 = bf16[4,16,96,128]{3,2,1,0:T(8,128)(2,1)S(1)} fusion(f32[4,16,1,128]{3,2,1,0:T(1,128)S(1)} %broadcast_in_dim.163, f32[4,16,95,128]{3,2,1,0:T(8,128)} %get-tuple-element.20, f32[4,16,95,128]{3,2,1,0:T(8,128)S(1)} %get-tuple-element.19, f32[4,16,1,128]{3,2,1,0:T(1,128)S(1)} %broadcast_in_dim.162, f32[4,1,96,128]{3,2,1,0:T(8,128)S(1)} %broadcast_in_dim.161, ...), kind=kLoop, calls=%fused_computation.46 | loop fusion | flops 17301504 | bytes 16687108 | tf_op jit(solution)/shard_map/convert_element_type | solution.py:79
  45.3 4.6 %collective-permute-start.4 = (bf16[1,16,96,128]{3,2,1,0:T(8,128)(2,1)S(1)}, bf16[1,16,96,128]{3,2,1,0:T(8,128)(2,1)S(1)}, u32[]{:S(2)}, u32[]{:S(2)}) collective-permute-start(bf16[1,16,96,128]{3,2,1,0:T(8,128)(2,1)S(1)} %get-tuple-element.33), channel_id=1, source_target_pairs={{0,1},{1,2},{2,3},{4,5},{5,6},{6,7},{8,9},{9,10},{10,11},{12,13},{... | collective-permute-start | bytes 1179656 | tf_op jit(solution)/shard_map/ppermute | solution.py:18
  51.9 5.2 %collective-permute-done.4 = bf16[1,16,96,128]{3,2,1,0:T(8,128)(2,1)S(1)} collective-permute-done((bf16[1,16,96,128]{3,2,1,0:T(8,128)(2,1)S(1)}, bf16[1,16,96,128]{3,2,1,0:T(8,128)(2,1)S(1)}, u32[]{:S(2)}, u32[]{:S(2)}) %collective-permute-start.4) | collective-permute-done | bytes 393248 | tf_op jit(solution)/shard_map/ppermute | solution.py:18
  57.1 4.1 %collective-permute-done.5 = bf16[1,16,96,128]{3,2,1,0:T(8,128)(2,1)S(1)} collective-permute-done((bf16[1,16,96,128]{3,2,1,0:T(8,128)(2,1)S(1)}, bf16[1,16,96,128]{3,2,1,0:T(8,128)(2,1)S(1)}, u32[]{:S(2)}, u32[]{:S(2)}) %collective-permute-start.5) | collective-permute-done | bytes 393248 | tf_op jit(solution)/shard_map/ppermute | solution.py:20
  61.2 6.8 %fusion.31 = bf16[4,16,96,128]{3,2,1,0:T(8,128)(2,1)S(1)} fusion(f32[4,16,1,128]{3,2,1,0:T(1,128)S(1)} %broadcast_in_dim.163, f32[4,16,95,128]{3,2,1,0:T(8,128)S(1)} %get-tuple-element.38, f32[4,16,95,128]{3,2,1,0:T(8,128)S(1)} %get-tuple-element.37, f32[4,16,1,128]{3,2,1,0:T(1,128)S(1)} %broadcast_in_dim.162, f32[4,1,96,128]{3,2,1,0:T(8,128)S(1)} %broadcast_in_dim.161, ...), kind=kLoop, calls=%fused_computation.45 | loop fusion | flops 17301504 | bytes 16687108 | tf_op jit(solution)/shard_map/convert_element_type | solution.py:79
  69.3 3.4 %collective-permute-start.6 = (bf16[1,16,96,128]{3,2,1,0:T(8,128)(2,1)S(1)}, bf16[1,16,96,128]{3,2,1,0:T(8,128)(2,1)S(1)}, u32[]{:S(2)}, u32[]{:S(2)}) collective-permute-start(bf16[1,16,96,128]{3,2,1,0:T(8,128)(2,1)S(1)} %get-tuple-element.27), channel_id=1, source_target_pairs={{0,1},{1,2},{2,3},{4,5},{5,6},{6,7},{8,9},{9,10},{10,11},{12,13},{... | collective-permute-start | bytes 1179656 | tf_op jit(solution)/shard_map/ppermute | solution.py:18
  74.7 4.2 %collective-permute-done.6 = bf16[1,16,96,128]{3,2,1,0:T(8,128)(2,1)S(1)} collective-permute-done((bf16[1,16,96,128]{3,2,1,0:T(8,128)(2,1)S(1)}, bf16[1,16,96,128]{3,2,1,0:T(8,128)(2,1)S(1)}, u32[]{:S(2)}, u32[]{:S(2)}) %collective-permute-start.6) | collective-permute-done | bytes 393248 | tf_op jit(solution)/shard_map/ppermute | solution.py:18
  78.9 4.1 %collective-permute-done.7 = bf16[1,16,96,128]{3,2,1,0:T(8,128)(2,1)S(1)} collective-permute-done((bf16[1,16,96,128]{3,2,1,0:T(8,128)(2,1)S(1)}, bf16[1,16,96,128]{3,2,1,0:T(8,128)(2,1)S(1)}, u32[]{:S(2)}, u32[]{:S(2)}) %collective-permute-start.7) | collective-permute-done | bytes 393248 | tf_op jit(solution)/shard_map/ppermute | solution.py:20
  83.1 6.8 %fusion.30 = bf16[4,16,96,128]{3,2,1,0:T(8,128)(2,1)S(1)} fusion(f32[4,16,1,128]{3,2,1,0:T(1,128)S(1)} %broadcast_in_dim.163, f32[4,16,95,128]{3,2,1,0:T(8,128)S(1)} %get-tuple-element.32, f32[4,16,95,128]{3,2,1,0:T(8,128)S(1)} %get-tuple-element.31, f32[4,16,1,128]{3,2,1,0:T(1,128)S(1)} %broadcast_in_dim.162, f32[4,1,96,128]{3,2,1,0:T(8,128)S(1)} %broadcast_in_dim.161, ...), kind=kLoop, calls=%fused_computation.44 | loop fusion | flops 17301504 | bytes 16687108 | tf_op jit(solution)/shard_map/convert_element_type | solution.py:79
  93.2 3.4 %collective-permute-start.8 = (bf16[1,16,96,128]{3,2,1,0:T(8,128)(2,1)S(1)}, bf16[1,16,96,128]{3,2,1,0:T(8,128)(2,1)S(1)}, u32[]{:S(2)}, u32[]{:S(2)}) collective-permute-start(bf16[1,16,96,128]{3,2,1,0:T(8,128)(2,1)S(1)} %get-tuple-element.21), channel_id=1, source_target_pairs={{0,1},{1,2},{2,3},{4,5},{5,6},{6,7},{8,9},{9,10},{10,11},{12,13},{... | collective-permute-start | bytes 1179656 | tf_op jit(solution)/shard_map/ppermute | solution.py:18
  98.8 3.0 %collective-permute-done.8 = bf16[1,16,96,128]{3,2,1,0:T(8,128)(2,1)S(1)} collective-permute-done((bf16[1,16,96,128]{3,2,1,0:T(8,128)(2,1)S(1)}, bf16[1,16,96,128]{3,2,1,0:T(8,128)(2,1)S(1)}, u32[]{:S(2)}, u32[]{:S(2)}) %collective-permute-start.8) | collective-permute-done | bytes 393248 | tf_op jit(solution)/shard_map/ppermute | solution.py:18
  101.8 4.4 %collective-permute-done.9 = bf16[1,16,96,128]{3,2,1,0:T(8,128)(2,1)S(1)} collective-permute-done((bf16[1,16,96,128]{3,2,1,0:T(8,128)(2,1)S(1)}, bf16[1,16,96,128]{3,2,1,0:T(8,128)(2,1)S(1)}, u32[]{:S(2)}, u32[]{:S(2)}) %collective-permute-start.9) | collective-permute-done | bytes 393248 | tf_op jit(solution)/shard_map/ppermute | solution.py:20
  106.2 7.6 %fusion.47 = f32[128,128]{1,0:T(8,128)} fusion(bf16[4,16,96,128]{3,2,1,0:T(8,128)(2,1)S(1)} %fusion.30, f32[4,16,95,128]{3,2,1,0:T(8,128)S(1)} %get-tuple-element.26, f32[4,16,95,128]{3,2,1,0:T(8,128)S(1)} %get-tuple-element.25, f32[4,15,96,128]{3,2,1,0:T(8,128)S(1)} %get-tuple-element.24, f32[4,15,96,128]{3,2,1,0:T(8,128)S(1)} %get-tuple-element.23, ...), kind=kOutput, calls=%fused_computation.70 | convolution fusion | flops 216268800 | bytes 14721024 | tf_op jit(solution)/shard_map/dot_general | solution.py:106
  113.8 32.9 %all-reduce.7.cloned.1.call-done = (f32[128,128]{1,0:T(8,128)}, f32[128,128]{1,0:T(8,128)}) async-done(((f32[128,128]{1,0:T(8,128)}, f32[128,128]{1,0:T(8,128)}), (f32[128,128]{1,0:T(8,128)}, f32[128,128]{1,0:T(8,128)})) %all-reduce.7.cloned.1.call-update) | async-done | bytes 131088 | tf_op jit(solution)/shard_map/psum | solution.py:144
  148.7 11.7 %cholesky.36 = f32[128,128]{1,0:T(8,128)S(1)} custom-call(f32[128,128]{1,0:T(8,128)S(1)} %fusion.67), custom_call_target="Cholesky" | custom-call | tf_op jit(solution)/shard_map/jit(cholesky)/cholesky | solution.py:114
  161.8 10.0 %custom-call.25 = f32[1,128,128]{1,2,0:T(8,128)S(1)} custom-call(f32[1,128,128]{2,1,0:T(8,128)S(1)} %fusion.50), custom_call_target="InvertDiagBlocksLowerTriangular" | custom-call | tf_op jit(solution)/shard_map/jit(_cho_solve)/triangular_solve | solution.py:118
  184.7 2.9 %cholesky.126 = f32[32,32]{1,0:T(8,128)S(1)} custom-call(f32[32,32]{1,0:T(8,128)S(1)} %fusion.111), custom_call_target="Cholesky" | custom-call | tf_op jit(solution)/shard_map/jit(cholesky)/cholesky | solution.py:121
  193.8 2.9 %cholesky.137 = f32[32,32]{1,0:T(8,128)S(1)} custom-call(f32[32,32]{1,0:T(8,128)S(1)} %fusion.106), custom_call_target="Cholesky" | custom-call | tf_op jit(solution)/shard_map/jit(cholesky)/cholesky | solution.py:121
  202.0 2.9 %cholesky.148 = f32[32,32]{1,0:T(8,128)S(1)} custom-call(f32[32,32]{1,0:T(8,128)S(1)} %fusion.101), custom_call_target="Cholesky" | custom-call | tf_op jit(solution)/shard_map/jit(cholesky)/cholesky | solution.py:121
  210.4 3.6 %all-to-all-start = ((bf16[8,32,768]{2,1,0:T(8,128)(2,1)}), bf16[8,32,768]{2,1,0:T(8,128)(2,1)S(1)}, u32[]{:S(2)}, u32[]{:S(2)}) async-start(bf16[8,32,768]{2,1,0:T(8,128)(2,1)} %fusion.46), calls=%async_computation | async-start | bytes 786432 | tf_op jit(solution)/shard_map/all_to_all | solution.py:154
  214.2 8.1 %all-to-all-done = bf16[8,32,768]{2,1,0:T(8,128)(2,1)S(1)} async-done(((bf16[8,32,768]{2,1,0:T(8,128)(2,1)}), bf16[8,32,768]{2,1,0:T(8,128)(2,1)S(1)}, u32[]{:S(2)}, u32[]{:S(2)}) %all-to-all-start) | async-done | bytes 393248 | tf_op jit(solution)/shard_map/all_to_all | solution.py:154
  (114 shorter events, 59.3 us)
Async XLA Ops:
  6.5 165.2 %copy-start = (f32[1,128,32]{1,2,0:T(8,128)S(1)}, f32[1,128,32]{1,2,0:T(8,128)}, u32[]{:S(2)}) copy-start(f32[1,128,32]{1,2,0:T(8,128)} %param.17) | copy-start | bytes 49156
  6.5 140.2 %all-reduce.7.cloned.1.call-start = ((), (), s32[]{:S(2)}) async-start(), calls=%async_computation.1 | async-start | bytes 262144 | tf_op jit(solution)/shard_map/psum | solution.py:144
  7.9 24.9 %collective-permute-start = (s32[1,16,96]{2,1,0:T(8,128)}, s32[1,16,96]{2,1,0:T(8,128)}, u32[]{:S(2)}, u32[]{:S(2)}) collective-permute-start(s32[1,16,96]{2,1,0:T(8,128)} %get-tuple-element.47), channel_id=1, source_target_pairs={{0,1},{1,2},{2,3},{4,5},{5,6},{6,7},{8,9},{9,10},{10,11},{12,13},{... | collective-permute-start | bytes 18440 | tf_op jit(solution)/shard_map/ppermute | solution.py:18
  13.4 19.4 %collective-permute-start.1 = (s32[1,16,96]{2,1,0:T(8,128)}, s32[1,16,96]{2,1,0:T(8,128)}, u32[]{:S(2)}, u32[]{:S(2)}) collective-permute-start(s32[1,16,96]{2,1,0:T(8,128)} %get-tuple-element.48), channel_id=1, source_target_pairs={{1,0},{2,1},{3,2},{5,4},{6,5},{7,6},{9,8},{10,9},{11,10},{13,12},{... | collective-permute-start | bytes 18440 | tf_op jit(solution)/shard_map/ppermute | solution.py:20
  16.6 17.4 %collective-permute-start.2 = (bf16[1,16,96,128]{3,2,1,0:T(8,128)(2,1)}, bf16[1,16,96,128]{3,2,1,0:T(8,128)(2,1)}, u32[]{:S(2)}, u32[]{:S(2)}) collective-permute-start(bf16[1,16,96,128]{3,2,1,0:T(8,128)(2,1)} %get-tuple-element.39), channel_id=1, source_target_pairs={{0,1},{1,2},{2,3},{4,5},{5,6},{6,7},{8,9},{9,10},{10,11},{12,13},{... | collective-permute-start | bytes 1179656 | tf_op jit(solution)/shard_map/ppermute | solution.py:18
  21.9 12.1 %collective-permute-start.3 = (bf16[1,16,96,128]{3,2,1,0:T(8,128)(2,1)S(1)}, bf16[1,16,96,128]{3,2,1,0:T(8,128)(2,1)}, u32[]{:S(2)}, u32[]{:S(2)}) collective-permute-start(bf16[1,16,96,128]{3,2,1,0:T(8,128)(2,1)S(1)} %get-tuple-element.40), channel_id=1, source_target_pairs={{1,0},{2,1},{3,2},{5,4},{6,5},{7,6},{9,8},{10,9},{11,10},{13,12},{... | collective-permute-start | bytes 1179656 | tf_op jit(solution)/shard_map/ppermute | solution.py:20
  45.3 11.8 %collective-permute-start.4 = (bf16[1,16,96,128]{3,2,1,0:T(8,128)(2,1)S(1)}, bf16[1,16,96,128]{3,2,1,0:T(8,128)(2,1)S(1)}, u32[]{:S(2)}, u32[]{:S(2)}) collective-permute-start(bf16[1,16,96,128]{3,2,1,0:T(8,128)(2,1)S(1)} %get-tuple-element.33), channel_id=1, source_target_pairs={{0,1},{1,2},{2,3},{4,5},{5,6},{6,7},{8,9},{9,10},{10,11},{12,13},{... | collective-permute-start | bytes 1179656 | tf_op jit(solution)/shard_map/ppermute | solution.py:18
  49.9 11.3 %collective-permute-start.5 = (bf16[1,16,96,128]{3,2,1,0:T(8,128)(2,1)S(1)}, bf16[1,16,96,128]{3,2,1,0:T(8,128)(2,1)S(1)}, u32[]{:S(2)}, u32[]{:S(2)}) collective-permute-start(bf16[1,16,96,128]{3,2,1,0:T(8,128)(2,1)S(1)} %get-tuple-element.34), channel_id=1, source_target_pairs={{1,0},{2,1},{3,2},{5,4},{6,5},{7,6},{9,8},{10,9},{11,10},{13,12},{... | collective-permute-start | bytes 1179656 | tf_op jit(solution)/shard_map/ppermute | solution.py:20
  69.3 9.7 %collective-permute-start.6 = (bf16[1,16,96,128]{3,2,1,0:T(8,128)(2,1)S(1)}, bf16[1,16,96,128]{3,2,1,0:T(8,128)(2,1)S(1)}, u32[]{:S(2)}, u32[]{:S(2)}) collective-permute-start(bf16[1,16,96,128]{3,2,1,0:T(8,128)(2,1)S(1)} %get-tuple-element.27), channel_id=1, source_target_pairs={{0,1},{1,2},{2,3},{4,5},{5,6},{6,7},{8,9},{9,10},{10,11},{12,13},{... | collective-permute-start | bytes 1179656 | tf_op jit(solution)/shard_map/ppermute | solution.py:18
  72.6 10.4 %collective-permute-start.7 = (bf16[1,16,96,128]{3,2,1,0:T(8,128)(2,1)S(1)}, bf16[1,16,96,128]{3,2,1,0:T(8,128)(2,1)S(1)}, u32[]{:S(2)}, u32[]{:S(2)}) collective-permute-start(bf16[1,16,96,128]{3,2,1,0:T(8,128)(2,1)S(1)} %get-tuple-element.28), channel_id=1, source_target_pairs={{1,0},{2,1},{3,2},{5,4},{6,5},{7,6},{9,8},{10,9},{11,10},{13,12},{... | collective-permute-start | bytes 1179656 | tf_op jit(solution)/shard_map/ppermute | solution.py:20
  93.2 8.6 %collective-permute-start.8 = (bf16[1,16,96,128]{3,2,1,0:T(8,128)(2,1)S(1)}, bf16[1,16,96,128]{3,2,1,0:T(8,128)(2,1)S(1)}, u32[]{:S(2)}, u32[]{:S(2)}) collective-permute-start(bf16[1,16,96,128]{3,2,1,0:T(8,128)(2,1)S(1)} %get-tuple-element.21), channel_id=1, source_target_pairs={{0,1},{1,2},{2,3},{4,5},{5,6},{6,7},{8,9},{9,10},{10,11},{12,13},{... | collective-permute-start | bytes 1179656 | tf_op jit(solution)/shard_map/ppermute | solution.py:18
  96.6 9.7 %collective-permute-start.9 = (bf16[1,16,96,128]{3,2,1,0:T(8,128)(2,1)S(1)}, bf16[1,16,96,128]{3,2,1,0:T(8,128)(2,1)S(1)}, u32[]{:S(2)}, u32[]{:S(2)}) collective-permute-start(bf16[1,16,96,128]{3,2,1,0:T(8,128)(2,1)S(1)} %get-tuple-element.22), channel_id=1, source_target_pairs={{1,0},{2,1},{3,2},{5,4},{6,5},{7,6},{9,8},{10,9},{11,10},{13,12},{... | collective-permute-start | bytes 1179656 | tf_op jit(solution)/shard_map/ppermute | solution.py:20
  146.8 46.5 %copy-start.1 = (f32[128,128]{1,0:T(8,128)S(1)}, f32[128,128]{1,0:T(8,128)}, u32[]{:S(2)}) copy-start(f32[128,128]{1,0:T(8,128)} %get-tuple-element.6) | copy-start | bytes 196612
  173.4 40.6 %copy-start.2 = (s32[8,8]{1,0:T(8,128)S(1)}, s32[8,8]{1,0:T(8,128)}, u32[]{:S(2)}) copy-start(s32[8,8]{1,0:T(8,128)} %param.18) | copy-start | bytes 772
  210.4 12.0 %all-to-all-start = ((bf16[8,32,768]{2,1,0:T(8,128)(2,1)}), bf16[8,32,768]{2,1,0:T(8,128)(2,1)S(1)}, u32[]{:S(2)}, u32[]{:S(2)}) async-start(bf16[8,32,768]{2,1,0:T(8,128)(2,1)} %fusion.46), calls=%async_computation | async-start | bytes 786432 | tf_op jit(solution)/shard_map/all_to_all | solution.py:154
Sparse Core Ops, SparseCore 0:
  113.9 32.7 all-reduce.6
where the time goes:
time: 231 us; the launch traced here: 230 us
  other arithmetic  80.1 us (35%)
  waiting for transfers between devices  66.2 us (29%)
  starting transfers between devices  32.3 us (14%)
  matrix products  20.5 us (9%)
  local copies, waits for them, and re-layouts  16.8 us (7%)
  between operations  14 us (6%)
    psum x1, waiting for transfers between devices, on_device(): mass_sum, stiff_sum = lax.psum((mass_part, stiff_part), 'sub')  32.9 us
    convert_element_type x3, other arithmetic, relax(): jnp.where(inside[:, None, None, None], updated, jnp.float32(0.0))  23.4 us
    ppermute x5, starting transfers between devices, with_halo(): lax.ppermute(tail, axis, [(i, (i + 1) % count) for i in range(ends)])  22.1 us
    another operation x12, other arithmetic, subspace(): lower = jnp.linalg.cholesky(inner)  14.4 us
    ppermute x5, waiting for transfers between devices, with_halo(): lax.ppermute(head, axis, [((i + 1) % count, i) for i in range(ends)])  12.7 us
    ppermute x5, waiting for transfers between devices, with_halo(): lax.ppermute(tail, axis, [(i, (i + 1) % count) for i in range(ends)])  12.4 us
    another operation x3, other arithmetic, subspace(): factor = jnp.linalg.cholesky(stiff_gram)  12.4 us
    another operation x8, other arithmetic, subspace(): jax.scipy.linalg.solve_triangular(lower, solved.T, lower=True)  12.3 us
  transfers between devices with their start and end apart: 12, of which 8 were waited for; matrix products, arithmetic and copies ran while one was open for 7% of the time, Pallas kernels for 0%

commit v1 on v0

--- a/solution.py
+++ b/solution.py
@@ -1,6 +1,10 @@
+import functools
+
 import jax
 import jax.numpy as jnp
 from jax import lax
+from jax.experimental import pallas as pl
+from jax.experimental.pallas import tpu as pltpu
 from jax.sharding import PartitionSpec as P
 
 SWEEPS = 3
@@ -107,20 +111,107 @@
     return (mass_part, stiff_part)
 
 
-def subspace(mass_sum, stiff_sum, start, cell_count):
-    highest = lax.Precision.HIGHEST
-    mass_gram = mass_sum / cell_count
-    stiff_gram = (stiff_sum + stiff_sum.T) * (0.5 / cell_count)
-    factor = jnp.linalg.cholesky(stiff_gram)
-    mode_block = start
-    for step in range(ITERS):
-        right_side = jnp.dot(mass_gram, mode_block, precision=highest)
-        solved = jax.scipy.linalg.cho_solve((factor, True), right_side)
-        inner = jnp.dot(solved.T, jnp.dot(mass_gram, solved, precision=highest), precision=highest)
-        inner = 0.5 * (inner + inner.T)
-        lower = jnp.linalg.cholesky(inner)
-        mode_block = jax.scipy.linalg.solve_triangular(lower, solved.T, lower=True).T
-    return mode_block
+def lane_copy(tile, lane):
+    return jnp.broadcast_to(tile[:, lane : lane + 1], (8, 128))
+
+
+def row_copy(tile, row):
+    return jnp.broadcast_to(tile[row : row + 1, :], (8, tile.shape[1]))
+
+
+def solve_spd(left, right):
+    size = left.shape[0]
+    count = size // 8
+    sub = lax.broadcasted_iota(jnp.int32, (8, 128), 0)
+    lhs = [left[8 * t : 8 * t + 8] for t in range(count)]
+    rhs = [right[8 * t : 8 * t + 8] for t in range(count)]
+    for k in range(count):
+        cols = [lane_copy(lhs[k], 8 * k + j) for j in range(8)]
+        panel_l, panel_r = lhs[k], rhs[k]
+        for j in range(8):
+            recip = 1.0 / row_copy(cols[j], j)
+            here = sub == j
+            mult = jnp.where(here, recip, -cols[j] * recip)
+            for l in range(j + 1, 8):
+                cols[l] = jnp.where(here, 0.0, cols[l]) + mult * row_copy(cols[l], j)
+            panel_l = jnp.where(here, 0.0, panel_l) + mult * row_copy(panel_l, j)
+            panel_r = jnp.where(here, 0.0, panel_r) + mult * row_copy(panel_r, j)
+        rows_l = [row_copy(panel_l, j) for j in range(8)]
+        rows_r = [row_copy(panel_r, j) for j in range(8)]
+        order = list(range(k + 1, count)) + list(range(k))
+        for t in order:
+            tile_cols = [lane_copy(lhs[t], 8 * k + j) for j in range(8)]
+            if k + 1 < count:
+                lhs[t] = lhs[t] - tree([tile_cols[j] * rows_l[j] for j in range(8)])
+            rhs[t] = rhs[t] - tree([tile_cols[j] * rows_r[j] for j in range(8)])
+        lhs[k], rhs[k] = panel_l, panel_r
+    return jnp.concatenate(rhs, axis=0)
+
+
+def tree(terms):
+    while len(terms) > 1:
+        terms = [a + b for a, b in zip(terms[::2], terms[1::2])] + terms[len(terms) & ~1 :]
+    return terms[0]
+
+
+def whiten(inner, block):
+    size = inner.shape[0]
+    count = size // 8
+    sub = lax.broadcasted_iota(jnp.int32, (8, 128), 0)
+    lhs = [inner[8 * t : 8 * t + 8] for t in range(count)]
+    rhs = [block[8 * t : 8 * t + 8] for t in range(count)]
+    done = []
+    for k in range(count):
+        live = range(k, count)
+        cols = {t: [lane_copy(lhs[t], 8 * k + j) for j in range(8)] for t in live}
+        scale = None
+        for j in range(8):
+            pivot = row_copy(cols[k][j], j)
+            recip = 1.0 / pivot
+            root = lax.rsqrt(pivot)
+            scale = root if scale is None else jnp.where(sub >= j, root, scale)
+            head = {l: row_copy(cols[k][l], j) for l in range(j + 1, 8)}
+            row_l, row_r = row_copy(lhs[k], j), row_copy(rhs[k], j)
+            for t in live:
+                mult = cols[t][j] * recip
+                if t == k:
+                    mult = jnp.where(sub > j, mult, 0.0)
+                for l in range(j + 1, 8):
+                    cols[t][l] = cols[t][l] - mult * head[l]
+                lhs[t] = lhs[t] - mult[:, : row_l.shape[1]] * row_l
+                rhs[t] = rhs[t] - mult * row_r
+        done.append(rhs[k] * scale)
+    return jnp.concatenate(done, axis=0)
+
+
+def dot(a, b, dims):
+    return lax.dot_general(
+        a, b, (dims, ((), ())), precision=lax.Precision.HIGHEST, preferred_element_type=jnp.float32
+    )
+
+
+def modes_kernel(cell_count, *refs):
+    *part_refs, start_ref, snap_ref, out_ref = refs
+    mass = part_refs[0][0]
+    stiff = part_refs[0][1]
+    for part in part_refs[1:]:
+        mass = mass + part[0]
+        stiff = stiff + part[1]
+    mass = mass * (1.0 / cell_count)
+    stiff = (stiff + stiff.T) * (0.5 / cell_count)
+    step = solve_spd(stiff, mass)
+    form = dot(step, dot(mass, step, ((1,), (0,))), ((0,), (0,)))
+    block = start_ref[...]
+    for _ in range(ITERS):
+        weighted = dot(block, form, ((1,), (0,)))
+        solved = dot(block, step, ((1,), (1,)))
+        inner = dot(weighted, block, ((1,), (1,)))
+        block = whiten(inner, solved)
+    modes = block.astype(jnp.bfloat16)
+    for piece in range(out_ref.shape[0]):
+        out_ref[piece] = lax.dot_general(
+            modes, snap_ref[piece], (((1,), (1,)), ((), ())), preferred_element_type=jnp.float32
+        ).astype(jnp.bfloat16)
 
 
 def on_device(snap_init, channel_map, yface_vals, zface_vals, face_of, start_block, correlation):
@@ -141,16 +232,23 @@
     kappa_local = kappa_edge[1:-1]
     stiff_apply = stiffness(field_edge, kappa_edge, base_plane - 1, plane_count)
     mass_part, stiff_part = gram_terms(snapshots, kappa_local, stiff_apply)
-    mass_sum, stiff_sum = lax.psum((mass_part, stiff_part), "sub")
+    own = jnp.stack([mass_part, stiff_part])
+    subs = lax.axis_size("sub")
+    parts = [own] + [
+        lax.ppermute(own, "sub", [(i, (i + shift) % subs) for i in range(subs)])
+        for shift in range(1, subs)
+    ]
     cell_count = float(plane_count * snapshots.shape[1] * snapshots.shape[2])
-    mode_block = subspace(mass_sum, stiff_sum, start_block[0], cell_count)
     owner_count = lax.axis_size("nbhd")
     width = snapshots.shape[-1]
     piece_cells = snapshots.size // width // owner_count
     blocks = snapshots.reshape(owner_count, piece_cells, width)
-    pieces = jnp.einsum(
-        "pcs,sm->pmc", blocks, mode_block.astype(jnp.bfloat16), preferred_element_type=jnp.float32
-    ).astype(jnp.bfloat16)
+    modes = start_block.shape[-1]
+    pieces = pl.pallas_call(
+        functools.partial(modes_kernel, cell_count),
+        out_shape=jax.ShapeDtypeStruct((owner_count, modes, piece_cells), jnp.bfloat16),
+        compiler_params=pltpu.CompilerParams(vmem_limit_bytes=32 * 2**20),
+    )(*parts, start_block[0].T, blocks)
     received = lax.all_to_all(pieces, "nbhd", split_axis=0, concat_axis=0, tiled=True)
     column = lax.dynamic_slice_in_dim(correlation, lax.axis_index("nbhd"), 1, axis=1)[:, 0]
     result = received * column.astype(jnp.bfloat16)[:, None, None]

time: 231 us -> 140 us (0.61)
  other arithmetic: 80.1 us -> 29.4 us
  waiting for transfers between devices: 66.2 us -> 40.3 us
  between operations: 14 us -> 0.31 us
  matrix products: 20.5 us -> 8.41 us
  Pallas kernels: 0 us -> 11.4 us
    another operation x25 -> x1, other arithmetic: 49.8 us -> 0.01 us  [on_device(): own = jnp.stack([mass_part, stiff_part])]
    psum x1 -> x0, waiting for transfers between devices: 32.9 us -> none  [on_device(): mass_sum, stiff_sum = lax.psum((mass_part, stiff_part), 'sub')]
    pallas_call x0 -> x1, Pallas kernels: none -> 11.4 us  [on_device(): pl.pallas_call(functools.partial(modes_kernel, cell_count), out_shape=jax...]
    dot_general x13 -> x0, matrix products: 7.82 us -> none  [the longest x4 3.3 us: subspace(): right_side = jnp.dot(mass_gram, mode_block, precision=highest)]
    ppermute x0 -> x3, waiting for transfers between devices: none -> 7 us  [on_device(): lax.ppermute(own, 'sub', [(i, (i + shift) % subs) for i in range(subs)])]
    another operation x12 -> x0, matrix products: 3.01 us -> none  [the longest x8 2.07 us: subspace(): solved = jax.scipy.linalg.cho_solve((factor, True), right_side)]
  transfers between devices with their start and end apart: 12 -> 14, of which waited for: 8 -> 9; matrix products, arithmetic and copies ran while one was open for 7% -> 11% of each run, Pallas kernels for 0% -> 0%
where the time goes in v1:
time: 140 us; the launch traced here: 139 us
  waiting for transfers between devices  40.3 us (29%)
  starting transfers between devices  33.9 us (24%)
  other arithmetic  29.4 us (21%)
  local copies, waits for them, and re-layouts  15.1 us (11%)
  Pallas kernels  11.4 us (8%)
  matrix products  8.41 us (6%)
    convert_element_type x3, other arithmetic, relax(): jnp.where(inside[:, None, None, None], updated, jnp.float32(0.0))  23.4 us
    ppermute x5, starting transfers between devices, with_halo(): lax.ppermute(tail, axis, [(i, (i + 1) % count) for i in range(ends)])  21.5 us
    ppermute x5, waiting for transfers between devices, with_halo(): lax.ppermute(head, axis, [((i + 1) % count, i) for i in range(ends)])  12.7 us
    ppermute x5, waiting for transfers between devices, with_halo(): lax.ppermute(tail, axis, [(i, (i + 1) % count) for i in range(ends)])  12.4 us
    pallas_call x1, Pallas kernels, on_device(): pl.pallas_call(functools.partial(modes_kernel, cell_count), out_shape=jax...  11.4 us
    all_to_all x1, waiting for transfers between devices, on_device(): lax.all_to_all(pieces, 'nbhd', split_axis=0, concat_axis=0, tiled=True)  8.15 us
    ppermute x3, waiting for transfers between devices, on_device(): lax.ppermute(own, 'sub', [(i, (i + shift) % subs) for i in range(subs)])  7 us
    dot_general x1, matrix products, gram_terms(): lax.dot_general(flat, stiff_flat, dims, preferred_element_type=jnp.float32)  6.95 us
  transfers between devices with their start and end apart: 14, of which 9 were waited for; matrix products, arithmetic and copies ran while one was open for 11% of the time, Pallas kernels for 0%

profile of v1, /device:TPU:0, one launch (start us, length us, event | category | flops | bytes accessed | tf_op | source)
XLA Modules:
  0.0 138.9 jit_solution(12621438124979855548)
XLA Ops:
  1.3 4.9 %collective-permute-start = (s32[1,16,96]{2,1,0:T(8,128)}, s32[1,16,96]{2,1,0:T(8,128)S(1)}, u32[]{:S(2)}, u32[]{:S(2)}) collective-permute-start(s32[1,16,96]{2,1,0:T(8,128)} %get-tuple-element.42), channel_id=1, source_target_pairs={{0,1},{1,2},{2,3},{4,5},{5,6},{6,7},{8,9},{9,10},{10,11},{12,13},{... | collective-permute-start | bytes 18440 | tf_op jit(solution)/shard_map/ppermute | solution.py:22
  7.5 1.9 %slice_bitcast_fusion.1 = (bf16[1,16,96,128]{3,2,1,0:T(8,128)(2,1)}, bf16[1,16,96,128]{3,2,1,0:T(8,128)(2,1)S(1)}) fusion(bf16[1,4,16,96,128]{4,3,2,1,0:T(8,128)(2,1)} %param.7), kind=kLoop, calls=%fused_computation.72 | loop fusion | bytes 1572864 | tf_op jit(solution)/shard_map/slice | solution.py:19
  9.5 5.3 %collective-permute-start.2 = (bf16[1,16,96,128]{3,2,1,0:T(8,128)(2,1)}, bf16[1,16,96,128]{3,2,1,0:T(8,128)(2,1)}, u32[]{:S(2)}, u32[]{:S(2)}) collective-permute-start(bf16[1,16,96,128]{3,2,1,0:T(8,128)(2,1)} %get-tuple-element.34), channel_id=1, source_target_pairs={{0,1},{1,2},{2,3},{4,5},{5,6},{6,7},{8,9},{9,10},{10,11},{12,13},{... | collective-permute-start | bytes 1179656 | tf_op jit(solution)/shard_map/ppermute | solution.py:22
  16.0 1.8 %bitcast_convert_fusion = f32[4,16,96,128]{3,2,1,0:T(8,128)S(1)} fusion(bf16[1,4,16,96,128]{4,3,2,1,0:T(8,128)(2,1)} %param.7), kind=kLoop, calls=%fused_computation.106 | loop fusion | flops 786432 | bytes 4718592 | tf_op jit(solution)/shard_map/convert_element_type | solution.py:49
  17.9 3.3 %fusion.57 = (f32[4,15,96,128]{3,2,1,0:T(8,128)}, f32[4,15,96,128]{3,2,1,0:T(8,128)}) fusion(f32[4,16,96,128]{3,2,1,0:T(8,128)S(1)} %bitcast_convert_fusion), kind=kLoop, calls=%fused_computation.108 | loop fusion | bytes 11796480 | tf_op jit(solution)/shard_map/slice | solution.py:53
  21.1 2.4 %fusion.58 = (f32[4,16,95,128]{3,2,1,0:T(8,128)S(1)}, f32[4,16,95,128]{3,2,1,0:T(8,128)}) fusion(f32[4,16,96,128]{3,2,1,0:T(8,128)S(1)} %bitcast_convert_fusion), kind=kLoop, calls=%fused_computation.109 | loop fusion | bytes 12451840 | tf_op jit(solution)/shard_map/slice | solution.py:59
  26.9 9.9 %fusion.32 = bf16[4,16,96,128]{3,2,1,0:T(8,128)(2,1)S(1)} fusion(f32[4,16,1,128]{3,2,1,0:T(1,128)S(1)} %broadcast_in_dim.160, f32[4,16,95,128]{3,2,1,0:T(8,128)} %get-tuple-element.15, f32[4,16,95,128]{3,2,1,0:T(8,128)S(1)} %get-tuple-element.14, f32[4,16,1,128]{3,2,1,0:T(1,128)S(1)} %broadcast_in_dim.159, f32[4,1,96,128]{3,2,1,0:T(8,128)S(1)} %broadcast_in_dim.158, ...), kind=kLoop, calls=%fused_computation.46 | loop fusion | flops 17301504 | bytes 16687108 | tf_op jit(solution)/shard_map/convert_element_type | solution.py:83
  38.1 4.6 %collective-permute-start.4 = (bf16[1,16,96,128]{3,2,1,0:T(8,128)(2,1)S(1)}, bf16[1,16,96,128]{3,2,1,0:T(8,128)(2,1)S(1)}, u32[]{:S(2)}, u32[]{:S(2)}) collective-permute-start(bf16[1,16,96,128]{3,2,1,0:T(8,128)(2,1)S(1)} %get-tuple-element.28), channel_id=1, source_target_pairs={{0,1},{1,2},{2,3},{4,5},{5,6},{6,7},{8,9},{9,10},{10,11},{12,13},{... | collective-permute-start | bytes 1179656 | tf_op jit(solution)/shard_map/ppermute | solution.py:22
  44.7 5.2 %collective-permute-done.4 = bf16[1,16,96,128]{3,2,1,0:T(8,128)(2,1)S(1)} collective-permute-done((bf16[1,16,96,128]{3,2,1,0:T(8,128)(2,1)S(1)}, bf16[1,16,96,128]{3,2,1,0:T(8,128)(2,1)S(1)}, u32[]{:S(2)}, u32[]{:S(2)}) %collective-permute-start.4) | collective-permute-done | bytes 393248 | tf_op jit(solution)/shard_map/ppermute | solution.py:22
  49.9 4.1 %collective-permute-done.5 = bf16[1,16,96,128]{3,2,1,0:T(8,128)(2,1)S(1)} collective-permute-done((bf16[1,16,96,128]{3,2,1,0:T(8,128)(2,1)S(1)}, bf16[1,16,96,128]{3,2,1,0:T(8,128)(2,1)S(1)}, u32[]{:S(2)}, u32[]{:S(2)}) %collective-permute-start.5) | collective-permute-done | bytes 393248 | tf_op jit(solution)/shard_map/ppermute | solution.py:24
  54.0 6.8 %fusion.31 = bf16[4,16,96,128]{3,2,1,0:T(8,128)(2,1)S(1)} fusion(f32[4,16,1,128]{3,2,1,0:T(1,128)S(1)} %broadcast_in_dim.160, f32[4,16,95,128]{3,2,1,0:T(8,128)S(1)} %get-tuple-element.33, f32[4,16,95,128]{3,2,1,0:T(8,128)S(1)} %get-tuple-element.32, f32[4,16,1,128]{3,2,1,0:T(1,128)S(1)} %broadcast_in_dim.159, f32[4,1,96,128]{3,2,1,0:T(8,128)S(1)} %broadcast_in_dim.158, ...), kind=kLoop, calls=%fused_computation.45 | loop fusion | flops 17301504 | bytes 16687108 | tf_op jit(solution)/shard_map/convert_element_type | solution.py:83
  62.1 3.3 %collective-permute-start.6 = (bf16[1,16,96,128]{3,2,1,0:T(8,128)(2,1)S(1)}, bf16[1,16,96,128]{3,2,1,0:T(8,128)(2,1)S(1)}, u32[]{:S(2)}, u32[]{:S(2)}) collective-permute-start(bf16[1,16,96,128]{3,2,1,0:T(8,128)(2,1)S(1)} %get-tuple-element.22), channel_id=1, source_target_pairs={{0,1},{1,2},{2,3},{4,5},{5,6},{6,7},{8,9},{9,10},{10,11},{12,13},{... | collective-permute-start | bytes 1179656 | tf_op jit(solution)/shard_map/ppermute | solution.py:22
  67.5 4.2 %collective-permute-done.6 = bf16[1,16,96,128]{3,2,1,0:T(8,128)(2,1)S(1)} collective-permute-done((bf16[1,16,96,128]{3,2,1,0:T(8,128)(2,1)S(1)}, bf16[1,16,96,128]{3,2,1,0:T(8,128)(2,1)S(1)}, u32[]{:S(2)}, u32[]{:S(2)}) %collective-permute-start.6) | collective-permute-done | bytes 393248 | tf_op jit(solution)/shard_map/ppermute | solution.py:22
  71.7 4.1 %collective-permute-done.7 = bf16[1,16,96,128]{3,2,1,0:T(8,128)(2,1)S(1)} collective-permute-done((bf16[1,16,96,128]{3,2,1,0:T(8,128)(2,1)S(1)}, bf16[1,16,96,128]{3,2,1,0:T(8,128)(2,1)S(1)}, u32[]{:S(2)}, u32[]{:S(2)}) %collective-permute-start.7) | collective-permute-done | bytes 393248 | tf_op jit(solution)/shard_map/ppermute | solution.py:24
  75.9 6.8 %fusion.30 = bf16[4,16,96,128]{3,2,1,0:T(8,128)(2,1)S(1)} fusion(f32[4,16,1,128]{3,2,1,0:T(1,128)S(1)} %broadcast_in_dim.160, f32[4,16,95,128]{3,2,1,0:T(8,128)S(1)} %get-tuple-element.27, f32[4,16,95,128]{3,2,1,0:T(8,128)S(1)} %get-tuple-element.26, f32[4,16,1,128]{3,2,1,0:T(1,128)S(1)} %broadcast_in_dim.159, f32[4,1,96,128]{3,2,1,0:T(8,128)S(1)} %broadcast_in_dim.158, ...), kind=kLoop, calls=%fused_computation.44 | loop fusion | flops 17301504 | bytes 16687108 | tf_op jit(solution)/shard_map/convert_element_type | solution.py:83
  85.4 3.4 %collective-permute-start.8 = (bf16[1,16,96,128]{3,2,1,0:T(8,128)(2,1)S(1)}, bf16[1,16,96,128]{3,2,1,0:T(8,128)(2,1)S(1)}, u32[]{:S(2)}, u32[]{:S(2)}) collective-permute-start(bf16[1,16,96,128]{3,2,1,0:T(8,128)(2,1)S(1)} %get-tuple-element.16), channel_id=1, source_target_pairs={{0,1},{1,2},{2,3},{4,5},{5,6},{6,7},{8,9},{9,10},{10,11},{12,13},{... | collective-permute-start | bytes 1179656 | tf_op jit(solution)/shard_map/ppermute | solution.py:22
  91.0 3.0 %collective-permute-done.8 = bf16[1,16,96,128]{3,2,1,0:T(8,128)(2,1)S(1)} collective-permute-done((bf16[1,16,96,128]{3,2,1,0:T(8,128)(2,1)S(1)}, bf16[1,16,96,128]{3,2,1,0:T(8,128)(2,1)S(1)}, u32[]{:S(2)}, u32[]{:S(2)}) %collective-permute-start.8) | collective-permute-done | bytes 393248 | tf_op jit(solution)/shard_map/ppermute | solution.py:22
  94.0 4.4 %collective-permute-done.9 = bf16[1,16,96,128]{3,2,1,0:T(8,128)(2,1)S(1)} collective-permute-done((bf16[1,16,96,128]{3,2,1,0:T(8,128)(2,1)S(1)}, bf16[1,16,96,128]{3,2,1,0:T(8,128)(2,1)S(1)}, u32[]{:S(2)}, u32[]{:S(2)}) %collective-permute-start.9) | collective-permute-done | bytes 393248 | tf_op jit(solution)/shard_map/ppermute | solution.py:24
  98.4 7.0 %fusion.46 = f32[1,128,128]{2,1,0:T(8,128)S(1)} fusion(bf16[4,16,96,128]{3,2,1,0:T(8,128)(2,1)S(1)} %fusion.30, f32[4,16,95,128]{3,2,1,0:T(8,128)S(1)} %get-tuple-element.21, f32[4,16,95,128]{3,2,1,0:T(8,128)S(1)} %get-tuple-element.20, f32[4,15,96,128]{3,2,1,0:T(8,128)S(1)} %get-tuple-element.19, f32[4,15,96,128]{3,2,1,0:T(8,128)S(1)} %get-tuple-element.18, ...), kind=kOutput, calls=%fused_computation.68 | convolution fusion | flops 216268800 | bytes 14721024 | tf_op jit(solution)/shard_map/dot_general | solution.py:110
  107.5 4.1 %collective-permute-done.12.refs_3_ = f32[2,128,128]{2,1,0:T(8,128)S(1)} collective-permute-done((f32[2,128,128]{2,1,0:T(8,128)S(1)}, f32[2,128,128]{2,1,0:T(8,128)S(1)}, u32[]{:S(2)}, u32[]{:S(2)}) %collective-permute-start.12) | collective-permute-done | bytes 131104 | tf_op jit(solution)/shard_map/ppermute | solution.py:238
  111.6 2.9 %collective-permute-done.11.refs_2_ = f32[2,128,128]{2,1,0:T(8,128)S(1)} collective-permute-done((f32[2,128,128]{2,1,0:T(8,128)S(1)}, f32[2,128,128]{2,1,0:T(8,128)S(1)}, u32[]{:S(2)}, u32[]{:S(2)}) %collective-permute-start.11) | collective-permute-done | bytes 131104 | tf_op jit(solution)/shard_map/ppermute | solution.py:238
  114.5 11.4 %shard_map.73 = bf16[8,32,768]{2,1,0:T(8,128)(2,1)} custom-call(f32[2,128,128]{2,1,0:T(8,128)S(1)} %pad_maximum_fusion.21.refs_0_, f32[2,128,128]{2,1,0:T(8,128)S(1)} %collective-permute-done.10.refs_1_, f32[2,128,128]{2,1,0:T(8,128)S(1)} %collective-permute-done.11.refs_2_, f32[2,128,128]{2,1,0:T(8,128)S(1)} %collective-permute-done.12.refs_3_, ...), custom_call_target="tpu_custom_call" | custom-call | tf_op jit(solution)/shard_map/pallas_call | solution.py:247
  126.0 3.7 %all-to-all-start = ((bf16[8,32,768]{2,1,0:T(8,128)(2,1)}), bf16[8,32,768]{2,1,0:T(8,128)(2,1)S(1)}, u32[]{:S(2)}, u32[]{:S(2)}) async-start(bf16[8,32,768]{2,1,0:T(8,128)(2,1)} %shard_map.73), calls=%async_computation | async-start | bytes 786432 | tf_op jit(solution)/shard_map/all_to_all | solution.py:252
  129.9 8.1 %all-to-all-done = bf16[8,32,768]{2,1,0:T(8,128)(2,1)S(1)} async-done(((bf16[8,32,768]{2,1,0:T(8,128)(2,1)}), bf16[8,32,768]{2,1,0:T(8,128)(2,1)S(1)}, u32[]{:S(2)}, u32[]{:S(2)}) %all-to-all-start) | async-done | bytes 393248 | tf_op jit(solution)/shard_map/all_to_all | solution.py:252
  (47 shorter events, 21.9 us)
Async XLA Ops:
  1.3 24.4 %collective-permute-start = (s32[1,16,96]{2,1,0:T(8,128)}, s32[1,16,96]{2,1,0:T(8,128)S(1)}, u32[]{:S(2)}, u32[]{:S(2)}) collective-permute-start(s32[1,16,96]{2,1,0:T(8,128)} %get-tuple-element.42), channel_id=1, source_target_pairs={{0,1},{1,2},{2,3},{4,5},{5,6},{6,7},{8,9},{9,10},{10,11},{12,13},{... | collective-permute-start | bytes 18440 | tf_op jit(solution)/shard_map/ppermute | solution.py:22
  6.2 19.4 %collective-permute-start.1 = (s32[1,16,96]{2,1,0:T(8,128)}, s32[1,16,96]{2,1,0:T(8,128)S(1)}, u32[]{:S(2)}, u32[]{:S(2)}) collective-permute-start(s32[1,16,96]{2,1,0:T(8,128)} %get-tuple-element.43), channel_id=1, source_target_pairs={{1,0},{2,1},{3,2},{5,4},{6,5},{7,6},{9,8},{10,9},{11,10},{13,12},{... | collective-permute-start | bytes 18440 | tf_op jit(solution)/shard_map/ppermute | solution.py:24
  9.5 17.4 %collective-permute-start.2 = (bf16[1,16,96,128]{3,2,1,0:T(8,128)(2,1)}, bf16[1,16,96,128]{3,2,1,0:T(8,128)(2,1)}, u32[]{:S(2)}, u32[]{:S(2)}) collective-permute-start(bf16[1,16,96,128]{3,2,1,0:T(8,128)(2,1)} %get-tuple-element.34), channel_id=1, source_target_pairs={{0,1},{1,2},{2,3},{4,5},{5,6},{6,7},{8,9},{9,10},{10,11},{12,13},{... | collective-permute-start | bytes 1179656 | tf_op jit(solution)/shard_map/ppermute | solution.py:22
  14.7 12.1 %collective-permute-start.3 = (bf16[1,16,96,128]{3,2,1,0:T(8,128)(2,1)S(1)}, bf16[1,16,96,128]{3,2,1,0:T(8,128)(2,1)}, u32[]{:S(2)}, u32[]{:S(2)}) collective-permute-start(bf16[1,16,96,128]{3,2,1,0:T(8,128)(2,1)S(1)} %get-tuple-element.35), channel_id=1, source_target_pairs={{1,0},{2,1},{3,2},{5,4},{6,5},{7,6},{9,8},{10,9},{11,10},{13,12},{... | collective-permute-start | bytes 1179656 | tf_op jit(solution)/shard_map/ppermute | solution.py:24
  38.1 11.8 %collective-permute-start.4 = (bf16[1,16,96,128]{3,2,1,0:T(8,128)(2,1)S(1)}, bf16[1,16,96,128]{3,2,1,0:T(8,128)(2,1)S(1)}, u32[]{:S(2)}, u32[]{:S(2)}) collective-permute-start(bf16[1,16,96,128]{3,2,1,0:T(8,128)(2,1)S(1)} %get-tuple-element.28), channel_id=1, source_target_pairs={{0,1},{1,2},{2,3},{4,5},{5,6},{6,7},{8,9},{9,10},{10,11},{12,13},{... | collective-permute-start | bytes 1179656 | tf_op jit(solution)/shard_map/ppermute | solution.py:22
  42.7 11.3 %collective-permute-start.5 = (bf16[1,16,96,128]{3,2,1,0:T(8,128)(2,1)S(1)}, bf16[1,16,96,128]{3,2,1,0:T(8,128)(2,1)S(1)}, u32[]{:S(2)}, u32[]{:S(2)}) collective-permute-start(bf16[1,16,96,128]{3,2,1,0:T(8,128)(2,1)S(1)} %get-tuple-element.29), channel_id=1, source_target_pairs={{1,0},{2,1},{3,2},{5,4},{6,5},{7,6},{9,8},{10,9},{11,10},{13,12},{... | collective-permute-start | bytes 1179656 | tf_op jit(solution)/shard_map/ppermute | solution.py:24
  62.1 9.6 %collective-permute-start.6 = (bf16[1,16,96,128]{3,2,1,0:T(8,128)(2,1)S(1)}, bf16[1,16,96,128]{3,2,1,0:T(8,128)(2,1)S(1)}, u32[]{:S(2)}, u32[]{:S(2)}) collective-permute-start(bf16[1,16,96,128]{3,2,1,0:T(8,128)(2,1)S(1)} %get-tuple-element.22), channel_id=1, source_target_pairs={{0,1},{1,2},{2,3},{4,5},{5,6},{6,7},{8,9},{9,10},{10,11},{12,13},{... | collective-permute-start | bytes 1179656 | tf_op jit(solution)/shard_map/ppermute | solution.py:22
  65.4 10.4 %collective-permute-start.7 = (bf16[1,16,96,128]{3,2,1,0:T(8,128)(2,1)S(1)}, bf16[1,16,96,128]{3,2,1,0:T(8,128)(2,1)S(1)}, u32[]{:S(2)}, u32[]{:S(2)}) collective-permute-start(bf16[1,16,96,128]{3,2,1,0:T(8,128)(2,1)S(1)} %get-tuple-element.23), channel_id=1, source_target_pairs={{1,0},{2,1},{3,2},{5,4},{6,5},{7,6},{9,8},{10,9},{11,10},{13,12},{... | collective-permute-start | bytes 1179656 | tf_op jit(solution)/shard_map/ppermute | solution.py:24
  85.4 8.6 %collective-permute-start.8 = (bf16[1,16,96,128]{3,2,1,0:T(8,128)(2,1)S(1)}, bf16[1,16,96,128]{3,2,1,0:T(8,128)(2,1)S(1)}, u32[]{:S(2)}, u32[]{:S(2)}) collective-permute-start(bf16[1,16,96,128]{3,2,1,0:T(8,128)(2,1)S(1)} %get-tuple-element.16), channel_id=1, source_target_pairs={{0,1},{1,2},{2,3},{4,5},{5,6},{6,7},{8,9},{9,10},{10,11},{12,13},{... | collective-permute-start | bytes 1179656 | tf_op jit(solution)/shard_map/ppermute | solution.py:22
  88.8 9.7 %collective-permute-start.9 = (bf16[1,16,96,128]{3,2,1,0:T(8,128)(2,1)S(1)}, bf16[1,16,96,128]{3,2,1,0:T(8,128)(2,1)S(1)}, u32[]{:S(2)}, u32[]{:S(2)}) collective-permute-start(bf16[1,16,96,128]{3,2,1,0:T(8,128)(2,1)S(1)} %get-tuple-element.17), channel_id=1, source_target_pairs={{1,0},{2,1},{3,2},{5,4},{6,5},{7,6},{9,8},{10,9},{11,10},{13,12},{... | collective-permute-start | bytes 1179656 | tf_op jit(solution)/shard_map/ppermute | solution.py:24
  98.4 16.1 %copy-start = (f32[1,128,32]{1,2,0:T(8,128)S(1)}, f32[1,128,32]{1,2,0:T(8,128)}, u32[]{:S(2)}) copy-start(f32[1,128,32]{1,2,0:T(8,128)} %param.12) | copy-start | bytes 49156
  105.4 24.3 %copy-start.1 = (s32[8,8]{1,0:T(8,128)S(1)}, s32[8,8]{1,0:T(8,128)}, u32[]{:S(2)}) copy-start(s32[8,8]{1,0:T(8,128)} %param.13) | copy-start | bytes 772
  105.4 6.2 %collective-permute-start.12 = (f32[2,128,128]{2,1,0:T(8,128)S(1)}, f32[2,128,128]{2,1,0:T(8,128)S(1)}, u32[]{:S(2)}, u32[]{:S(2)}) collective-permute-start(f32[2,128,128]{2,1,0:T(8,128)S(1)} %pad_maximum_fusion.21.refs_0_), channel_id=1, source_target_pairs={{0,3},{1,0},{2,1},{3,2},{4,7},{5,4},{6,5},{7,6},{8,11},{9,8},{10,9... | collective-permute-start | bytes 393224 | tf_op jit(solution)/shard_map/ppermute | solution.py:238
  105.5 9.0 %collective-permute-start.11 = (f32[2,128,128]{2,1,0:T(8,128)S(1)}, f32[2,128,128]{2,1,0:T(8,128)S(1)}, u32[]{:S(2)}, u32[]{:S(2)}) collective-permute-start(f32[2,128,128]{2,1,0:T(8,128)S(1)} %pad_maximum_fusion.21.refs_0_), channel_id=1, source_target_pairs={{0,2},{1,3},{2,0},{3,1},{4,6},{5,7},{6,4},{7,5},{8,10},{9,11},{10,... | collective-permute-start | bytes 393224 | tf_op jit(solution)/shard_map/ppermute | solution.py:238
  107.2 7.3 %collective-permute-start.10 = (f32[2,128,128]{2,1,0:T(8,128)S(1)}, f32[2,128,128]{2,1,0:T(8,128)S(1)}, u32[]{:S(2)}, u32[]{:S(2)}) collective-permute-start(f32[2,128,128]{2,1,0:T(8,128)S(1)} %pad_maximum_fusion.21.refs_0_), channel_id=1, source_target_pairs={{0,1},{1,2},{2,3},{3,0},{4,5},{5,6},{6,7},{7,4},{8,9},{9,10},{10,1... | collective-permute-start | bytes 393224 | tf_op jit(solution)/shard_map/ppermute | solution.py:238
  126.0 12.1 %all-to-all-start = ((bf16[8,32,768]{2,1,0:T(8,128)(2,1)}), bf16[8,32,768]{2,1,0:T(8,128)(2,1)S(1)}, u32[]{:S(2)}, u32[]{:S(2)}) async-start(bf16[8,32,768]{2,1,0:T(8,128)(2,1)} %shard_map.73), calls=%async_computation | async-start | bytes 786432 | tf_op jit(solution)/shard_map/all_to_all | solution.py:252

commit v2 on v1

v2 whole, which is shorter than its diff:
```python
import functools

import jax
import jax.numpy as jnp
from jax import lax
from jax.experimental import pallas as pl
from jax.experimental.pallas import tpu as pltpu
from jax.sharding import PartitionSpec as P

SWEEPS = 3
ITERS = 4


def harmonic(left_k, right_k):
    return 2.0 * left_k * right_k / (left_k + right_k)


def coefficients(classes, planes, first, last):
    kappa = jnp.exp2(2.0 * classes.astype(jnp.float32))
    length = classes.shape[0]
    depth = (length - planes) // 2
    place = jnp.arange(length, dtype=jnp.int32)[:, None, None]
    outside = (first & (place < depth)) | (last & (place >= depth + planes))
    x_face = harmonic(kappa[1:], kappa[:-1])
    x_face = jnp.where(outside[:-1], kappa[1:], jnp.where(outside[1:], kappa[:-1], x_face))
    centre = kappa[1:-1]
    y_face = harmonic(centre[:, 1:], centre[:, :-1])
    y_face = jnp.concatenate([centre[:, :1], y_face, centre[:, -1:]], axis=1)
    z_face = harmonic(centre[:, :, 1:], centre[:, :, :-1])
    z_face = jnp.concatenate([centre[:, :, :1], z_face, centre[:, :, -1:]], axis=2)
    denom = (
        x_face[:-1]
        + x_face[1:]
        + y_face[:, :-1]
        + y_face[:, 1:]
        + z_face[:, :, :-1]
        + z_face[:, :, 1:]
    )
    scale = jnp.where(outside[1:-1], 0.0, 1.0 / denom)
    z_face = jnp.pad(z_face, ((0, 0), (0, 0), (0, 7)))
    mass = kappa[depth : depth + planes] * (1.0 / 16.0)
    return [jnp.swapaxes(item, 1, 2) for item in (x_face, y_face, z_face, scale, mass)]


def relax_kernel(
    own,
    low,
    high,
    x_col,
    y_col,
    z_col,
    scale_col,
    mass_col,
    y_vals,
    z_vals,
    face_ids,
    snap,
    gram,
    state,
    x_face,
    y_face,
    z_face,
    scale,
    ghost,
    both,
):
    planes, rows_y, rows_z, width = own.shape
    length = state.shape[0]
    inner = pl.ds(8, rows_z)

    def fill(src, base):
        def body(p, carry):
            for y in range(rows_y):
                state[base + p, y, inner] = src[p, y].astype(jnp.float32)
            return carry

        lax.fori_loop(0, planes, body, 0)

    fill(low, 0)
    fill(own, planes)
    fill(high, 2 * planes)
    ids = face_ids[...]
    picks = [(ids == side).astype(jnp.float32) for side in range(4)]
    ghost[0] = y_vals[...].astype(jnp.float32) * picks[0]
    ghost[1] = y_vals[...].astype(jnp.float32) * picks[1]
    z_low = z_vals[...].astype(jnp.float32) * picks[2]
    z_high = z_vals[...].astype(jnp.float32) * picks[3]

    def edges(p, carry):
        for y in range(rows_y):
            state[p, y, pl.ds(7, 1)] = z_low[y : y + 1]
            state[p, y, pl.ds(8 + rows_z, 1)] = z_high[y : y + 1]
        return carry

    lax.fori_loop(0, length, edges, 0)

    def spread(dst, src):
        def body(p, carry):
            columns = src[p]
            for y in range(dst.shape[1]):
                dst[p, y] = jnp.broadcast_to(columns[:, y : y + 1], (columns.shape[0], width))
            return carry

        lax.fori_loop(0, dst.shape[0], body, 0)

    spread(x_face, x_col)
    spread(y_face, y_col)
    spread(z_face, z_col)
    spread(scale, scale_col)

    for sweep in range(1, SWEEPS + 1):

        def body(e, carry, sweep=sweep):
            slot = e - sweep + 1
            for y in range(rows_y):
                below = ghost[0] if y == 0 else state[slot, y - 1, inner]
                above = ghost[1] if y == rows_y - 1 else state[slot, y + 1, inner]
                numer = (
                    x_face[e - 1, y] * state[slot - 1, y, inner]
                    + x_face[e, y] * state[slot + 1, y, inner]
                    + y_face[e - 1, y] * below
                    + y_face[e - 1, y + 1] * above
                    + z_face[e - 1, y, pl.ds(0, rows_z)] * state[slot, y, pl.ds(7, rows_z)]
                    + z_face[e - 1, y, pl.ds(1, rows_z)] * state[slot, y, pl.ds(9, rows_z)]
                )
                fresh = (numer * scale[e - 1, y]).astype(jnp.bfloat16)
                state[slot - 1, y, inner] = fresh.astype(jnp.float32)
            return carry

        lax.fori_loop(sweep, length - sweep, body, 0)

    for p in range(planes):
        e = planes + p
        slot = e - SWEEPS
        mass = mass_col[p]
        for y in range(rows_y):
            state[slot, y, pl.ds(7, 1)] = jnp.zeros((1, width), jnp.float32)
            state[slot, y, pl.ds(8 + rows_z, 1)] = jnp.zeros((1, width), jnp.float32)
        for y in range(rows_y):
            rows = pl.ds(y * rows_z, rows_z)
            middle = state[slot, y, inner]
            faces = [
                x_face[e - 1, y],
                x_face[e, y],
                y_face[e - 1, y],
                y_face[e - 1, y + 1],
                z_face[e - 1, y, pl.ds(0, rows_z)],
                z_face[e - 1, y, pl.ds(1, rows_z)],
            ]
            numer = faces[0] * state[slot - 1, y, inner] + faces[1] * state[slot + 1, y, inner]
            if y > 0:
                numer = numer + faces[2] * state[slot, y - 1, inner]
            if y < rows_y - 1:
                numer = numer + faces[3] * state[slot, y + 1, inner]
            numer = (
                numer
                + faces[4] * state[slot, y, pl.ds(7, rows_z)]
                + faces[5] * state[slot, y, pl.ds(9, rows_z)]
            )
            denom = faces[0] + faces[1] + faces[2] + faces[3] + faces[4] + faces[5]
            snap[p, rows] = middle.astype(jnp.bfloat16)
            both[rows, pl.ds(0, width)] = (
                middle * jnp.broadcast_to(mass[:, y : y + 1], (rows_z, width))
            ).astype(jnp.bfloat16)
            both[rows, pl.ds(width, width)] = (denom * middle - numer).astype(jnp.bfloat16)
        part = lax.dot_general(
            snap[p], both[...], (((0,), (0,)), ((), ())), preferred_element_type=jnp.float32
        )
        for item in range(2):
            piece = part[:, item * width : (item + 1) * width]
            gram[item] = piece if p == 0 else gram[item] + piece


def shift_planes(array, up):
    count = lax.axis_size("sub")
    pairs = [(i, i + 1) for i in range(count - 1)]
    if not up:
        pairs = [(j, i) for i, j in pairs]
    return lax.ppermute(array, "sub", pairs)


def relax(initial, classes, y_vals, z_vals, face_ids):
    planes, rows_y, rows_z, width = initial.shape
    index = lax.axis_index("sub")
    subs = lax.axis_size("sub")
    packed = classes.astype(jnp.bfloat16)
    class_low = shift_planes(packed, True)
    class_high = shift_planes(packed, False)
    low = shift_planes(initial, True)
    high = shift_planes(initial, False)
    extended = jnp.concatenate([class_low, packed, class_high], axis=0)
    columns = coefficients(extended, planes, index == 0, index == subs - 1)
    length = 3 * planes
    scratch = [
        (length, rows_y, rows_z + 16),
        (length - 1, rows_y, rows_z),
        (length - 2, rows_y + 1, rows_z),
        (length - 2, rows_y, rows_z + 8),
        (length - 2, rows_y, rows_z),
        (2, rows_z),
    ]
    return pl.pallas_call(
        relax_kernel,
        out_shape=[
            jax.ShapeDtypeStruct((planes, rows_y * rows_z, width), jnp.bfloat16),
            jax.ShapeDtypeStruct((2, width, width), jnp.float32),
        ],
        scratch_shapes=[pltpu.VMEM(shape + (width,), jnp.float32) for shape in scratch]
        + [pltpu.VMEM((rows_y * rows_z, 2 * width), jnp.bfloat16)],
        compiler_params=pltpu.CompilerParams(vmem_limit_bytes=60 * 2**20),
    )(initial, low, high, *columns, y_vals, z_vals, face_ids[None])


def lane_copy(tile, lane):
    return jnp.broadcast_to(tile[:, lane : lane + 1], (8, 128))


def row_copy(tile, row):
    return jnp.broadcast_to(tile[row : row + 1, :], (8, tile.shape[1]))


def solve_spd(left, right):
    size = left.shape[0]
    count = size // 8
    sub = lax.broadcasted_iota(jnp.int32, (8, 128), 0)
    lhs = [left[8 * t : 8 * t + 8] for t in range(count)]
    rhs = [right[8 * t : 8 * t + 8] for t in range(count)]
    for k in range(count):
        cols = [lane_copy(lhs[k], 8 * k + j) for j in range(8)]
        panel_l, panel_r = lhs[k], rhs[k]
        for j in range(8):
            recip = 1.0 / row_copy(cols[j], j)
            here = sub == j
            mult = jnp.where(here, recip, -cols[j] * recip)
            for l in range(j + 1, 8):
                cols[l] = jnp.where(here, 0.0, cols[l]) + mult * row_copy(cols[l], j)
            panel_l = jnp.where(here, 0.0, panel_l) + mult * row_copy(panel_l, j)
            panel_r = jnp.where(here, 0.0, panel_r) + mult * row_copy(panel_r, j)
        rows_l = [row_copy(panel_l, j) for j in range(8)]
        rows_r = [row_copy(panel_r, j) for j in range(8)]
        order = list(range(k + 1, count)) + list(range(k))
        for t in order:
            tile_cols = [lane_copy(lhs[t], 8 * k + j) for j in range(8)]
            if k + 1 < count:
                lhs[t] = lhs[t] - tree([tile_cols[j] * rows_l[j] for j in range(8)])
            rhs[t] = rhs[t] - tree([tile_cols[j] * rows_r[j] for j in range(8)])
        lhs[k], rhs[k] = panel_l, panel_r
    return jnp.concatenate(rhs, axis=0)


def tree(terms):
    while len(terms) > 1:
        terms = [a + b for a, b in zip(terms[::2], terms[1::2])] + terms[len(terms) & ~1 :]
    return terms[0]


def whiten(inner, block):
    size = inner.shape[0]
    count = size // 8
    sub = lax.broadcasted_iota(jnp.int32, (8, 128), 0)
    lhs = [inner[8 * t : 8 * t + 8] for t in range(count)]
    rhs = [block[8 * t : 8 * t + 8] for t in range(count)]
    done = []
    for k in range(count):
        live = range(k, count)
        cols = {t: [lane_copy(lhs[t], 8 * k + j) for j in range(8)] for t in live}
        scale = None
        for j in range(8):
            pivot = row_copy(cols[k][j], j)
            recip = 1.0 / pivot
            root = lax.rsqrt(pivot)
            scale = root if scale is None else jnp.where(sub >= j, root, scale)
            head = {l: row_copy(cols[k][l], j) for l in range(j + 1, 8)}
            row_l, row_r = row_copy(lhs[k], j), row_copy(rhs[k], j)
            for t in live:
                mult = cols[t][j] * recip
                if t == k:
                    mult = jnp.where(sub > j, mult, 0.0)
                for l in range(j + 1, 8):
                    cols[t][l] = cols[t][l] - mult * head[l]
                lhs[t] = lhs[t] - mult[:, : row_l.shape[1]] * row_l
                rhs[t] = rhs[t] - mult * row_r
        done.append(rhs[k] * scale)
    return jnp.concatenate(done, axis=0)


def dot(a, b, dims):
    return lax.dot_general(
        a, b, (dims, ((), ())), precision=lax.Precision.HIGHEST, preferred_element_type=jnp.float32
    )


def modes_kernel(cell_count, *refs):
    *part_refs, start_ref, snap_ref, out_ref = refs
    mass = part_refs[0][0]
    stiff = part_refs[0][1]
    for part in part_refs[1:]:
        mass = mass + part[0]
        stiff = stiff + part[1]
    mass = mass * (1.0 / cell_count)
    stiff = (stiff + stiff.T) * (0.5 / cell_count)
    step = solve_spd(stiff, mass)
    form = dot(step, dot(mass, step, ((1,), (0,))), ((0,), (0,)))
    block = start_ref[...]
    for _ in range(ITERS):
        weighted = dot(block, form, ((1,), (0,)))
        solved = dot(block, step, ((1,), (1,)))
        inner = dot(weighted, block, ((1,), (1,)))
        block = whiten(inner, solved)
    modes = block.astype(jnp.bfloat16)
    for piece in range(out_ref.shape[0]):
        out_ref[piece] = lax.dot_general(
            modes, snap_ref[piece], (((1,), (1,)), ((), ())), preferred_element_type=jnp.float32
        ).astype(jnp.bfloat16)


def on_device(snap_init, channel_map, yface_vals, zface_vals, face_of, start_block, correlation):
    subs = lax.axis_size("sub")
    snapshots, own = relax(
        snap_init[0], channel_map[0], yface_vals[0], zface_vals[0], face_of[0]
    )
    parts = [own] + [
        lax.ppermute(own, "sub", [(i, (i + shift) % subs) for i in range(subs)])
        for shift in range(1, subs)
    ]
    cell_count = float(subs * snapshots.shape[0] * snapshots.shape[1])
    owner_count = lax.axis_size("nbhd")
    width = snapshots.shape[-1]
    piece_cells = snapshots.size // width // owner_count
    blocks = snapshots.reshape(owner_count, piece_cells, width)
    modes = start_block.shape[-1]
    pieces = pl.pallas_call(
        functools.partial(modes_kernel, cell_count),
        out_shape=jax.ShapeDtypeStruct((owner_count, modes, piece_cells), jnp.bfloat16),
        compiler_params=pltpu.CompilerParams(vmem_limit_bytes=32 * 2**20),
    )(*parts, start_block[0].T, blocks)
    received = lax.all_to_all(pieces, "nbhd", split_axis=0, concat_axis=0, tiled=True)
    column = lax.dynamic_slice_in_dim(correlation, lax.axis_index("nbhd"), 1, axis=1)[:, 0]
    result = received * column.astype(jnp.bfloat16)[:, None, None]
    return result[None, None]


def solution(mesh):
    return jax.shard_map(
        on_device,
        mesh=mesh,
        in_specs=(
            P("nbhd", "sub", None, None, None),
            P("nbhd", "sub", None, None),
            P("nbhd", None, None),
            P("nbhd", None, None),
            P("nbhd", None),
            P("nbhd", None, None),
            P(),
        ),
        out_specs=P("nbhd", "sub", None, None, None),
        check_vma=False,
    )
```

time: 140 us -> 122 us (0.87)
  Pallas kernels: 11.4 us -> 44.3 us
  other arithmetic: 29.4 us -> 7.31 us
  local copies, waits for them, and re-layouts: 15.1 us -> 2.98 us
  starting transfers between devices: 33.9 us -> 23.3 us
  matrix products: 8.41 us -> 0 us
  waiting for transfers between devices: 40.3 us -> 43.7 us
    pallas_call x0 -> x1, Pallas kernels: none -> 32.9 us  [relax(): pl.pallas_call(relax_kernel, out_shape=[jax.ShapeDtypeStruct((planes, row...]
    convert_element_type x4 -> x1, other arithmetic: 25.3 us -> 0.76 us  [relax(): packed = classes.astype(jnp.bfloat16)]
    slice x16 -> x2, local copies, waits for them, and re-layouts: 15 us -> 0.21 us  [the longest x1 0.2 us: coefficients(): y_face = jnp.concatenate([centre[:, :1], y_face, centre[:, -1:]], axis=1)]
    ppermute x10 -> x4, starting transfers between devices: 28.1 us -> 13.9 us  [shift_planes(): return lax.ppermute(array, 'sub', pairs)]
    dot_general x2 -> x0, matrix products: 8.41 us -> none  [the longest x1 6.95 us: gram_terms(): lax.dot_general(flat, stiff_flat, dims, preferred_element_type=jnp.float32)]
    transpose x0 -> x5, other arithmetic: none -> 4.96 us  [coefficients(): jnp.swapaxes(item, 1, 2)]
    ppermute x3, starting transfers between devices: 2.07 us -> 5.68 us  [on_device(): lax.ppermute(own, 'sub', [(i, (i + shift) % subs) for i in range(subs)])]
    ppermute x3, waiting for transfers between devices: 7 us -> 9.52 us  [on_device(): lax.ppermute(own, 'sub', [(i, (i + shift) % subs) for i in range(subs)])]
  transfers between devices with their start and end apart: 14 -> 8, of which waited for: 9 -> 5; matrix products, arithmetic and copies ran while one was open for 11% -> 5% of each run, Pallas kernels for 0% -> 0%
where the time goes in v2:
time: 122 us
  Pallas kernels  44.3 us (36%)
  waiting for transfers between devices  43.7 us (36%)
  starting transfers between devices  23.3 us (19%)
  other arithmetic  7.31 us (6%)
  local copies, waits for them, and re-layouts  2.98 us (2%)
    pallas_call x1, Pallas kernels, relax(): pl.pallas_call(relax_kernel, out_shape=[jax.ShapeDtypeStruct((planes, row...  32.9 us
    ppermute x4, waiting for transfers between devices, shift_planes(): return lax.ppermute(array, 'sub', pairs)  26 us
    ppermute x4, starting transfers between devices, shift_planes(): return lax.ppermute(array, 'sub', pairs)  13.9 us
    pallas_call x1, Pallas kernels, on_device(): pl.pallas_call(functools.partial(modes_kernel, cell_count), out_shape=jax...  11.4 us
    ppermute x3, waiting for transfers between devices, on_device(): lax.ppermute(own, 'sub', [(i, (i + shift) % subs) for i in range(subs)])  9.52 us
    all_to_all x1, waiting for transfers between devices, on_device(): lax.all_to_all(pieces, 'nbhd', split_axis=0, concat_axis=0, tiled=True)  8.15 us
    ppermute x3, starting transfers between devices, on_device(): lax.ppermute(own, 'sub', [(i, (i + shift) % subs) for i in range(subs)])  5.68 us
    transpose x5, other arithmetic, coefficients(): jnp.swapaxes(item, 1, 2)  4.96 us
  transfers between devices with their start and end apart: 8, of which 5 were waited for; matrix products, arithmetic and copies ran while one was open for 5% of the time, Pallas kernels for 0%

profile of v2, /device:TPU:0, one launch (start us, length us, event | category | flops | bytes accessed | tf_op | source)
XLA Modules:
  0.0 121.6 jit_solution(17524735730762207509)
XLA Ops:
  0.0 0.8 convert_bitcast_fusion
  0.8 1.3 %collective-permute-start.3 = (bf16[4,16,96]{2,1,0:T(8,128)(2,1)S(1)}, bf16[4,16,96]{2,1,0:T(8,128)(2,1)S(1)}, u32[]{:S(2)}, u32[]{:S(2)}) collective-permute-start(bf16[4,16,96]{2,1,0:T(8,128)(2,1)S(1)} %convert_bitcast_fusion), channel_id=1, source_target_pairs={{1,0},{2,1},{3,2},{5,4},{6,5},{7,6},{9,8},{10,9},{11,10},{13,12},{... | collective-permute-start | bytes 36872 | tf_op jit(solution)/shard_map/ppermute | solution.py:179
  2.1 5.6 %collective-permute-start.2 = (bf16[4,16,96]{2,1,0:T(8,128)(2,1)S(1)}, bf16[4,16,96]{2,1,0:T(8,128)(2,1)S(1)}, u32[]{:S(2)}, u32[]{:S(2)}) collective-permute-start(bf16[4,16,96]{2,1,0:T(8,128)(2,1)S(1)} %convert_bitcast_fusion), channel_id=1, source_target_pairs={{0,1},{1,2},{2,3},{4,5},{5,6},{6,7},{8,9},{9,10},{10,11},{12,13},{... | collective-permute-start | bytes 36872 | tf_op jit(solution)/shard_map/ppermute | solution.py:179
  7.6 1.3 %collective-permute-start.1 = (bf16[4,16,96,128]{3,2,1,0:T(8,128)(2,1)}, bf16[4,16,96,128]{3,2,1,0:T(8,128)(2,1)S(1)}, u32[]{:S(2)}, u32[]{:S(2)}) collective-permute-start(bf16[4,16,96,128]{3,2,1,0:T(8,128)(2,1)} %bitcast.29), channel_id=1, source_target_pairs={{1,0},{2,1},{3,2},{5,4},{6,5},{7,6},{9,8},{10,9},{11,10},{13,12},{... | collective-permute-start | bytes 4718600 | tf_op jit(solution)/shard_map/ppermute | solution.py:179
  8.9 5.7 %collective-permute-start = (bf16[4,16,96,128]{3,2,1,0:T(8,128)(2,1)}, bf16[4,16,96,128]{3,2,1,0:T(8,128)(2,1)}, u32[]{:S(2)}, u32[]{:S(2)}) collective-permute-start(bf16[4,16,96,128]{3,2,1,0:T(8,128)(2,1)} %bitcast.30), channel_id=1, source_target_pairs={{0,1},{1,2},{2,3},{4,5},{5,6},{6,7},{8,9},{9,10},{10,11},{12,13},{... | collective-permute-start | bytes 4718600 | tf_op jit(solution)/shard_map/ppermute | solution.py:179
  14.8 0.2 copy.33
  15.6 1.1 maximum_bitcast_fusion.y_col
  16.8 0.9 fusion.z_col
  17.7 0.7 fusion.8.mass_col
  18.6 1.2 %fusion.7.scale_col = f32[10,96,16]{2,1,0:T(8,128)} fusion(f32[10,16,1]{1,2,0:T(1,128)S(1)} %get-tuple-element.10, f32[10,16,95]{1,2,0:T(8,128)S(1)} %add_divide_fusion, f32[10,16,1]{1,2,0:T(1,128)S(1)} %get-tuple-element.9, f32[10,1,96]{1,2,0:T(8,128)S(1)} %get-tuple-element.12, f32[10,15,96]{1,2,0:T(8,128)S(1)} %add_divide_fusion.1, ...), kind=kLoop, calls=%fused_computation.15 | loop fusion | flops 168960 | bytes 311690 | tf_op jit(solution)/shard_map/transpose | solution.py:42
  19.9 1.0 fusion.12.x_col
  20.9 24.7 %collective-permute-done.1.high = bf16[4,16,96,128]{3,2,1,0:T(8,128)(2,1)S(1)} collective-permute-done((bf16[4,16,96,128]{3,2,1,0:T(8,128)(2,1)}, bf16[4,16,96,128]{3,2,1,0:T(8,128)(2,1)S(1)}, u32[]{:S(2)}, u32[]{:S(2)}) %collective-permute-start.1) | collective-permute-done | bytes 1572896 | tf_op jit(solution)/shard_map/ppermute | solution.py:179
  45.6 1.3 %collective-permute-done.low = bf16[4,16,96,128]{3,2,1,0:T(8,128)(2,1)} collective-permute-done((bf16[4,16,96,128]{3,2,1,0:T(8,128)(2,1)}, bf16[4,16,96,128]{3,2,1,0:T(8,128)(2,1)}, u32[]{:S(2)}, u32[]{:S(2)}) %collective-permute-start) | collective-permute-done | bytes 1572896 | tf_op jit(solution)/shard_map/ppermute | solution.py:179
  46.9 32.9 %shard_map.73 = (bf16[4,1536,128]{2,1,0:T(8,128)(2,1)}, f32[2,128,128]{2,1,0:T(8,128)}) custom-call(bf16[4,16,96,128]{3,2,1,0:T(8,128)(2,1)} %bitcast.31, bf16[4,16,96,128]{3,2,1,0:T(8,128)(2,1)} %collective-permute-done.low, bf16[4,16,96,128]{3,2,1,0:T(8,128)(2,1)} %copy-done.3, f32[11,96,16]{2,1,0:T(8,128)} %fusion.12.x_col, ...), custom_call_target="tpu_custom_call" | custom-call | tf_op jit(solution)/shard_map/pallas_call | solution.py:202
  79.7 4.8 %collective-permute-start.6 = (f32[2,128,128]{2,1,0:T(8,128)}, f32[2,128,128]{2,1,0:T(8,128)S(1)}, u32[]{:S(2)}, u32[]{:S(2)}) collective-permute-start(f32[2,128,128]{2,1,0:T(8,128)} %get-tuple-element.7.refs_0_), channel_id=1, source_target_pairs={{0,3},{1,0},{2,1},{3,2},{4,7},{5,4},{6,5},{7,6},{8,11},{9,8},{10,9... | collective-permute-start | bytes 393224 | tf_op jit(solution)/shard_map/ppermute | solution.py:323
  84.5 0.9 collective-permute-start.4
  85.4 3.2 %collective-permute-done.6.refs_3_ = f32[2,128,128]{2,1,0:T(8,128)S(1)} collective-permute-done((f32[2,128,128]{2,1,0:T(8,128)}, f32[2,128,128]{2,1,0:T(8,128)S(1)}, u32[]{:S(2)}, u32[]{:S(2)}) %collective-permute-start.6) | collective-permute-done | bytes 131104 | tf_op jit(solution)/shard_map/ppermute | solution.py:323
  88.7 6.3 %collective-permute-done.5.refs_2_ = f32[2,128,128]{2,1,0:T(8,128)S(1)} collective-permute-done((f32[2,128,128]{2,1,0:T(8,128)}, f32[2,128,128]{2,1,0:T(8,128)S(1)}, u32[]{:S(2)}, u32[]{:S(2)}) %collective-permute-start.5) | collective-permute-done | bytes 131104 | tf_op jit(solution)/shard_map/ppermute | solution.py:323
  94.9 1.4 %copy-done = bf16[4,1536,128]{2,1,0:T(8,128)(2,1)S(1)} copy-done((bf16[4,1536,128]{2,1,0:T(8,128)(2,1)S(1)}, bf16[4,1536,128]{2,1,0:T(8,128)(2,1)}, u32[]{:S(2)}) %copy-start) | copy-done | bytes 1572888
  96.4 0.9 copy-done.1
  97.3 11.4 %shard_map.74 = bf16[8,32,768]{2,1,0:T(8,128)(2,1)} custom-call(f32[2,128,128]{2,1,0:T(8,128)S(1)} %copy-done.1, f32[2,128,128]{2,1,0:T(8,128)S(1)} %collective-permute-done.4.refs_1_, f32[2,128,128]{2,1,0:T(8,128)S(1)} %collective-permute-done.5.refs_2_, f32[2,128,128]{2,1,0:T(8,128)S(1)} %collective-permute-done.6.refs_3_, f32[32,128]{1,0:T(8,128)S(1)} %bitcast.28, ...), custom_call_target="tpu_custom_call" | custom-call | tf_op jit(solution)/shard_map/pallas_call | solution.py:332
  108.7 3.7 %all-to-all-start = ((bf16[8,32,768]{2,1,0:T(8,128)(2,1)}), bf16[8,32,768]{2,1,0:T(8,128)(2,1)S(1)}, u32[]{:S(2)}, u32[]{:S(2)}) async-start(bf16[8,32,768]{2,1,0:T(8,128)(2,1)} %shard_map.74), calls=%async_computation | async-start | bytes 786432 | tf_op jit(solution)/shard_map/all_to_all | solution.py:337
  112.6 8.1 %all-to-all-done = bf16[8,32,768]{2,1,0:T(8,128)(2,1)S(1)} async-done(((bf16[8,32,768]{2,1,0:T(8,128)(2,1)}), bf16[8,32,768]{2,1,0:T(8,128)(2,1)S(1)}, u32[]{:S(2)}, u32[]{:S(2)}) %all-to-all-start) | async-done | bytes 393248 | tf_op jit(solution)/shard_map/all_to_all | solution.py:337
  120.8 0.8 multiply_bitcast_fusion
  (23 shorter events, 1.2 us)
Async XLA Ops:
  0.8 14.0 %collective-permute-start.3 = (bf16[4,16,96]{2,1,0:T(8,128)(2,1)S(1)}, bf16[4,16,96]{2,1,0:T(8,128)(2,1)S(1)}, u32[]{:S(2)}, u32[]{:S(2)}) collective-permute-start(bf16[4,16,96]{2,1,0:T(8,128)(2,1)S(1)} %convert_bitcast_fusion), channel_id=1, source_target_pairs={{1,0},{2,1},{3,2},{5,4},{6,5},{7,6},{9,8},{10,9},{11,10},{13,12},{... | collective-permute-start | bytes 36872 | tf_op jit(solution)/shard_map/ppermute | solution.py:179
  2.1 12.8 %collective-permute-start.2 = (bf16[4,16,96]{2,1,0:T(8,128)(2,1)S(1)}, bf16[4,16,96]{2,1,0:T(8,128)(2,1)S(1)}, u32[]{:S(2)}, u32[]{:S(2)}) collective-permute-start(bf16[4,16,96]{2,1,0:T(8,128)(2,1)S(1)} %convert_bitcast_fusion), channel_id=1, source_target_pairs={{0,1},{1,2},{2,3},{4,5},{5,6},{6,7},{8,9},{9,10},{10,11},{12,13},{... | collective-permute-start | bytes 36872 | tf_op jit(solution)/shard_map/ppermute | solution.py:179
  7.6 38.0 %collective-permute-start.1 = (bf16[4,16,96,128]{3,2,1,0:T(8,128)(2,1)}, bf16[4,16,96,128]{3,2,1,0:T(8,128)(2,1)S(1)}, u32[]{:S(2)}, u32[]{:S(2)}) collective-permute-start(bf16[4,16,96,128]{3,2,1,0:T(8,128)(2,1)} %bitcast.29), channel_id=1, source_target_pairs={{1,0},{2,1},{3,2},{5,4},{6,5},{7,6},{9,8},{10,9},{11,10},{13,12},{... | collective-permute-start | bytes 4718600 | tf_op jit(solution)/shard_map/ppermute | solution.py:179
  8.9 38.0 %collective-permute-start = (bf16[4,16,96,128]{3,2,1,0:T(8,128)(2,1)}, bf16[4,16,96,128]{3,2,1,0:T(8,128)(2,1)}, u32[]{:S(2)}, u32[]{:S(2)}) collective-permute-start(bf16[4,16,96,128]{3,2,1,0:T(8,128)(2,1)} %bitcast.30), channel_id=1, source_target_pairs={{0,1},{1,2},{2,3},{4,5},{5,6},{6,7},{8,9},{9,10},{10,11},{12,13},{... | collective-permute-start | bytes 4718600 | tf_op jit(solution)/shard_map/ppermute | solution.py:179
  45.6 1.3 %copy-start.3 = (bf16[4,16,96,128]{3,2,1,0:T(8,128)(2,1)}, bf16[4,16,96,128]{3,2,1,0:T(8,128)(2,1)S(1)}, u32[]{:S(2)}) copy-start(bf16[4,16,96,128]{3,2,1,0:T(8,128)(2,1)S(1)} %collective-permute-done.1.high) | copy-start | bytes 4718596
  46.9 48.1 %copy-start.2 = (f32[1,128,32]{1,2,0:T(8,128)S(1)}, f32[1,128,32]{1,2,0:T(8,128)}, u32[]{:S(2)}) copy-start(f32[1,128,32]{1,2,0:T(8,128)} %param.12) | copy-start | bytes 49156
  79.7 8.9 %collective-permute-start.6 = (f32[2,128,128]{2,1,0:T(8,128)}, f32[2,128,128]{2,1,0:T(8,128)S(1)}, u32[]{:S(2)}, u32[]{:S(2)}) collective-permute-start(f32[2,128,128]{2,1,0:T(8,128)} %get-tuple-element.7.refs_0_), channel_id=1, source_target_pairs={{0,3},{1,0},{2,1},{3,2},{4,7},{5,4},{6,5},{7,6},{8,11},{9,8},{10,9... | collective-permute-start | bytes 393224 | tf_op jit(solution)/shard_map/ppermute | solution.py:323
  84.5 10.4 %collective-permute-start.5 = (f32[2,128,128]{2,1,0:T(8,128)}, f32[2,128,128]{2,1,0:T(8,128)S(1)}, u32[]{:S(2)}, u32[]{:S(2)}) collective-permute-start(f32[2,128,128]{2,1,0:T(8,128)} %get-tuple-element.7.refs_0_), channel_id=1, source_target_pairs={{0,2},{1,3},{2,0},{3,1},{4,6},{5,7},{6,4},{7,5},{8,10},{9,11},{10,... | collective-permute-start | bytes 393224 | tf_op jit(solution)/shard_map/ppermute | solution.py:323
  84.5 10.4 %collective-permute-start.4 = (f32[2,128,128]{2,1,0:T(8,128)}, f32[2,128,128]{2,1,0:T(8,128)S(1)}, u32[]{:S(2)}, u32[]{:S(2)}) collective-permute-start(f32[2,128,128]{2,1,0:T(8,128)} %get-tuple-element.7.refs_0_), channel_id=1, source_target_pairs={{0,1},{1,2},{2,3},{3,0},{4,5},{5,6},{6,7},{7,4},{8,9},{9,10},{10,1... | collective-permute-start | bytes 393224 | tf_op jit(solution)/shard_map/ppermute | solution.py:323
  94.9 1.4 %copy-start = (bf16[4,1536,128]{2,1,0:T(8,128)(2,1)S(1)}, bf16[4,1536,128]{2,1,0:T(8,128)(2,1)}, u32[]{:S(2)}) copy-start(bf16[4,1536,128]{2,1,0:T(8,128)(2,1)} %get-tuple-element.8) | copy-start | bytes 4718596
  96.4 0.9 copy-start.1
  97.3 15.2 %copy-start.4 = (s32[8,8]{1,0:T(8,128)S(1)}, s32[8,8]{1,0:T(8,128)}, u32[]{:S(2)}) copy-start(s32[8,8]{1,0:T(8,128)} %param.13) | copy-start | bytes 772
  108.7 12.1 %all-to-all-start = ((bf16[8,32,768]{2,1,0:T(8,128)(2,1)}), bf16[8,32,768]{2,1,0:T(8,128)(2,1)S(1)}, u32[]{:S(2)}, u32[]{:S(2)}) async-start(bf16[8,32,768]{2,1,0:T(8,128)(2,1)} %shard_map.74), calls=%async_computation | async-start | bytes 786432 | tf_op jit(solution)/shard_map/all_to_all | solution.py:337

commit v3 on v2

v3 whole, which is shorter than its diff:
```python
import functools

import jax
import jax.numpy as jnp
from jax import lax
from jax.experimental import pallas as pl
from jax.experimental.pallas import tpu as pltpu
from jax.sharding import PartitionSpec as P

SWEEPS = 3
ITERS = 4


def harmonic(left_k, right_k):
    return 2.0 * left_k * right_k / (left_k + right_k)


def coefficients(classes, planes, first, last, lanes):
    kappa = jnp.exp2(2.0 * classes.astype(jnp.float32))
    length, rows_y, rows_z = kappa.shape
    depth = (length - planes) // 2
    place = jnp.arange(length, dtype=jnp.int32)[:, None, None]
    outside = (first & (place < depth)) | (last & (place >= depth + planes))
    x_face = harmonic(kappa[1:], kappa[:-1])
    x_face = jnp.where(outside[:-1], kappa[1:], jnp.where(outside[1:], kappa[:-1], x_face))
    centre = kappa[1:-1]
    y_face = harmonic(centre[:, 1:], centre[:, :-1])
    y_face = jnp.concatenate([centre[:, :1], y_face, centre[:, -1:]], axis=1)
    z_face = harmonic(centre[:, :, 1:], centre[:, :, :-1])
    z_face = jnp.concatenate([centre[:, :, :1], z_face, centre[:, :, -1:]], axis=2)
    faces = [
        x_face[:-1],
        x_face[1:],
        y_face[:, :-1],
        y_face[:, 1:],
        z_face[:, :, :-1],
        z_face[:, :, 1:],
    ]
    denom = faces[0] + faces[1] + faces[2] + faces[3] + faces[4] + faces[5]
    scale = jnp.where(outside[1:-1], 0.0, 1.0 / denom)
    empty = jnp.zeros_like(denom)
    sweep = jnp.stack([face * scale for face in faces] + [empty, empty], axis=2)
    sweep = jnp.pad(sweep, ((1, 1), (0, 0), (0, 0), (0, lanes - rows_z)))
    own = slice(depth - 1, depth - 1 + planes)
    plane = jnp.arange(planes, dtype=jnp.int32)[:, None, None]
    row_y = jnp.arange(rows_y, dtype=jnp.int32)[None, :, None]
    row_z = jnp.arange(rows_z, dtype=jnp.int32)[None, None, :]
    upper_half = row_y >= rows_y // 2
    counted = [
        jnp.where(plane > 0, 1.0, jnp.where(first | ~upper_half, 0.0, 2.0)),
        jnp.where(plane < planes - 1, 1.0, jnp.where(last | upper_half, 0.0, 2.0)),
        jnp.where(row_y > 0, 1.0, 0.0),
        jnp.where(row_y < rows_y - 1, 1.0, 0.0),
        jnp.where(row_z > 0, 1.0, 0.0),
        jnp.where(row_z < rows_z - 1, 1.0, 0.0),
    ]
    rows = [face[own] * share for face, share in zip(faces, counted)]
    rows += [denom[own], kappa[depth : depth + planes] * (1.0 / 16.0)]
    stiff = jnp.pad(jnp.stack(rows, axis=2), ((0, 0), (0, 0), (0, 0), (0, lanes - rows_z)))
    return sweep, stiff


def relax_kernel(
    own,
    low,
    high,
    sweep_rows,
    stiff_rows,
    y_vals,
    z_vals,
    face_ids,
    snap,
    gram,
    state_a,
    state_b,
    pad_rows,
    both,
):
    planes, rows_y, rows_z, width = own.shape
    length = state_a.shape[0]
    lanes = state_a.shape[3]
    half = rows_y // 2
    bf16 = jnp.bfloat16
    row = lax.broadcasted_iota(jnp.int32, (width, width), 0)
    col = lax.broadcasted_iota(jnp.int32, (width, width), 1)
    eye = jnp.where(row == col, 1.0, 0.0).astype(bf16)
    valid = lax.broadcasted_iota(jnp.int32, (width, lanes), 1) < rows_z

    def turn(lines):
        return lax.dot_general(
            eye, lines, (((1,), (1,)), ((), ())), preferred_element_type=jnp.float32
        )

    ids = face_ids[...]
    picks = [(ids == side).astype(jnp.float32) for side in range(4)]
    spare = lanes - rows_z
    place = lax.broadcasted_iota(jnp.int32, (spare, width), 0)
    z_all = z_vals[...].astype(jnp.float32)
    z_low = z_all * picks[2]
    z_high = z_all * picks[3]
    for y in range(rows_y):
        rows = jnp.where(place == 0, z_high[y : y + 1], 0.0)
        pad_rows[y] = jnp.where(place == spare - 1, z_low[y : y + 1], rows).astype(bf16)
    y_all = y_vals[...].astype(jnp.float32)
    blank = jnp.zeros((spare, width), bf16)
    ghost_low = turn(jnp.concatenate([(y_all * picks[0]).astype(bf16), blank], axis=0))
    ghost_high = turn(jnp.concatenate([(y_all * picks[1]).astype(bf16), blank], axis=0))

    def edges(e, carry):
        for state in (state_a, state_b):
            state[e, 0] = ghost_low
            state[e, rows_y + 1] = ghost_high
        return carry

    lax.fori_loop(0, length, edges, 0)

    def fill(get, e, y_from, y_to):
        for y in range(y_from, y_to, 2):
            lines = turn(
                jnp.concatenate([get(y), pad_rows[y], get(y + 1), pad_rows[y + 1]], axis=0)
            )
            state_a[e, y + 1] = lines[:, :lanes]
            state_a[e, y + 2] = lines[:, lanes:]

    def fill_planes(i, carry):
        fill(lambda y: own[i, y], planes + i, 0, rows_y)
        return carry

    def fill_sides(i, carry):
        fill(lambda y: low[half + i * rows_y + y], 1 + i, 0, rows_y)
        fill(lambda y: high[i * rows_y + y], 2 * planes + i, 0, rows_y)
        return carry

    lax.fori_loop(0, planes, fill_planes, 0)
    lax.fori_loop(0, planes - 1, fill_sides, 0)
    fill(lambda y: low[y - half], 0, half, rows_y)
    fill(lambda y: high[(planes - 1) * rows_y + y], length - 1, 0, half)

    def relax_line(src, dst, e, y, keep):
        middle = src[e, y + 1]
        rows = sweep_rows[e, y]
        fresh = (
            rows[0:1] * src[e - 1, y + 1]
            + rows[1:2] * src[e + 1, y + 1]
            + rows[2:3] * src[e, y]
            + rows[3:4] * src[e, y + 2]
            + rows[4:5] * pltpu.roll(middle, 1, 1)
            + rows[5:6] * pltpu.roll(middle, lanes - 1, 1)
        )
        fresh = fresh.astype(bf16).astype(jnp.float32)
        dst[e, y + 1] = jnp.where(valid, fresh, middle) if keep else fresh

    group = 4

    def relax_rows(src, dst, e, y_from, y_to, keep):
        def body(i, carry):
            for j in range(group):
                relax_line(src, dst, e, y_from + i * group + j, keep)
            return carry

        lax.fori_loop(0, (y_to - y_from) // group, body, 0)

    buffers = (state_a, state_b)
    for sweep in range(1, SWEEPS + 1):
        src, dst = buffers[(sweep - 1) % 2], buffers[sweep % 2]
        keep = sweep < SWEEPS

        def body(e, carry, src=src, dst=dst, keep=keep):
            relax_rows(src, dst, e, 0, rows_y, keep)
            return carry

        first = planes - SWEEPS - 1 + sweep
        lax.fori_loop(first + 1, length - 1 - first, body, 0)
        relax_rows(src, dst, first, half, rows_y, keep)
        relax_rows(src, dst, length - 1 - first, 0, half, keep)
    final = buffers[SWEEPS % 2]

    def stiffness(p, total):
        e = planes + p

        def body(y, carry):
            middle = final[e, y + 1]
            rows = stiff_rows[p, y]
            numer = (
                rows[0:1] * final[e - 1, y + 1]
                + rows[1:2] * final[e + 1, y + 1]
                + rows[2:3] * final[e, y]
                + rows[3:4] * final[e, y + 2]
                + rows[4:5] * pltpu.roll(middle, 1, 1)
                + rows[5:6] * pltpu.roll(middle, lanes - 1, 1)
            )
            spot = pl.ds(y * lanes, lanes)
            snap[p, :, spot] = middle.astype(bf16)
            both[pl.ds(0, width), spot] = (rows[7:8] * middle).astype(bf16)
            both[pl.ds(width, width), spot] = (rows[6:7] * middle - numer).astype(bf16)
            return carry

        for y in range(rows_y):
            body(y, 0)
        return total + lax.dot_general(
            snap[p], both[...], (((1,), (1,)), ((), ())), preferred_element_type=jnp.float32
        )

    total = lax.fori_loop(0, planes, stiffness, jnp.zeros((width, 2 * width), jnp.float32))
    mass = total[:, :width]
    stiff = total[:, width:]
    stiff = stiff + stiff.T
    gram[pl.ds(0, width)] = jnp.where(row > col, stiff, mass)
    diagonal = jnp.sum(jnp.where(row == col, stiff, 0.0), axis=0, keepdims=True)
    gram[pl.ds(width, 8)] = jnp.broadcast_to(diagonal, (8, width))


def shift_planes(array, up):
    count = lax.axis_size("sub")
    pairs = [(i, i + 1) for i in range(count - 1)]
    if not up:
        pairs = [(j, i) for i, j in pairs]
    return lax.ppermute(array, "sub", pairs)


def relax(initial, classes, y_vals, z_vals, face_ids):
    planes, rows_y, rows_z, width = initial.shape
    lanes = 128
    index = lax.axis_index("sub")
    subs = lax.axis_size("sub")
    packed = classes.astype(jnp.bfloat16)
    lines = initial.reshape(planes * rows_y, rows_z, width)
    half = rows_y // 2
    low = shift_planes(lines[half:], True)
    high = shift_planes(lines[:-half], False)
    class_low = shift_planes(packed, True)
    class_high = shift_planes(packed, False)
    extended = jnp.concatenate([class_low, packed, class_high], axis=0)
    sweep_rows, stiff_rows = coefficients(extended, planes, index == 0, index == subs - 1, lanes)
    state = pltpu.VMEM((3 * planes, rows_y + 2, width, lanes), jnp.float32)
    return pl.pallas_call(
        relax_kernel,
        out_shape=[
            jax.ShapeDtypeStruct((planes, width, rows_y * lanes), jnp.bfloat16),
            jax.ShapeDtypeStruct((width + 8, width), jnp.float32),
        ],
        scratch_shapes=[
            state,
            state,
            pltpu.VMEM((rows_y, lanes - rows_z, width), jnp.bfloat16),
            pltpu.VMEM((2 * width, rows_y * lanes), jnp.bfloat16),
        ],
        compiler_params=pltpu.CompilerParams(vmem_limit_bytes=56 * 2**20),
    )(initial, low, high, sweep_rows, stiff_rows, y_vals, z_vals, face_ids[None])


def lane_copy(tile, lane):
    return jnp.broadcast_to(tile[:, lane : lane + 1], (8, 128))


def row_copy(tile, row):
    return jnp.broadcast_to(tile[row : row + 1, :], (8, tile.shape[1]))


def solve_spd(left, right):
    size = left.shape[0]
    count = size // 8
    sub = lax.broadcasted_iota(jnp.int32, (8, 128), 0)
    lhs = [left[8 * t : 8 * t + 8] for t in range(count)]
    rhs = [right[8 * t : 8 * t + 8] for t in range(count)]
    for k in range(count):
        cols = [lane_copy(lhs[k], 8 * k + j) for j in range(8)]
        panel_l, panel_r = lhs[k], rhs[k]
        for j in range(8):
            recip = 1.0 / row_copy(cols[j], j)
            here = sub == j
            mult = jnp.where(here, recip, -cols[j] * recip)
            for l in range(j + 1, 8):
                cols[l] = jnp.where(here, 0.0, cols[l]) + mult * row_copy(cols[l], j)
            panel_l = jnp.where(here, 0.0, panel_l) + mult * row_copy(panel_l, j)
            panel_r = jnp.where(here, 0.0, panel_r) + mult * row_copy(panel_r, j)
        rows_l = [row_copy(panel_l, j) for j in range(8)]
        rows_r = [row_copy(panel_r, j) for j in range(8)]
        order = list(range(k + 1, count)) + list(range(k))
        for t in order:
            tile_cols = [lane_copy(lhs[t], 8 * k + j) for j in range(8)]
            if k + 1 < count:
                lhs[t] = lhs[t] - tree([tile_cols[j] * rows_l[j] for j in range(8)])
            rhs[t] = rhs[t] - tree([tile_cols[j] * rows_r[j] for j in range(8)])
        lhs[k], rhs[k] = panel_l, panel_r
    return jnp.concatenate(rhs, axis=0)


def tree(terms):
    while len(terms) > 1:
        terms = [a + b for a, b in zip(terms[::2], terms[1::2])] + terms[len(terms) & ~1 :]
    return terms[0]


def whiten(inner, block):
    size = inner.shape[0]
    count = size // 8
    sub = lax.broadcasted_iota(jnp.int32, (8, 128), 0)
    lhs = [inner[8 * t : 8 * t + 8] for t in range(count)]
    rhs = [block[8 * t : 8 * t + 8] for t in range(count)]
    done = []
    for k in range(count):
        live = range(k, count)
        cols = {t: [lane_copy(lhs[t], 8 * k + j) for j in range(8)] for t in live}
        scale = None
        for j in range(8):
            pivot = row_copy(cols[k][j], j)
            recip = 1.0 / pivot
            root = lax.rsqrt(pivot)
            scale = root if scale is None else jnp.where(sub >= j, root, scale)
            head = {l: row_copy(cols[k][l], j) for l in range(j + 1, 8)}
            row_l, row_r = row_copy(lhs[k], j), row_copy(rhs[k], j)
            for t in live:
                mult = cols[t][j] * recip
                if t == k:
                    mult = jnp.where(sub > j, mult, 0.0)
                for l in range(j + 1, 8):
                    cols[t][l] = cols[t][l] - mult * head[l]
                lhs[t] = lhs[t] - mult[:, : row_l.shape[1]] * row_l
                rhs[t] = rhs[t] - mult * row_r
        done.append(rhs[k] * scale)
    return jnp.concatenate(done, axis=0)


def dot(a, b, dims):
    return lax.dot_general(
        a, b, (dims, ((), ())), precision=lax.Precision.HIGHEST, preferred_element_type=jnp.float32
    )


def modes_kernel(cell_count, rows_z, *refs):
    *part_refs, start_ref, snap_ref, out_ref = refs
    total = part_refs[0][...]
    for part in part_refs[1:]:
        total = total + part[...]
    width = total.shape[1]
    row = lax.broadcasted_iota(jnp.int32, (width, width), 0)
    col = lax.broadcasted_iota(jnp.int32, (width, width), 1)
    packed = total[:width]
    turned = packed.T
    mass = jnp.where(row <= col, packed, turned) * (1.0 / cell_count)
    stiff = jnp.where(row > col, packed, jnp.where(row < col, turned, total[width : width + 1]))
    stiff = stiff * (0.5 / cell_count)
    step = solve_spd(stiff, mass)
    form = dot(step, dot(mass, step, ((1,), (0,))), ((0,), (0,)))
    block = start_ref[...]
    for _ in range(ITERS):
        weighted = dot(block, form, ((1,), (0,)))
        solved = dot(block, step, ((1,), (1,)))
        inner = dot(weighted, block, ((1,), (1,)))
        block = whiten(inner, solved)
    modes = block.astype(jnp.bfloat16)
    planes, _, columns = snap_ref.shape
    lanes = 128
    rows_y = columns // lanes
    piece_rows = planes * rows_y // out_ref.shape[0]
    for p in range(planes):
        basis = jnp.dot(modes, snap_ref[p], preferred_element_type=jnp.float32)
        for y in range(rows_y):
            piece, spot = divmod(p * rows_y + y, piece_rows)
            out_ref[piece, :, pl.ds(spot * rows_z, rows_z)] = basis[
                :, y * lanes : y * lanes + rows_z
            ].astype(jnp.bfloat16)


def on_device(snap_init, channel_map, yface_vals, zface_vals, face_of, start_block, correlation):
    subs = lax.axis_size("sub")
    owner_count = lax.axis_size("nbhd")
    planes, rows_y, rows_z, width = snap_init.shape[1:]
    snapshots, own = relax(
        snap_init[0], channel_map[0], yface_vals[0], zface_vals[0], face_of[0]
    )
    parts = [own] + [
        lax.ppermute(own, "sub", [(i, (i + shift) % subs) for i in range(subs)])
        for shift in range(1, subs)
    ]
    cells = planes * rows_y * rows_z
    modes = start_block.shape[-1]
    pieces = pl.pallas_call(
        functools.partial(modes_kernel, float(subs * cells), rows_z),
        out_shape=jax.ShapeDtypeStruct((owner_count, modes, cells // owner_count), jnp.bfloat16),
        compiler_params=pltpu.CompilerParams(vmem_limit_bytes=32 * 2**20),
    )(*parts, start_block[0].T, snapshots)
    received = lax.all_to_all(pieces, "nbhd", split_axis=0, concat_axis=0, tiled=True)
    column = lax.dynamic_slice_in_dim(correlation, lax.axis_index("nbhd"), 1, axis=1)[:, 0]
    result = received * column.astype(jnp.bfloat16)[:, None, None]
    return result[None, None]


def solution(mesh):
    return jax.shard_map(
        on_device,
        mesh=mesh,
        in_specs=(
            P("nbhd", "sub", None, None, None),
            P("nbhd", "sub", None, None),
            P("nbhd", None, None),
            P("nbhd", None, None),
            P("nbhd", None),
            P("nbhd", None, None),
            P(),
        ),
        out_specs=P("nbhd", "sub", None, None, None),
        check_vma=False,
    )
```

time: 122 us -> 112 us (0.918)
  waiting for transfers between devices: 43.7 us -> 29.3 us
  local copies, waits for them, and re-layouts: 2.98 us -> 12.8 us
  Pallas kernels: 44.3 us -> 39.6 us
    ppermute x4, waiting for transfers between devices: 26 us -> 15.7 us  [shift_planes(): return lax.ppermute(array, 'sub', pairs)]
    transpose x5 -> x0, other arithmetic: 4.96 us -> none  [coefficients(): jnp.swapaxes(item, 1, 2)]
    pallas_call x2, Pallas kernels: 44.3 us -> 39.6 us  [the longest x1 28.2 us: relax(): pl.pallas_call(relax_kernel, out_shape=[jax.ShapeDtypeStruct((planes, wid...]
    another operation x0 -> x3, local copies, waits for them, and re-layouts: none -> 4.57 us  [the longest x2 3.35 us: coefficients(): sweep = jnp.stack([face * scale for face in faces] + [empty, empty], axis=2)]
    mul x0 -> x6, other arithmetic: none -> 4.41 us  [the longest x3 2.1 us: coefficients(): rows = [face[own] * share for face, share in zip(faces, counted)]]
    ppermute x3, waiting for transfers between devices: 9.52 us -> 5.38 us  [on_device(): lax.ppermute(own, 'sub', [(i, (i + shift) % subs) for i in range(subs)])]
    slice x0 -> x2, local copies, waits for them, and re-layouts: none -> 3.66 us  [the longest x1 3.04 us: relax(): high = shift_planes(lines[:-half], False)]
    pad x0 -> x2, local copies, waits for them, and re-layouts: none -> 1.71 us  [the longest x1 0.98 us: coefficients(): sweep = jnp.pad(sweep, ((1, 1), (0, 0), (0, 0), (0, lanes - rows_z)))]
  transfers between devices with their start and end apart: 8 -> 8, of which waited for: 5 -> 6; matrix products, arithmetic and copies ran while one was open for 5% -> 14% of each run, Pallas kernels for 0% -> 0%
where the time goes in v3:
time: 112 us
  Pallas kernels  39.6 us (35%)
  waiting for transfers between devices  29.3 us (26%)
  starting transfers between devices  23.2 us (21%)
  local copies, waits for them, and re-layouts  12.8 us (11%)
  other arithmetic  6.55 us (6%)
    pallas_call x1, Pallas kernels, relax(): pl.pallas_call(relax_kernel, out_shape=[jax.ShapeDtypeStruct((planes, wid...  28.2 us
    ppermute x4, waiting for transfers between devices, shift_planes(): return lax.ppermute(array, 'sub', pairs)  15.7 us
    ppermute x4, starting transfers between devices, shift_planes(): return lax.ppermute(array, 'sub', pairs)  13.8 us
    pallas_call x1, Pallas kernels, on_device(): pl.pallas_call(functools.partial(modes_kernel, float(subs * cells), rows_...  11.3 us
    all_to_all x1, waiting for transfers between devices, on_device(): lax.all_to_all(pieces, 'nbhd', split_axis=0, concat_axis=0, tiled=True)  8.15 us
    ppermute x3, starting transfers between devices, on_device(): lax.ppermute(own, 'sub', [(i, (i + shift) % subs) for i in range(subs)])  5.67 us
    ppermute x3, waiting for transfers between devices, on_device(): lax.ppermute(own, 'sub', [(i, (i + shift) % subs) for i in range(subs)])  5.38 us
    all_to_all x1, starting transfers between devices, on_device(): lax.all_to_all(pieces, 'nbhd', split_axis=0, concat_axis=0, tiled=True)  3.72 us
  transfers between devices with their start and end apart: 8, of which 6 were waited for; matrix products, arithmetic and copies ran while one was open for 14% of the time, Pallas kernels for 0%

profile of v3, /device:TPU:0, one launch (start us, length us, event | category | flops | bytes accessed | tf_op | source)
XLA Modules:
  0.0 111.5 jit_solution(10039261032826868277)
XLA Ops:
  0.0 0.8 convert_bitcast_fusion
  0.8 1.3 %collective-permute-start.3 = (bf16[4,16,96]{2,1,0:T(8,128)(2,1)S(1)}, bf16[4,16,96]{2,1,0:T(8,128)(2,1)S(1)}, u32[]{:S(2)}, u32[]{:S(2)}) collective-permute-start(bf16[4,16,96]{2,1,0:T(8,128)(2,1)S(1)} %convert_bitcast_fusion), channel_id=1, source_target_pairs={{1,0},{2,1},{3,2},{5,4},{6,5},{7,6},{9,8},{10,9},{11,10},{13,12},{... | collective-permute-start | bytes 36872 | tf_op jit(solution)/shard_map/ppermute | solution.py:218
  2.1 5.6 %collective-permute-start.2 = (bf16[4,16,96]{2,1,0:T(8,128)(2,1)S(1)}, bf16[4,16,96]{2,1,0:T(8,128)(2,1)S(1)}, u32[]{:S(2)}, u32[]{:S(2)}) collective-permute-start(bf16[4,16,96]{2,1,0:T(8,128)(2,1)S(1)} %convert_bitcast_fusion), channel_id=1, source_target_pairs={{0,1},{1,2},{2,3},{4,5},{5,6},{6,7},{8,9},{9,10},{10,11},{12,13},{... | collective-permute-start | bytes 36872 | tf_op jit(solution)/shard_map/ppermute | solution.py:218
  7.6 3.0 %fusion.13 = (bf16[56,96,128]{2,1,0:T(8,128)(2,1)}, bf16[56,96,128]{2,1,0:T(8,128)(2,1)S(1)}) fusion(bf16[64,96,128]{2,1,0:T(8,128)(2,1)} %bitcast.58), kind=kLoop, calls=%fused_computation.53 | loop fusion | bytes 5505024 | tf_op jit(solution)/shard_map/slice | solution.py:230
  10.7 1.3 %collective-permute-start.1 = (bf16[56,96,128]{2,1,0:T(8,128)(2,1)}, bf16[56,96,128]{2,1,0:T(8,128)(2,1)S(1)}, u32[]{:S(2)}, u32[]{:S(2)}) collective-permute-start(bf16[56,96,128]{2,1,0:T(8,128)(2,1)} %get-tuple-element.11), channel_id=1, source_target_pairs={{1,0},{2,1},{3,2},{5,4},{6,5},{7,6},{9,8},{10,9},{11,10},{13,12},{... | collective-permute-start | bytes 4128776 | tf_op jit(solution)/shard_map/ppermute | solution.py:218
  11.9 5.7 %collective-permute-start = (bf16[56,96,128]{2,1,0:T(8,128)(2,1)S(1)}, bf16[56,96,128]{2,1,0:T(8,128)(2,1)}, u32[]{:S(2)}, u32[]{:S(2)}) collective-permute-start(bf16[56,96,128]{2,1,0:T(8,128)(2,1)S(1)} %get-tuple-element.12), channel_id=1, source_target_pairs={{0,1},{1,2},{2,3},{4,5},{5,6},{6,7},{8,9},{9,10},{10,11},{12,13},{... | collective-permute-start | bytes 4128776 | tf_op jit(solution)/shard_map/ppermute | solution.py:218
  21.8 1.2 %stack.67 = f32[4,16,8,96]{3,2,1,0:T(8,128)S(1)} concatenate(f32[4,16,1,96]{3,2,1,0:T(1,128)} %bitcast.73, f32[4,16,1,96]{3,2,1,0:T(1,128)} %bitcast.72, f32[4,16,1,96]{3,2,1,0:T(1,128)} %bitcast.67, f32[4,16,1,96]{3,2,1,0:T(1,128)S(1)} %bitcast.66, f32[4,16,1,96]{3,2,1,0:T(1,128)} %bitcast.69, f32[4,16,1,96]{3,2,1,0:T(1,128)} %bitcast.68, f32[4,16,1,96]{3,2,1,0:T(1,128)} %bitcast.70, ...), dimensions={2} | concatenate | bytes 393216 | tf_op jit(solution)/shard_map/stack | solution.py:59
  23.7 1.6 %fusion = (f32[10,16,96]{2,1,0:T(8,128)}, f32[10,16,96]{2,1,0:T(8,128)}, f32[10,16,96]{2,1,0:T(8,128)}, f32[10,16,96]{2,1,0:T(8,128)}, f32[10,16,96]{2,1,0:T(8,128)}) fusion(f32[10,1,96]{2,1,0:T(1,128)} %copy-done.4, f32[10,15,96]{2,1,0:T(8,128)S(1)} %add_divide_fusion.1, f32[10,16,96]{2,1,0:T(8,128)S(1)} %get-tuple-element.10, pred[10]{0:T(512)(128)(4,1)} %copy-done.6, ...), kind=kLoop, calls=%fused_computation.21 | loop fusion | flops 153600 | bytes 618250 | tf_op jit(solution)/shard_map/mul | solution.py:42
  26.0 2.6 %stack.58 = f32[10,16,8,96]{3,2,1,0:T(8,128)S(1)} concatenate(f32[10,16,1,96]{3,2,1,0:T(1,128)} %bitcast.64, f32[10,16,1,96]{3,2,1,0:T(1,128)} %bitcast.65, f32[10,16,1,96]{3,2,1,0:T(1,128)} %bitcast.62, f32[10,16,1,96]{3,2,1,0:T(1,128)} %bitcast.61, f32[10,16,1,96]{3,2,1,0:T(1,128)} %bitcast.63, f32[10,16,1,96]{3,2,1,0:T(1,128)S(1)} %bitcast.60, f32[10,16,2,96]{3,2,1,0:T(2,128)} %stack.57), dimensions={2} | concatenate | bytes 983040 | tf_op jit(solution)/shard_map/stack | solution.py:42
  28.7 1.0 pad.8.sweep_rows
  29.6 14.8 %collective-permute-done.1.high = bf16[56,96,128]{2,1,0:T(8,128)(2,1)S(1)} collective-permute-done((bf16[56,96,128]{2,1,0:T(8,128)(2,1)}, bf16[56,96,128]{2,1,0:T(8,128)(2,1)S(1)}, u32[]{:S(2)}, u32[]{:S(2)}) %collective-permute-start.1) | collective-permute-done | bytes 1376288 | tf_op jit(solution)/shard_map/ppermute | solution.py:218
  44.4 1.0 collective-permute-done.low
  45.5 28.2 %shard_map.73 = (bf16[4,128,2048]{2,1,0:T(8,128)(2,1)}, f32[136,128]{1,0:T(8,128)}) custom-call(bf16[4,16,96,128]{3,2,1,0:T(8,128)(2,1)} %bitcast.59, bf16[56,96,128]{2,1,0:T(8,128)(2,1)} %collective-permute-done.low, bf16[56,96,128]{2,1,0:T(8,128)(2,1)} %copy-done.3, f32[12,16,8,128]{3,2,1,0:T(8,128)} %pad.8.sweep_rows, f32[4,16,8,128]{3,2,1,0:T(8,128)} %pad.9.stiff_rows, ...), custom_call_target="tpu_custom_call" | custom-call | tf_op jit(solution)/shard_map/pallas_call | solution.py:236
  73.7 4.7 %collective-permute-start.6 = (f32[136,128]{1,0:T(8,128)}, f32[136,128]{1,0:T(8,128)S(1)}, u32[]{:S(2)}, u32[]{:S(2)}) collective-permute-start(f32[136,128]{1,0:T(8,128)} %get-tuple-element.7.refs_0_), channel_id=1, source_target_pairs={{0,3},{1,0},{2,1},{3,2},{4,7},{5,4},{6,5},{7,6},{8,11},{9,8},{10,9... | collective-permute-start | bytes 208904 | tf_op jit(solution)/shard_map/ppermute | solution.py:374
  78.5 0.9 collective-permute-start.4
  79.4 1.3 %collective-permute-done.6.refs_3_ = f32[136,128]{1,0:T(8,128)S(1)} collective-permute-done((f32[136,128]{1,0:T(8,128)}, f32[136,128]{1,0:T(8,128)S(1)}, u32[]{:S(2)}, u32[]{:S(2)}) %collective-permute-start.6) | collective-permute-done | bytes 69664 | tf_op jit(solution)/shard_map/ppermute | solution.py:374
  80.7 3.2 %collective-permute-done.5.refs_2_ = f32[136,128]{1,0:T(8,128)S(1)} collective-permute-done((f32[136,128]{1,0:T(8,128)}, f32[136,128]{1,0:T(8,128)S(1)}, u32[]{:S(2)}, u32[]{:S(2)}) %collective-permute-start.5) | collective-permute-done | bytes 69664 | tf_op jit(solution)/shard_map/ppermute | solution.py:374
  83.9 0.9 collective-permute-done.4.refs_1_
  84.8 1.6 %copy-done = bf16[4,128,2048]{2,1,0:T(8,128)(2,1)S(1)} copy-done((bf16[4,128,2048]{2,1,0:T(8,128)(2,1)S(1)}, bf16[4,128,2048]{2,1,0:T(8,128)(2,1)}, u32[]{:S(2)}) %copy-start) | copy-done | bytes 2097176
  86.4 0.9 copy-done.1
  87.3 11.3 %shard_map.74 = bf16[8,32,768]{2,1,0:T(8,128)(2,1)} custom-call(f32[136,128]{1,0:T(8,128)S(1)} %copy-done.1, f32[136,128]{1,0:T(8,128)S(1)} %collective-permute-done.4.refs_1_, f32[136,128]{1,0:T(8,128)S(1)} %collective-permute-done.5.refs_2_, f32[136,128]{1,0:T(8,128)S(1)} %collective-permute-done.6.refs_3_, f32[32,128]{1,0:T(8,128)S(1)} %bitcast.57, ...), custom_call_target="tpu_custom_call" | custom-call | tf_op jit(solution)/shard_map/pallas_call | solution.py:379
  98.6 3.7 %all-to-all-start = ((bf16[8,32,768]{2,1,0:T(8,128)(2,1)}), bf16[8,32,768]{2,1,0:T(8,128)(2,1)S(1)}, u32[]{:S(2)}, u32[]{:S(2)}) async-start(bf16[8,32,768]{2,1,0:T(8,128)(2,1)} %shard_map.74), calls=%async_computation | async-start | bytes 786432 | tf_op jit(solution)/shard_map/all_to_all | solution.py:384
  102.5 8.1 %all-to-all-done = bf16[8,32,768]{2,1,0:T(8,128)(2,1)S(1)} async-done(((bf16[8,32,768]{2,1,0:T(8,128)(2,1)}), bf16[8,32,768]{2,1,0:T(8,128)(2,1)S(1)}, u32[]{:S(2)}, u32[]{:S(2)}) %all-to-all-start) | async-done | bytes 393248 | tf_op jit(solution)/shard_map/all_to_all | solution.py:384
  110.7 0.8 multiply_bitcast_fusion
  (40 shorter events, 5.8 us)
Async XLA Ops:
  0.8 17.1 %collective-permute-start.3 = (bf16[4,16,96]{2,1,0:T(8,128)(2,1)S(1)}, bf16[4,16,96]{2,1,0:T(8,128)(2,1)S(1)}, u32[]{:S(2)}, u32[]{:S(2)}) collective-permute-start(bf16[4,16,96]{2,1,0:T(8,128)(2,1)S(1)} %convert_bitcast_fusion), channel_id=1, source_target_pairs={{1,0},{2,1},{3,2},{5,4},{6,5},{7,6},{9,8},{10,9},{11,10},{13,12},{... | collective-permute-start | bytes 36872 | tf_op jit(solution)/shard_map/ppermute | solution.py:218
  2.1 15.9 %collective-permute-start.2 = (bf16[4,16,96]{2,1,0:T(8,128)(2,1)S(1)}, bf16[4,16,96]{2,1,0:T(8,128)(2,1)S(1)}, u32[]{:S(2)}, u32[]{:S(2)}) collective-permute-start(bf16[4,16,96]{2,1,0:T(8,128)(2,1)S(1)} %convert_bitcast_fusion), channel_id=1, source_target_pairs={{0,1},{1,2},{2,3},{4,5},{5,6},{6,7},{8,9},{9,10},{10,11},{12,13},{... | collective-permute-start | bytes 36872 | tf_op jit(solution)/shard_map/ppermute | solution.py:218
  10.7 33.7 %collective-permute-start.1 = (bf16[56,96,128]{2,1,0:T(8,128)(2,1)}, bf16[56,96,128]{2,1,0:T(8,128)(2,1)S(1)}, u32[]{:S(2)}, u32[]{:S(2)}) collective-permute-start(bf16[56,96,128]{2,1,0:T(8,128)(2,1)} %get-tuple-element.11), channel_id=1, source_target_pairs={{1,0},{2,1},{3,2},{5,4},{6,5},{7,6},{9,8},{10,9},{11,10},{13,12},{... | collective-permute-start | bytes 4128776 | tf_op jit(solution)/shard_map/ppermute | solution.py:218
  11.9 33.4 %collective-permute-start = (bf16[56,96,128]{2,1,0:T(8,128)(2,1)S(1)}, bf16[56,96,128]{2,1,0:T(8,128)(2,1)}, u32[]{:S(2)}, u32[]{:S(2)}) collective-permute-start(bf16[56,96,128]{2,1,0:T(8,128)(2,1)S(1)} %get-tuple-element.12), channel_id=1, source_target_pairs={{0,1},{1,2},{2,3},{4,5},{5,6},{6,7},{8,9},{9,10},{10,11},{12,13},{... | collective-permute-start | bytes 4128776 | tf_op jit(solution)/shard_map/ppermute | solution.py:218
  17.7 4.0 %copy-start.6 = (pred[10]{0:T(512)(128)(4,1)}, pred[10]{0:T(512)(128)(4,1)S(1)}, u32[]{:S(2)}) copy-start(pred[10]{0:T(512)(128)(4,1)S(1)} %slice_bitcast_fusion) | copy-start | bytes 34
  18.3 3.5 %copy-start.4 = (f32[10,1,96]{2,1,0:T(1,128)}, f32[10,1,96]{2,1,0:T(1,128)S(1)}, u32[]{:S(2)}) copy-start(f32[10,1,96]{2,1,0:T(1,128)S(1)} %get-tuple-element.18) | copy-start | bytes 11524
  44.4 1.1 copy-start.3
  45.5 39.3 %copy-start.2 = (f32[1,128,32]{1,2,0:T(8,128)S(1)}, f32[1,128,32]{1,2,0:T(8,128)}, u32[]{:S(2)}) copy-start(f32[1,128,32]{1,2,0:T(8,128)} %param.12) | copy-start | bytes 49156
  73.7 7.0 %collective-permute-start.6 = (f32[136,128]{1,0:T(8,128)}, f32[136,128]{1,0:T(8,128)S(1)}, u32[]{:S(2)}, u32[]{:S(2)}) collective-permute-start(f32[136,128]{1,0:T(8,128)} %get-tuple-element.7.refs_0_), channel_id=1, source_target_pairs={{0,3},{1,0},{2,1},{3,2},{4,7},{5,4},{6,5},{7,6},{8,11},{9,8},{10,9... | collective-permute-start | bytes 208904 | tf_op jit(solution)/shard_map/ppermute | solution.py:374
  78.5 5.4 %collective-permute-start.5 = (f32[136,128]{1,0:T(8,128)}, f32[136,128]{1,0:T(8,128)S(1)}, u32[]{:S(2)}, u32[]{:S(2)}) collective-permute-start(f32[136,128]{1,0:T(8,128)} %get-tuple-element.7.refs_0_), channel_id=1, source_target_pairs={{0,2},{1,3},{2,0},{3,1},{4,6},{5,7},{6,4},{7,5},{8,10},{9,11},{10,... | collective-permute-start | bytes 208904 | tf_op jit(solution)/shard_map/ppermute | solution.py:374
  78.5 6.3 %collective-permute-start.4 = (f32[136,128]{1,0:T(8,128)}, f32[136,128]{1,0:T(8,128)S(1)}, u32[]{:S(2)}, u32[]{:S(2)}) collective-permute-start(f32[136,128]{1,0:T(8,128)} %get-tuple-element.7.refs_0_), channel_id=1, source_target_pairs={{0,1},{1,2},{2,3},{3,0},{4,5},{5,6},{6,7},{7,4},{8,9},{9,10},{10,1... | collective-permute-start | bytes 208904 | tf_op jit(solution)/shard_map/ppermute | solution.py:374
  84.8 1.6 %copy-start = (bf16[4,128,2048]{2,1,0:T(8,128)(2,1)S(1)}, bf16[4,128,2048]{2,1,0:T(8,128)(2,1)}, u32[]{:S(2)}) copy-start(bf16[4,128,2048]{2,1,0:T(8,128)(2,1)} %get-tuple-element.8.refs_5_) | copy-start | bytes 6291460
  86.4 0.9 copy-start.1
  87.3 15.1 %copy-start.5 = (s32[8,8]{1,0:T(8,128)S(1)}, s32[8,8]{1,0:T(8,128)}, u32[]{:S(2)}) copy-start(s32[8,8]{1,0:T(8,128)} %param.13) | copy-start | bytes 772
  98.6 12.1 %all-to-all-start = ((bf16[8,32,768]{2,1,0:T(8,128)(2,1)}), bf16[8,32,768]{2,1,0:T(8,128)(2,1)S(1)}, u32[]{:S(2)}, u32[]{:S(2)}) async-start(bf16[8,32,768]{2,1,0:T(8,128)(2,1)} %shard_map.74), calls=%async_computation | async-start | bytes 786432 | tf_op jit(solution)/shard_map/all_to_all | solution.py:384

commit v4 on v3

--- a/solution.py
+++ b/solution.py
@@ -80,11 +80,13 @@
     length = state_a.shape[0]
     lanes = state_a.shape[3]
     half = rows_y // 2
+    spare_lines = low.shape[0] - planes * rows_y + half
     bf16 = jnp.bfloat16
     row = lax.broadcasted_iota(jnp.int32, (width, width), 0)
     col = lax.broadcasted_iota(jnp.int32, (width, width), 1)
     eye = jnp.where(row == col, 1.0, 0.0).astype(bf16)
-    valid = lax.broadcasted_iota(jnp.int32, (width, lanes), 1) < rows_z
+    part = 16
+    valid = lax.broadcasted_iota(jnp.int32, (part, lanes), 1) < rows_z
 
     def turn(lines):
         return lax.dot_general(
@@ -127,30 +129,33 @@
         return carry
 
     def fill_sides(i, carry):
-        fill(lambda y: low[half + i * rows_y + y], 1 + i, 0, rows_y)
-        fill(lambda y: high[i * rows_y + y], 2 * planes + i, 0, rows_y)
+        fill(lambda y: low[spare_lines + half + i * rows_y + y], 1 + i, 0, rows_y)
+        fill(lambda y: high[spare_lines + i * rows_y + y], 2 * planes + i, 0, rows_y)
         return carry
 
     lax.fori_loop(0, planes, fill_planes, 0)
     lax.fori_loop(0, planes - 1, fill_sides, 0)
-    fill(lambda y: low[y - half], 0, half, rows_y)
-    fill(lambda y: high[(planes - 1) * rows_y + y], length - 1, 0, half)
+    fill(lambda y: low[spare_lines + y - half], 0, half, rows_y)
+    fill(lambda y: high[spare_lines + (planes - 1) * rows_y + y], length - 1, 0, half)
 
     def relax_line(src, dst, e, y, keep):
-        middle = src[e, y + 1]
         rows = sweep_rows[e, y]
-        fresh = (
-            rows[0:1] * src[e - 1, y + 1]
-            + rows[1:2] * src[e + 1, y + 1]
-            + rows[2:3] * src[e, y]
-            + rows[3:4] * src[e, y + 2]
-            + rows[4:5] * pltpu.roll(middle, 1, 1)
-            + rows[5:6] * pltpu.roll(middle, lanes - 1, 1)
-        )
-        fresh = fresh.astype(bf16).astype(jnp.float32)
-        dst[e, y + 1] = jnp.where(valid, fresh, middle) if keep else fresh
-
-    group = 4
+        weights = [jnp.broadcast_to(rows[k : k + 1], (part, lanes)) for k in range(6)]
+        for start in range(0, width, part):
+            some = pl.ds(start, part)
+            middle = src[e, y + 1, some]
+            fresh = (
+                weights[0] * src[e - 1, y + 1, some]
+                + weights[1] * src[e + 1, y + 1, some]
+                + weights[2] * src[e, y, some]
+                + weights[3] * src[e, y + 2, some]
+                + weights[4] * pltpu.roll(middle, 1, 1)
+                + weights[5] * pltpu.roll(middle, lanes - 1, 1)
+            )
+            fresh = fresh.astype(bf16).astype(jnp.float32)
+            dst[e, y + 1, some] = jnp.where(valid, fresh, middle) if keep else fresh
+
+    group = 2
 
     def relax_rows(src, dst, e, y_from, y_to, keep):
         def body(i, carry):
@@ -178,25 +183,27 @@
     def stiffness(p, total):
         e = planes + p
 
-        def body(y, carry):
-            middle = final[e, y + 1]
+        def line(y):
             rows = stiff_rows[p, y]
-            numer = (
-                rows[0:1] * final[e - 1, y + 1]
-                + rows[1:2] * final[e + 1, y + 1]
-                + rows[2:3] * final[e, y]
-                + rows[3:4] * final[e, y + 2]
-                + rows[4:5] * pltpu.roll(middle, 1, 1)
-                + rows[5:6] * pltpu.roll(middle, lanes - 1, 1)
-            )
+            weights = [jnp.broadcast_to(rows[k : k + 1], (part, lanes)) for k in range(8)]
             spot = pl.ds(y * lanes, lanes)
-            snap[p, :, spot] = middle.astype(bf16)
-            both[pl.ds(0, width), spot] = (rows[7:8] * middle).astype(bf16)
-            both[pl.ds(width, width), spot] = (rows[6:7] * middle - numer).astype(bf16)
-            return carry
+            for start in range(0, width, part):
+                some = pl.ds(start, part)
+                middle = final[e, y + 1, some]
+                numer = (
+                    weights[0] * final[e - 1, y + 1, some]
+                    + weights[1] * final[e + 1, y + 1, some]
+                    + weights[2] * final[e, y, some]
+                    + weights[3] * final[e, y + 2, some]
+                    + weights[4] * pltpu.roll(middle, 1, 1)
+                    + weights[5] * pltpu.roll(middle, lanes - 1, 1)
+                )
+                snap[p, some, spot] = middle.astype(bf16)
+                both[some, spot] = (weights[7] * middle).astype(bf16)
+                both[pl.ds(width + start, part), spot] = (weights[6] * middle - numer).astype(bf16)
 
         for y in range(rows_y):
-            body(y, 0)
+            line(y)
         return total + lax.dot_general(
             snap[p], both[...], (((1,), (1,)), ((), ())), preferred_element_type=jnp.float32
         )
@@ -223,14 +230,21 @@
     lanes = 128
     index = lax.axis_index("sub")
     subs = lax.axis_size("sub")
-    packed = classes.astype(jnp.bfloat16)
     lines = initial.reshape(planes * rows_y, rows_z, width)
+    count = planes * rows_y
     half = rows_y // 2
-    low = shift_planes(lines[half:], True)
-    high = shift_planes(lines[:-half], False)
-    class_low = shift_planes(packed, True)
-    class_high = shift_planes(packed, False)
-    extended = jnp.concatenate([class_low, packed, class_high], axis=0)
+    marks = classes.astype(jnp.bfloat16).reshape(count, rows_z).T
+    marks = jnp.pad(marks, ((0, 0), (0, -count % width)))
+    marks = jnp.swapaxes(marks.reshape(rows_z, -1, width), 0, 1)
+    low = shift_planes(jnp.concatenate([marks, lines[half:]], axis=0), True)
+    high = shift_planes(jnp.concatenate([marks, lines[:-half]], axis=0), False)
+    spare = marks.shape[0]
+
+    def unmark(halo):
+        flat = jnp.swapaxes(halo[:spare], 0, 1).reshape(rows_z, spare * width)
+        return flat[:, :count].T.reshape(planes, rows_y, rows_z).astype(jnp.int32)
+
+    extended = jnp.concatenate([unmark(low), classes, unmark(high)], axis=0)
     sweep_rows, stiff_rows = coefficients(extended, planes, index == 0, index == subs - 1, lanes)
     state = pltpu.VMEM((3 * planes, rows_y + 2, width, lanes), jnp.float32)
     return pl.pallas_call(
@@ -329,7 +343,9 @@
 
 
 def modes_kernel(cell_count, rows_z, *refs):
-    *part_refs, start_ref, snap_ref, out_ref = refs
+    *part_refs, start_ref, snap_hbm, out_ref, snap_ref, sem = refs
+    fetch = pltpu.make_async_copy(snap_hbm, snap_ref, sem)
+    fetch.start()
     total = part_refs[0][...]
     for part in part_refs[1:]:
         total = total + part[...]
@@ -350,6 +366,7 @@
         inner = dot(weighted, block, ((1,), (1,)))
         block = whiten(inner, solved)
     modes = block.astype(jnp.bfloat16)
+    fetch.wait()
     planes, _, columns = snap_ref.shape
     lanes = 128
     rows_y = columns // lanes
@@ -379,7 +396,13 @@
     pieces = pl.pallas_call(
         functools.partial(modes_kernel, float(subs * cells), rows_z),
         out_shape=jax.ShapeDtypeStruct((owner_count, modes, cells // owner_count), jnp.bfloat16),
-        compiler_params=pltpu.CompilerParams(vmem_limit_bytes=32 * 2**20),
+        in_specs=[pl.BlockSpec(memory_space=pltpu.VMEM)] * (subs + 1)
+        + [pl.BlockSpec(memory_space=pl.ANY)],
+        scratch_shapes=[
+            pltpu.VMEM(snapshots.shape, snapshots.dtype),
+            pltpu.SemaphoreType.DMA,
+        ],
+        compiler_params=pltpu.CompilerParams(vmem_limit_bytes=56 * 2**20),
     )(*parts, start_block[0].T, snapshots)
     received = lax.all_to_all(pieces, "nbhd", split_axis=0, concat_axis=0, tiled=True)
     column = lax.dynamic_slice_in_dim(correlation, lax.axis_index("nbhd"), 1, axis=1)[:, 0]

time: 112 us -> 121 us (1.080)
  waiting for transfers between devices: 29.3 us -> 43.3 us
  Pallas kernels: 39.6 us -> 48.1 us
  starting transfers between devices: 23.2 us -> 16.2 us
  local copies, waits for them, and re-layouts: 12.8 us -> 7.72 us
  other arithmetic: 6.55 us -> 5.21 us
    ppermute x4 -> x2, waiting for transfers between devices: 15.7 us -> 29.8 us  [shift_planes(): return lax.ppermute(array, 'sub', pairs)]
    ppermute x4 -> x2, starting transfers between devices: 13.8 us -> 6.92 us  [shift_planes(): return lax.ppermute(array, 'sub', pairs)]
    pallas_call x1, Pallas kernels: 28.2 us -> 34.6 us  [relax(): pl.pallas_call(relax_kernel, out_shape=[jax.ShapeDtypeStruct((planes, wid...]
    pallas_call x1, Pallas kernels: 11.3 us -> 13.5 us  [on_device(): pl.pallas_call(functools.partial(modes_kernel, float(subs * cells), rows_...]
    unnamed x14 -> x24, local copies, waits for them, and re-layouts: 2.61 us -> 0.66 us
    mul x3, other arithmetic: 2.1 us -> 0.24 us  [coefficients(): rows = [face[own] * share for face, share in zip(faces, counted)]]
    concatenate x0 -> x1, other arithmetic: none -> 1.79 us  [relax(): high = shift_planes(jnp.concatenate([marks, lines[:-half]], axis=0), False)]
  transfers between devices with their start and end apart: 8 -> 6, of which waited for: 6 -> 6; matrix products, arithmetic and copies ran while one was open for 14% -> 0% of each run, Pallas kernels for 0% -> 0%
where the time goes in v4:
time: 121 us
  Pallas kernels  48.1 us (40%)
  waiting for transfers between devices  43.3 us (36%)
  starting transfers between devices  16.2 us (13%)
  local copies, waits for them, and re-layouts  7.72 us (6%)
  other arithmetic  5.21 us (4%)
    pallas_call x1, Pallas kernels, relax(): pl.pallas_call(relax_kernel, out_shape=[jax.ShapeDtypeStruct((planes, wid...  34.6 us
    ppermute x2, waiting for transfers between devices, shift_planes(): return lax.ppermute(array, 'sub', pairs)  29.8 us
    pallas_call x1, Pallas kernels, on_device(): pl.pallas_call(functools.partial(modes_kernel, float(subs * cells), rows_...  13.5 us
    all_to_all x1, waiting for transfers between devices, on_device(): lax.all_to_all(pieces, 'nbhd', split_axis=0, concat_axis=0, tiled=True)  8.15 us
    ppermute x2, starting transfers between devices, shift_planes(): return lax.ppermute(array, 'sub', pairs)  6.92 us
    ppermute x3, starting transfers between devices, on_device(): lax.ppermute(own, 'sub', [(i, (i + shift) % subs) for i in range(subs)])  5.57 us
    ppermute x3, waiting for transfers between devices, on_device(): lax.ppermute(own, 'sub', [(i, (i + shift) % subs) for i in range(subs)])  5.39 us
    all_to_all x1, starting transfers between devices, on_device(): lax.all_to_all(pieces, 'nbhd', split_axis=0, concat_axis=0, tiled=True)  3.74 us
  transfers between devices with their start and end apart: 6, of which 6 were waited for; matrix products, arithmetic and copies ran while one was open for 0% of the time, Pallas kernels for 0%

profile of v4, /device:TPU:0, one launch (start us, length us, event | category | flops | bytes accessed | tf_op | source)
XLA Modules:
  0.0 120.9 jit_solution(15245432305291422075)
XLA Ops:
  0.0 0.8 convert_element_type.44
  0.9 1.9 %fusion.15 = (bf16[56,96,128]{2,1,0:T(8,128)(2,1)S(1)}, bf16[56,96,128]{2,1,0:T(8,128)(2,1)S(1)}) fusion(bf16[64,96,128]{2,1,0:T(8,128)(2,1)} %bitcast.70), kind=kLoop, calls=%fused_computation.61 | loop fusion | bytes 5505024 | tf_op jit(solution)/shard_map/slice | solution.py:240
  2.8 1.8 %pad_maximum_fusion = (bf16[57,96,128]{2,1,0:T(8,128)(2,1)}, bf16[57,96,128]{2,1,0:T(8,128)(2,1)}) fusion(bf16[1,96,128]{2,1,0:T(8,128)(2,1)S(1)} %pad_bitcast_fusion, bf16[56,96,128]{2,1,0:T(8,128)(2,1)S(1)} %get-tuple-element.11, bf16[56,96,128]{2,1,0:T(8,128)(2,1)S(1)} %get-tuple-element.12), kind=kLoop, calls=%fused_computation | loop fusion | flops 1400832 | bytes 5578752 | tf_op jit(solution)/shard_map/concatenate | solution.py:240
  4.6 1.3 %collective-permute-start.1 = (bf16[57,96,128]{2,1,0:T(8,128)(2,1)}, bf16[57,96,128]{2,1,0:T(8,128)(2,1)S(1)}, u32[]{:S(2)}, u32[]{:S(2)}) collective-permute-start(bf16[57,96,128]{2,1,0:T(8,128)(2,1)} %get-tuple-element.30), channel_id=1, source_target_pairs={{1,0},{2,1},{3,2},{5,4},{6,5},{7,6},{9,8},{10,9},{11,10},{13,12},{... | collective-permute-start | bytes 4202504 | tf_op jit(solution)/shard_map/ppermute | solution.py:225
  5.9 5.6 %collective-permute-start = (bf16[57,96,128]{2,1,0:T(8,128)(2,1)}, bf16[57,96,128]{2,1,0:T(8,128)(2,1)S(1)}, u32[]{:S(2)}, u32[]{:S(2)}) collective-permute-start(bf16[57,96,128]{2,1,0:T(8,128)(2,1)} %get-tuple-element.31), channel_id=1, source_target_pairs={{0,1},{1,2},{2,3},{4,5},{5,6},{6,7},{8,9},{9,10},{10,11},{12,13},{... | collective-permute-start | bytes 4202504 | tf_op jit(solution)/shard_map/ppermute | solution.py:225
  11.9 28.6 %collective-permute-done.1.high = bf16[57,96,128]{2,1,0:T(8,128)(2,1)S(1)} collective-permute-done((bf16[57,96,128]{2,1,0:T(8,128)(2,1)}, bf16[57,96,128]{2,1,0:T(8,128)(2,1)S(1)}, u32[]{:S(2)}, u32[]{:S(2)}) %collective-permute-start.1) | collective-permute-done | bytes 1400864 | tf_op jit(solution)/shard_map/ppermute | solution.py:225
  40.5 1.2 collective-permute-done.low
  42.4 0.9 fusion.2
  43.6 0.4 stack.67
  44.0 0.7 pad.14.stiff_rows
  44.8 2.5 %stack.58 = f32[10,16,8,96]{3,2,1,0:T(8,128)S(1)} concatenate(f32[10,16,1,96]{3,2,1,0:T(1,128)S(1)} %bitcast.76, f32[10,16,1,96]{3,2,1,0:T(1,128)S(1)} %bitcast.77, f32[10,16,1,96]{3,2,1,0:T(1,128)S(1)} %bitcast.74, f32[10,16,1,96]{3,2,1,0:T(1,128)S(1)} %bitcast.73, f32[10,16,1,96]{3,2,1,0:T(1,128)S(1)} %bitcast.75, f32[10,16,1,96]{3,2,1,0:T(1,128)S(1)} %bitcast.72, ...), dimensions={2} | concatenate | bytes 983040 | tf_op jit(solution)/shard_map/stack | solution.py:42
  47.3 1.0 pad.13.sweep_rows
  48.3 34.6 %shard_map.73 = (bf16[4,128,2048]{2,1,0:T(8,128)(2,1)}, f32[136,128]{1,0:T(8,128)}) custom-call(bf16[4,16,96,128]{3,2,1,0:T(8,128)(2,1)} %bitcast.71, bf16[57,96,128]{2,1,0:T(8,128)(2,1)} %copy-done.1, bf16[57,96,128]{2,1,0:T(8,128)(2,1)} %copy-done, f32[12,16,8,128]{3,2,1,0:T(8,128)} %pad.13.sweep_rows, f32[4,16,8,128]{3,2,1,0:T(8,128)} %pad.14.stiff_rows, ...), custom_call_target="tpu_custom_call" | custom-call | tf_op jit(solution)/shard_map/pallas_call | solution.py:250
  82.9 4.6 %collective-permute-start.4 = (f32[136,128]{1,0:T(8,128)}, f32[136,128]{1,0:T(8,128)S(1)}, u32[]{:S(2)}, u32[]{:S(2)}) collective-permute-start(f32[136,128]{1,0:T(8,128)} %get-tuple-element.7.refs_0_), channel_id=1, source_target_pairs={{0,3},{1,0},{2,1},{3,2},{4,7},{5,4},{6,5},{7,6},{8,11},{9,8},{10,9... | collective-permute-start | bytes 208904 | tf_op jit(solution)/shard_map/ppermute | solution.py:391
  87.5 0.9 collective-permute-start.2
  88.4 1.3 %collective-permute-done.4.refs_3_ = f32[136,128]{1,0:T(8,128)S(1)} collective-permute-done((f32[136,128]{1,0:T(8,128)}, f32[136,128]{1,0:T(8,128)S(1)}, u32[]{:S(2)}, u32[]{:S(2)}) %collective-permute-start.4) | collective-permute-done | bytes 69664 | tf_op jit(solution)/shard_map/ppermute | solution.py:391
  89.8 3.2 %collective-permute-done.3.refs_2_ = f32[136,128]{1,0:T(8,128)S(1)} collective-permute-done((f32[136,128]{1,0:T(8,128)}, f32[136,128]{1,0:T(8,128)S(1)}, u32[]{:S(2)}, u32[]{:S(2)}) %collective-permute-start.3) | collective-permute-done | bytes 69664 | tf_op jit(solution)/shard_map/ppermute | solution.py:391
  92.9 0.9 collective-permute-done.2.refs_1_
  93.8 0.6 copy-done.10
  94.4 13.5 %shard_map.74 = bf16[8,32,768]{2,1,0:T(8,128)(2,1)} custom-call(f32[136,128]{1,0:T(8,128)} %get-tuple-element.7.refs_0_, f32[136,128]{1,0:T(8,128)} %copy-done.10, f32[136,128]{1,0:T(8,128)} %copy-done.9, f32[136,128]{1,0:T(8,128)} %copy-done.8, f32[32,128]{1,0:T(8,128)} %bitcast.92, bf16[4,128,2048]{2,1,0:T(8,128)(2,1)} %get-tuple-element.8.refs_5_), custom_call_target="tpu_custom_call" | custom-call | tf_op jit(solution)/shard_map/pallas_call | solution.py:396
  108.0 3.7 %all-to-all-start = ((bf16[8,32,768]{2,1,0:T(8,128)(2,1)}), bf16[8,32,768]{2,1,0:T(8,128)(2,1)S(1)}, u32[]{:S(2)}, u32[]{:S(2)}) async-start(bf16[8,32,768]{2,1,0:T(8,128)(2,1)} %shard_map.74), calls=%async_computation | async-start | bytes 786432 | tf_op jit(solution)/shard_map/all_to_all | solution.py:407
  111.7 0.2 fusion.14
  111.9 8.1 %all-to-all-done = bf16[8,32,768]{2,1,0:T(8,128)(2,1)S(1)} async-done(((bf16[8,32,768]{2,1,0:T(8,128)(2,1)}), bf16[8,32,768]{2,1,0:T(8,128)(2,1)S(1)}, u32[]{:S(2)}, u32[]{:S(2)}) %all-to-all-start) | async-done | bytes 393248 | tf_op jit(solution)/shard_map/all_to_all | solution.py:407
  120.1 0.8 multiply_bitcast_fusion
  (55 shorter events, 1.4 us)
Async XLA Ops:
  2.8 39.0 %copy-start.7 = (s32[1,4,16,96]{3,2,1,0:T(8,128)S(1)}, s32[1,4,16,96]{3,2,1,0:T(8,128)}, u32[]{:S(2)}) copy-start(s32[1,4,16,96]{3,2,1,0:T(8,128)} %param.8) | copy-start | bytes 73732
  4.6 35.8 %collective-permute-start.1 = (bf16[57,96,128]{2,1,0:T(8,128)(2,1)}, bf16[57,96,128]{2,1,0:T(8,128)(2,1)S(1)}, u32[]{:S(2)}, u32[]{:S(2)}) collective-permute-start(bf16[57,96,128]{2,1,0:T(8,128)(2,1)} %get-tuple-element.30), channel_id=1, source_target_pairs={{1,0},{2,1},{3,2},{5,4},{6,5},{7,6},{9,8},{10,9},{11,10},{13,12},{... | collective-permute-start | bytes 4202504 | tf_op jit(solution)/shard_map/ppermute | solution.py:225
  5.9 35.8 %collective-permute-start = (bf16[57,96,128]{2,1,0:T(8,128)(2,1)}, bf16[57,96,128]{2,1,0:T(8,128)(2,1)S(1)}, u32[]{:S(2)}, u32[]{:S(2)}) collective-permute-start(bf16[57,96,128]{2,1,0:T(8,128)(2,1)} %get-tuple-element.31), channel_id=1, source_target_pairs={{0,1},{1,2},{2,3},{4,5},{5,6},{6,7},{8,9},{9,10},{10,11},{12,13},{... | collective-permute-start | bytes 4202504 | tf_op jit(solution)/shard_map/ppermute | solution.py:225
  40.5 2.8 %copy-start = (bf16[57,96,128]{2,1,0:T(8,128)(2,1)}, bf16[57,96,128]{2,1,0:T(8,128)(2,1)S(1)}, u32[]{:S(2)}) copy-start(bf16[57,96,128]{2,1,0:T(8,128)(2,1)S(1)} %collective-permute-done.1.high) | copy-start | bytes 4202500
  41.7 1.5 %copy-start.1 = (bf16[57,96,128]{2,1,0:T(8,128)(2,1)}, bf16[57,96,128]{2,1,0:T(8,128)(2,1)S(1)}, u32[]{:S(2)}) copy-start(bf16[57,96,128]{2,1,0:T(8,128)(2,1)S(1)} %collective-permute-done.low) | copy-start | bytes 4202500
  43.3 1.5 %copy-start.2 = (f32[10,16,96]{2,1,0:T(8,128)S(1)}, f32[10,16,96]{2,1,0:T(8,128)}, u32[]{:S(2)}) copy-start(f32[10,16,96]{2,1,0:T(8,128)} %get-tuple-element.15) | copy-start | bytes 184324
  43.3 1.5 %copy-start.3 = (f32[10,16,96]{2,1,0:T(8,128)S(1)}, f32[10,16,96]{2,1,0:T(8,128)}, u32[]{:S(2)}) copy-start(f32[10,16,96]{2,1,0:T(8,128)} %get-tuple-element.16) | copy-start | bytes 184324
  43.3 1.5 %copy-start.4 = (f32[10,16,96]{2,1,0:T(8,128)S(1)}, f32[10,16,96]{2,1,0:T(8,128)}, u32[]{:S(2)}) copy-start(f32[10,16,96]{2,1,0:T(8,128)} %get-tuple-element.23) | copy-start | bytes 184324
  43.3 1.5 %copy-start.5 = (f32[10,16,96]{2,1,0:T(8,128)S(1)}, f32[10,16,96]{2,1,0:T(8,128)}, u32[]{:S(2)}) copy-start(f32[10,16,96]{2,1,0:T(8,128)} %get-tuple-element.24) | copy-start | bytes 184324
  43.3 1.5 %copy-start.6 = (f32[10,16,96]{2,1,0:T(8,128)S(1)}, f32[10,16,96]{2,1,0:T(8,128)}, u32[]{:S(2)}) copy-start(f32[10,16,96]{2,1,0:T(8,128)} %get-tuple-element.25) | copy-start | bytes 184324
  82.9 6.9 %collective-permute-start.4 = (f32[136,128]{1,0:T(8,128)}, f32[136,128]{1,0:T(8,128)S(1)}, u32[]{:S(2)}, u32[]{:S(2)}) collective-permute-start(f32[136,128]{1,0:T(8,128)} %get-tuple-element.7.refs_0_), channel_id=1, source_target_pairs={{0,3},{1,0},{2,1},{3,2},{4,7},{5,4},{6,5},{7,6},{8,11},{9,8},{10,9... | collective-permute-start | bytes 208904 | tf_op jit(solution)/shard_map/ppermute | solution.py:391
  87.5 5.4 %collective-permute-start.3 = (f32[136,128]{1,0:T(8,128)}, f32[136,128]{1,0:T(8,128)S(1)}, u32[]{:S(2)}, u32[]{:S(2)}) collective-permute-start(f32[136,128]{1,0:T(8,128)} %get-tuple-element.7.refs_0_), channel_id=1, source_target_pairs={{0,2},{1,3},{2,0},{3,1},{4,6},{5,7},{6,4},{7,5},{8,10},{9,11},{10,... | collective-permute-start | bytes 208904 | tf_op jit(solution)/shard_map/ppermute | solution.py:391
  87.5 6.3 %collective-permute-start.2 = (f32[136,128]{1,0:T(8,128)}, f32[136,128]{1,0:T(8,128)S(1)}, u32[]{:S(2)}, u32[]{:S(2)}) collective-permute-start(f32[136,128]{1,0:T(8,128)} %get-tuple-element.7.refs_0_), channel_id=1, source_target_pairs={{0,1},{1,2},{2,3},{3,0},{4,5},{5,6},{6,7},{7,4},{8,9},{9,10},{10,1... | collective-permute-start | bytes 208904 | tf_op jit(solution)/shard_map/ppermute | solution.py:391
  89.8 4.1 %copy-start.8 = (f32[136,128]{1,0:T(8,128)}, f32[136,128]{1,0:T(8,128)S(1)}, u32[]{:S(2)}) copy-start(f32[136,128]{1,0:T(8,128)S(1)} %collective-permute-done.4.refs_3_) | copy-start | bytes 208900
  92.9 0.9 copy-start.9
  93.8 0.6 copy-start.10
  94.4 17.3 %copy-start.11 = (s32[8,8]{1,0:T(8,128)S(1)}, s32[8,8]{1,0:T(8,128)}, u32[]{:S(2)}) copy-start(s32[8,8]{1,0:T(8,128)} %param.13) | copy-start | bytes 772
  108.0 12.1 %all-to-all-start = ((bf16[8,32,768]{2,1,0:T(8,128)(2,1)}), bf16[8,32,768]{2,1,0:T(8,128)(2,1)S(1)}, u32[]{:S(2)}, u32[]{:S(2)}) async-start(bf16[8,32,768]{2,1,0:T(8,128)(2,1)} %shard_map.74), calls=%async_computation | async-start | bytes 786432 | tf_op jit(solution)/shard_map/all_to_all | solution.py:407

commit v5 on v3

v5 whole, which is shorter than its diff:
```python
import functools

import jax
import jax.numpy as jnp
from jax import lax
from jax.experimental import pallas as pl
from jax.experimental.pallas import tpu as pltpu
from jax.sharding import PartitionSpec as P

SWEEPS = 3
ITERS = 4


def harmonic(left_k, right_k):
    return 2.0 * left_k * right_k / (left_k + right_k)


LANES = 128


def weight_rows(kappa_ref, weights, stiff_rows, lines, first, last, rows_y, rows_z):
    total = kappa_ref.shape[0]
    depth = (total - lines) // 2
    kappa = kappa_ref[...]
    shape = kappa.shape
    line = lax.broadcasted_iota(jnp.int32, shape, 0)
    row_z = lax.broadcasted_iota(jnp.int32, shape, 1)
    row_y = lax.rem(line, rows_y)

    def face(other, edge):
        return jnp.where(edge, kappa, harmonic(kappa, other))

    top = depth + lines
    faces = [
        face(pltpu.roll(kappa, rows_y, 0), (line >= depth) & (line < depth + rows_y * first)),
        face(pltpu.roll(kappa, total - rows_y, 0), (line >= top - rows_y * last) & (line < top)),
        face(pltpu.roll(kappa, 1, 0), row_y == 0),
        face(pltpu.roll(kappa, total - 1, 0), row_y == rows_y - 1),
        face(pltpu.roll(kappa, 1, 1), row_z == 0),
        face(pltpu.roll(kappa, LANES - 1, 1), row_z == rows_z - 1),
    ]
    denom = faces[0] + faces[1] + faces[2] + faces[3] + faces[4] + faces[5]
    outside = (line < depth * first) | (line >= total - depth * last) | (row_z >= rows_z)
    scale = jnp.where(outside, 0.0, 1.0 / denom)
    for k in range(6):
        weights[k] = faces[k] * scale
    upper = row_y >= rows_y // 2
    low_edge = line < depth + rows_y
    high_edge = line >= top - rows_y
    low_cross = jnp.where(upper, 2.0 - 2.0 * first.astype(jnp.float32), 0.0)
    high_cross = jnp.where(upper, 0.0, 2.0 - 2.0 * last.astype(jnp.float32))
    shares = [
        jnp.where(low_edge, low_cross, 1.0),
        jnp.where(high_edge, high_cross, 1.0),
        jnp.where(row_y == 0, 0.0, 1.0),
        jnp.where(row_y == rows_y - 1, 0.0, 1.0),
        jnp.where(row_z == 0, 0.0, 1.0),
        jnp.where(row_z == rows_z - 1, 0.0, 1.0),
    ]
    rows = [item * share for item, share in zip(faces, shares)] + [denom, kappa * (1.0 / 16.0)]
    inside = (row_z < rows_z)[depth:top]
    for k in range(8):
        stiff_rows[k] = jnp.where(inside, rows[k][depth:top], 0.0)


def turned(lines):
    width = lines.shape[1]
    row = lax.broadcasted_iota(jnp.int32, (width, width), 0)
    col = lax.broadcasted_iota(jnp.int32, (width, width), 1)
    eye = jnp.where(row == col, 1.0, 0.0).astype(jnp.bfloat16)
    return lax.dot_general(eye, lines, (((1,), (1,)), ((), ())), preferred_element_type=jnp.float32)


def place(line, rows_y):
    return lax.div(line, rows_y), lax.rem(line, rows_y)


def fill(state, source, skip, count, first_line, pad_rows):
    rows_y = pad_rows.shape[0]
    group = 4

    def body(i, carry):
        done = []
        for j in range(0, group, 2):
            at = i * group + j
            e, y = place(first_line + at, rows_y)
            lines = [source[skip + at], pad_rows[y], source[skip + at + 1], pad_rows[y + 1]]
            done.append((e, y, turned(jnp.concatenate(lines, axis=0))))
        for e, y, both in done:
            state[e, y + 1] = both[:, :LANES]
            state[e, y + 2] = both[:, LANES:]
        return carry

    lax.fori_loop(0, count // group, body, 0)


def neighbour_sum(src, e, y, rows, some, middle):
    return (
        rows[0] * src[e - 1, y + 1, some]
        + rows[1] * src[e + 1, y + 1, some]
        + rows[2] * src[e, y, some]
        + rows[3] * src[e, y + 2, some]
        + rows[4] * pltpu.roll(middle, 1, 1)
        + rows[5] * pltpu.roll(middle, LANES - 1, 1)
    )


PART = 64


def relax_lines(src, dst, weights, first_line, count, rows_y, rows_z, keep):
    width = src.shape[2]
    group = 4
    valid = lax.broadcasted_iota(jnp.int32, (PART, LANES), 1) < rows_z

    def body(i, carry):
        waiting = []
        for j in range(group):
            line = first_line + i * group + j
            e, y = place(line, rows_y)
            rows = [weights[k, pl.ds(line, 1)] for k in range(6)]
            for start in range(0, width, PART):
                some = pl.ds(start, PART)
                middle = src[e, y + 1, some]
                fresh = neighbour_sum(src, e, y, rows, some, middle)
                fresh = fresh.astype(jnp.bfloat16).astype(jnp.float32)
                if keep:
                    fresh = jnp.where(valid, fresh, middle)
                waiting.append((e, y, some, fresh))
                if len(waiting) > 1:
                    e0, y0, some0, value = waiting.pop(0)
                    dst[e0, y0 + 1, some0] = value
        for e0, y0, some0, value in waiting:
            dst[e0, y0 + 1, some0] = value
        return carry

    lax.fori_loop(0, count // group, body, 0)


def near_kernel(
    flags,
    own,
    near_a,
    near_b,
    classes,
    y_vals,
    z_vals,
    face_ids,
    hand_a,
    hand_b,
    weights,
    stiff_rows,
    pad_rows,
    state_a,
    state_b,
    kappa,
    sems,
):
    lines, rows_z, width = own.shape
    rows_y = pad_rows.shape[0]
    planes = lines // rows_y
    near = lines // 2
    bf16 = jnp.bfloat16
    even, first, last = flags[0], flags[1], flags[2]
    one = jnp.int32(1)

    def powers(marks):
        return jnp.left_shift(one, 2 * marks).astype(jnp.float32)

    base_a = pl.multiple_of(even * (2 * lines), 8)
    base_b = pl.multiple_of((1 - even) * (2 * lines), 8)
    kappa[...] = jnp.ones(kappa.shape, jnp.float32)
    kappa[pl.ds(lines, lines), pl.ds(0, rows_z)] = powers(classes[...])
    kappa[pl.ds(base_a, lines)] = powers(near_a[0][:lines].astype(jnp.float32).astype(jnp.int32))
    kappa[pl.ds(base_b, lines)] = powers(near_b[0][:lines].astype(jnp.float32).astype(jnp.int32))
    weight_rows(kappa, weights, stiff_rows, lines, first, last, rows_y, rows_z)

    ids = face_ids[...]
    picks = [(ids == side).astype(jnp.float32) for side in range(4)]
    spare = LANES - rows_z
    spot = lax.broadcasted_iota(jnp.int32, (spare, width), 0)
    z_all = z_vals[...].astype(jnp.float32)
    z_low = z_all * picks[2]
    z_high = z_all * picks[3]
    for y in range(rows_y):
        rows = jnp.where(spot == 0, z_high[y : y + 1], 0.0)
        pad_rows[y] = jnp.where(spot == spare - 1, z_low[y : y + 1], rows).astype(bf16)
    y_all = y_vals[...].astype(jnp.float32)
    blank = jnp.zeros((spare, width), bf16)
    ghost_low = turned(jnp.concatenate([(y_all * picks[0]).astype(bf16), blank], axis=0))
    ghost_high = turned(jnp.concatenate([(y_all * picks[1]).astype(bf16), blank], axis=0))
    for e in range(planes - 2, 2 * planes + 2):
        for state in (state_a, state_b):
            state[e, 0] = ghost_low
            state[e, rows_y + 1] = ghost_high

    fill(state_a, own, 0, lines, lines, pad_rows)
    fill(state_a, near_a, 1, near, near + even * (lines + near), pad_rows)
    fill(state_a, near_b, 1, near, near + (1 - even) * (lines + near), pad_rows)

    sent = []

    def send(state, hand, e, count, offset):
        copy = pltpu.make_async_copy(
            state.at[pl.ds(e, count)], hand.at[pl.ds(e - offset, count)], sems.at[len(sent)]
        )
        copy.start()
        sent.append(copy)

    step = functools.partial(relax_lines, weights=weights, rows_y=rows_y, rows_z=rows_z)
    send(state_a, hand_a, planes - 2, 2, planes - 2)
    send(state_a, hand_a, 2 * planes, 2, planes - 2)
    step(state_a, state_b, first_line=lines - rows_y, count=lines + 2 * rows_y, keep=True)
    send(state_b, hand_b, planes - 1, 2, planes - 1)
    send(state_b, hand_b, 2 * planes - 1, 2, planes - 1)
    step(state_b, state_a, first_line=lines, count=lines, keep=True)
    send(state_a, hand_a, planes, planes, planes - 2)
    step(state_a, state_b, first_line=lines + rows_y, count=lines - 2 * rows_y, keep=False)
    send(state_b, hand_b, planes + 1, planes - 2, planes - 1)
    for copy in sent:
        copy.wait()


def far_kernel(
    flags,
    far_a,
    far_b,
    weights,
    stiff_rows,
    pad_rows,
    hand_a,
    hand_b,
    snap,
    gram,
    state_a,
    state_b,
    both,
    sems,
):
    planes, width, _ = snap.shape
    rows_y = pad_rows.shape[0]
    rows_z = far_a.shape[1]
    lines = planes * rows_y
    half = rows_y // 2
    even = flags[0]
    bf16 = jnp.bfloat16
    taken = []

    def take(dst, src):
        copy = pltpu.make_async_copy(src, dst, sems.at[len(taken)])
        copy.start()
        taken.append(copy)

    top = rows_y + 1
    a_off, b_off = planes - 2, planes - 1
    take(state_a.at[pl.ds(a_off, 2)], hand_a.at[pl.ds(0, 2)])
    take(state_a.at[pl.ds(2 * planes, 2)], hand_a.at[pl.ds(2 * planes - a_off, 2)])
    take(state_a.at[1, top], hand_a.at[0, top])
    take(state_a.at[3 * planes - 2, 0], hand_a.at[0, 0])
    take(state_b.at[pl.ds(b_off, 2)], hand_b.at[pl.ds(0, 2)])
    take(state_b.at[pl.ds(2 * planes - 1, 2)], hand_b.at[pl.ds(2 * planes - 1 - b_off, 2)])
    take(state_b.at[2, top], hand_b.at[0, top])
    take(state_b.at[3 * planes - 3, 0], hand_b.at[0, 0])
    take(state_a.at[pl.ds(planes, planes)], hand_a.at[pl.ds(planes - a_off, planes)])
    take(state_b.at[pl.ds(planes + 1, planes - 2)], hand_b.at[pl.ds(planes + 1 - b_off, planes - 2)])

    far = far_a.shape[0]
    low_line = half
    high_line = 3 * lines - half - far
    fill(state_a, far_a, 0, far, low_line + even * (high_line - low_line), pad_rows)
    fill(state_a, far_b, 0, far, high_line - even * (high_line - low_line), pad_rows)

    waits = {1: range(0, 4), 2: range(4, 8), 3: range(8, 9)}
    buffers = (state_a, state_b)
    for sweep in range(1, SWEEPS + 1):
        for k in waits[sweep]:
            taken[k].wait()
        src, dst = buffers[(sweep - 1) % 2], buffers[sweep % 2]
        for first_line in (half + sweep * rows_y, 3 * lines - half - far - sweep * rows_y):
            relax_lines(src, dst, weights, first_line, far, rows_y, rows_z, sweep < SWEEPS)
    taken[9].wait()
    final = buffers[SWEEPS % 2]

    def stiffness(p, total):
        e = planes + p
        waiting = []

        def store(y, some, below, values):
            spot = pl.ds(y * LANES, LANES)
            snap[p, some, spot] = values[0]
            both[some, spot] = values[1]
            both[below, spot] = values[2]

        for y in range(rows_y):
            rows = [stiff_rows[k, pl.ds(p * rows_y + y, 1)] for k in range(8)]
            for start in range(0, width, PART):
                some = pl.ds(start, PART)
                middle = final[e, y + 1, some]
                numer = neighbour_sum(final, e, y, rows, some, middle)
                values = [middle, rows[7] * middle, rows[6] * middle - numer]
                values = [value.astype(bf16) for value in values]
                waiting.append((y, some, pl.ds(width + start, PART), values))
                if len(waiting) > 1:
                    store(*waiting.pop(0))
        for item in waiting:
            store(*item)
        return total + lax.dot_general(
            snap[p], both[...], (((1,), (1,)), ((), ())), preferred_element_type=jnp.float32
        )

    total = lax.fori_loop(0, planes, stiffness, jnp.zeros((width, 2 * width), jnp.float32))
    mass = total[:, :width]
    stiff = total[:, width:]
    stiff = stiff + stiff.T
    row = lax.broadcasted_iota(jnp.int32, (width, width), 0)
    col = lax.broadcasted_iota(jnp.int32, (width, width), 1)
    gram[pl.ds(0, width)] = jnp.where(row > col, stiff, mass)
    diagonal = jnp.sum(jnp.where(row == col, stiff, 0.0), axis=0, keepdims=True)
    gram[pl.ds(width, 8)] = jnp.broadcast_to(diagonal, (8, width))


def swap(array, start):
    count = lax.axis_size("sub")
    pairs = [(i, i + 1) for i in range(start, count - 1, 2)]
    return lax.ppermute(array, "sub", pairs + [(j, i) for i, j in pairs])


def relax(initial, classes, y_vals, z_vals, face_ids):
    planes, rows_y, rows_z, width = initial.shape
    index = lax.axis_index("sub")
    subs = lax.axis_size("sub")
    even = (index + 1) % 2
    flags = jnp.stack([even, index == 0, index == subs - 1, 0]).astype(jnp.int32)
    lines = initial.reshape(planes * rows_y, rows_z, width)
    count = planes * rows_y
    near, far, half = 2 * rows_y, 2 * rows_y - rows_y // 2, rows_y // 2
    marks = classes.astype(jnp.bfloat16).reshape(1, count, rows_z)
    marks = jnp.pad(marks, ((0, 0), (0, rows_z - count), (0, width - rows_z)))

    def near_part(upward):
        part = lax.dynamic_slice_in_dim(lines, upward * (count - near), near, axis=0)
        return jnp.concatenate([marks, part], axis=0)

    def far_part(upward):
        start = upward * half + (1 - upward) * near
        return lax.dynamic_slice_in_dim(lines, start, far, axis=0)

    near_a = swap(near_part(even), 0)
    near_b = swap(near_part(1 - even), 1)
    far_a = swap(far_part(even), 0)
    far_b = swap(far_part(1 - even), 1)

    vmem = pl.BlockSpec(memory_space=pltpu.VMEM)
    smem = pl.BlockSpec(memory_space=pltpu.SMEM)
    hbm = pl.BlockSpec(memory_space=pltpu.HBM)
    state = pltpu.VMEM((3 * planes, rows_y + 2, width, LANES), jnp.float32)
    params = pltpu.CompilerParams(vmem_limit_bytes=48 * 2**20)
    hand_a, hand_b, weights, stiff_rows, pad_rows = pl.pallas_call(
        near_kernel,
        out_shape=[
            jax.ShapeDtypeStruct((planes + 4, rows_y + 2, width, LANES), jnp.float32),
            jax.ShapeDtypeStruct((planes + 2, rows_y + 2, width, LANES), jnp.float32),
            jax.ShapeDtypeStruct((6, 3 * count, LANES), jnp.float32),
            jax.ShapeDtypeStruct((8, count, LANES), jnp.float32),
            jax.ShapeDtypeStruct((rows_y, LANES - rows_z, width), jnp.bfloat16),
        ],
        in_specs=[smem] + [vmem] * 7,
        out_specs=[hbm, hbm, vmem, vmem, vmem],
        scratch_shapes=[
            state,
            state,
            pltpu.VMEM((3 * count, LANES), jnp.float32),
            pltpu.SemaphoreType.DMA((6,)),
        ],
        compiler_params=params,
    )(
        flags,
        lines,
        near_a,
        near_b,
        classes.reshape(count, rows_z),
        y_vals,
        z_vals,
        face_ids[None],
    )
    return pl.pallas_call(
        far_kernel,
        out_shape=[
            jax.ShapeDtypeStruct((planes, width, rows_y * LANES), jnp.bfloat16),
            jax.ShapeDtypeStruct((width + 8, width), jnp.float32),
        ],
        in_specs=[smem] + [vmem] * 5 + [hbm] * 2,
        out_specs=[vmem, vmem],
        scratch_shapes=[
            state,
            state,
            pltpu.VMEM((2 * width, rows_y * LANES), jnp.bfloat16),
            pltpu.SemaphoreType.DMA((10,)),
        ],
        compiler_params=params,
    )(flags, far_a, far_b, weights, stiff_rows, pad_rows, hand_a, hand_b)


def lane_copy(tile, lane):
    return jnp.broadcast_to(tile[:, lane : lane + 1], (8, 128))


def row_copy(tile, row):
    return jnp.broadcast_to(tile[row : row + 1, :], (8, tile.shape[1]))


def solve_spd(left, right):
    size = left.shape[0]
    count = size // 8
    sub = lax.broadcasted_iota(jnp.int32, (8, 128), 0)
    lhs = [left[8 * t : 8 * t + 8] for t in range(count)]
    rhs = [right[8 * t : 8 * t + 8] for t in range(count)]
    for k in range(count):
        cols = [lane_copy(lhs[k], 8 * k + j) for j in range(8)]
        panel_l, panel_r = lhs[k], rhs[k]
        for j in range(8):
            recip = 1.0 / row_copy(cols[j], j)
            here = sub == j
            mult = jnp.where(here, recip, -cols[j] * recip)
            for l in range(j + 1, 8):
                cols[l] = jnp.where(here, 0.0, cols[l]) + mult * row_copy(cols[l], j)
            panel_l = jnp.where(here, 0.0, panel_l) + mult * row_copy(panel_l, j)
            panel_r = jnp.where(here, 0.0, panel_r) + mult * row_copy(panel_r, j)
        rows_l = [row_copy(panel_l, j) for j in range(8)]
        rows_r = [row_copy(panel_r, j) for j in range(8)]
        order = list(range(k + 1, count)) + list(range(k))
        for t in order:
            tile_cols = [lane_copy(lhs[t], 8 * k + j) for j in range(8)]
            if k + 1 < count:
                lhs[t] = lhs[t] - tree([tile_cols[j] * rows_l[j] for j in range(8)])
            rhs[t] = rhs[t] - tree([tile_cols[j] * rows_r[j] for j in range(8)])
        lhs[k], rhs[k] = panel_l, panel_r
    return jnp.concatenate(rhs, axis=0)


def tree(terms):
    while len(terms) > 1:
        terms = [a + b for a, b in zip(terms[::2], terms[1::2])] + terms[len(terms) & ~1 :]
    return terms[0]


def whiten(inner, block):
    size = inner.shape[0]
    count = size // 8
    sub = lax.broadcasted_iota(jnp.int32, (8, 128), 0)
    lhs = [inner[8 * t : 8 * t + 8] for t in range(count)]
    rhs = [block[8 * t : 8 * t + 8] for t in range(count)]
    done = []
    for k in range(count):
        live = range(k, count)
        cols = {t: [lane_copy(lhs[t], 8 * k + j) for j in range(8)] for t in live}
        scale = None
        for j in range(8):
            pivot = row_copy(cols[k][j], j)
            recip = 1.0 / pivot
            root = lax.rsqrt(pivot)
            scale = root if scale is None else jnp.where(sub >= j, root, scale)
            head = {l: row_copy(cols[k][l], j) for l in range(j + 1, 8)}
            row_l, row_r = row_copy(lhs[k], j), row_copy(rhs[k], j)
            for t in live:
                mult = cols[t][j] * recip
                if t == k:
                    mult = jnp.where(sub > j, mult, 0.0)
                for l in range(j + 1, 8):
                    cols[t][l] = cols[t][l] - mult * head[l]
                lhs[t] = lhs[t] - mult[:, : row_l.shape[1]] * row_l
                rhs[t] = rhs[t] - mult * row_r
        done.append(rhs[k] * scale)
    return jnp.concatenate(done, axis=0)


def dot(a, b, dims):
    return lax.dot_general(
        a, b, (dims, ((), ())), precision=lax.Precision.HIGHEST, preferred_element_type=jnp.float32
    )


def modes_kernel(cell_count, rows_z, *refs):
    *part_refs, start_ref, snap_hbm, out_ref, snap_ref, sem = refs
    fetch = pltpu.make_async_copy(snap_hbm, snap_ref, sem)
    fetch.start()
    total = part_refs[0][...]
    for part in part_refs[1:]:
        total = total + part[...]
    width = total.shape[1]
    row = lax.broadcasted_iota(jnp.int32, (width, width), 0)
    col = lax.broadcasted_iota(jnp.int32, (width, width), 1)
    packed = total[:width]
    turned = packed.T
    mass = jnp.where(row <= col, packed, turned) * (1.0 / cell_count)
    stiff = jnp.where(row > col, packed, jnp.where(row < col, turned, total[width : width + 1]))
    stiff = stiff * (0.5 / cell_count)
    step = solve_spd(stiff, mass)
    form = dot(step, dot(mass, step, ((1,), (0,))), ((0,), (0,)))
    block = start_ref[...]
    for _ in range(ITERS):
        weighted = dot(block, form, ((1,), (0,)))
        solved = dot(block, step, ((1,), (1,)))
        inner = dot(weighted, block, ((1,), (1,)))
        block = whiten(inner, solved)
    modes = block.astype(jnp.bfloat16)
    fetch.wait()
    planes, _, columns = snap_ref.shape
    lanes = LANES
    rows_y = columns // lanes
    piece_rows = planes * rows_y // out_ref.shape[0]
    for p in range(planes):
        basis = jnp.dot(modes, snap_ref[p], preferred_element_type=jnp.float32)
        for y in range(rows_y):
            piece, spot = divmod(p * rows_y + y, piece_rows)
            out_ref[piece, :, pl.ds(spot * rows_z, rows_z)] = basis[
                :, y * lanes : y * lanes + rows_z
            ].astype(jnp.bfloat16)


def on_device(snap_init, channel_map, yface_vals, zface_vals, face_of, start_block, correlation):
    subs = lax.axis_size("sub")
    owner_count = lax.axis_size("nbhd")
    planes, rows_y, rows_z, width = snap_init.shape[1:]
    snapshots, own = relax(
        snap_init[0], channel_map[0], yface_vals[0], zface_vals[0], face_of[0]
    )
    parts = [own] + [
        lax.ppermute(own, "sub", [(i, (i + shift) % subs) for i in range(subs)])
        for shift in range(1, subs)
    ]
    cells = planes * rows_y * rows_z
    modes = start_block.shape[-1]
    pieces = pl.pallas_call(
        functools.partial(modes_kernel, float(subs * cells), rows_z),
        out_shape=jax.ShapeDtypeStruct((owner_count, modes, cells // owner_count), jnp.bfloat16),
        in_specs=[pl.BlockSpec(memory_space=pltpu.VMEM)] * (subs + 1)
        + [pl.BlockSpec(memory_space=pltpu.HBM)],
        scratch_shapes=[
            pltpu.VMEM(snapshots.shape, snapshots.dtype),
            pltpu.SemaphoreType.DMA,
        ],
        compiler_params=pltpu.CompilerParams(vmem_limit_bytes=24 * 2**20),
    )(*parts, start_block[0].T, snapshots)
    received = lax.all_to_all(pieces, "nbhd", split_axis=0, concat_axis=0, tiled=True)
    column = lax.dynamic_slice_in_dim(correlation, lax.axis_index("nbhd"), 1, axis=1)[:, 0]
    result = received * column.astype(jnp.bfloat16)[:, None, None]
    return result[None, None]


def solution(mesh):
    return jax.shard_map(
        on_device,
        mesh=mesh,
        in_specs=(
            P("nbhd", "sub", None, None, None),
            P("nbhd", "sub", None, None),
            P("nbhd", None, None),
            P("nbhd", None, None),
            P("nbhd", None),
            P("nbhd", None, None),
            P(),
        ),
        out_specs=P("nbhd", "sub", None, None, None),
        check_vma=False,
    )
```

time: 112 us -> 100 us (0.89)
  local copies, waits for them, and re-layouts: 12.8 us -> 2.61 us
  Pallas kernels: 39.6 us -> 47.6 us
  starting transfers between devices: 23.2 us -> 16.9 us
  other arithmetic: 6.55 us -> 3.16 us
    pallas_call x1 -> x2, Pallas kernels: 28.2 us -> 36.1 us  [the longest x1 19.3 us: relax(): pl.pallas_call(near_kernel, out_shape=[jax.ShapeDtypeStruct((planes + 4,...]
    ppermute x4, starting transfers between devices: 13.8 us -> 9.17 us  [swap(): return lax.ppermute(array, 'sub', pairs + [(j, i) for i, j in pairs])]
    another operation x3 -> x0, local copies, waits for them, and re-layouts: 4.57 us -> none  [the longest x2 3.35 us: coefficients(): sweep = jnp.stack([face * scale for face in faces] + [empty, empty], axis=2)]
    mul x6 -> x0, other arithmetic: 4.41 us -> none  [the longest x3 2.1 us: coefficients(): rows = [face[own] * share for face, share in zip(faces, counted)]]
    slice x4 -> x0, local copies, waits for them, and re-layouts: 3.75 us -> none  [the longest x1 3.04 us: relax(): high = shift_planes(lines[:-half], False)]
    dynamic_slice x0 -> x2, local copies, waits for them, and re-layouts: none -> 2.58 us  [the longest x1 1.47 us: near_part(): lax.dynamic_slice_in_dim(lines, upward * (count - near), near, axis=0)]
    unnamed x14, local copies, waits for them, and re-layouts: 2.61 us -> 0.03 us
    pad x2 -> x0, local copies, waits for them, and re-layouts: 1.71 us -> none  [the longest x1 0.98 us: coefficients(): sweep = jnp.pad(sweep, ((1, 1), (0, 0), (0, 0), (0, lanes - rows_z)))]
  transfers between devices with their start and end apart: 8 -> 8, of which waited for: 6 -> 5; matrix products, arithmetic and copies ran while one was open for 14% -> 1% of each run, Pallas kernels for 0% -> 19%
where the time goes in v5:
time: 100 us; the launch traced here: 99.7 us
  Pallas kernels  47.6 us (48%)
  waiting for transfers between devices  29.3 us (29%)
  starting transfers between devices  16.9 us (17%)
  other arithmetic  3.16 us (3%)
  local copies, waits for them, and re-layouts  2.61 us (3%)
    pallas_call x1, Pallas kernels, relax(): pl.pallas_call(near_kernel, out_shape=[jax.ShapeDtypeStruct((planes + 4,...  19.3 us
    pallas_call x1, Pallas kernels, relax(): pl.pallas_call(far_kernel, out_shape=[jax.ShapeDtypeStruct((planes, width...  16.8 us
    ppermute x4, waiting for transfers between devices, swap(): return lax.ppermute(array, 'sub', pairs + [(j, i) for i, j in pairs])  15.5 us
    pallas_call x1, Pallas kernels, on_device(): pl.pallas_call(functools.partial(modes_kernel, float(subs * cells), rows_...  11.5 us
    ppermute x4, starting transfers between devices, swap(): return lax.ppermute(array, 'sub', pairs + [(j, i) for i, j in pairs])  9.17 us
    all_to_all x1, waiting for transfers between devices, on_device(): lax.all_to_all(pieces, 'nbhd', split_axis=0, concat_axis=0, tiled=True)  8.15 us
    ppermute x3, waiting for transfers between devices, on_device(): lax.ppermute(own, 'sub', [(i, (i + shift) % subs) for i in range(subs)])  5.66 us
    ppermute x3, starting transfers between devices, on_device(): lax.ppermute(own, 'sub', [(i, (i + shift) % subs) for i in range(subs)])  4.02 us
  transfers between devices with their start and end apart: 8, of which 5 were waited for; matrix products, arithmetic and copies ran while one was open for 1% of the time, Pallas kernels for 19%

profile of v5, /device:TPU:0, one launch (start us, length us, event | category | flops | bytes accessed | tf_op | source)
XLA Modules:
  0.0 99.7 jit_solution(14897578880729094686)
XLA Ops:
  0.0 0.8 convert_element_type.27
  0.8 1.5 %constant_dynamic-slice_fusion = (bf16[32,96,128]{2,1,0:T(8,128)(2,1)S(1)}, bf16[32,96,128]{2,1,0:T(8,128)(2,1)S(1)}) fusion(bf16[64,96,128]{2,1,0:T(8,128)(2,1)} %bitcast.13, s32[]{:T(128)S(6)} %select_n.26, s32[]{:T(128)S(6)} %select_n.25), kind=kLoop, calls=%fused_computation.7 | loop fusion | bytes 3145736 | tf_op jit(solution)/shard_map/dynamic_slice | solution.py:341
  2.2 0.0 copy-start
  2.3 1.3 %fusion.2 = (bf16[33,96,128]{2,1,0:T(8,128)(2,1)}, bf16[33,96,128]{2,1,0:T(8,128)(2,1)}) fusion(bf16[1,64,96]{2,1,0:T(8,128)(2,1)S(1)} %bitcast.20, bf16[32,96,128]{2,1,0:T(8,128)(2,1)S(1)} %get-tuple-element.19, bf16[32,96,128]{2,1,0:T(8,128)(2,1)S(1)} %get-tuple-element.20), kind=kLoop, calls=%fused_computation.3 | loop fusion | flops 3649536 | bytes 3207168 | tf_op jit(solution)/shard_map/concatenate | solution.py:342
  3.6 0.8 collective-permute-start.3
  4.4 5.9 %collective-permute-start.2 = (bf16[33,96,128]{2,1,0:T(8,128)(2,1)}, bf16[33,96,128]{2,1,0:T(8,128)(2,1)S(1)}, u32[]{:S(2)}, u32[]{:S(2)}) collective-permute-start(bf16[33,96,128]{2,1,0:T(8,128)(2,1)} %get-tuple-element.24), channel_id=1, source_target_pairs={{0,1},{2,3},{1,0},{3,2},{4,5},{6,7},{5,4},{7,6},{8,9},{10,11},{9,8... | collective-permute-start | bytes 2433032 | tf_op jit(solution)/shard_map/ppermute | solution.py:325
  10.3 1.1 %constant_dynamic-slice_fusion.2 = (bf16[24,96,128]{2,1,0:T(8,128)(2,1)}, bf16[24,96,128]{2,1,0:T(8,128)(2,1)}) fusion(bf16[64,96,128]{2,1,0:T(8,128)(2,1)S(1)} %bitcast.14, s32[]{:T(128)S(6)} %select_n.24, s32[]{:T(128)S(6)} %select_n.23), kind=kLoop, calls=%fused_computation.9 | loop fusion | bytes 2359304 | tf_op jit(solution)/shard_map/dynamic_slice | solution.py:346
  11.4 1.5 %collective-permute-start.1 = (bf16[24,96,128]{2,1,0:T(8,128)(2,1)}, bf16[24,96,128]{2,1,0:T(8,128)(2,1)}, u32[]{:S(2)}, u32[]{:S(2)}) collective-permute-start(bf16[24,96,128]{2,1,0:T(8,128)(2,1)} %get-tuple-element.21), channel_id=1, source_target_pairs={{1,2},{2,1},{5,6},{6,5},{9,10},{10,9},{13,14},{14,13},{17,18},{18,... | collective-permute-start | bytes 1769480 | tf_op jit(solution)/shard_map/ppermute | solution.py:325
  12.9 1.0 collective-permute-start
  13.9 0.1 pad_add_fusion.flags
  13.9 15.5 %collective-permute-done.2.near_a = bf16[33,96,128]{2,1,0:T(8,128)(2,1)S(1)} collective-permute-done((bf16[33,96,128]{2,1,0:T(8,128)(2,1)}, bf16[33,96,128]{2,1,0:T(8,128)(2,1)S(1)}, u32[]{:S(2)}, u32[]{:S(2)}) %collective-permute-start.2) | collective-permute-done | bytes 811040 | tf_op jit(solution)/shard_map/ppermute | solution.py:325
  29.4 19.3 %shard_map.73 = (f32[8,18,128,128]{3,2,1,0:T(8,128)}, f32[6,18,128,128]{3,2,1,0:T(8,128)}, f32[6,192,128]{2,1,0:T(8,128)S(1)}, f32[8,64,128]{2,1,0:T(8,128)S(1)}, bf16[16,32,128]{2,1,0:T(8,128)(2,1)S(1)}) custom-call(s32[4]{0:T(128)S(1)} %pad_add_fusion.flags, bf16[64,96,128]{2,1,0:T(8,128)(2,1)S(1)} %bitcast.15, ...), custom_call_target="tpu_custom_call" | custom-call | tf_op jit(solution)/shard_map/pallas_call | solution.py:358
  48.7 16.8 %shard_map.74 = (bf16[4,128,2048]{2,1,0:T(8,128)(2,1)S(1)}, f32[136,128]{1,0:T(8,128)S(1)}) custom-call(s32[4]{0:T(128)S(1)} %pad_add_fusion.flags, bf16[24,96,128]{2,1,0:T(8,128)(2,1)} %collective-permute-done.far_a, bf16[24,96,128]{2,1,0:T(8,128)(2,1)} %collective-permute-done.1.far_b, f32[6,192,128]{2,1,0:T(8,128)S(1)} %get-tuple-element.12.weights, ...), custom_call_target="tpu_custom_call" | custom-call | tf_op jit(solution)/shard_map/pallas_call | solution.py:386
  65.6 1.4 %collective-permute-start.6 = (f32[136,128]{1,0:T(8,128)S(1)}, f32[136,128]{1,0:T(8,128)S(1)}, u32[]{:S(2)}, u32[]{:S(2)}) collective-permute-start(f32[136,128]{1,0:T(8,128)S(1)} %get-tuple-element.17.refs_0_), channel_id=1, source_target_pairs={{0,3},{1,0},{2,1},{3,2},{4,7},{5,4},{6,5},{7,6},{8,11},{9,8},{10,9... | collective-permute-start | bytes 208904 | tf_op jit(solution)/shard_map/ppermute | solution.py:529
  67.0 2.2 %collective-permute-start.5 = (f32[136,128]{1,0:T(8,128)S(1)}, f32[136,128]{1,0:T(8,128)S(1)}, u32[]{:S(2)}, u32[]{:S(2)}) collective-permute-start(f32[136,128]{1,0:T(8,128)S(1)} %get-tuple-element.17.refs_0_), channel_id=1, source_target_pairs={{0,2},{1,3},{2,0},{3,1},{4,6},{5,7},{6,4},{7,5},{8,10},{9,11},{10,... | collective-permute-start | bytes 208904 | tf_op jit(solution)/shard_map/ppermute | solution.py:529
  69.2 0.5 collective-permute-start.4
  69.6 0.7 collective-permute-done.6.refs_3_
  70.3 3.0 %collective-permute-done.5.refs_2_ = f32[136,128]{1,0:T(8,128)S(1)} collective-permute-done((f32[136,128]{1,0:T(8,128)S(1)}, f32[136,128]{1,0:T(8,128)S(1)}, u32[]{:S(2)}, u32[]{:S(2)}) %collective-permute-start.5) | collective-permute-done | bytes 69664 | tf_op jit(solution)/shard_map/ppermute | solution.py:529
  73.2 2.0 %collective-permute-done.4.refs_1_ = f32[136,128]{1,0:T(8,128)S(1)} collective-permute-done((f32[136,128]{1,0:T(8,128)S(1)}, f32[136,128]{1,0:T(8,128)S(1)}, u32[]{:S(2)}, u32[]{:S(2)}) %collective-permute-start.4) | collective-permute-done | bytes 69664 | tf_op jit(solution)/shard_map/ppermute | solution.py:529
  75.3 11.5 %shard_map.75 = bf16[8,32,768]{2,1,0:T(8,128)(2,1)} custom-call(f32[136,128]{1,0:T(8,128)S(1)} %get-tuple-element.17.refs_0_, f32[136,128]{1,0:T(8,128)S(1)} %collective-permute-done.4.refs_1_, f32[136,128]{1,0:T(8,128)S(1)} %collective-permute-done.5.refs_2_, f32[136,128]{1,0:T(8,128)S(1)} %collective-permute-done.6.refs_3_, f32[32,128]{1,0:T(8,128)S(1)} %bitcast.18, ...), custom_call_target="tpu_custom_call" | custom-call | tf_op jit(solution)/shard_map/pallas_call | solution.py:534
  86.8 3.7 %all-to-all-start = ((bf16[8,32,768]{2,1,0:T(8,128)(2,1)}), bf16[8,32,768]{2,1,0:T(8,128)(2,1)S(1)}, u32[]{:S(2)}, u32[]{:S(2)}) async-start(bf16[8,32,768]{2,1,0:T(8,128)(2,1)} %shard_map.75), calls=%async_computation | async-start | bytes 786432 | tf_op jit(solution)/shard_map/all_to_all | solution.py:545
  90.5 0.2 fusion.3
  90.7 8.1 %all-to-all-done = bf16[8,32,768]{2,1,0:T(8,128)(2,1)S(1)} async-done(((bf16[8,32,768]{2,1,0:T(8,128)(2,1)}), bf16[8,32,768]{2,1,0:T(8,128)(2,1)S(1)}, u32[]{:S(2)}, u32[]{:S(2)}) %all-to-all-start) | async-done | bytes 393248 | tf_op jit(solution)/shard_map/all_to_all | solution.py:545
  98.9 0.8 multiply_bitcast_fusion
  (16 shorter events, 0.0 us)
Async XLA Ops:
  2.2 8.0 %copy-start = (bf16[1,4,16,96,128]{4,3,2,1,0:T(8,128)(2,1)S(1)}, bf16[1,4,16,96,128]{4,3,2,1,0:T(8,128)(2,1)}, u32[]{:S(2)}) copy-start(bf16[1,4,16,96,128]{4,3,2,1,0:T(8,128)(2,1)} %param.7) | copy-start | bytes 4718596
  3.5 25.9 %copy-start.1 = (s32[1,4,16,96]{3,2,1,0:T(8,128)S(1)}, s32[1,4,16,96]{3,2,1,0:T(8,128)}, u32[]{:S(2)}) copy-start(s32[1,4,16,96]{3,2,1,0:T(8,128)} %param.8) | copy-start | bytes 73732
  3.5 25.9 %copy-start.2 = (bf16[1,96,128]{2,1,0:T(8,128)(2,1)S(1)}, bf16[1,96,128]{2,1,0:T(8,128)(2,1)}, u32[]{:S(2)}) copy-start(bf16[1,96,128]{2,1,0:T(8,128)(2,1)} %param.9) | copy-start | bytes 73732
  3.5 25.9 %copy-start.4 = (bf16[1,16,128]{2,1,0:T(8,128)(2,1)S(1)}, bf16[1,16,128]{2,1,0:T(8,128)(2,1)}, u32[]{:S(2)}) copy-start(bf16[1,16,128]{2,1,0:T(8,128)(2,1)} %param.10) | copy-start | bytes 12292
  3.6 25.9 %copy-start.5 = (s32[1,128]{1,0:T(1,128)S(1)}, s32[1,128]{1,0:T(1,128)}, u32[]{:S(2)}) copy-start(s32[1,128]{1,0:T(1,128)} %face_ids.1) | copy-start | bytes 1540
  3.6 10.4 %collective-permute-start.3 = (bf16[33,96,128]{2,1,0:T(8,128)(2,1)}, bf16[33,96,128]{2,1,0:T(8,128)(2,1)S(1)}, u32[]{:S(2)}, u32[]{:S(2)}) collective-permute-start(bf16[33,96,128]{2,1,0:T(8,128)(2,1)} %get-tuple-element.23), channel_id=1, source_target_pairs={{1,2},{2,1},{5,6},{6,5},{9,10},{10,9},{13,14},{14,13},{17,18},{18,... | collective-permute-start | bytes 2433032 | tf_op jit(solution)/shard_map/ppermute | solution.py:325
  4.4 25.0 %collective-permute-start.2 = (bf16[33,96,128]{2,1,0:T(8,128)(2,1)}, bf16[33,96,128]{2,1,0:T(8,128)(2,1)S(1)}, u32[]{:S(2)}, u32[]{:S(2)}) collective-permute-start(bf16[33,96,128]{2,1,0:T(8,128)(2,1)} %get-tuple-element.24), channel_id=1, source_target_pairs={{0,1},{2,3},{1,0},{3,2},{4,5},{6,7},{5,4},{7,6},{8,9},{10,11},{9,8... | collective-permute-start | bytes 2433032 | tf_op jit(solution)/shard_map/ppermute | solution.py:325
  11.4 37.3 %collective-permute-start.1 = (bf16[24,96,128]{2,1,0:T(8,128)(2,1)}, bf16[24,96,128]{2,1,0:T(8,128)(2,1)}, u32[]{:S(2)}, u32[]{:S(2)}) collective-permute-start(bf16[24,96,128]{2,1,0:T(8,128)(2,1)} %get-tuple-element.21), channel_id=1, source_target_pairs={{1,2},{2,1},{5,6},{6,5},{9,10},{10,9},{13,14},{14,13},{17,18},{18,... | collective-permute-start | bytes 1769480 | tf_op jit(solution)/shard_map/ppermute | solution.py:325
  12.9 35.8 %collective-permute-start = (bf16[24,96,128]{2,1,0:T(8,128)(2,1)}, bf16[24,96,128]{2,1,0:T(8,128)(2,1)}, u32[]{:S(2)}, u32[]{:S(2)}) collective-permute-start(bf16[24,96,128]{2,1,0:T(8,128)(2,1)} %get-tuple-element.22), channel_id=1, source_target_pairs={{0,1},{2,3},{1,0},{3,2},{4,5},{6,7},{5,4},{7,6},{8,9},{10,11},{9,8... | collective-permute-start | bytes 1769480 | tf_op jit(solution)/shard_map/ppermute | solution.py:325
  48.7 26.5 %copy-start.3 = (f32[1,128,32]{1,2,0:T(8,128)S(1)}, f32[1,128,32]{1,2,0:T(8,128)}, u32[]{:S(2)}) copy-start(f32[1,128,32]{1,2,0:T(8,128)} %param.12) | copy-start | bytes 49156
  65.6 4.7 %collective-permute-start.6 = (f32[136,128]{1,0:T(8,128)S(1)}, f32[136,128]{1,0:T(8,128)S(1)}, u32[]{:S(2)}, u32[]{:S(2)}) collective-permute-start(f32[136,128]{1,0:T(8,128)S(1)} %get-tuple-element.17.refs_0_), channel_id=1, source_target_pairs={{0,3},{1,0},{2,1},{3,2},{4,7},{5,4},{6,5},{7,6},{8,11},{9,8},{10,9... | collective-permute-start | bytes 208904 | tf_op jit(solution)/shard_map/ppermute | solution.py:529
  67.0 6.3 %collective-permute-start.5 = (f32[136,128]{1,0:T(8,128)S(1)}, f32[136,128]{1,0:T(8,128)S(1)}, u32[]{:S(2)}, u32[]{:S(2)}) collective-permute-start(f32[136,128]{1,0:T(8,128)S(1)} %get-tuple-element.17.refs_0_), channel_id=1, source_target_pairs={{0,2},{1,3},{2,0},{3,1},{4,6},{5,7},{6,4},{7,5},{8,10},{9,11},{10,... | collective-permute-start | bytes 208904 | tf_op jit(solution)/shard_map/ppermute | solution.py:529
  69.2 6.1 %collective-permute-start.4 = (f32[136,128]{1,0:T(8,128)S(1)}, f32[136,128]{1,0:T(8,128)S(1)}, u32[]{:S(2)}, u32[]{:S(2)}) collective-permute-start(f32[136,128]{1,0:T(8,128)S(1)} %get-tuple-element.17.refs_0_), channel_id=1, source_target_pairs={{0,1},{1,2},{2,3},{3,0},{4,5},{5,6},{6,7},{7,4},{8,9},{9,10},{10,1... | collective-permute-start | bytes 208904 | tf_op jit(solution)/shard_map/ppermute | solution.py:529
  75.3 15.3 %copy-start.6 = (s32[8,8]{1,0:T(8,128)S(1)}, s32[8,8]{1,0:T(8,128)}, u32[]{:S(2)}) copy-start(s32[8,8]{1,0:T(8,128)} %param.13) | copy-start | bytes 772
  86.8 12.1 %all-to-all-start = ((bf16[8,32,768]{2,1,0:T(8,128)(2,1)}), bf16[8,32,768]{2,1,0:T(8,128)(2,1)S(1)}, u32[]{:S(2)}, u32[]{:S(2)}) async-start(bf16[8,32,768]{2,1,0:T(8,128)(2,1)} %shard_map.75), calls=%async_computation | async-start | bytes 786432 | tf_op jit(solution)/shard_map/all_to_all | solution.py:545

commit v6 on v5

--- a/solution.py
+++ b/solution.py
@@ -45,18 +45,20 @@
     for k in range(6):
         weights[k] = faces[k] * scale
     upper = row_y >= rows_y // 2
-    low_edge = line < depth + rows_y
-    high_edge = line >= top - rows_y
+    plane = lax.div(line - depth, rows_y)
+    planes = lines // rows_y
     low_cross = jnp.where(upper, 2.0 - 2.0 * first.astype(jnp.float32), 0.0)
     high_cross = jnp.where(upper, 0.0, 2.0 - 2.0 * last.astype(jnp.float32))
     shares = [
-        jnp.where(low_edge, low_cross, 1.0),
-        jnp.where(high_edge, high_cross, 1.0),
+        jnp.where(plane == 0, low_cross, jnp.where(plane == 1, 0.0, 1.0)),
+        jnp.where(plane == planes - 1, high_cross, jnp.where(plane == planes - 2, 0.0, 1.0)),
         jnp.where(row_y == 0, 0.0, 1.0),
         jnp.where(row_y == rows_y - 1, 0.0, 1.0),
         jnp.where(row_z == 0, 0.0, 1.0),
         jnp.where(row_z == rows_z - 1, 0.0, 1.0),
     ]
+    shares[0] = jnp.where(plane == planes - 1, 2.0, shares[0])
+    shares[1] = jnp.where(plane == 0, 2.0, shares[1])
     rows = [item * share for item, share in zip(faces, shares)] + [denom, kappa * (1.0 / 16.0)]
     inside = (row_z < rows_z)[depth:top]
     for k in range(8):
@@ -77,18 +79,24 @@
 
 def fill(state, source, skip, count, first_line, pad_rows):
     rows_y = pad_rows.shape[0]
-    group = 4
+    group = 16 if count % 16 == 0 else 8
 
     def body(i, carry):
-        done = []
+        waiting = []
+
+        def store(e, y, both):
+            state[e, y + 1] = both[:, :LANES]
+            state[e, y + 2] = both[:, LANES:]
+
         for j in range(0, group, 2):
             at = i * group + j
             e, y = place(first_line + at, rows_y)
             lines = [source[skip + at], pad_rows[y], source[skip + at + 1], pad_rows[y + 1]]
-            done.append((e, y, turned(jnp.concatenate(lines, axis=0))))
-        for e, y, both in done:
-            state[e, y + 1] = both[:, :LANES]
-            state[e, y + 2] = both[:, LANES:]
+            waiting.append((e, y, turned(jnp.concatenate(lines, axis=0))))
+            if len(waiting) > 1:
+                store(*waiting.pop(0))
+        for item in waiting:
+            store(*item)
         return carry
 
     lax.fori_loop(0, count // group, body, 0)
@@ -110,7 +118,7 @@
 
 def relax_lines(src, dst, weights, first_line, count, rows_y, rows_z, keep):
     width = src.shape[2]
-    group = 4
+    group = 8
     valid = lax.broadcasted_iota(jnp.int32, (PART, LANES), 1) < rows_z
 
     def body(i, carry):
@@ -137,44 +145,63 @@
     lax.fori_loop(0, count // group, body, 0)
 
 
-def near_kernel(
+def gram_terms(final, places, planes, stiff_rows, snap, both, total):
+    _, width, columns = snap.shape
+    rows_y = columns // LANES
+    for item, e in enumerate(places):
+        p = e - planes
+        waiting = []
+
+        def store(y, some, below, values, item=item):
+            spot = pl.ds(y * LANES, LANES)
+            snap[item, some, spot] = values[0]
+            both[some, spot] = values[1]
+            both[below, spot] = values[2]
+
+        for y in range(rows_y):
+            rows = [stiff_rows[k, pl.ds(p * rows_y + y, 1)] for k in range(8)]
+            for start in range(0, width, PART):
+                some = pl.ds(start, PART)
+                middle = final[e, y + 1, some]
+                numer = neighbour_sum(final, e, y, rows, some, middle)
+                values = [middle, rows[7] * middle, rows[6] * middle - numer]
+                values = [value.astype(jnp.bfloat16) for value in values]
+                waiting.append((y, some, pl.ds(width + start, PART), values))
+                if len(waiting) > 1:
+                    store(*waiting.pop(0))
+        for entry in waiting:
+            store(*entry)
+        total = total + lax.dot_general(
+            snap[item], both[...], (((1,), (1,)), ((), ())), preferred_element_type=jnp.float32
+        )
+    return total
+
+
+def powers(marks):
+    return jnp.left_shift(jnp.int32(1), 2 * marks).astype(jnp.float32)
+
+
+def own_kernel(
     flags,
     own,
-    near_a,
-    near_b,
     classes,
     y_vals,
     z_vals,
     face_ids,
-    hand_a,
-    hand_b,
-    weights,
-    stiff_rows,
+    hand,
+    inner,
     pad_rows,
     state_a,
     state_b,
     kappa,
+    weights,
+    stiff_rows,
     sems,
 ):
     lines, rows_z, width = own.shape
     rows_y = pad_rows.shape[0]
     planes = lines // rows_y
-    near = lines // 2
     bf16 = jnp.bfloat16
-    even, first, last = flags[0], flags[1], flags[2]
-    one = jnp.int32(1)
-
-    def powers(marks):
-        return jnp.left_shift(one, 2 * marks).astype(jnp.float32)
-
-    base_a = pl.multiple_of(even * (2 * lines), 8)
-    base_b = pl.multiple_of((1 - even) * (2 * lines), 8)
-    kappa[...] = jnp.ones(kappa.shape, jnp.float32)
-    kappa[pl.ds(lines, lines), pl.ds(0, rows_z)] = powers(classes[...])
-    kappa[pl.ds(base_a, lines)] = powers(near_a[0][:lines].astype(jnp.float32).astype(jnp.int32))
-    kappa[pl.ds(base_b, lines)] = powers(near_b[0][:lines].astype(jnp.float32).astype(jnp.int32))
-    weight_rows(kappa, weights, stiff_rows, lines, first, last, rows_y, rows_z)
-
     ids = face_ids[...]
     picks = [(ids == side).astype(jnp.float32) for side in range(4)]
     spare = LANES - rows_z
@@ -189,20 +216,84 @@
     blank = jnp.zeros((spare, width), bf16)
     ghost_low = turned(jnp.concatenate([(y_all * picks[0]).astype(bf16), blank], axis=0))
     ghost_high = turned(jnp.concatenate([(y_all * picks[1]).astype(bf16), blank], axis=0))
-    for e in range(planes - 2, 2 * planes + 2):
+    for e in range(planes, 2 * planes):
         for state in (state_a, state_b):
             state[e, 0] = ghost_low
             state[e, rows_y + 1] = ghost_high
-
     fill(state_a, own, 0, lines, lines, pad_rows)
+    sends = [
+        pltpu.make_async_copy(state_a.at[pl.ds(planes, planes)], hand, sems.at[0]),
+        pltpu.make_async_copy(state_b.at[pl.ds(planes + 1, planes - 2)], inner, sems.at[1]),
+    ]
+    sends[0].start()
+    kappa[...] = jnp.ones(kappa.shape, jnp.float32)
+    kappa[pl.ds(lines, lines), pl.ds(0, rows_z)] = powers(classes[...])
+    weight_rows(kappa, weights, stiff_rows, lines, flags[1], flags[2], rows_y, rows_z)
+    middle = (lines + rows_y, lines - 2 * rows_y)
+    relax_lines(state_a, state_b, weights, *middle, rows_y, rows_z, True)
+    sends[1].start()
+    for copy in sends:
+        copy.wait()
+
+
+def near_kernel(
+    flags,
+    near_a,
+    near_b,
+    classes,
+    pad_rows,
+    hand,
+    inner,
+    hand_a,
+    hand_b,
+    weights,
+    stiff_rows,
+    snap,
+    gram,
+    state_a,
+    state_b,
+    kappa,
+    both,
+    sems,
+):
+    lines = classes.shape[0]
+    rows_z = near_a.shape[1]
+    rows_y = pad_rows.shape[0]
+    planes = lines // rows_y
+    near = lines // 2
+    even, first, last = flags[0], flags[1], flags[2]
+    taken = [
+        pltpu.make_async_copy(hand, state_a.at[pl.ds(planes, planes)], sems.at[0]),
+        pltpu.make_async_copy(inner, state_b.at[pl.ds(planes + 1, planes - 2)], sems.at[1]),
+    ]
+    for copy in taken:
+        copy.start()
+
+    base_a = pl.multiple_of(even * (2 * lines), 8)
+    base_b = pl.multiple_of((1 - even) * (2 * lines), 8)
+    kappa[...] = jnp.ones(kappa.shape, jnp.float32)
+    kappa[pl.ds(lines, lines), pl.ds(0, rows_z)] = powers(classes[...])
+    kappa[pl.ds(base_a, lines)] = powers(near_a[0][:lines].astype(jnp.float32).astype(jnp.int32))
+    kappa[pl.ds(base_b, lines)] = powers(near_b[0][:lines].astype(jnp.float32).astype(jnp.int32))
+    weight_rows(kappa, weights, stiff_rows, lines, first, last, rows_y, rows_z)
     fill(state_a, near_a, 1, near, near + even * (lines + near), pad_rows)
     fill(state_a, near_b, 1, near, near + (1 - even) * (lines + near), pad_rows)
+    for copy in taken:
+        copy.wait()
+    ghost_low = state_a[planes, 0]
+    ghost_high = state_a[planes, rows_y + 1]
+    for e in (planes - 2, planes - 1, 2 * planes, 2 * planes + 1):
+        state_a[e, 0] = ghost_low
+        state_a[e, rows_y + 1] = ghost_high
+    for e in (planes - 1, planes, 2 * planes - 1, 2 * planes):
+        state_b[e, 0] = ghost_low
+        state_b[e, rows_y + 1] = ghost_high
 
     sent = []
 
-    def send(state, hand, e, count, offset):
+    def send(state, to, e, count, offset):
         copy = pltpu.make_async_copy(
-            state.at[pl.ds(e, count)], hand.at[pl.ds(e - offset, count)], sems.at[len(sent)]
+            state.at[pl.ds(e, count)], to.at[pl.ds(e - offset, count)], sems.at[2 + len(sent)]
         )
         copy.start()
         sent.append(copy)
@@ -210,13 +301,17 @@
     step = functools.partial(relax_lines, weights=weights, rows_y=rows_y, rows_z=rows_z)
     send(state_a, hand_a, planes - 2, 2, planes - 2)
     send(state_a, hand_a, 2 * planes, 2, planes - 2)
-    step(state_a, state_b, first_line=lines - rows_y, count=lines + 2 * rows_y, keep=True)
+    step(state_a, state_b, first_line=lines - rows_y, count=2 * rows_y, keep=True)
+    step(state_a, state_b, first_line=2 * lines - rows_y, count=2 * rows_y, keep=True)
     send(state_b, hand_b, planes - 1, 2, planes - 1)
     send(state_b, hand_b, 2 * planes - 1, 2, planes - 1)
     step(state_b, state_a, first_line=lines, count=lines, keep=True)
     send(state_a, hand_a, planes, planes, planes - 2)
     step(state_a, state_b, first_line=lines + rows_y, count=lines - 2 * rows_y, keep=False)
     send(state_b, hand_b, planes + 1, planes - 2, planes - 1)
+    inside = range(planes + 1, 2 * planes - 1)
+    blank = jnp.zeros(gram.shape, jnp.float32)
+    gram[...] = gram_terms(state_b, inside, planes, stiff_rows, snap, both, blank)
     for copy in sent:
         copy.wait()
 
@@ -228,6 +323,7 @@
     weights,
     stiff_rows,
     pad_rows,
+    near_gram,
     hand_a,
     hand_b,
     snap,
@@ -237,13 +333,13 @@
     both,
     sems,
 ):
-    planes, width, _ = snap.shape
+    width = snap.shape[1]
     rows_y = pad_rows.shape[0]
     rows_z = far_a.shape[1]
-    lines = planes * rows_y
+    lines = stiff_rows.shape[1]
+    planes = lines // rows_y
     half = rows_y // 2
     even = flags[0]
-    bf16 = jnp.bfloat16
     taken = []
 
     def take(dst, src):
@@ -281,34 +377,8 @@
     taken[9].wait()
     final = buffers[SWEEPS % 2]
 
-    def stiffness(p, total):
-        e = planes + p
-        waiting = []
-
-        def store(y, some, below, values):
-            spot = pl.ds(y * LANES, LANES)
-            snap[p, some, spot] = values[0]
-            both[some, spot] = values[1]
-            both[below, spot] = values[2]
-
-        for y in range(rows_y):
-            rows = [stiff_rows[k, pl.ds(p * rows_y + y, 1)] for k in range(8)]
-            for start in range(0, width, PART):
-                some = pl.ds(start, PART)
-                middle = final[e, y + 1, some]
-                numer = neighbour_sum(final, e, y, rows, some, middle)
-                values = [middle, rows[7] * middle, rows[6] * middle - numer]
-                values = [value.astype(bf16) for value in values]
-                waiting.append((y, some, pl.ds(width + start, PART), values))
-                if len(waiting) > 1:
-                    store(*waiting.pop(0))
-        for item in waiting:
-            store(*item)
-        return total + lax.dot_general(
-            snap[p], both[...], (((1,), (1,)), ((), ())), preferred_element_type=jnp.float32
-        )
-
-    total = lax.fori_loop(0, planes, stiffness, jnp.zeros((width, 2 * width), jnp.float32))
+    outer = (planes, 2 * planes - 1)
+    total = gram_terms(final, outer, planes, stiff_rows, snap, both, near_gram[...])
     mass = total[:, :width]
     stiff = total[:, width:]
     stiff = stiff + stiff.T
@@ -355,50 +425,60 @@
     hbm = pl.BlockSpec(memory_space=pltpu.HBM)
     state = pltpu.VMEM((3 * planes, rows_y + 2, width, LANES), jnp.float32)
     params = pltpu.CompilerParams(vmem_limit_bytes=48 * 2**20)
-    hand_a, hand_b, weights, stiff_rows, pad_rows = pl.pallas_call(
+    kappa = pltpu.VMEM((3 * count, LANES), jnp.float32)
+    both = pltpu.VMEM((2 * width, rows_y * LANES), jnp.bfloat16)
+
+    def slab(depth):
+        return jax.ShapeDtypeStruct((depth, rows_y + 2, width, LANES), jnp.float32)
+
+    def sems(number):
+        return pltpu.SemaphoreType.DMA((number,))
+
+    def kept(depth):
+        return jax.ShapeDtypeStruct((depth, width, rows_y * LANES), jnp.bfloat16)
+
+    rows = [
+        jax.ShapeDtypeStruct((6, 3 * count, LANES), jnp.float32),
+        jax.ShapeDtypeStruct((8, count, LANES), jnp.float32),
+    ]
+    flat_classes = classes.reshape(count, rows_z)
+    hand, inner, pad_rows = pl.pallas_call(
+        own_kernel,
+        out_shape=[
+            slab(planes),
+            slab(planes - 2),
+            jax.ShapeDtypeStruct((rows_y, LANES - rows_z, width), jnp.bfloat16),
+        ],
+        in_specs=[smem] + [vmem] * 5,
+        out_specs=[hbm, hbm, vmem],
+        scratch_shapes=[state, state, kappa]
+        + [pltpu.VMEM(item.shape, item.dtype) for item in rows]
+        + [sems(2)],
+        compiler_params=params,
+    )(flags, lines, flat_classes, y_vals, z_vals, face_ids[None])
+    hand_a, hand_b, weights, stiff_rows, snap_near, gram_near = pl.pallas_call(
         near_kernel,
         out_shape=[
-            jax.ShapeDtypeStruct((planes + 4, rows_y + 2, width, LANES), jnp.float32),
-            jax.ShapeDtypeStruct((planes + 2, rows_y + 2, width, LANES), jnp.float32),
-            jax.ShapeDtypeStruct((6, 3 * count, LANES), jnp.float32),
-            jax.ShapeDtypeStruct((8, count, LANES), jnp.float32),
-            jax.ShapeDtypeStruct((rows_y, LANES - rows_z, width), jnp.bfloat16),
+            slab(planes + 4),
+            slab(planes + 2),
+            *rows,
+            kept(planes - 2),
+            jax.ShapeDtypeStruct((width, 2 * width), jnp.float32),
         ],
-        in_specs=[smem] + [vmem] * 7,
-        out_specs=[hbm, hbm, vmem, vmem, vmem],
-        scratch_shapes=[
-            state,
-            state,
-            pltpu.VMEM((3 * count, LANES), jnp.float32),
-            pltpu.SemaphoreType.DMA((6,)),
-        ],
+        in_specs=[smem] + [vmem] * 4 + [hbm] * 2,
+        out_specs=[hbm, hbm] + [vmem] * 4,
+        scratch_shapes=[state, state, kappa, both, sems(8)],
         compiler_params=params,
-    )(
-        flags,
-        lines,
-        near_a,
-        near_b,
-        classes.reshape(count, rows_z),
-        y_vals,
-        z_vals,
-        face_ids[None],
-    )
-    return pl.pallas_call(
+    )(flags, near_a, near_b, flat_classes, pad_rows, hand, inner)
+    snap_far, gram = pl.pallas_call(
         far_kernel,
-        out_shape=[
-            jax.ShapeDtypeStruct((planes, width, rows_y * LANES), jnp.bfloat16),
-            jax.ShapeDtypeStruct((width + 8, width), jnp.float32),
-        ],
-        in_specs=[smem] + [vmem] * 5 + [hbm] * 2,
+        out_shape=[kept(2), jax.ShapeDtypeStruct((width + 8, width), jnp.float32)],
+        in_specs=[smem] + [vmem] * 6 + [hbm] * 2,
         out_specs=[vmem, vmem],
-        scratch_shapes=[
-            state,
-            state,
-            pltpu.VMEM((2 * width, rows_y * LANES), jnp.bfloat16),
-            pltpu.SemaphoreType.DMA((10,)),
-        ],
+        scratch_shapes=[state, state, both, sems(10)],
         compiler_params=params,
-    )(flags, far_a, far_b, weights, stiff_rows, pad_rows, hand_a, hand_b)
+    )(flags, far_a, far_b, weights, stiff_rows, pad_rows, gram_near, hand_a, hand_b)
+    return snap_near, snap_far, gram
 
 
 def lane_copy(tile, lane):
@@ -419,7 +499,7 @@
         cols = [lane_copy(lhs[k], 8 * k + j) for j in range(8)]
         panel_l, panel_r = lhs[k], rhs[k]
         for j in range(8):
-            recip = 1.0 / row_copy(cols[j], j)
+            recip = pl.reciprocal(row_copy(cols[j], j), approx=True)
             here = sub == j
             mult = jnp.where(here, recip, -cols[j] * recip)
             for l in range(j + 1, 8):
@@ -457,7 +537,7 @@
         scale = None
         for j in range(8):
             pivot = row_copy(cols[k][j], j)
-            recip = 1.0 / pivot
+            recip = pl.reciprocal(pivot, approx=True)
             root = lax.rsqrt(pivot)
             scale = root if scale is None else jnp.where(sub >= j, root, scale)
             head = {l: row_copy(cols[k][l], j) for l in range(j + 1, 8)}
@@ -481,9 +561,15 @@
 
 
 def modes_kernel(cell_count, rows_z, *refs):
-    *part_refs, start_ref, snap_hbm, out_ref, snap_ref, sem = refs
-    fetch = pltpu.make_async_copy(snap_hbm, snap_ref, sem)
-    fetch.start()
+    mask_ref, *part_refs, start_ref, near_hbm, far_hbm, out_ref, snap_ref, sems = refs
+    planes, _, columns = snap_ref.shape
+    places = [(far_hbm, 0, 0, 1), (near_hbm, 0, 1, planes - 2), (far_hbm, 1, planes - 1, 1)]
+    fetches = [
+        pltpu.make_async_copy(src.at[pl.ds(at, n)], snap_ref.at[pl.ds(to, n)], sems.at[k])
+        for k, (src, at, to, n) in enumerate(places)
+    ]
+    for fetch in fetches:
+        fetch.start()
     total = part_refs[0][...]
     for part in part_refs[1:]:
         total = total + part[...]
@@ -504,8 +590,8 @@
         inner = dot(weighted, block, ((1,), (1,)))
         block = whiten(inner, solved)
     modes = block.astype(jnp.bfloat16)
-    fetch.wait()
-    planes, _, columns = snap_ref.shape
+    for fetch in fetches:
+        fetch.wait()
     lanes = LANES
     rows_y = columns // lanes
     piece_rows = planes * rows_y // out_ref.shape[0]
@@ -513,16 +599,16 @@
         basis = jnp.dot(modes, snap_ref[p], preferred_element_type=jnp.float32)
         for y in range(rows_y):
             piece, spot = divmod(p * rows_y + y, piece_rows)
-            out_ref[piece, :, pl.ds(spot * rows_z, rows_z)] = basis[
-                :, y * lanes : y * lanes + rows_z
-            ].astype(jnp.bfloat16)
+            values = basis[:, y * lanes : y * lanes + rows_z].astype(jnp.bfloat16)
+            wanted = mask_ref[piece] != 0
+            out_ref[piece, :, pl.ds(spot * rows_z, rows_z)] = jnp.where(wanted, values, 0.0)
 
 
 def on_device(snap_init, channel_map, yface_vals, zface_vals, face_of, start_block, correlation):
     subs = lax.axis_size("sub")
     owner_count = lax.axis_size("nbhd")
     planes, rows_y, rows_z, width = snap_init.shape[1:]
-    snapshots, own = relax(
+    snap_near, snap_far, own = relax(
         snap_init[0], channel_map[0], yface_vals[0], zface_vals[0], face_of[0]
     )
     parts = [own] + [
@@ -531,21 +617,21 @@
     ]
     cells = planes * rows_y * rows_z
     modes = start_block.shape[-1]
+    mask = lax.dynamic_slice_in_dim(correlation, lax.axis_index("nbhd"), 1, axis=0)[0]
     pieces = pl.pallas_call(
         functools.partial(modes_kernel, float(subs * cells), rows_z),
         out_shape=jax.ShapeDtypeStruct((owner_count, modes, cells // owner_count), jnp.bfloat16),
-        in_specs=[pl.BlockSpec(memory_space=pltpu.VMEM)] * (subs + 1)
-        + [pl.BlockSpec(memory_space=pltpu.HBM)],
+        in_specs=[pl.BlockSpec(memory_space=pltpu.SMEM)]
+        + [pl.BlockSpec(memory_space=pltpu.VMEM)] * (subs + 1)
+        + [pl.BlockSpec(memory_space=pltpu.HBM)] * 2,
         scratch_shapes=[
-            pltpu.VMEM(snapshots.shape, snapshots.dtype),
-            pltpu.SemaphoreType.DMA,
+            pltpu.VMEM((planes, width, rows_y * LANES), jnp.bfloat16),
+            pltpu.SemaphoreType.DMA((3,)),
         ],
         compiler_params=pltpu.CompilerParams(vmem_limit_bytes=24 * 2**20),
-    )(*parts, start_block[0].T, snapshots)
+    )(mask, *parts, start_block[0].T, snap_near, snap_far)
     received = lax.all_to_all(pieces, "nbhd", split_axis=0, concat_axis=0, tiled=True)
-    column = lax.dynamic_slice_in_dim(correlation, lax.axis_index("nbhd"), 1, axis=1)[:, 0]
-    result = received * column.astype(jnp.bfloat16)[:, None, None]
-    return result[None, None]
+    return received[None, None]
 
 
 def solution(mesh):

time: 100 us -> 87.9 us (0.88)
  waiting for transfers between devices: 29.3 us -> 9.11 us
  blocking collectives: 0 us -> 11.9 us
  Pallas kernels: 47.6 us -> 41.7 us
  starting transfers between devices: 16.9 us -> 19.1 us
  other arithmetic: 3.16 us -> 2.15 us
    all_to_all x0 -> x1, blocking collectives: none -> 11.9 us  [on_device(): lax.all_to_all(pieces, 'nbhd', split_axis=0, concat_axis=0, tiled=True)]
    ppermute x4, waiting for transfers between devices: 15.5 us -> 7.18 us  [swap(): return lax.ppermute(array, 'sub', pairs + [(j, i) for i, j in pairs])]
    all_to_all x1 -> x0, waiting for transfers between devices: 8.15 us -> none  [on_device(): lax.all_to_all(pieces, 'nbhd', split_axis=0, concat_axis=0, tiled=True)]
    pallas_call x2 -> x3, Pallas kernels: 36.1 us -> 30.4 us  [the longest x1 13.2 us: relax(): pl.pallas_call(far_kernel, out_shape=[kept(2), jax.ShapeDtypeStruct((widt...]
    ppermute x3, starting transfers between devices: 4.02 us -> 9.54 us  [on_device(): lax.ppermute(own, 'sub', [(i, (i + shift) % subs) for i in range(subs)])]
    all_to_all x1 -> x0, starting transfers between devices: 3.73 us -> none  [on_device(): lax.all_to_all(pieces, 'nbhd', split_axis=0, concat_axis=0, tiled=True)]
    ppermute x3, waiting for transfers between devices: 5.66 us -> 1.93 us  [on_device(): lax.ppermute(own, 'sub', [(i, (i + shift) % subs) for i in range(subs)])]
  transfers between devices with their start and end apart: 8 -> 7, of which waited for: 5 -> 3; matrix products, arithmetic and copies ran while one was open for 1% -> 1% of each run, Pallas kernels for 19% -> 20%
where the time goes in v6:
time: 87.9 us; the launch traced here: 87.5 us
  Pallas kernels  41.7 us (47%)
  starting transfers between devices  19.1 us (22%)
  blocking collectives  11.9 us (14%)
  waiting for transfers between devices  9.11 us (10%)
  local copies, waits for them, and re-layouts  3.39 us (4%)
  other arithmetic  2.15 us (2%)
    pallas_call x1, Pallas kernels, relax(): pl.pallas_call(far_kernel, out_shape=[kept(2), jax.ShapeDtypeStruct((widt...  13.2 us
    pallas_call x1, Pallas kernels, relax(): pl.pallas_call(near_kernel, out_shape=[slab(planes + 4), slab(planes + 2)...  13.1 us
    all_to_all x1, blocking collectives, on_device(): lax.all_to_all(pieces, 'nbhd', split_axis=0, concat_axis=0, tiled=True)  11.9 us
    pallas_call x1, Pallas kernels, on_device(): pl.pallas_call(functools.partial(modes_kernel, float(subs * cells), rows_...  11.3 us
    ppermute x4, starting transfers between devices, swap(): return lax.ppermute(array, 'sub', pairs + [(j, i) for i, j in pairs])  9.6 us
    ppermute x3, starting transfers between devices, on_device(): lax.ppermute(own, 'sub', [(i, (i + shift) % subs) for i in range(subs)])  9.54 us
    ppermute x4, waiting for transfers between devices, swap(): return lax.ppermute(array, 'sub', pairs + [(j, i) for i, j in pairs])  7.18 us
    pallas_call x1, Pallas kernels, relax(): pl.pallas_call(own_kernel, out_shape=[slab(planes), slab(planes - 2), jax...  4.13 us
  transfers between devices with their start and end apart: 7, of which 3 were waited for; matrix products, arithmetic and copies ran while one was open for 1% of the time, Pallas kernels for 20%

profile of v6, /device:TPU:0, one launch (start us, length us, event | category | flops | bytes accessed | tf_op | source)
XLA Modules:
  0.0 87.5 jit_solution(15915967161858954659)
XLA Ops:
  0.0 0.8 convert_element_type.17
  0.8 1.5 %constant_dynamic-slice_fusion = (bf16[32,96,128]{2,1,0:T(8,128)(2,1)S(1)}, bf16[32,96,128]{2,1,0:T(8,128)(2,1)S(1)}) fusion(bf16[64,96,128]{2,1,0:T(8,128)(2,1)} %bitcast.14, s32[]{:T(128)S(6)} %select_n.27, s32[]{:T(128)S(6)} %select_n.26), kind=kLoop, calls=%fused_computation.4 | loop fusion | bytes 3145736 | tf_op jit(solution)/shard_map/dynamic_slice | solution.py:411
  2.3 0.0 copy-start.1
  2.3 1.3 %fusion.2 = (bf16[33,96,128]{2,1,0:T(8,128)(2,1)}, bf16[33,96,128]{2,1,0:T(8,128)(2,1)}) fusion(bf16[1,64,96]{2,1,0:T(8,128)(2,1)S(1)} %bitcast.23, bf16[32,96,128]{2,1,0:T(8,128)(2,1)S(1)} %get-tuple-element.27, bf16[32,96,128]{2,1,0:T(8,128)(2,1)S(1)} %get-tuple-element.28), kind=kLoop, calls=%fused_computation.3 | loop fusion | flops 3649536 | bytes 3207168 | tf_op jit(solution)/shard_map/concatenate | solution.py:412
  3.6 3.1 %collective-permute-start.2 = (bf16[33,96,128]{2,1,0:T(8,128)(2,1)}, bf16[33,96,128]{2,1,0:T(8,128)(2,1)S(1)}, u32[]{:S(2)}, u32[]{:S(2)}) collective-permute-start(bf16[33,96,128]{2,1,0:T(8,128)(2,1)} %get-tuple-element.32), channel_id=1, source_target_pairs={{0,1},{2,3},{1,0},{3,2},{4,5},{6,7},{5,4},{7,6},{8,9},{10,11},{9,8... | collective-permute-start | bytes 2433032 | tf_op jit(solution)/shard_map/ppermute | solution.py:395
  6.7 0.7 collective-permute-start.3
  7.4 1.1 %constant_dynamic-slice_fusion.2 = (bf16[24,96,128]{2,1,0:T(8,128)(2,1)}, bf16[24,96,128]{2,1,0:T(8,128)(2,1)}) fusion(bf16[64,96,128]{2,1,0:T(8,128)(2,1)S(1)} %bitcast.15, s32[]{:T(128)S(6)} %select_n.25, s32[]{:T(128)S(6)} %select_n.24), kind=kLoop, calls=%fused_computation.6 | loop fusion | bytes 2359304 | tf_op jit(solution)/shard_map/dynamic_slice | solution.py:416
  8.5 4.3 %collective-permute-start = (bf16[24,96,128]{2,1,0:T(8,128)(2,1)}, bf16[24,96,128]{2,1,0:T(8,128)(2,1)}, u32[]{:S(2)}, u32[]{:S(2)}) collective-permute-start(bf16[24,96,128]{2,1,0:T(8,128)(2,1)} %get-tuple-element.30), channel_id=1, source_target_pairs={{0,1},{2,3},{1,0},{3,2},{4,5},{6,7},{5,4},{7,6},{8,9},{10,11},{9,8... | collective-permute-start | bytes 1769480 | tf_op jit(solution)/shard_map/ppermute | solution.py:395
  12.9 1.5 %collective-permute-start.1 = (bf16[24,96,128]{2,1,0:T(8,128)(2,1)}, bf16[24,96,128]{2,1,0:T(8,128)(2,1)}, u32[]{:S(2)}, u32[]{:S(2)}) collective-permute-start(bf16[24,96,128]{2,1,0:T(8,128)(2,1)} %get-tuple-element.29), channel_id=1, source_target_pairs={{1,2},{2,1},{5,6},{6,5},{9,10},{10,9},{13,14},{14,13},{17,18},{18,... | collective-permute-start | bytes 1769480 | tf_op jit(solution)/shard_map/ppermute | solution.py:395
  14.4 0.1 pad_add_fusion.flags
  14.5 4.1 %shard_map.73 = (f32[4,18,128,128]{3,2,1,0:T(8,128)}, f32[2,18,128,128]{3,2,1,0:T(8,128)S(1)}, bf16[16,32,128]{2,1,0:T(8,128)(2,1)S(1)}) custom-call(s32[4]{0:T(128)S(1)} %pad_add_fusion.flags, bf16[64,96,128]{2,1,0:T(8,128)(2,1)S(1)} %bitcast.16, s32[64,96]{1,0:T(8,128)S(1)} %bitcast.17, bf16[96,128]{1,0:T(8,128)(2,1)S(1)} %bitcast.19, ...), custom_call_target="tpu_custom_call" | custom-call | tf_op jit(solution)/shard_map/pallas_call | solution.py:445
  18.6 7.2 %collective-permute-done.2.near_a = bf16[33,96,128]{2,1,0:T(8,128)(2,1)S(1)} collective-permute-done((bf16[33,96,128]{2,1,0:T(8,128)(2,1)}, bf16[33,96,128]{2,1,0:T(8,128)(2,1)S(1)}, u32[]{:S(2)}, u32[]{:S(2)}) %collective-permute-start.2) | collective-permute-done | bytes 811040 | tf_op jit(solution)/shard_map/ppermute | solution.py:395
  25.8 0.0 collective-permute-done.3.near_b
  25.8 13.1 %shard_map.74 = (f32[8,18,128,128]{3,2,1,0:T(8,128)}, f32[6,18,128,128]{3,2,1,0:T(8,128)}, f32[6,192,128]{2,1,0:T(8,128)S(1)}, f32[8,64,128]{2,1,0:T(8,128)S(1)}...) custom-call(s32[4]{0:T(128)S(1)} %pad_add_fusion.flags, ...), custom_call_target="tpu_custom_call" | custom-call | tf_op jit(solution)/shard_map/pallas_call | solution.py:459
  38.9 0.0 copy-start.4
  38.9 13.2 %shard_map.75 = (bf16[2,128,2048]{2,1,0:T(8,128)(2,1)S(1)}, f32[136,128]{1,0:T(8,128)S(1)}) custom-call(s32[4]{0:T(128)S(1)} %pad_add_fusion.flags, bf16[24,96,128]{2,1,0:T(8,128)(2,1)} %collective-permute-done.far_a, bf16[24,96,128]{2,1,0:T(8,128)(2,1)} %collective-permute-done.1.far_b, f32[6,192,128]{2,1,0:T(8,128)S(1)} %get-tuple-element.19.weights, ...), custom_call_target="tpu_custom_call" | custom-call | tf_op jit(solution)/shard_map/pallas_call | solution.py:473
  52.1 5.1 %collective-permute-start.4 = (f32[136,128]{1,0:T(8,128)S(1)}, f32[136,128]{1,0:T(8,128)S(1)}, u32[]{:S(2)}, u32[]{:S(2)}) collective-permute-start(f32[136,128]{1,0:T(8,128)S(1)} %get-tuple-element.24.refs_1_), channel_id=1, source_target_pairs={{0,1},{1,2},{2,3},{3,0},{4,5},{5,6},{6,7},{7,4},{8,9},{9,10},{10,1... | collective-permute-start | bytes 208904 | tf_op jit(solution)/shard_map/ppermute | solution.py:615
  57.2 1.6 %collective-permute-start.5 = (f32[136,128]{1,0:T(8,128)S(1)}, f32[136,128]{1,0:T(8,128)S(1)}, u32[]{:S(2)}, u32[]{:S(2)}) collective-permute-start(f32[136,128]{1,0:T(8,128)S(1)} %get-tuple-element.24.refs_1_), channel_id=1, source_target_pairs={{0,2},{1,3},{2,0},{3,1},{4,6},{5,7},{6,4},{7,5},{8,10},{9,11},{10,... | collective-permute-start | bytes 208904 | tf_op jit(solution)/shard_map/ppermute | solution.py:615
  58.8 2.8 %collective-permute-start.6 = (f32[136,128]{1,0:T(8,128)S(1)}, f32[136,128]{1,0:T(8,128)S(1)}, u32[]{:S(2)}, u32[]{:S(2)}) collective-permute-start(f32[136,128]{1,0:T(8,128)S(1)} %get-tuple-element.24.refs_1_), channel_id=1, source_target_pairs={{0,3},{1,0},{2,1},{3,2},{4,7},{5,4},{6,5},{7,6},{8,11},{9,8},{10,9... | collective-permute-start | bytes 208904 | tf_op jit(solution)/shard_map/ppermute | solution.py:615
  61.6 0.8 collective-permute-done.5.refs_3_
  62.4 1.1 %collective-permute-done.6.refs_4_ = f32[136,128]{1,0:T(8,128)S(1)} collective-permute-done((f32[136,128]{1,0:T(8,128)S(1)}, f32[136,128]{1,0:T(8,128)S(1)}, u32[]{:S(2)}, u32[]{:S(2)}) %collective-permute-start.6) | collective-permute-done | bytes 69664 | tf_op jit(solution)/shard_map/ppermute | solution.py:615
  63.6 11.3 %shard_map.76 = bf16[8,32,768]{2,1,0:T(8,128)(2,1)S(1)} custom-call(s32[8]{0:T(128)S(1)} %fusion.3.refs_0_, f32[136,128]{1,0:T(8,128)S(1)} %get-tuple-element.24.refs_1_, f32[136,128]{1,0:T(8,128)S(1)} %collective-permute-done.4.refs_2_, f32[136,128]{1,0:T(8,128)S(1)} %collective-permute-done.5.refs_3_, f32[136,128]{1,0:T(8,128)S(1)} %collective-permute-done.6.refs_4_, ...), custom_call_target="tpu_custom_call" | custom-call | tf_op jit(solution)/shard_map/pallas_call | solution.py:621
  74.9 11.9 %all_to_all.5 = bf16[8,32,768]{2,1,0:T(8,128)(2,1)S(1)} all-to-all(bf16[8,32,768]{2,1,0:T(8,128)(2,1)S(1)} %shard_map.76), channel_id=1, replica_groups=mesh['nbhd'=8,'sub'=4] {'nbhd'}, dimensions={0} | all-to-all | bytes 786432 | tf_op jit(solution)/shard_map/all_to_all | solution.py:633
  86.8 0.7 copy.9
  (16 shorter events, 0.0 us)
Async XLA Ops:
  0.0 61.6 %copy-start = (s32[8,8]{1,0:T(8,128)S(1)}, s32[8,8]{1,0:T(8,128)}, u32[]{:S(2)}) copy-start(s32[8,8]{1,0:T(8,128)} %param.13) | copy-start | bytes 772
  2.3 5.1 %copy-start.1 = (bf16[1,4,16,96,128]{4,3,2,1,0:T(8,128)(2,1)S(1)}, bf16[1,4,16,96,128]{4,3,2,1,0:T(8,128)(2,1)}, u32[]{:S(2)}) copy-start(bf16[1,4,16,96,128]{4,3,2,1,0:T(8,128)(2,1)} %param.7) | copy-start | bytes 4718596
  3.6 10.9 %copy-start.2 = (s32[1,4,16,96]{3,2,1,0:T(8,128)S(1)}, s32[1,4,16,96]{3,2,1,0:T(8,128)}, u32[]{:S(2)}) copy-start(s32[1,4,16,96]{3,2,1,0:T(8,128)} %param.8) | copy-start | bytes 73732
  3.6 10.9 %copy-start.3 = (bf16[1,96,128]{2,1,0:T(8,128)(2,1)S(1)}, bf16[1,96,128]{2,1,0:T(8,128)(2,1)}, u32[]{:S(2)}) copy-start(bf16[1,96,128]{2,1,0:T(8,128)(2,1)} %param.9) | copy-start | bytes 73732
  3.6 10.9 %copy-start.5 = (bf16[1,16,128]{2,1,0:T(8,128)(2,1)S(1)}, bf16[1,16,128]{2,1,0:T(8,128)(2,1)}, u32[]{:S(2)}) copy-start(bf16[1,16,128]{2,1,0:T(8,128)(2,1)} %param.10) | copy-start | bytes 12292
  3.6 10.9 %copy-start.6 = (s32[1,128]{1,0:T(1,128)S(1)}, s32[1,128]{1,0:T(1,128)}, u32[]{:S(2)}) copy-start(s32[1,128]{1,0:T(1,128)} %face_ids.1) | copy-start | bytes 1540
  3.6 22.2 %collective-permute-start.2 = (bf16[33,96,128]{2,1,0:T(8,128)(2,1)}, bf16[33,96,128]{2,1,0:T(8,128)(2,1)S(1)}, u32[]{:S(2)}, u32[]{:S(2)}) collective-permute-start(bf16[33,96,128]{2,1,0:T(8,128)(2,1)} %get-tuple-element.32), channel_id=1, source_target_pairs={{0,1},{2,3},{1,0},{3,2},{4,5},{6,7},{5,4},{7,6},{8,9},{10,11},{9,8... | collective-permute-start | bytes 2433032 | tf_op jit(solution)/shard_map/ppermute | solution.py:395
  6.7 19.1 %collective-permute-start.3 = (bf16[33,96,128]{2,1,0:T(8,128)(2,1)}, bf16[33,96,128]{2,1,0:T(8,128)(2,1)S(1)}, u32[]{:S(2)}, u32[]{:S(2)}) collective-permute-start(bf16[33,96,128]{2,1,0:T(8,128)(2,1)} %get-tuple-element.31), channel_id=1, source_target_pairs={{1,2},{2,1},{5,6},{6,5},{9,10},{10,9},{13,14},{14,13},{17,18},{18,... | collective-permute-start | bytes 2433032 | tf_op jit(solution)/shard_map/ppermute | solution.py:395
  8.5 30.3 %collective-permute-start = (bf16[24,96,128]{2,1,0:T(8,128)(2,1)}, bf16[24,96,128]{2,1,0:T(8,128)(2,1)}, u32[]{:S(2)}, u32[]{:S(2)}) collective-permute-start(bf16[24,96,128]{2,1,0:T(8,128)(2,1)} %get-tuple-element.30), channel_id=1, source_target_pairs={{0,1},{2,3},{1,0},{3,2},{4,5},{6,7},{5,4},{7,6},{8,9},{10,11},{9,8... | collective-permute-start | bytes 1769480 | tf_op jit(solution)/shard_map/ppermute | solution.py:395
  12.9 26.0 %collective-permute-start.1 = (bf16[24,96,128]{2,1,0:T(8,128)(2,1)}, bf16[24,96,128]{2,1,0:T(8,128)(2,1)}, u32[]{:S(2)}, u32[]{:S(2)}) collective-permute-start(bf16[24,96,128]{2,1,0:T(8,128)(2,1)} %get-tuple-element.29), channel_id=1, source_target_pairs={{1,2},{2,1},{5,6},{6,5},{9,10},{10,9},{13,14},{14,13},{17,18},{18,... | collective-permute-start | bytes 1769480 | tf_op jit(solution)/shard_map/ppermute | solution.py:395
  38.9 24.7 %copy-start.4 = (f32[1,128,32]{1,2,0:T(8,128)S(1)}, f32[1,128,32]{1,2,0:T(8,128)}, u32[]{:S(2)}) copy-start(f32[1,128,32]{1,2,0:T(8,128)} %param.12) | copy-start | bytes 49156
  52.1 9.6 %collective-permute-start.4 = (f32[136,128]{1,0:T(8,128)S(1)}, f32[136,128]{1,0:T(8,128)S(1)}, u32[]{:S(2)}, u32[]{:S(2)}) collective-permute-start(f32[136,128]{1,0:T(8,128)S(1)} %get-tuple-element.24.refs_1_), channel_id=1, source_target_pairs={{0,1},{1,2},{2,3},{3,0},{4,5},{5,6},{6,7},{7,4},{8,9},{9,10},{10,1... | collective-permute-start | bytes 208904 | tf_op jit(solution)/shard_map/ppermute | solution.py:615
  57.2 5.2 %collective-permute-start.5 = (f32[136,128]{1,0:T(8,128)S(1)}, f32[136,128]{1,0:T(8,128)S(1)}, u32[]{:S(2)}, u32[]{:S(2)}) collective-permute-start(f32[136,128]{1,0:T(8,128)S(1)} %get-tuple-element.24.refs_1_), channel_id=1, source_target_pairs={{0,2},{1,3},{2,0},{3,1},{4,6},{5,7},{6,4},{7,5},{8,10},{9,11},{10,... | collective-permute-start | bytes 208904 | tf_op jit(solution)/shard_map/ppermute | solution.py:615
  58.8 4.8 %collective-permute-start.6 = (f32[136,128]{1,0:T(8,128)S(1)}, f32[136,128]{1,0:T(8,128)S(1)}, u32[]{:S(2)}, u32[]{:S(2)}) collective-permute-start(f32[136,128]{1,0:T(8,128)S(1)} %get-tuple-element.24.refs_1_), channel_id=1, source_target_pairs={{0,3},{1,0},{2,1},{3,2},{4,7},{5,4},{6,5},{7,6},{8,11},{9,8},{10,9... | collective-permute-start | bytes 208904 | tf_op jit(solution)/shard_map/ppermute | solution.py:615

commit v7 on v6

--- a/solution.py
+++ b/solution.py
@@ -188,15 +188,12 @@
     y_vals,
     z_vals,
     face_ids,
-    hand,
-    inner,
-    pad_rows,
     state_a,
     state_b,
+    pad_rows,
     kappa,
     weights,
     stiff_rows,
-    sems,
 ):
     lines, rows_z, width = own.shape
     rows_y = pad_rows.shape[0]
@@ -216,104 +213,63 @@
     blank = jnp.zeros((spare, width), bf16)
     ghost_low = turned(jnp.concatenate([(y_all * picks[0]).astype(bf16), blank], axis=0))
     ghost_high = turned(jnp.concatenate([(y_all * picks[1]).astype(bf16), blank], axis=0))
-    for e in range(planes, 2 * planes):
+
+    def edges(e, carry):
         for state in (state_a, state_b):
             state[e, 0] = ghost_low
             state[e, rows_y + 1] = ghost_high
+        return carry
+
+    lax.fori_loop(1, state_a.shape[0] - 1, edges, 0)
     fill(state_a, own, 0, lines, lines, pad_rows)
-    sends = [
-        pltpu.make_async_copy(state_a.at[pl.ds(planes, planes)], hand, sems.at[0]),
-        pltpu.make_async_copy(state_b.at[pl.ds(planes + 1, planes - 2)], inner, sems.at[1]),
-    ]
-    sends[0].start()
     kappa[...] = jnp.ones(kappa.shape, jnp.float32)
     kappa[pl.ds(lines, lines), pl.ds(0, rows_z)] = powers(classes[...])
     weight_rows(kappa, weights, stiff_rows, lines, flags[1], flags[2], rows_y, rows_z)
     middle = (lines + rows_y, lines - 2 * rows_y)
     relax_lines(state_a, state_b, weights, *middle, rows_y, rows_z, True)
-    sends[1].start()
-    for copy in sends:
-        copy.wait()
 
 
 def near_kernel(
     flags,
     near_a,
     near_b,
+    class_a,
+    class_b,
     classes,
     pad_rows,
-    hand,
-    inner,
-    hand_a,
-    hand_b,
+    old_a,
+    old_b,
+    state_a,
+    state_b,
     weights,
     stiff_rows,
     snap,
     gram,
-    state_a,
-    state_b,
     kappa,
     both,
-    sems,
 ):
-    lines = classes.shape[0]
-    rows_z = near_a.shape[1]
+    del old_a, old_b
+    lines, rows_z = classes.shape
     rows_y = pad_rows.shape[0]
-    planes = lines // rows_y
     near = lines // 2
     even, first, last = flags[0], flags[1], flags[2]
-    taken = [
-        pltpu.make_async_copy(hand, state_a.at[pl.ds(planes, planes)], sems.at[0]),
-        pltpu.make_async_copy(inner, state_b.at[pl.ds(planes + 1, planes - 2)], sems.at[1]),
-    ]
-    for copy in taken:
-        copy.start()
-
     base_a = pl.multiple_of(even * (2 * lines), 8)
     base_b = pl.multiple_of((1 - even) * (2 * lines), 8)
     kappa[...] = jnp.ones(kappa.shape, jnp.float32)
-    kappa[pl.ds(lines, lines), pl.ds(0, rows_z)] = powers(classes[...])
-    kappa[pl.ds(base_a, lines)] = powers(near_a[0][:lines].astype(jnp.float32).astype(jnp.int32))
-    kappa[pl.ds(base_b, lines)] = powers(near_b[0][:lines].astype(jnp.float32).astype(jnp.int32))
+    for base, marks in ((lines, classes), (base_a, class_a), (base_b, class_b)):
+        kappa[pl.ds(base, lines), pl.ds(0, rows_z)] = powers(marks[...])
     weight_rows(kappa, weights, stiff_rows, lines, first, last, rows_y, rows_z)
-    fill(state_a, near_a, 1, near, near + even * (lines + near), pad_rows)
-    fill(state_a, near_b, 1, near, near + (1 - even) * (lines + near), pad_rows)
-    for copy in taken:
-        copy.wait()
-    ghost_low = state_a[planes, 0]
-    ghost_high = state_a[planes, rows_y + 1]
-    for e in (planes - 2, planes - 1, 2 * planes, 2 * planes + 1):
-        state_a[e, 0] = ghost_low
-        state_a[e, rows_y + 1] = ghost_high
-    for e in (planes - 1, planes, 2 * planes - 1, 2 * planes):
-        state_b[e, 0] = ghost_low
-        state_b[e, rows_y + 1] = ghost_high
-
-    sent = []
-
-    def send(state, to, e, count, offset):
-        copy = pltpu.make_async_copy(
-            state.at[pl.ds(e, count)], to.at[pl.ds(e - offset, count)], sems.at[2 + len(sent)]
-        )
-        copy.start()
-        sent.append(copy)
-
+    fill(state_a, near_a, 0, near, near + even * (lines + near), pad_rows)
+    fill(state_a, near_b, 0, near, near + (1 - even) * (lines + near), pad_rows)
     step = functools.partial(relax_lines, weights=weights, rows_y=rows_y, rows_z=rows_z)
-    send(state_a, hand_a, planes - 2, 2, planes - 2)
-    send(state_a, hand_a, 2 * planes, 2, planes - 2)
     step(state_a, state_b, first_line=lines - rows_y, count=2 * rows_y, keep=True)
     step(state_a, state_b, first_line=2 * lines - rows_y, count=2 * rows_y, keep=True)
-    send(state_b, hand_b, planes - 1, 2, planes - 1)
-    send(state_b, hand_b, 2 * planes - 1, 2, planes - 1)
     step(state_b, state_a, first_line=lines, count=lines, keep=True)
-    send(state_a, hand_a, planes, planes, planes - 2)
     step(state_a, state_b, first_line=lines + rows_y, count=lines - 2 * rows_y, keep=False)
-    send(state_b, hand_b, planes + 1, planes - 2, planes - 1)
+    planes = lines // rows_y
     inside = range(planes + 1, 2 * planes - 1)
     blank = jnp.zeros(gram.shape, jnp.float32)
     gram[...] = gram_terms(state_b, inside, planes, stiff_rows, snap, both, blank)
-    for copy in sent:
-        copy.wait()
 
 
 def far_kernel(
@@ -324,59 +280,32 @@
     stiff_rows,
     pad_rows,
     near_gram,
-    hand_a,
-    hand_b,
+    old_a,
+    old_b,
+    state_a,
+    state_b,
     snap,
     gram,
-    state_a,
-    state_b,
     both,
-    sems,
 ):
+    del old_a, old_b
     width = snap.shape[1]
     rows_y = pad_rows.shape[0]
-    rows_z = far_a.shape[1]
+    far, rows_z = far_a.shape[:2]
     lines = stiff_rows.shape[1]
     planes = lines // rows_y
     half = rows_y // 2
     even = flags[0]
-    taken = []
-
-    def take(dst, src):
-        copy = pltpu.make_async_copy(src, dst, sems.at[len(taken)])
-        copy.start()
-        taken.append(copy)
-
-    top = rows_y + 1
-    a_off, b_off = planes - 2, planes - 1
-    take(state_a.at[pl.ds(a_off, 2)], hand_a.at[pl.ds(0, 2)])
-    take(state_a.at[pl.ds(2 * planes, 2)], hand_a.at[pl.ds(2 * planes - a_off, 2)])
-    take(state_a.at[1, top], hand_a.at[0, top])
-    take(state_a.at[3 * planes - 2, 0], hand_a.at[0, 0])
-    take(state_b.at[pl.ds(b_off, 2)], hand_b.at[pl.ds(0, 2)])
-    take(state_b.at[pl.ds(2 * planes - 1, 2)], hand_b.at[pl.ds(2 * planes - 1 - b_off, 2)])
-    take(state_b.at[2, top], hand_b.at[0, top])
-    take(state_b.at[3 * planes - 3, 0], hand_b.at[0, 0])
-    take(state_a.at[pl.ds(planes, planes)], hand_a.at[pl.ds(planes - a_off, planes)])
-    take(state_b.at[pl.ds(planes + 1, planes - 2)], hand_b.at[pl.ds(planes + 1 - b_off, planes - 2)])
-
-    far = far_a.shape[0]
     low_line = half
     high_line = 3 * lines - half - far
     fill(state_a, far_a, 0, far, low_line + even * (high_line - low_line), pad_rows)
     fill(state_a, far_b, 0, far, high_line - even * (high_line - low_line), pad_rows)
-
-    waits = {1: range(0, 4), 2: range(4, 8), 3: range(8, 9)}
     buffers = (state_a, state_b)
     for sweep in range(1, SWEEPS + 1):
-        for k in waits[sweep]:
-            taken[k].wait()
         src, dst = buffers[(sweep - 1) % 2], buffers[sweep % 2]
         for first_line in (half + sweep * rows_y, 3 * lines - half - far - sweep * rows_y):
             relax_lines(src, dst, weights, first_line, far, rows_y, rows_z, sweep < SWEEPS)
-    taken[9].wait()
     final = buffers[SWEEPS % 2]
-
     outer = (planes, 2 * planes - 1)
     total = gram_terms(final, outer, planes, stiff_rows, snap, both, near_gram[...])
     mass = total[:, :width]
@@ -404,12 +333,8 @@
     lines = initial.reshape(planes * rows_y, rows_z, width)
     count = planes * rows_y
     near, far, half = 2 * rows_y, 2 * rows_y - rows_y // 2, rows_y // 2
-    marks = classes.astype(jnp.bfloat16).reshape(1, count, rows_z)
-    marks = jnp.pad(marks, ((0, 0), (0, rows_z - count), (0, width - rows_z)))
-
     def near_part(upward):
-        part = lax.dynamic_slice_in_dim(lines, upward * (count - near), near, axis=0)
-        return jnp.concatenate([marks, part], axis=0)
+        return lax.dynamic_slice_in_dim(lines, upward * (count - near), near, axis=0)
 
     def far_part(upward):
         start = upward * half + (1 - upward) * near
@@ -417,67 +342,85 @@
 
     near_a = swap(near_part(even), 0)
     near_b = swap(near_part(1 - even), 1)
+    flat_classes = classes.reshape(count, rows_z)
+    class_a = swap(flat_classes, 0)
+    class_b = swap(flat_classes, 1)
     far_a = swap(far_part(even), 0)
     far_b = swap(far_part(1 - even), 1)
 
     vmem = pl.BlockSpec(memory_space=pltpu.VMEM)
     smem = pl.BlockSpec(memory_space=pltpu.SMEM)
-    hbm = pl.BlockSpec(memory_space=pltpu.HBM)
     state = pltpu.VMEM((3 * planes, rows_y + 2, width, LANES), jnp.float32)
-    params = pltpu.CompilerParams(vmem_limit_bytes=48 * 2**20)
     kappa = pltpu.VMEM((3 * count, LANES), jnp.float32)
     both = pltpu.VMEM((2 * width, rows_y * LANES), jnp.bfloat16)
-
-    def slab(depth):
-        return jax.ShapeDtypeStruct((depth, rows_y + 2, width, LANES), jnp.float32)
-
-    def sems(number):
-        return pltpu.SemaphoreType.DMA((number,))
+    params = pltpu.CompilerParams(vmem_limit_bytes=14 * 2**20)
 
     def kept(depth):
         return jax.ShapeDtypeStruct((depth, width, rows_y * LANES), jnp.bfloat16)
+
+    def held(item):
+        return pltpu.with_memory_space_constraint(item, pltpu.VMEM)
 
     rows = [
         jax.ShapeDtypeStruct((6, 3 * count, LANES), jnp.float32),
         jax.ShapeDtypeStruct((8, count, LANES), jnp.float32),
     ]
-    flat_classes = classes.reshape(count, rows_z)
-    hand, inner, pad_rows = pl.pallas_call(
+    state_a, state_b, pad_rows = pl.pallas_call(
         own_kernel,
         out_shape=[
-            slab(planes),
-            slab(planes - 2),
+            state,
+            state,
             jax.ShapeDtypeStruct((rows_y, LANES - rows_z, width), jnp.bfloat16),
         ],
         in_specs=[smem] + [vmem] * 5,
-        out_specs=[hbm, hbm, vmem],
-        scratch_shapes=[state, state, kappa]
-        + [pltpu.VMEM(item.shape, item.dtype) for item in rows]
-        + [sems(2)],
+        out_specs=[vmem] * 3,
+        scratch_shapes=[kappa] + [pltpu.VMEM(item.shape, item.dtype) for item in rows],
         compiler_params=params,
     )(flags, lines, flat_classes, y_vals, z_vals, face_ids[None])
-    hand_a, hand_b, weights, stiff_rows, snap_near, gram_near = pl.pallas_call(
+    state_a, state_b, weights, stiff_rows, snap_near, gram_near = pl.pallas_call(
         near_kernel,
         out_shape=[
-            slab(planes + 4),
-            slab(planes + 2),
+            state,
+            state,
             *rows,
             kept(planes - 2),
             jax.ShapeDtypeStruct((width, 2 * width), jnp.float32),
         ],
-        in_specs=[smem] + [vmem] * 4 + [hbm] * 2,
-        out_specs=[hbm, hbm] + [vmem] * 4,
-        scratch_shapes=[state, state, kappa, both, sems(8)],
+        in_specs=[smem] + [vmem] * 8,
+        out_specs=[vmem] * 6,
+        scratch_shapes=[kappa, both],
+        input_output_aliases={7: 0, 8: 1},
         compiler_params=params,
-    )(flags, near_a, near_b, flat_classes, pad_rows, hand, inner)
-    snap_far, gram = pl.pallas_call(
+    )(
+        flags,
+        near_a,
+        near_b,
+        class_a,
+        class_b,
+        flat_classes,
+        pad_rows,
+        held(state_a),
+        held(state_b),
+    )
+    _, _, snap_far, gram = pl.pallas_call(
         far_kernel,
-        out_shape=[kept(2), jax.ShapeDtypeStruct((width + 8, width), jnp.float32)],
-        in_specs=[smem] + [vmem] * 6 + [hbm] * 2,
-        out_specs=[vmem, vmem],
-        scratch_shapes=[state, state, both, sems(10)],
+        out_shape=[state, state, kept(2), jax.ShapeDtypeStruct((width + 8, width), jnp.float32)],
+        in_specs=[smem] + [vmem] * 8,
+        out_specs=[vmem] * 4,
+        scratch_shapes=[both],
+        input_output_aliases={7: 0, 8: 1},
         compiler_params=params,
-    )(flags, far_a, far_b, weights, stiff_rows, pad_rows, gram_near, hand_a, hand_b)
+    )(
+        flags,
+        far_a,
+        far_b,
+        weights,
+        stiff_rows,
+        pad_rows,
+        gram_near,
+        held(state_a),
+        held(state_b),
+    )
     return snap_near, snap_far, gram
 
 
@@ -487,34 +430,54 @@
 
 def row_copy(tile, row):
     return jnp.broadcast_to(tile[row : row + 1, :], (8, tile.shape[1]))
+
+
+def eliminate(cols, panels):
+    grid = {(i, j): row_copy(cols[j], i) for j in range(8) for i in range(j, 8)}
+    rows = [[row_copy(panel, i) for panel in panels] for i in range(8)]
+    factor, pivots, recips = {}, [], []
+    for j in range(8):
+        pivot = grid[j, j]
+        recip = pl.reciprocal(pivot, approx=True)
+        pivots.append(pivot)
+        recips.append(recip)
+        for i in range(j + 1, 8):
+            factor[i, j] = grid[i, j] * recip
+            for k in range(j + 1, i + 1):
+                grid[i, k] = grid[i, k] - factor[i, j] * grid[k, j]
+            rows[i] = [a - factor[i, j][:, : a.shape[1]] * b for a, b in zip(rows[i], rows[j])]
+    solved = [[a * recips[i][:, : a.shape[1]] for a in rows[i]] for i in range(8)]
+    for i in range(7, 0, -1):
+        for j in range(i):
+            solved[j] = [
+                a - factor[i, j][:, : a.shape[1]] * b for a, b in zip(solved[j], solved[i])
+            ]
+    return rows, pivots, solved
+
+
+def gather_rows(rows):
+    sub = lax.broadcasted_iota(jnp.int32, rows[0].shape, 0)
+    out = rows[0]
+    for i in range(1, 8):
+        out = jnp.where(sub == i, rows[i], out)
+    return out
 
 
 def solve_spd(left, right):
     size = left.shape[0]
     count = size // 8
-    sub = lax.broadcasted_iota(jnp.int32, (8, 128), 0)
     lhs = [left[8 * t : 8 * t + 8] for t in range(count)]
     rhs = [right[8 * t : 8 * t + 8] for t in range(count)]
     for k in range(count):
         cols = [lane_copy(lhs[k], 8 * k + j) for j in range(8)]
-        panel_l, panel_r = lhs[k], rhs[k]
-        for j in range(8):
-            recip = pl.reciprocal(row_copy(cols[j], j), approx=True)
-            here = sub == j
-            mult = jnp.where(here, recip, -cols[j] * recip)
-            for l in range(j + 1, 8):
-                cols[l] = jnp.where(here, 0.0, cols[l]) + mult * row_copy(cols[l], j)
-            panel_l = jnp.where(here, 0.0, panel_l) + mult * row_copy(panel_l, j)
-            panel_r = jnp.where(here, 0.0, panel_r) + mult * row_copy(panel_r, j)
-        rows_l = [row_copy(panel_l, j) for j in range(8)]
-        rows_r = [row_copy(panel_r, j) for j in range(8)]
-        order = list(range(k + 1, count)) + list(range(k))
-        for t in order:
+        _, _, solved = eliminate(cols, [lhs[k], rhs[k]])
+        for t in list(range(k + 1, count)) + list(range(k)):
             tile_cols = [lane_copy(lhs[t], 8 * k + j) for j in range(8)]
             if k + 1 < count:
-                lhs[t] = lhs[t] - tree([tile_cols[j] * rows_l[j] for j in range(8)])
-            rhs[t] = rhs[t] - tree([tile_cols[j] * rows_r[j] for j in range(8)])
-        lhs[k], rhs[k] = panel_l, panel_r
+                lhs[t] = lhs[t] - tree([tile_cols[j] * solved[j][0] for j in range(8)])
+            rhs[t] = rhs[t] - tree([tile_cols[j] * solved[j][1] for j in range(8)])
+        lhs[k] = gather_rows([solved[j][0] for j in range(8)])
+        rhs[k] = gather_rows([solved[j][1] for j in range(8)])
     return jnp.concatenate(rhs, axis=0)
 
 
@@ -527,30 +490,17 @@
 def whiten(inner, block):
     size = inner.shape[0]
     count = size // 8
-    sub = lax.broadcasted_iota(jnp.int32, (8, 128), 0)
     lhs = [inner[8 * t : 8 * t + 8] for t in range(count)]
     rhs = [block[8 * t : 8 * t + 8] for t in range(count)]
     done = []
     for k in range(count):
-        live = range(k, count)
-        cols = {t: [lane_copy(lhs[t], 8 * k + j) for j in range(8)] for t in live}
-        scale = None
-        for j in range(8):
-            pivot = row_copy(cols[k][j], j)
-            recip = pl.reciprocal(pivot, approx=True)
-            root = lax.rsqrt(pivot)
-            scale = root if scale is None else jnp.where(sub >= j, root, scale)
-            head = {l: row_copy(cols[k][l], j) for l in range(j + 1, 8)}
-            row_l, row_r = row_copy(lhs[k], j), row_copy(rhs[k], j)
-            for t in live:
-                mult = cols[t][j] * recip
-                if t == k:
-                    mult = jnp.where(sub > j, mult, 0.0)
-                for l in range(j + 1, 8):
-                    cols[t][l] = cols[t][l] - mult * head[l]
-                lhs[t] = lhs[t] - mult[:, : row_l.shape[1]] * row_l
-                rhs[t] = rhs[t] - mult * row_r
-        done.append(rhs[k] * scale)
+        cols = [lane_copy(lhs[k], 8 * k + j) for j in range(8)]
+        rows, pivots, solved = eliminate(cols, [lhs[k], rhs[k]])
+        done.append(gather_rows([rows[j][1] * lax.rsqrt(pivots[j]) for j in range(8)]))
+        for t in range(k + 1, count):
+            tile_cols = [lane_copy(lhs[t], 8 * k + j) for j in range(8)]
+            lhs[t] = lhs[t] - tree([tile_cols[j][:, :size] * solved[j][0] for j in range(8)])
+            rhs[t] = rhs[t] - tree([tile_cols[j] * solved[j][1] for j in range(8)])
     return jnp.concatenate(done, axis=0)
 
 

time: 87.9 us -> 103 us (1.17)
  waiting for transfers between devices: 9.11 us -> 24.9 us
  local copies, waits for them, and re-layouts: 3.39 us -> 9.81 us
  Pallas kernels: 41.7 us -> 37.3 us
  other arithmetic: 2.15 us -> 0.08 us
    ppermute x4 -> x6, waiting for transfers between devices: 7.18 us -> 21.9 us  [swap(): return lax.ppermute(array, 'sub', pairs + [(j, i) for i, j in pairs])]
    pallas_call x3, Pallas kernels: 30.4 us -> 24.8 us  [the longest x1 11 us: relax(): pl.pallas_call(near_kernel, out_shape=[state, state, *rows, kept(planes -...]
    unnamed x15, local copies, waits for them, and re-layouts: 0.78 us -> 5 us
    ppermute x3, starting transfers between devices: 9.54 us -> 7.44 us  [on_device(): lax.ppermute(own, 'sub', [(i, (i + shift) % subs) for i in range(subs)])]
    concatenate x1 -> x0, other arithmetic: 1.29 us -> none  [near_part(): return jnp.concatenate([marks, part], axis=0)]
    dynamic_slice x1, local copies, waits for them, and re-layouts: 1.47 us -> 2.66 us  [near_part(): lax.dynamic_slice_in_dim(lines, upward * (count - near), near, axis=0)]
    pallas_call x1, Pallas kernels: 11.3 us -> 12.5 us  [on_device(): pl.pallas_call(functools.partial(modes_kernel, float(subs * cells), rows_...]
    ppermute x4 -> x6, starting transfers between devices: 9.6 us -> 10.7 us  [swap(): return lax.ppermute(array, 'sub', pairs + [(j, i) for i, j in pairs])]
  transfers between devices with their start and end apart: 7 -> 9, of which waited for: 3 -> 2; matrix products, arithmetic and copies ran while one was open for 1% -> 2% of each run, Pallas kernels for 20% -> 14%
where the time goes in v7:
time: 103 us; the launch traced here: 102 us
  Pallas kernels  37.3 us (36%)
  waiting for transfers between devices  24.9 us (24%)
  starting transfers between devices  18.1 us (18%)
  blocking collectives  11.8 us (11%)
  local copies, waits for them, and re-layouts  9.81 us (10%)
    ppermute x6, waiting for transfers between devices, swap(): return lax.ppermute(array, 'sub', pairs + [(j, i) for i, j in pairs])  21.9 us
    pallas_call x1, Pallas kernels, on_device(): pl.pallas_call(functools.partial(modes_kernel, float(subs * cells), rows_...  12.5 us
    all_to_all x1, blocking collectives, on_device(): lax.all_to_all(pieces, 'nbhd', split_axis=0, concat_axis=0, tiled=True)  11.8 us
    pallas_call x1, Pallas kernels, relax(): pl.pallas_call(near_kernel, out_shape=[state, state, *rows, kept(planes -...  11 us
    ppermute x6, starting transfers between devices, swap(): return lax.ppermute(array, 'sub', pairs + [(j, i) for i, j in pairs])  10.7 us
    pallas_call x1, Pallas kernels, relax(): pl.pallas_call(far_kernel, out_shape=[state, state, kept(2), jax.ShapeDty...  10.2 us
    ppermute x3, starting transfers between devices, on_device(): lax.ppermute(own, 'sub', [(i, (i + shift) % subs) for i in range(subs)])  7.44 us
    unnamed x15, local copies, waits for them, and re-layouts  5 us
  transfers between devices with their start and end apart: 9, of which 2 were waited for; matrix products, arithmetic and copies ran while one was open for 2% of the time, Pallas kernels for 14%

profile of v7, /device:TPU:0, one launch (start us, length us, event | category | flops | bytes accessed | tf_op | source)
XLA Modules:
  0.0 102.3 jit_solution(5045817325580943962)
XLA Ops:
  0.0 2.7 %constant_dynamic-slice_fusion = (bf16[32,96,128]{2,1,0:T(8,128)(2,1)}, bf16[32,96,128]{2,1,0:T(8,128)(2,1)}) fusion(bf16[64,96,128]{2,1,0:T(8,128)(2,1)} %bitcast.13, s32[]{:T(128)S(6)} %select_n.27, s32[]{:T(128)S(6)} %select_n.26), kind=kLoop, calls=%fused_computation | loop fusion | bytes 3145736 | tf_op jit(solution)/shard_map/dynamic_slice | solution.py:337
  2.7 3.0 %collective-permute-start.2 = (bf16[32,96,128]{2,1,0:T(8,128)(2,1)}, bf16[32,96,128]{2,1,0:T(8,128)(2,1)S(1)}, u32[]{:S(2)}, u32[]{:S(2)}) collective-permute-start(bf16[32,96,128]{2,1,0:T(8,128)(2,1)} %get-tuple-element.28), channel_id=1, source_target_pairs={{0,1},{2,3},{1,0},{3,2},{4,5},{6,7},{5,4},{7,6},{8,9},{10,11},{9,8... | collective-permute-start | bytes 2359304 | tf_op jit(solution)/shard_map/ppermute | solution.py:324
  5.7 0.7 collective-permute-start.3
  6.4 2.1 %constant_dynamic-slice_fusion.2 = (bf16[24,96,128]{2,1,0:T(8,128)(2,1)S(1)}, bf16[24,96,128]{2,1,0:T(8,128)(2,1)}) fusion(bf16[64,96,128]{2,1,0:T(8,128)(2,1)} %bitcast.14, s32[]{:T(128)S(6)} %select_n.25, s32[]{:T(128)S(6)} %select_n.24), kind=kLoop, calls=%fused_computation.2 | loop fusion | bytes 2359304 | tf_op jit(solution)/shard_map/dynamic_slice | solution.py:341
  8.6 4.3 %collective-permute-start = (bf16[24,96,128]{2,1,0:T(8,128)(2,1)}, bf16[24,96,128]{2,1,0:T(8,128)(2,1)S(1)}, u32[]{:S(2)}, u32[]{:S(2)}) collective-permute-start(bf16[24,96,128]{2,1,0:T(8,128)(2,1)} %get-tuple-element.30), channel_id=1, source_target_pairs={{0,1},{2,3},{1,0},{3,2},{4,5},{6,7},{5,4},{7,6},{8,9},{10,11},{9,8... | collective-permute-start | bytes 1769480 | tf_op jit(solution)/shard_map/ppermute | solution.py:324
  12.9 0.7 collective-permute-start.1
  13.6 1.3 %collective-permute-start.4 = (s32[64,96]{1,0:T(8,128)}, s32[64,96]{1,0:T(8,128)S(1)}, u32[]{:S(2)}, u32[]{:S(2)}) collective-permute-start(s32[64,96]{1,0:T(8,128)} %bitcast.16), channel_id=1, source_target_pairs={{0,1},{2,3},{1,0},{3,2},{4,5},{6,7},{5,4},{7,6},{8,9},{10,11},{9,8... | collective-permute-start | bytes 73736 | tf_op jit(solution)/shard_map/ppermute | solution.py:324
  14.9 21.9 %collective-permute-done.4.class_a = s32[64,96]{1,0:T(8,128)S(1)} collective-permute-done((s32[64,96]{1,0:T(8,128)}, s32[64,96]{1,0:T(8,128)S(1)}, u32[]{:S(2)}, u32[]{:S(2)}) %collective-permute-start.4) | collective-permute-done | bytes 24608 | tf_op jit(solution)/shard_map/ppermute | solution.py:324
  36.8 0.7 collective-permute-start.5
  37.4 0.1 pad_add_fusion.flags
  37.5 1.4 %copy-done.1 = bf16[1,4,16,96,128]{4,3,2,1,0:T(8,128)(2,1)S(1)} copy-done((bf16[1,4,16,96,128]{4,3,2,1,0:T(8,128)(2,1)S(1)}, bf16[1,4,16,96,128]{4,3,2,1,0:T(8,128)(2,1)}, u32[]{:S(2)}) %copy-start.1) | copy-done | bytes 1572888
  38.9 0.8 copy-done.2
  39.7 0.7 copy-done.3
  40.4 0.7 copy-done.5
  41.1 0.7 copy-done.6
  41.8 3.7 %shard_map.73 = (f32[12,18,128,128]{3,2,1,0:T(8,128)S(1)}, f32[12,18,128,128]{3,2,1,0:T(8,128)S(1)}, bf16[16,32,128]{2,1,0:T(8,128)(2,1)S(1)}) custom-call(s32[4]{0:T(128)S(1)} %pad_add_fusion.flags, bf16[64,96,128]{2,1,0:T(8,128)(2,1)S(1)} %bitcast.15, s32[64,96]{1,0:T(8,128)S(1)} %bitcast.18, bf16[96,128]{1,0:T(8,128)(2,1)S(1)} %bitcast.20, ...), custom_call_target="tpu_custom_call" | custom-call | tf_op jit(solution)/shard_map/pallas_call | solution.py:368
  45.5 11.0 %shard_map.74 = (f32[12,18,128,128]{3,2,1,0:T(8,128)S(1)}, f32[12,18,128,128]{3,2,1,0:T(8,128)S(1)}, f32[6,192,128]{2,1,0:T(8,128)S(1)}, f32[8,64,128]{2,1,0:T(8...) custom-call(s32[4]{0:T(128)S(1)} %pad_add_fusion.flags, ...), custom_call_target="tpu_custom_call", output_to_operand_aliasing={{0}: (7, {}), {1}: (8, {})} | custom-call | tf_op jit(solution)/shard_map/pallas_call | solution.py:380
  56.5 10.2 %shard_map.75 = (f32[12,18,128,128]{3,2,1,0:T(8,128)S(1)}, f32[12,18,128,128]{3,2,1,0:T(8,128)S(1)}, bf16[2,128,2048]{2,1,0:T(8,128)(2,1)S(1)}, f32[136,128]{1,0:T(8,128)S(1)}) custom-call(s32[4]{0:T(128)S(1)} %pad_add_fusion.flags, bf16[24,96,128]{2,1,0:T(8,128)(2,1)S(1)} %collective-permute-done.far_a, ...), custom_call_target="tpu_custom_call", output_to_operand_aliasing={{0}: (7, {}), {1}: (8, {})} | custom-call | tf_op jit(solution)/shard_map/pallas_call | solution.py:405
  66.7 4.6 %collective-permute-start.6 = (f32[136,128]{1,0:T(8,128)S(1)}, f32[136,128]{1,0:T(8,128)S(1)}, u32[]{:S(2)}, u32[]{:S(2)}) collective-permute-start(f32[136,128]{1,0:T(8,128)S(1)} %get-tuple-element.24.refs_1_), channel_id=1, source_target_pairs={{0,1},{1,2},{2,3},{3,0},{4,5},{5,6},{6,7},{7,4},{8,9},{9,10},{10,1... | collective-permute-start | bytes 208904 | tf_op jit(solution)/shard_map/ppermute | solution.py:565
  71.3 2.8 %collective-permute-start.8 = (f32[136,128]{1,0:T(8,128)S(1)}, f32[136,128]{1,0:T(8,128)S(1)}, u32[]{:S(2)}, u32[]{:S(2)}) collective-permute-start(f32[136,128]{1,0:T(8,128)S(1)} %get-tuple-element.24.refs_1_), channel_id=1, source_target_pairs={{0,3},{1,0},{2,1},{3,2},{4,7},{5,4},{6,5},{7,6},{8,11},{9,8},{10,9... | collective-permute-start | bytes 208904 | tf_op jit(solution)/shard_map/ppermute | solution.py:565
  74.1 3.0 %collective-permute-done.7.refs_3_ = f32[136,128]{1,0:T(8,128)S(1)} collective-permute-done((f32[136,128]{1,0:T(8,128)S(1)}, f32[136,128]{1,0:T(8,128)S(1)}, u32[]{:S(2)}, u32[]{:S(2)}) %collective-permute-start.7) | collective-permute-done | bytes 69664 | tf_op jit(solution)/shard_map/ppermute | solution.py:565
  77.1 12.5 %shard_map.76 = bf16[8,32,768]{2,1,0:T(8,128)(2,1)S(1)} custom-call(s32[8]{0:T(128)S(1)} %fusion.refs_0_, f32[136,128]{1,0:T(8,128)S(1)} %get-tuple-element.24.refs_1_, f32[136,128]{1,0:T(8,128)S(1)} %collective-permute-done.6.refs_2_, f32[136,128]{1,0:T(8,128)S(1)} %collective-permute-done.7.refs_3_, f32[136,128]{1,0:T(8,128)S(1)} %collective-permute-done.8.refs_4_, ...), custom_call_target="tpu_custom_call" | custom-call | tf_op jit(solution)/shard_map/pallas_call | solution.py:571
  89.7 11.8 %all_to_all.5 = bf16[8,32,768]{2,1,0:T(8,128)(2,1)S(1)} all-to-all(bf16[8,32,768]{2,1,0:T(8,128)(2,1)S(1)} %shard_map.76), channel_id=1, replica_groups=mesh['nbhd'=8,'sub'=4] {'nbhd'}, dimensions={0} | all-to-all | bytes 786432 | tf_op jit(solution)/shard_map/all_to_all | solution.py:583
  101.5 0.7 copy.17
  (18 shorter events, 0.0 us)
Async XLA Ops:
  0.0 74.1 %copy-start = (s32[8,8]{1,0:T(8,128)S(1)}, s32[8,8]{1,0:T(8,128)}, u32[]{:S(2)}) copy-start(s32[8,8]{1,0:T(8,128)} %param.13) | copy-start | bytes 772
  2.7 42.8 %collective-permute-start.2 = (bf16[32,96,128]{2,1,0:T(8,128)(2,1)}, bf16[32,96,128]{2,1,0:T(8,128)(2,1)S(1)}, u32[]{:S(2)}, u32[]{:S(2)}) collective-permute-start(bf16[32,96,128]{2,1,0:T(8,128)(2,1)} %get-tuple-element.28), channel_id=1, source_target_pairs={{0,1},{2,3},{1,0},{3,2},{4,5},{6,7},{5,4},{7,6},{8,9},{10,11},{9,8... | collective-permute-start | bytes 2359304 | tf_op jit(solution)/shard_map/ppermute | solution.py:324
  5.7 39.8 %collective-permute-start.3 = (bf16[32,96,128]{2,1,0:T(8,128)(2,1)}, bf16[32,96,128]{2,1,0:T(8,128)(2,1)S(1)}, u32[]{:S(2)}, u32[]{:S(2)}) collective-permute-start(bf16[32,96,128]{2,1,0:T(8,128)(2,1)} %get-tuple-element.27), channel_id=1, source_target_pairs={{1,2},{2,1},{5,6},{6,5},{9,10},{10,9},{13,14},{14,13},{17,18},{18,... | collective-permute-start | bytes 2359304 | tf_op jit(solution)/shard_map/ppermute | solution.py:324
  8.6 47.9 %collective-permute-start = (bf16[24,96,128]{2,1,0:T(8,128)(2,1)}, bf16[24,96,128]{2,1,0:T(8,128)(2,1)S(1)}, u32[]{:S(2)}, u32[]{:S(2)}) collective-permute-start(bf16[24,96,128]{2,1,0:T(8,128)(2,1)} %get-tuple-element.30), channel_id=1, source_target_pairs={{0,1},{2,3},{1,0},{3,2},{4,5},{6,7},{5,4},{7,6},{8,9},{10,11},{9,8... | collective-permute-start | bytes 1769480 | tf_op jit(solution)/shard_map/ppermute | solution.py:324
  12.9 43.6 %collective-permute-start.1 = (bf16[24,96,128]{2,1,0:T(8,128)(2,1)S(1)}, bf16[24,96,128]{2,1,0:T(8,128)(2,1)S(1)}, u32[]{:S(2)}, u32[]{:S(2)}) collective-permute-start(bf16[24,96,128]{2,1,0:T(8,128)(2,1)S(1)} %get-tuple-element.29), channel_id=1, source_target_pairs={{1,2},{2,1},{5,6},{6,5},{9,10},{10,9},{13,14},{14,13},{17,18},{18,... | collective-permute-start | bytes 1769480 | tf_op jit(solution)/shard_map/ppermute | solution.py:324
  13.6 23.2 %collective-permute-start.4 = (s32[64,96]{1,0:T(8,128)}, s32[64,96]{1,0:T(8,128)S(1)}, u32[]{:S(2)}, u32[]{:S(2)}) collective-permute-start(s32[64,96]{1,0:T(8,128)} %bitcast.16), channel_id=1, source_target_pairs={{0,1},{2,3},{1,0},{3,2},{4,5},{6,7},{5,4},{7,6},{8,9},{10,11},{9,8... | collective-permute-start | bytes 73736 | tf_op jit(solution)/shard_map/ppermute | solution.py:324
  36.8 8.7 %collective-permute-start.5 = (s32[64,96]{1,0:T(8,128)}, s32[64,96]{1,0:T(8,128)S(1)}, u32[]{:S(2)}, u32[]{:S(2)}) collective-permute-start(s32[64,96]{1,0:T(8,128)} %bitcast.17), channel_id=1, source_target_pairs={{1,2},{2,1},{5,6},{6,5},{9,10},{10,9},{13,14},{14,13},{17,18},{18,... | collective-permute-start | bytes 73736 | tf_op jit(solution)/shard_map/ppermute | solution.py:324
  37.5 1.4 %copy-start.1 = (bf16[1,4,16,96,128]{4,3,2,1,0:T(8,128)(2,1)S(1)}, bf16[1,4,16,96,128]{4,3,2,1,0:T(8,128)(2,1)}, u32[]{:S(2)}) copy-start(bf16[1,4,16,96,128]{4,3,2,1,0:T(8,128)(2,1)} %param.7) | copy-start | bytes 4718596
  38.9 0.8 copy-start.2
  39.7 0.7 copy-start.3
  40.4 0.7 copy-start.5
  41.1 0.7 copy-start.6
  56.5 20.6 %copy-start.4 = (f32[1,128,32]{1,2,0:T(8,128)S(1)}, f32[1,128,32]{1,2,0:T(8,128)}, u32[]{:S(2)}) copy-start(f32[1,128,32]{1,2,0:T(8,128)} %param.12) | copy-start | bytes 49156
  66.7 7.5 %collective-permute-start.6 = (f32[136,128]{1,0:T(8,128)S(1)}, f32[136,128]{1,0:T(8,128)S(1)}, u32[]{:S(2)}, u32[]{:S(2)}) collective-permute-start(f32[136,128]{1,0:T(8,128)S(1)} %get-tuple-element.24.refs_1_), channel_id=1, source_target_pairs={{0,1},{1,2},{2,3},{3,0},{4,5},{5,6},{6,7},{7,4},{8,9},{9,10},{10,1... | collective-permute-start | bytes 208904 | tf_op jit(solution)/shard_map/ppermute | solution.py:565
  71.3 5.8 %collective-permute-start.7 = (f32[136,128]{1,0:T(8,128)S(1)}, f32[136,128]{1,0:T(8,128)S(1)}, u32[]{:S(2)}, u32[]{:S(2)}) collective-permute-start(f32[136,128]{1,0:T(8,128)S(1)} %get-tuple-element.24.refs_1_), channel_id=1, source_target_pairs={{0,2},{1,3},{2,0},{3,1},{4,6},{5,7},{6,4},{7,5},{8,10},{9,11},{10,... | collective-permute-start | bytes 208904 | tf_op jit(solution)/shard_map/ppermute | solution.py:565
  71.3 5.8 %collective-permute-start.8 = (f32[136,128]{1,0:T(8,128)S(1)}, f32[136,128]{1,0:T(8,128)S(1)}, u32[]{:S(2)}, u32[]{:S(2)}) collective-permute-start(f32[136,128]{1,0:T(8,128)S(1)} %get-tuple-element.24.refs_1_), channel_id=1, source_target_pairs={{0,3},{1,0},{2,1},{3,2},{4,7},{5,4},{6,5},{7,6},{8,11},{9,8},{10,9... | collective-permute-start | bytes 208904 | tf_op jit(solution)/shard_map/ppermute | solution.py:565

commit v8 on v7

--- a/solution.py
+++ b/solution.py
@@ -116,25 +116,28 @@
 PART = 64
 
 
-def relax_lines(src, dst, weights, first_line, count, rows_y, rows_z, keep):
+def relax_lines(src, dst, weights, first_lines, count, rows_y, rows_z, keep):
     width = src.shape[2]
     group = 8
+    total = weights.shape[1] // rows_y
+    src_skip = (total - src.shape[0]) // 2
+    dst_skip = (total - dst.shape[0]) // 2
     valid = lax.broadcasted_iota(jnp.int32, (PART, LANES), 1) < rows_z
 
     def body(i, carry):
         waiting = []
-        for j in range(group):
-            line = first_line + i * group + j
+        for j in range(group * len(first_lines)):
+            line = first_lines[j // group] + i * group + j % group
             e, y = place(line, rows_y)
             rows = [weights[k, pl.ds(line, 1)] for k in range(6)]
             for start in range(0, width, PART):
                 some = pl.ds(start, PART)
-                middle = src[e, y + 1, some]
-                fresh = neighbour_sum(src, e, y, rows, some, middle)
+                middle = src[e - src_skip, y + 1, some]
+                fresh = neighbour_sum(src, e - src_skip, y, rows, some, middle)
                 fresh = fresh.astype(jnp.bfloat16).astype(jnp.float32)
                 if keep:
                     fresh = jnp.where(valid, fresh, middle)
-                waiting.append((e, y, some, fresh))
+                waiting.append((e - dst_skip, y, some, fresh))
                 if len(waiting) > 1:
                     e0, y0, some0, value = waiting.pop(0)
                     dst[e0, y0 + 1, some0] = value
@@ -150,6 +153,7 @@
     rows_y = columns // LANES
     for item, e in enumerate(places):
         p = e - planes
+        e = e - (3 * planes - final.shape[0]) // 2
         waiting = []
 
         def store(y, some, below, values, item=item):
@@ -181,6 +185,37 @@
     return jnp.left_shift(jnp.int32(1), 2 * marks).astype(jnp.float32)
 
 
+def pack_kernel(flags, class_map, lines, near_a, near_b, far_a, far_b, classes, sems):
+    count, rows_z = classes.shape
+    far = far_a.shape[0]
+    near = near_a.shape[0] - 1
+    upward = flags[0]
+    fetch = pltpu.make_async_copy(class_map, classes, sems.at[4])
+    fetch.start()
+    copies = []
+    for out, skip, size, start in (
+        (near_a, 1, near, upward * (count - near)),
+        (near_b, 1, near, (1 - upward) * (count - near)),
+        (far_a, 0, far, near - upward * far),
+        (far_b, 0, far, near - (1 - upward) * far),
+    ):
+        copies.append(
+            pltpu.make_async_copy(
+                lines.at[pl.ds(start, size)], out.at[pl.ds(skip, size)], sems.at[len(copies)]
+            )
+        )
+        copies[-1].start()
+    fetch.wait()
+    marks = classes[...].astype(jnp.float32).astype(jnp.bfloat16)
+    width = near_a.shape[2]
+    marks = jnp.concatenate([marks, jnp.zeros((count, width - rows_z), jnp.bfloat16)], axis=1)
+    for out in (near_a, near_b):
+        out[0, pl.ds(0, count)] = marks
+        out[0, pl.ds(count, rows_z - count)] = jnp.zeros((rows_z - count, width), jnp.bfloat16)
+    for copy in copies:
+        copy.wait()
+
+
 def own_kernel(
     flags,
     own,
@@ -191,6 +226,9 @@
     state_a,
     state_b,
     pad_rows,
+    last_a,
+    last_b,
+    own_kappa,
     kappa,
     weights,
     stiff_rows,
@@ -215,27 +253,29 @@
     ghost_high = turned(jnp.concatenate([(y_all * picks[1]).astype(bf16), blank], axis=0))
 
     def edges(e, carry):
-        for state in (state_a, state_b):
-            state[e, 0] = ghost_low
-            state[e, rows_y + 1] = ghost_high
+        for state, at in ((state_a, e + 1), (state_b, e)):
+            state[at, 0] = ghost_low
+            state[at, rows_y + 1] = ghost_high
         return carry
 
-    lax.fori_loop(1, state_a.shape[0] - 1, edges, 0)
+    lax.fori_loop(0, state_b.shape[0], edges, 0)
     fill(state_a, own, 0, lines, lines, pad_rows)
     kappa[...] = jnp.ones(kappa.shape, jnp.float32)
     kappa[pl.ds(lines, lines), pl.ds(0, rows_z)] = powers(classes[...])
+    own_kappa[...] = kappa[pl.ds(lines, lines)]
     weight_rows(kappa, weights, stiff_rows, lines, flags[1], flags[2], rows_y, rows_z)
-    middle = (lines + rows_y, lines - 2 * rows_y)
-    relax_lines(state_a, state_b, weights, *middle, rows_y, rows_z, True)
+    inside = lines - 2 * rows_y
+    relax_lines(state_a, state_b, weights, (lines + rows_y,), inside, rows_y, rows_z, True)
+    half = rows_y // 2
+    for out, upward in ((last_a, flags[0]), (last_b, 1 - flags[0])):
+        out[...] = own[pl.ds(upward * half + (1 - upward) * (lines - rows_y), half)]
 
 
 def near_kernel(
     flags,
     near_a,
     near_b,
-    class_a,
-    class_b,
-    classes,
+    own_kappa,
     pad_rows,
     old_a,
     old_b,
@@ -249,33 +289,57 @@
     both,
 ):
     del old_a, old_b
-    lines, rows_z = classes.shape
+    lines = own_kappa.shape[0]
+    rows_z = near_a.shape[1]
     rows_y = pad_rows.shape[0]
     near = lines // 2
     even, first, last = flags[0], flags[1], flags[2]
     base_a = pl.multiple_of(even * (2 * lines), 8)
     base_b = pl.multiple_of((1 - even) * (2 * lines), 8)
     kappa[...] = jnp.ones(kappa.shape, jnp.float32)
-    for base, marks in ((lines, classes), (base_a, class_a), (base_b, class_b)):
-        kappa[pl.ds(base, lines), pl.ds(0, rows_z)] = powers(marks[...])
+    kappa[pl.ds(lines, lines)] = own_kappa[...]
+    for base, part in ((base_a, near_a), (base_b, near_b)):
+        marks = part[0][:lines].astype(jnp.float32).astype(jnp.int32)
+        kappa[pl.ds(base, lines)] = powers(marks)
     weight_rows(kappa, weights, stiff_rows, lines, first, last, rows_y, rows_z)
-    fill(state_a, near_a, 0, near, near + even * (lines + near), pad_rows)
-    fill(state_a, near_b, 0, near, near + (1 - even) * (lines + near), pad_rows)
+    fill(state_a, near_a, 1, near, near + even * (lines + near), pad_rows)
+    fill(state_a, near_b, 1, near, near + (1 - even) * (lines + near), pad_rows)
     step = functools.partial(relax_lines, weights=weights, rows_y=rows_y, rows_z=rows_z)
-    step(state_a, state_b, first_line=lines - rows_y, count=2 * rows_y, keep=True)
-    step(state_a, state_b, first_line=2 * lines - rows_y, count=2 * rows_y, keep=True)
-    step(state_b, state_a, first_line=lines, count=lines, keep=True)
-    step(state_a, state_b, first_line=lines + rows_y, count=lines - 2 * rows_y, keep=False)
+    ends = (lines - rows_y, 2 * lines - rows_y)
+    step(state_a, state_b, first_lines=ends, count=2 * rows_y, keep=True)
+    step(state_b, state_a, first_lines=(lines,), count=lines, keep=True)
+    inner = (lines + rows_y,)
+    step(state_a, state_b, first_lines=inner, count=lines - 2 * rows_y, keep=False)
     planes = lines // rows_y
     inside = range(planes + 1, 2 * planes - 1)
     blank = jnp.zeros(gram.shape, jnp.float32)
     gram[...] = gram_terms(state_b, inside, planes, stiff_rows, snap, both, blank)
 
 
-def far_kernel(
+def advance(buffers, weights, low_line, count, total, rows_y, rows_z):
+    for sweep in range(1, SWEEPS + 1):
+        src, dst = buffers[(sweep - 1) % 2], buffers[sweep % 2]
+        low = low_line + sweep * rows_y
+        ends = (low, total - low - count)
+        relax_lines(src, dst, weights, ends, count, rows_y, rows_z, sweep < SWEEPS)
+
+
+def far_kernel(flags, far_a, far_b, weights, pad_rows, old_a, old_b, state_a, state_b):
+    del old_a, old_b
+    rows_y = pad_rows.shape[0]
+    count, rows_z = far_a.shape[:2]
+    total = weights.shape[1]
+    even = flags[0]
+    shift = even * (total - 2 * rows_y - count)
+    fill(state_a, far_a, 0, count, rows_y + shift, pad_rows)
+    fill(state_a, far_b, 0, count, total - rows_y - count - shift, pad_rows)
+    advance((state_a, state_b), weights, rows_y, count, total, rows_y, rows_z)
+
+
+def last_kernel(
     flags,
-    far_a,
-    far_b,
+    last_a,
+    last_b,
     weights,
     stiff_rows,
     pad_rows,
@@ -291,20 +355,14 @@
     del old_a, old_b
     width = snap.shape[1]
     rows_y = pad_rows.shape[0]
-    far, rows_z = far_a.shape[:2]
-    lines = stiff_rows.shape[1]
-    planes = lines // rows_y
-    half = rows_y // 2
-    even = flags[0]
-    low_line = half
-    high_line = 3 * lines - half - far
-    fill(state_a, far_a, 0, far, low_line + even * (high_line - low_line), pad_rows)
-    fill(state_a, far_b, 0, far, high_line - even * (high_line - low_line), pad_rows)
+    count, rows_z = last_a.shape[:2]
+    planes = stiff_rows.shape[1] // rows_y
+    lines = weights.shape[1]
+    shift = flags[0] * (lines - 3 * count)
+    fill(state_a, last_a, 0, count, count + shift, pad_rows)
+    fill(state_a, last_b, 0, count, lines - 2 * count - shift, pad_rows)
     buffers = (state_a, state_b)
-    for sweep in range(1, SWEEPS + 1):
-        src, dst = buffers[(sweep - 1) % 2], buffers[sweep % 2]
-        for first_line in (half + sweep * rows_y, 3 * lines - half - far - sweep * rows_y):
-            relax_lines(src, dst, weights, first_line, far, rows_y, rows_z, sweep < SWEEPS)
+    advance(buffers, weights, count, count, lines, rows_y, rows_z)
     final = buffers[SWEEPS % 2]
     outer = (planes, 2 * planes - 1)
     total = gram_terms(final, outer, planes, stiff_rows, snap, both, near_gram[...])
@@ -332,31 +390,22 @@
     flags = jnp.stack([even, index == 0, index == subs - 1, 0]).astype(jnp.int32)
     lines = initial.reshape(planes * rows_y, rows_z, width)
     count = planes * rows_y
-    near, far, half = 2 * rows_y, 2 * rows_y - rows_y // 2, rows_y // 2
-    def near_part(upward):
-        return lax.dynamic_slice_in_dim(lines, upward * (count - near), near, axis=0)
-
-    def far_part(upward):
-        start = upward * half + (1 - upward) * near
-        return lax.dynamic_slice_in_dim(lines, start, far, axis=0)
-
-    near_a = swap(near_part(even), 0)
-    near_b = swap(near_part(1 - even), 1)
+    near, half = 2 * rows_y, rows_y // 2
     flat_classes = classes.reshape(count, rows_z)
-    class_a = swap(flat_classes, 0)
-    class_b = swap(flat_classes, 1)
-    far_a = swap(far_part(even), 0)
-    far_b = swap(far_part(1 - even), 1)
-
+    part = functools.partial(jax.ShapeDtypeStruct, dtype=initial.dtype)
     vmem = pl.BlockSpec(memory_space=pltpu.VMEM)
     smem = pl.BlockSpec(memory_space=pltpu.SMEM)
-    state = pltpu.VMEM((3 * planes, rows_y + 2, width, LANES), jnp.float32)
+    first_state = pltpu.VMEM((3 * planes, rows_y + 2, width, LANES), jnp.float32)
+    second_state = pltpu.VMEM((3 * planes - 2, rows_y + 2, width, LANES), jnp.float32)
     kappa = pltpu.VMEM((3 * count, LANES), jnp.float32)
     both = pltpu.VMEM((2 * width, rows_y * LANES), jnp.bfloat16)
-    params = pltpu.CompilerParams(vmem_limit_bytes=14 * 2**20)
+    params = pltpu.CompilerParams(vmem_limit_bytes=8 * 2**20)
 
     def kept(depth):
         return jax.ShapeDtypeStruct((depth, width, rows_y * LANES), jnp.bfloat16)
+
+    def in_hbm(item):
+        return pltpu.with_memory_space_constraint(item, pltpu.HBM)
 
     def held(item):
         return pltpu.with_memory_space_constraint(item, pltpu.VMEM)
@@ -365,46 +414,69 @@
         jax.ShapeDtypeStruct((6, 3 * count, LANES), jnp.float32),
         jax.ShapeDtypeStruct((8, count, LANES), jnp.float32),
     ]
-    state_a, state_b, pad_rows = pl.pallas_call(
+    near_a, near_b, far_a, far_b = pl.pallas_call(
+        pack_kernel,
+        out_shape=[part((near + 1, rows_z, width))] * 2 + [part((rows_y, rows_z, width))] * 2,
+        in_specs=[smem] + [pl.BlockSpec(memory_space=pltpu.HBM)] * 2,
+        out_specs=[vmem] * 4,
+        scratch_shapes=[
+            pltpu.VMEM((count, rows_z), jnp.int32),
+            pltpu.SemaphoreType.DMA((5,)),
+        ],
+        compiler_params=params,
+    )(flags, in_hbm(flat_classes), in_hbm(lines))
+    near_a = swap(near_a, 0)
+    near_b = swap(near_b, 1)
+    far_a = swap(far_a, 0)
+    far_b = swap(far_b, 1)
+    state_a, state_b, pad_rows, last_a, last_b, own_kappa = pl.pallas_call(
         own_kernel,
         out_shape=[
-            state,
-            state,
-            jax.ShapeDtypeStruct((rows_y, LANES - rows_z, width), jnp.bfloat16),
+            first_state,
+            second_state,
+            part((rows_y, LANES - rows_z, width)),
+            part((half, rows_z, width)),
+            part((half, rows_z, width)),
+            jax.ShapeDtypeStruct((count, LANES), jnp.float32),
         ],
         in_specs=[smem] + [vmem] * 5,
-        out_specs=[vmem] * 3,
+        out_specs=[vmem] * 6,
         scratch_shapes=[kappa] + [pltpu.VMEM(item.shape, item.dtype) for item in rows],
         compiler_params=params,
     )(flags, lines, flat_classes, y_vals, z_vals, face_ids[None])
+    last_a = swap(last_a, 0)
+    last_b = swap(last_b, 1)
     state_a, state_b, weights, stiff_rows, snap_near, gram_near = pl.pallas_call(
         near_kernel,
         out_shape=[
-            state,
-            state,
+            first_state,
+            second_state,
             *rows,
             kept(planes - 2),
             jax.ShapeDtypeStruct((width, 2 * width), jnp.float32),
         ],
-        in_specs=[smem] + [vmem] * 8,
+        in_specs=[smem] + [vmem] * 6,
         out_specs=[vmem] * 6,
         scratch_shapes=[kappa, both],
-        input_output_aliases={7: 0, 8: 1},
+        input_output_aliases={5: 0, 6: 1},
         compiler_params=params,
-    )(
-        flags,
-        near_a,
-        near_b,
-        class_a,
-        class_b,
-        flat_classes,
-        pad_rows,
-        held(state_a),
-        held(state_b),
-    )
+    )(flags, near_a, near_b, own_kappa, pad_rows, held(state_a), held(state_b))
+    state_a, state_b = pl.pallas_call(
+        far_kernel,
+        out_shape=[first_state, second_state],
+        in_specs=[smem] + [vmem] * 6,
+        out_specs=[vmem] * 2,
+        input_output_aliases={5: 0, 6: 1},
+        compiler_params=params,
+    )(flags, far_a, far_b, weights, pad_rows, held(state_a), held(state_b))
     _, _, snap_far, gram = pl.pallas_call(
-        far_kernel,
-        out_shape=[state, state, kept(2), jax.ShapeDtypeStruct((width + 8, width), jnp.float32)],
+        last_kernel,
+        out_shape=[
+            first_state,
+            second_state,
+            kept(2),
+            jax.ShapeDtypeStruct((width + 8, width), jnp.float32),
+        ],
         in_specs=[smem] + [vmem] * 8,
         out_specs=[vmem] * 4,
         scratch_shapes=[both],
@@ -412,8 +484,8 @@
         compiler_params=params,
     )(
         flags,
-        far_a,
-        far_b,
+        last_a,
+        last_b,
         weights,
         stiff_rows,
         pad_rows,
@@ -432,52 +504,32 @@
     return jnp.broadcast_to(tile[row : row + 1, :], (8, tile.shape[1]))
 
 
-def eliminate(cols, panels):
-    grid = {(i, j): row_copy(cols[j], i) for j in range(8) for i in range(j, 8)}
-    rows = [[row_copy(panel, i) for panel in panels] for i in range(8)]
-    factor, pivots, recips = {}, [], []
-    for j in range(8):
-        pivot = grid[j, j]
-        recip = pl.reciprocal(pivot, approx=True)
-        pivots.append(pivot)
-        recips.append(recip)
-        for i in range(j + 1, 8):
-            factor[i, j] = grid[i, j] * recip
-            for k in range(j + 1, i + 1):
-                grid[i, k] = grid[i, k] - factor[i, j] * grid[k, j]
-            rows[i] = [a - factor[i, j][:, : a.shape[1]] * b for a, b in zip(rows[i], rows[j])]
-    solved = [[a * recips[i][:, : a.shape[1]] for a in rows[i]] for i in range(8)]
-    for i in range(7, 0, -1):
-        for j in range(i):
-            solved[j] = [
-                a - factor[i, j][:, : a.shape[1]] * b for a, b in zip(solved[j], solved[i])
-            ]
-    return rows, pivots, solved
-
-
-def gather_rows(rows):
-    sub = lax.broadcasted_iota(jnp.int32, rows[0].shape, 0)
-    out = rows[0]
-    for i in range(1, 8):
-        out = jnp.where(sub == i, rows[i], out)
-    return out
-
-
 def solve_spd(left, right):
     size = left.shape[0]
     count = size // 8
+    sub = lax.broadcasted_iota(jnp.int32, (8, 128), 0)
     lhs = [left[8 * t : 8 * t + 8] for t in range(count)]
     rhs = [right[8 * t : 8 * t + 8] for t in range(count)]
     for k in range(count):
         cols = [lane_copy(lhs[k], 8 * k + j) for j in range(8)]
-        _, _, solved = eliminate(cols, [lhs[k], rhs[k]])
-        for t in list(range(k + 1, count)) + list(range(k)):
+        panel_l, panel_r = lhs[k], rhs[k]
+        for j in range(8):
+            recip = pl.reciprocal(row_copy(cols[j], j), approx=True)
+            here = sub == j
+            mult = jnp.where(here, recip, -cols[j] * recip)
+            for l in range(j + 1, 8):
+                cols[l] = jnp.where(here, 0.0, cols[l]) + mult * row_copy(cols[l], j)
+            panel_l = jnp.where(here, 0.0, panel_l) + mult * row_copy(panel_l, j)
+            panel_r = jnp.where(here, 0.0, panel_r) + mult * row_copy(panel_r, j)
+        rows_l = [row_copy(panel_l, j) for j in range(8)]
+        rows_r = [row_copy(panel_r, j) for j in range(8)]
+        order = list(range(k + 1, count)) + list(range(k))
+        for t in order:
             tile_cols = [lane_copy(lhs[t], 8 * k + j) for j in range(8)]
             if k + 1 < count:
-                lhs[t] = lhs[t] - tree([tile_cols[j] * solved[j][0] for j in range(8)])
-            rhs[t] = rhs[t] - tree([tile_cols[j] * solved[j][1] for j in range(8)])
-        lhs[k] = gather_rows([solved[j][0] for j in range(8)])
-        rhs[k] = gather_rows([solved[j][1] for j in range(8)])
+                lhs[t] = lhs[t] - tree([tile_cols[j] * rows_l[j] for j in range(8)])
+            rhs[t] = rhs[t] - tree([tile_cols[j] * rows_r[j] for j in range(8)])
+        lhs[k], rhs[k] = panel_l, panel_r
     return jnp.concatenate(rhs, axis=0)
 
 
@@ -490,23 +542,46 @@
 def whiten(inner, block):
     size = inner.shape[0]
     count = size // 8
+    sub = lax.broadcasted_iota(jnp.int32, (8, 128), 0)
     lhs = [inner[8 * t : 8 * t + 8] for t in range(count)]
     rhs = [block[8 * t : 8 * t + 8] for t in range(count)]
     done = []
     for k in range(count):
-        cols = [lane_copy(lhs[k], 8 * k + j) for j in range(8)]
-        rows, pivots, solved = eliminate(cols, [lhs[k], rhs[k]])
-        done.append(gather_rows([rows[j][1] * lax.rsqrt(pivots[j]) for j in range(8)]))
-        for t in range(k + 1, count):
-            tile_cols = [lane_copy(lhs[t], 8 * k + j) for j in range(8)]
-            lhs[t] = lhs[t] - tree([tile_cols[j][:, :size] * solved[j][0] for j in range(8)])
-            rhs[t] = rhs[t] - tree([tile_cols[j] * solved[j][1] for j in range(8)])
+        live = range(k, count)
+        cols = {t: [lane_copy(lhs[t], 8 * k + j) for j in range(8)] for t in live}
+        scale = None
+        for j in range(8):
+            pivot = row_copy(cols[k][j], j)
+            recip = pl.reciprocal(pivot, approx=True)
+            root = lax.rsqrt(pivot)
+            scale = root if scale is None else jnp.where(sub >= j, root, scale)
+            head = {l: row_copy(cols[k][l], j) for l in range(j + 1, 8)}
+            row_l, row_r = row_copy(lhs[k], j), row_copy(rhs[k], j)
+            for t in live:
+                mult = cols[t][j] * recip
+                if t == k:
+                    mult = jnp.where(sub > j, mult, 0.0)
+                for l in range(j + 1, 8):
+                    cols[t][l] = cols[t][l] - mult * head[l]
+                lhs[t] = lhs[t] - mult[:, : row_l.shape[1]] * row_l
+                rhs[t] = rhs[t] - mult * row_r
+        done.append(rhs[k] * scale)
     return jnp.concatenate(done, axis=0)
 
 
-def dot(a, b, dims):
+def pieces_of(value):
+    high = value.astype(jnp.bfloat16)
+    return high, (value - high.astype(jnp.float32)).astype(jnp.bfloat16)
+
+
+def dot_rows(left, right):
+    left_high, left_low = pieces_of(left)
+    right_high, right_low = pieces_of(right)
     return lax.dot_general(
-        a, b, (dims, ((), ())), precision=lax.Precision.HIGHEST, preferred_element_type=jnp.float32
+        jnp.concatenate([left_high, left_high, left_low], axis=1),
+        jnp.concatenate([right_high, right_low, right_high], axis=1),
+        (((1,), (1,)), ((), ())),
+        preferred_element_type=jnp.float32,
     )
 
 
@@ -532,13 +607,14 @@
     stiff = jnp.where(row > col, packed, jnp.where(row < col, turned, total[width : width + 1]))
     stiff = stiff * (0.5 / cell_count)
     step = solve_spd(stiff, mass)
-    form = dot(step, dot(mass, step, ((1,), (0,))), ((0,), (0,)))
+    turned_step = step.T
+    form = dot_rows(turned_step, dot_rows(turned_step, mass))
+    both = jnp.concatenate([form, step], axis=0)
     block = start_ref[...]
     for _ in range(ITERS):
-        weighted = dot(block, form, ((1,), (0,)))
-        solved = dot(block, step, ((1,), (1,)))
-        inner = dot(weighted, block, ((1,), (1,)))
-        block = whiten(inner, solved)
+        products = dot_rows(block, both)
+        inner = dot_rows(products[:, :width], block)
+        block = whiten(inner, products[:, width:])
     modes = block.astype(jnp.bfloat16)
     for fetch in fetches:
         fetch.wait()

time: 103 us -> 96.4 us (0.936)
  waiting for transfers between devices: 24.9 us -> 5.34 us
  local copies, waits for them, and re-layouts: 9.81 us -> 23.7 us
  starting transfers between devices: 18.1 us -> 16.4 us
  Pallas kernels: 37.3 us -> 38.4 us
    ppermute x6, waiting for transfers between devices: 21.9 us -> 0.02 us  [swap(): return lax.ppermute(array, 'sub', pairs + [(j, i) for i, j in pairs])]
    unnamed x15 -> x23, local copies, waits for them, and re-layouts: 5 us -> 23.7 us
    dynamic_slice x2 -> x0, local copies, waits for them, and re-layouts: 4.81 us -> none  [the longest x1 2.66 us: near_part(): lax.dynamic_slice_in_dim(lines, upward * (count - near), near, axis=0)]
    pallas_call x3 -> x5, Pallas kernels: 24.8 us -> 27.5 us  [the longest x1 10.6 us: relax(): pl.pallas_call(near_kernel, out_shape=[first_state, second_state, *rows,...]
    ppermute x3, waiting for transfers between devices: 3.02 us -> 5.33 us  [on_device(): lax.ppermute(own, 'sub', [(i, (i + shift) % subs) for i in range(subs)])]
    ppermute x3, starting transfers between devices: 7.44 us -> 5.54 us  [on_device(): lax.ppermute(own, 'sub', [(i, (i + shift) % subs) for i in range(subs)])]
    pallas_call x1, Pallas kernels: 12.5 us -> 11 us  [on_device(): pl.pallas_call(functools.partial(modes_kernel, float(subs * cells), rows_...]
  transfers between devices with their start and end apart: 9 -> 9, of which waited for: 2 -> 3; matrix products, arithmetic and copies ran while one was open for 2% -> 0% of each run, Pallas kernels for 14% -> 21%
where the time goes in v8:
time: 96.4 us; the launch traced here: 95.9 us
  Pallas kernels  38.4 us (40%)
  local copies, waits for them, and re-layouts  23.7 us (25%)
  starting transfers between devices  16.4 us (17%)
  blocking collectives  11.9 us (12%)
  waiting for transfers between devices  5.34 us (6%)
    unnamed x23, local copies, waits for them, and re-layouts  23.7 us
    all_to_all x1, blocking collectives, on_device(): lax.all_to_all(pieces, 'nbhd', split_axis=0, concat_axis=0, tiled=True)  11.9 us
    pallas_call x1, Pallas kernels, on_device(): pl.pallas_call(functools.partial(modes_kernel, float(subs * cells), rows_...  11 us
    ppermute x6, starting transfers between devices, swap(): return lax.ppermute(array, 'sub', pairs + [(j, i) for i, j in pairs])  10.8 us
    pallas_call x1, Pallas kernels, relax(): pl.pallas_call(near_kernel, out_shape=[first_state, second_state, *rows,...  10.6 us
    ppermute x3, starting transfers between devices, on_device(): lax.ppermute(own, 'sub', [(i, (i + shift) % subs) for i in range(subs)])  5.54 us
    ppermute x3, waiting for transfers between devices, on_device(): lax.ppermute(own, 'sub', [(i, (i + shift) % subs) for i in range(subs)])  5.33 us
    pallas_call x1, Pallas kernels, relax(): pl.pallas_call(far_kernel, out_shape=[first_state, second_state], in_spec...  4.73 us
  transfers between devices with their start and end apart: 9, of which 3 were waited for; matrix products, arithmetic and copies ran while one was open for 0% of the time, Pallas kernels for 21%

profile of v8, /device:TPU:0, one launch (start us, length us, event | category | flops | bytes accessed | tf_op | source)
XLA Modules:
  0.0 95.9 jit_solution(4586137935197064051)
XLA Ops:
  0.1 3.2 %shard_map.74 = (bf16[33,96,128]{2,1,0:T(8,128)(2,1)S(1)}, bf16[33,96,128]{2,1,0:T(8,128)(2,1)}, bf16[16,96,128]{2,1,0:T(8,128)(2,1)}, bf16[16,96,128]{2,1,0:T(8,128)(2,1)S(1)}) custom-call(s32[4]{0:T(128)S(1)} %pad_add_fusion.flags, s32[64,96]{1,0:T(8,128)} %bitcast.15, bf16[64,96,128]{2,1,0:T(8,128)(2,1)} %bitcast.13), custom_call_target="tpu_custom_call" | custom-call | tf_op jit(solution)/shard_map/pallas_call | solution.py:417
  3.3 3.1 %collective-permute-start.2 = (bf16[33,96,128]{2,1,0:T(8,128)(2,1)S(1)}, bf16[33,96,128]{2,1,0:T(8,128)(2,1)S(1)}, u32[]{:S(2)}, u32[]{:S(2)}) collective-permute-start(bf16[33,96,128]{2,1,0:T(8,128)(2,1)S(1)} %get-tuple-element.27), channel_id=1, source_target_pairs={{0,1},{2,3},{1,0},{3,2},{4,5},{6,7},{5,4},{7,6},{8,9},{10,11},{9,8... | collective-permute-start | bytes 2433032 | tf_op jit(solution)/shard_map/ppermute | solution.py:382
  6.4 0.7 collective-permute-start.3
  7.1 4.4 %collective-permute-start.4 = (bf16[16,96,128]{2,1,0:T(8,128)(2,1)}, bf16[16,96,128]{2,1,0:T(8,128)(2,1)S(1)}, u32[]{:S(2)}, u32[]{:S(2)}) collective-permute-start(bf16[16,96,128]{2,1,0:T(8,128)(2,1)} %get-tuple-element.36), channel_id=1, source_target_pairs={{0,1},{2,3},{1,0},{3,2},{4,5},{6,7},{5,4},{7,6},{8,9},{10,11},{9,8... | collective-permute-start | bytes 1179656 | tf_op jit(solution)/shard_map/ppermute | solution.py:382
  12.2 1.4 %copy-done.5 = bf16[1,4,16,96,128]{4,3,2,1,0:T(8,128)(2,1)S(1)} copy-done((bf16[1,4,16,96,128]{4,3,2,1,0:T(8,128)(2,1)S(1)}, bf16[1,4,16,96,128]{4,3,2,1,0:T(8,128)(2,1)}, u32[]{:S(2)}) %copy-start.5) | copy-done | bytes 1572888
  13.6 0.8 copy-done.6
  14.4 0.7 copy-done.7
  16.5 4.5 %shard_map.73 = (f32[12,18,128,128]{3,2,1,0:T(8,128)S(1)}, f32[10,18,128,128]{3,2,1,0:T(8,128)S(1)}, bf16[16,32,128]{2,1,0:T(8,128)(2,1)S(1)}, bf16[8,96,128]{2,...) custom-call(s32[4]{0:T(128)S(1)} %pad_add_fusion.flags, bf16[64,96,128]{2,1,0:T(8,128)(2,1)S(1)} %bitcast.14, ...), custom_call_target="tpu_custom_call" | custom-call | tf_op jit(solution)/shard_map/pallas_call | solution.py:432
  21.0 5.0 %copy-done.1 = f32[12,18,128,128]{3,2,1,0:T(8,128)} copy-done((f32[12,18,128,128]{3,2,1,0:T(8,128)}, f32[12,18,128,128]{3,2,1,0:T(8,128)S(1)}, u32[]{:S(2)}) %copy-start.1) | copy-done | bytes 14155800
  26.0 4.3 %copy-done.3 = f32[10,18,128,128]{3,2,1,0:T(8,128)} copy-done((f32[10,18,128,128]{3,2,1,0:T(8,128)}, f32[10,18,128,128]{3,2,1,0:T(8,128)S(1)}, u32[]{:S(2)}) %copy-start.3) | copy-done | bytes 11796504
  30.3 1.3 %collective-permute-start = (bf16[8,96,128]{2,1,0:T(8,128)(2,1)}, bf16[8,96,128]{2,1,0:T(8,128)(2,1)S(1)}, u32[]{:S(2)}, u32[]{:S(2)}) collective-permute-start(bf16[8,96,128]{2,1,0:T(8,128)(2,1)} %get-tuple-element.25), channel_id=1, source_target_pairs={{0,1},{2,3},{1,0},{3,2},{4,5},{6,7},{5,4},{7,6},{8,9},{10,11},{9,8... | collective-permute-start | bytes 589832 | tf_op jit(solution)/shard_map/ppermute | solution.py:382
  32.3 5.0 %copy-done.2 = f32[12,18,128,128]{3,2,1,0:T(8,128)S(1)} copy-done((f32[12,18,128,128]{3,2,1,0:T(8,128)S(1)}, f32[12,18,128,128]{3,2,1,0:T(8,128)}, u32[]{:S(2)}) %copy-start.2) | copy-done | bytes 14155800
  37.3 4.3 %copy-done.4 = f32[10,18,128,128]{3,2,1,0:T(8,128)S(1)} copy-done((f32[10,18,128,128]{3,2,1,0:T(8,128)S(1)}, f32[10,18,128,128]{3,2,1,0:T(8,128)}, u32[]{:S(2)}) %copy-start.4) | copy-done | bytes 11796504
  41.7 10.6 %shard_map.75 = (f32[12,18,128,128]{3,2,1,0:T(8,128)S(1)}, f32[10,18,128,128]{3,2,1,0:T(8,128)S(1)}, f32[6,192,128]{2,1,0:T(8,128)S(1)}, f32[8,64,128]{2,1,0:T(8...) custom-call(s32[4]{0:T(128)S(1)} %pad_add_fusion.flags, ...), custom_call_target="tpu_custom_call", output_to_operand_aliasing={{0}: (5, {}), {1}: (6, {})} | custom-call | tf_op jit(solution)/shard_map/pallas_call | solution.py:449
  52.3 4.7 %shard_map.76 = (f32[12,18,128,128]{3,2,1,0:T(8,128)S(1)}, f32[10,18,128,128]{3,2,1,0:T(8,128)S(1)}) custom-call(s32[4]{0:T(128)S(1)} %pad_add_fusion.flags, bf16[16,96,128]{2,1,0:T(8,128)(2,1)S(1)} %collective-permute-done.4.far_a, bf16[16,96,128]{2,1,0:T(8,128)(2,1)S(1)} %collective-permute-done.5.far_b, ...), custom_call_target="tpu_custom_call", output_to_operand_aliasing={{0}: (5, {}), {1}: (6, {})} | custom-call | tf_op jit(solution)/shard_map/pallas_call | solution.py:464
  57.1 4.4 %shard_map.77 = (f32[12,18,128,128]{3,2,1,0:T(8,128)S(1)}, f32[10,18,128,128]{3,2,1,0:T(8,128)S(1)}, bf16[2,128,2048]{2,1,0:T(8,128)(2,1)S(1)}, f32[136,128]{1,0:T(8,128)S(1)}) custom-call(s32[4]{0:T(128)S(1)} %pad_add_fusion.flags, bf16[8,96,128]{2,1,0:T(8,128)(2,1)S(1)} %collective-permute-done.last_a, ...), custom_call_target="tpu_custom_call", output_to_operand_aliasing={{0}: (7, {}), {1}: (8, {})} | custom-call | tf_op jit(solution)/shard_map/pallas_call | solution.py:472
  61.5 3.0 %collective-permute-start.8 = (f32[136,128]{1,0:T(8,128)S(1)}, f32[136,128]{1,0:T(8,128)S(1)}, u32[]{:S(2)}, u32[]{:S(2)}) collective-permute-start(f32[136,128]{1,0:T(8,128)S(1)} %get-tuple-element.42.refs_1_), channel_id=1, source_target_pairs={{0,3},{1,0},{2,1},{3,2},{4,7},{5,4},{6,5},{7,6},{8,11},{9,8},{10,9... | collective-permute-start | bytes 208904 | tf_op jit(solution)/shard_map/ppermute | solution.py:641
  64.4 1.8 %collective-permute-start.7 = (f32[136,128]{1,0:T(8,128)S(1)}, f32[136,128]{1,0:T(8,128)S(1)}, u32[]{:S(2)}, u32[]{:S(2)}) collective-permute-start(f32[136,128]{1,0:T(8,128)S(1)} %get-tuple-element.42.refs_1_), channel_id=1, source_target_pairs={{0,2},{1,3},{2,0},{3,1},{4,6},{5,7},{6,4},{7,5},{8,10},{9,11},{10,... | collective-permute-start | bytes 208904 | tf_op jit(solution)/shard_map/ppermute | solution.py:641
  66.2 0.8 collective-permute-start.6
  67.3 3.7 %collective-permute-done.7.refs_3_ = f32[136,128]{1,0:T(8,128)S(1)} collective-permute-done((f32[136,128]{1,0:T(8,128)S(1)}, f32[136,128]{1,0:T(8,128)S(1)}, u32[]{:S(2)}, u32[]{:S(2)}) %collective-permute-start.7) | collective-permute-done | bytes 69664 | tf_op jit(solution)/shard_map/ppermute | solution.py:641
  71.0 1.4 %collective-permute-done.6.refs_2_ = f32[136,128]{1,0:T(8,128)S(1)} collective-permute-done((f32[136,128]{1,0:T(8,128)S(1)}, f32[136,128]{1,0:T(8,128)S(1)}, u32[]{:S(2)}, u32[]{:S(2)}) %collective-permute-start.6) | collective-permute-done | bytes 69664 | tf_op jit(solution)/shard_map/ppermute | solution.py:641
  72.4 11.0 %shard_map.78 = bf16[8,32,768]{2,1,0:T(8,128)(2,1)S(1)} custom-call(s32[8]{0:T(128)S(1)} %dynamic-slice_bitcast_fusion.refs_0_, f32[136,128]{1,0:T(8,128)S(1)} %get-tuple-element.42.refs_1_, f32[136,128]{1,0:T(8,128)S(1)} %collective-permute-done.6.refs_2_, f32[136,128]{1,0:T(8,128)S(1)} %collective-permute-done.7.refs_3_, ...), custom_call_target="tpu_custom_call" | custom-call | tf_op jit(solution)/shard_map/pallas_call | solution.py:647
  83.3 11.9 %all_to_all.5 = bf16[8,32,768]{2,1,0:T(8,128)(2,1)S(1)} all-to-all(bf16[8,32,768]{2,1,0:T(8,128)(2,1)S(1)} %shard_map.78), channel_id=1, replica_groups=mesh['nbhd'=8,'sub'=4] {'nbhd'}, dimensions={0} | all-to-all | bytes 786432 | tf_op jit(solution)/shard_map/all_to_all | solution.py:659
  95.2 0.7 copy.21
  (26 shorter events, 3.1 us)
Async XLA Ops:
  0.0 67.0 %copy-start = (s32[8,8]{1,0:T(8,128)S(1)}, s32[8,8]{1,0:T(8,128)}, u32[]{:S(2)}) copy-start(s32[8,8]{1,0:T(8,128)} %param.13) | copy-start | bytes 772
  3.3 28.3 %collective-permute-start.2 = (bf16[33,96,128]{2,1,0:T(8,128)(2,1)S(1)}, bf16[33,96,128]{2,1,0:T(8,128)(2,1)S(1)}, u32[]{:S(2)}, u32[]{:S(2)}) collective-permute-start(bf16[33,96,128]{2,1,0:T(8,128)(2,1)S(1)} %get-tuple-element.27), channel_id=1, source_target_pairs={{0,1},{2,3},{1,0},{3,2},{4,5},{6,7},{5,4},{7,6},{8,9},{10,11},{9,8... | collective-permute-start | bytes 2433032 | tf_op jit(solution)/shard_map/ppermute | solution.py:382
  6.4 25.9 %collective-permute-start.3 = (bf16[33,96,128]{2,1,0:T(8,128)(2,1)}, bf16[33,96,128]{2,1,0:T(8,128)(2,1)S(1)}, u32[]{:S(2)}, u32[]{:S(2)}) collective-permute-start(bf16[33,96,128]{2,1,0:T(8,128)(2,1)} %get-tuple-element.28), channel_id=1, source_target_pairs={{1,2},{2,1},{5,6},{6,5},{9,10},{10,9},{13,14},{14,13},{17,18},{18,... | collective-permute-start | bytes 2433032 | tf_op jit(solution)/shard_map/ppermute | solution.py:382
  7.1 45.2 %collective-permute-start.4 = (bf16[16,96,128]{2,1,0:T(8,128)(2,1)}, bf16[16,96,128]{2,1,0:T(8,128)(2,1)S(1)}, u32[]{:S(2)}, u32[]{:S(2)}) collective-permute-start(bf16[16,96,128]{2,1,0:T(8,128)(2,1)} %get-tuple-element.36), channel_id=1, source_target_pairs={{0,1},{2,3},{1,0},{3,2},{4,5},{6,7},{5,4},{7,6},{8,9},{10,11},{9,8... | collective-permute-start | bytes 1179656 | tf_op jit(solution)/shard_map/ppermute | solution.py:382
  11.5 40.8 %collective-permute-start.5 = (bf16[16,96,128]{2,1,0:T(8,128)(2,1)S(1)}, bf16[16,96,128]{2,1,0:T(8,128)(2,1)S(1)}, u32[]{:S(2)}, u32[]{:S(2)}) collective-permute-start(bf16[16,96,128]{2,1,0:T(8,128)(2,1)S(1)} %get-tuple-element.37), channel_id=1, source_target_pairs={{1,2},{2,1},{5,6},{6,5},{9,10},{10,9},{13,14},{14,13},{17,18},{18,... | collective-permute-start | bytes 1179656 | tf_op jit(solution)/shard_map/ppermute | solution.py:382
  12.2 1.4 %copy-start.5 = (bf16[1,4,16,96,128]{4,3,2,1,0:T(8,128)(2,1)S(1)}, bf16[1,4,16,96,128]{4,3,2,1,0:T(8,128)(2,1)}, u32[]{:S(2)}) copy-start(bf16[1,4,16,96,128]{4,3,2,1,0:T(8,128)(2,1)} %param.7) | copy-start | bytes 4718596
  13.6 0.8 copy-start.6
  14.4 0.7 copy-start.7
  15.1 0.7 copy-start.9
  15.8 0.7 copy-start.10
  21.0 5.0 %copy-start.1 = (f32[12,18,128,128]{3,2,1,0:T(8,128)}, f32[12,18,128,128]{3,2,1,0:T(8,128)S(1)}, u32[]{:S(2)}) copy-start(f32[12,18,128,128]{3,2,1,0:T(8,128)S(1)} %get-tuple-element.31.old_a) | copy-start | bytes 42467332
  26.0 4.3 %copy-start.3 = (f32[10,18,128,128]{3,2,1,0:T(8,128)}, f32[10,18,128,128]{3,2,1,0:T(8,128)S(1)}, u32[]{:S(2)}) copy-start(f32[10,18,128,128]{3,2,1,0:T(8,128)S(1)} %get-tuple-element.32.old_b) | copy-start | bytes 35389444
  30.3 26.7 %collective-permute-start = (bf16[8,96,128]{2,1,0:T(8,128)(2,1)}, bf16[8,96,128]{2,1,0:T(8,128)(2,1)S(1)}, u32[]{:S(2)}, u32[]{:S(2)}) collective-permute-start(bf16[8,96,128]{2,1,0:T(8,128)(2,1)} %get-tuple-element.25), channel_id=1, source_target_pairs={{0,1},{2,3},{1,0},{3,2},{4,5},{6,7},{5,4},{7,6},{8,9},{10,11},{9,8... | collective-permute-start | bytes 589832 | tf_op jit(solution)/shard_map/ppermute | solution.py:382
  31.6 25.5 %collective-permute-start.1 = (bf16[8,96,128]{2,1,0:T(8,128)(2,1)}, bf16[8,96,128]{2,1,0:T(8,128)(2,1)S(1)}, u32[]{:S(2)}, u32[]{:S(2)}) collective-permute-start(bf16[8,96,128]{2,1,0:T(8,128)(2,1)} %get-tuple-element.26), channel_id=1, source_target_pairs={{1,2},{2,1},{5,6},{6,5},{9,10},{10,9},{13,14},{14,13},{17,18},{18,... | collective-permute-start | bytes 589832 | tf_op jit(solution)/shard_map/ppermute | solution.py:382
  32.3 5.0 %copy-start.2 = (f32[12,18,128,128]{3,2,1,0:T(8,128)S(1)}, f32[12,18,128,128]{3,2,1,0:T(8,128)}, u32[]{:S(2)}) copy-start(f32[12,18,128,128]{3,2,1,0:T(8,128)} %copy-done.1) | copy-start | bytes 42467332
  37.3 4.4 %copy-start.4 = (f32[10,18,128,128]{3,2,1,0:T(8,128)S(1)}, f32[10,18,128,128]{3,2,1,0:T(8,128)}, u32[]{:S(2)}) copy-start(f32[10,18,128,128]{3,2,1,0:T(8,128)} %copy-done.3) | copy-start | bytes 35389444
  57.1 15.3 %copy-start.8 = (f32[1,128,32]{1,2,0:T(8,128)S(1)}, f32[1,128,32]{1,2,0:T(8,128)}, u32[]{:S(2)}) copy-start(f32[1,128,32]{1,2,0:T(8,128)} %param.12) | copy-start | bytes 49156
  61.5 5.8 %collective-permute-start.8 = (f32[136,128]{1,0:T(8,128)S(1)}, f32[136,128]{1,0:T(8,128)S(1)}, u32[]{:S(2)}, u32[]{:S(2)}) collective-permute-start(f32[136,128]{1,0:T(8,128)S(1)} %get-tuple-element.42.refs_1_), channel_id=1, source_target_pairs={{0,3},{1,0},{2,1},{3,2},{4,7},{5,4},{6,5},{7,6},{8,11},{9,8},{10,9... | collective-permute-start | bytes 208904 | tf_op jit(solution)/shard_map/ppermute | solution.py:641
  64.4 6.6 %collective-permute-start.7 = (f32[136,128]{1,0:T(8,128)S(1)}, f32[136,128]{1,0:T(8,128)S(1)}, u32[]{:S(2)}, u32[]{:S(2)}) collective-permute-start(f32[136,128]{1,0:T(8,128)S(1)} %get-tuple-element.42.refs_1_), channel_id=1, source_target_pairs={{0,2},{1,3},{2,0},{3,1},{4,6},{5,7},{6,4},{7,5},{8,10},{9,11},{10,... | collective-permute-start | bytes 208904 | tf_op jit(solution)/shard_map/ppermute | solution.py:641
  66.2 6.1 %collective-permute-start.6 = (f32[136,128]{1,0:T(8,128)S(1)}, f32[136,128]{1,0:T(8,128)S(1)}, u32[]{:S(2)}, u32[]{:S(2)}) collective-permute-start(f32[136,128]{1,0:T(8,128)S(1)} %get-tuple-element.42.refs_1_), channel_id=1, source_target_pairs={{0,1},{1,2},{2,3},{3,0},{4,5},{5,6},{6,7},{7,4},{8,9},{9,10},{10,1... | collective-permute-start | bytes 208904 | tf_op jit(solution)/shard_map/ppermute | solution.py:641

commit v9 on v8

--- a/solution.py
+++ b/solution.py
@@ -223,15 +223,18 @@
     y_vals,
     z_vals,
     face_ids,
-    state_a,
-    state_b,
+    hand,
+    inner,
     pad_rows,
     last_a,
     last_b,
     own_kappa,
+    state_a,
+    state_b,
     kappa,
     weights,
     stiff_rows,
+    sems,
 ):
     lines, rows_z, width = own.shape
     rows_y = pad_rows.shape[0]
@@ -253,22 +256,30 @@
     ghost_high = turned(jnp.concatenate([(y_all * picks[1]).astype(bf16), blank], axis=0))
 
     def edges(e, carry):
-        for state, at in ((state_a, e + 1), (state_b, e)):
+        for state, at in ((state_a, e), (state_b, e - 1)):
             state[at, 0] = ghost_low
             state[at, rows_y + 1] = ghost_high
         return carry
 
-    lax.fori_loop(0, state_b.shape[0], edges, 0)
+    lax.fori_loop(planes, 2 * planes, edges, 0)
     fill(state_a, own, 0, lines, lines, pad_rows)
+    sends = [
+        pltpu.make_async_copy(state_a.at[pl.ds(planes, planes)], hand, sems.at[0]),
+        pltpu.make_async_copy(state_b.at[pl.ds(planes, planes - 2)], inner, sems.at[1]),
+    ]
+    sends[0].start()
     kappa[...] = jnp.ones(kappa.shape, jnp.float32)
     kappa[pl.ds(lines, lines), pl.ds(0, rows_z)] = powers(classes[...])
     own_kappa[...] = kappa[pl.ds(lines, lines)]
     weight_rows(kappa, weights, stiff_rows, lines, flags[1], flags[2], rows_y, rows_z)
     inside = lines - 2 * rows_y
     relax_lines(state_a, state_b, weights, (lines + rows_y,), inside, rows_y, rows_z, True)
+    sends[1].start()
     half = rows_y // 2
     for out, upward in ((last_a, flags[0]), (last_b, 1 - flags[0])):
         out[...] = own[pl.ds(upward * half + (1 - upward) * (lines - rows_y), half)]
+    for copy in sends:
+        copy.wait()
 
 
 def near_kernel(
@@ -277,8 +288,8 @@
     near_b,
     own_kappa,
     pad_rows,
-    old_a,
-    old_b,
+    hand,
+    inner,
     state_a,
     state_b,
     weights,
@@ -287,12 +298,19 @@
     gram,
     kappa,
     both,
+    sems,
 ):
-    del old_a, old_b
     lines = own_kappa.shape[0]
     rows_z = near_a.shape[1]
     rows_y = pad_rows.shape[0]
     near = lines // 2
+    planes = lines // rows_y
+    taken = [
+        pltpu.make_async_copy(hand, state_a.at[pl.ds(planes, planes)], sems.at[0]),
+        pltpu.make_async_copy(inner, state_b.at[pl.ds(planes, planes - 2)], sems.at[1]),
+    ]
+    for copy in taken:
+        copy.start()
     even, first, last = flags[0], flags[1], flags[2]
     base_a = pl.multiple_of(even * (2 * lines), 8)
     base_b = pl.multiple_of((1 - even) * (2 * lines), 8)
@@ -304,13 +322,23 @@
     weight_rows(kappa, weights, stiff_rows, lines, first, last, rows_y, rows_z)
     fill(state_a, near_a, 1, near, near + even * (lines + near), pad_rows)
     fill(state_a, near_b, 1, near, near + (1 - even) * (lines + near), pad_rows)
+    for copy in taken:
+        copy.wait()
+    ghost_low = state_a[planes, 0]
+    ghost_high = state_a[planes, rows_y + 1]
+    for e in range(1, 3 * planes - 1):
+        if e not in range(planes, 2 * planes):
+            state_a[e, 0] = ghost_low
+            state_a[e, rows_y + 1] = ghost_high
+        if e not in range(planes + 1, 2 * planes - 1):
+            state_b[e - 1, 0] = ghost_low
+            state_b[e - 1, rows_y + 1] = ghost_high
     step = functools.partial(relax_lines, weights=weights, rows_y=rows_y, rows_z=rows_z)
     ends = (lines - rows_y, 2 * lines - rows_y)
     step(state_a, state_b, first_lines=ends, count=2 * rows_y, keep=True)
     step(state_b, state_a, first_lines=(lines,), count=lines, keep=True)
     inner = (lines + rows_y,)
     step(state_a, state_b, first_lines=inner, count=lines - 2 * rows_y, keep=False)
-    planes = lines // rows_y
     inside = range(planes + 1, 2 * planes - 1)
     blank = jnp.zeros(gram.shape, jnp.float32)
     gram[...] = gram_terms(state_b, inside, planes, stiff_rows, snap, both, blank)
@@ -395,6 +423,7 @@
     part = functools.partial(jax.ShapeDtypeStruct, dtype=initial.dtype)
     vmem = pl.BlockSpec(memory_space=pltpu.VMEM)
     smem = pl.BlockSpec(memory_space=pltpu.SMEM)
+    hbm = pl.BlockSpec(memory_space=pltpu.HBM)
     first_state = pltpu.VMEM((3 * planes, rows_y + 2, width, LANES), jnp.float32)
     second_state = pltpu.VMEM((3 * planes - 2, rows_y + 2, width, LANES), jnp.float32)
     kappa = pltpu.VMEM((3 * count, LANES), jnp.float32)
@@ -417,7 +446,7 @@
     near_a, near_b, far_a, far_b = pl.pallas_call(
         pack_kernel,
         out_shape=[part((near + 1, rows_z, width))] * 2 + [part((rows_y, rows_z, width))] * 2,
-        in_specs=[smem] + [pl.BlockSpec(memory_space=pltpu.HBM)] * 2,
+        in_specs=[smem] + [hbm] * 2,
         out_specs=[vmem] * 4,
         scratch_shapes=[
             pltpu.VMEM((count, rows_z), jnp.int32),
@@ -429,20 +458,22 @@
     near_b = swap(near_b, 1)
     far_a = swap(far_a, 0)
     far_b = swap(far_b, 1)
-    state_a, state_b, pad_rows, last_a, last_b, own_kappa = pl.pallas_call(
+    hand, inner, pad_rows, last_a, last_b, own_kappa = pl.pallas_call(
         own_kernel,
         out_shape=[
-            first_state,
-            second_state,
+            pltpu.HBM((planes,) + first_state.shape[1:], jnp.float32),
+            pltpu.HBM((planes - 2,) + first_state.shape[1:], jnp.float32),
             part((rows_y, LANES - rows_z, width)),
             part((half, rows_z, width)),
             part((half, rows_z, width)),
             jax.ShapeDtypeStruct((count, LANES), jnp.float32),
         ],
         in_specs=[smem] + [vmem] * 5,
-        out_specs=[vmem] * 6,
-        scratch_shapes=[kappa] + [pltpu.VMEM(item.shape, item.dtype) for item in rows],
-        compiler_params=params,
+        out_specs=[hbm] * 2 + [vmem] * 4,
+        scratch_shapes=[first_state, second_state, kappa]
+        + [pltpu.VMEM(item.shape, item.dtype) for item in rows]
+        + [pltpu.SemaphoreType.DMA((2,))],
+        compiler_params=pltpu.CompilerParams(vmem_limit_bytes=40 * 2**20),
     )(flags, lines, flat_classes, y_vals, z_vals, face_ids[None])
     last_a = swap(last_a, 0)
     last_b = swap(last_b, 1)
@@ -455,12 +486,11 @@
             kept(planes - 2),
             jax.ShapeDtypeStruct((width, 2 * width), jnp.float32),
         ],
-        in_specs=[smem] + [vmem] * 6,
+        in_specs=[smem] + [vmem] * 4 + [hbm] * 2,
         out_specs=[vmem] * 6,
-        scratch_shapes=[kappa, both],
-        input_output_aliases={5: 0, 6: 1},
+        scratch_shapes=[kappa, both, pltpu.SemaphoreType.DMA((2,))],
         compiler_params=params,
-    )(flags, near_a, near_b, own_kappa, pad_rows, held(state_a), held(state_b))
+    )(flags, near_a, near_b, own_kappa, pad_rows, in_hbm(hand), in_hbm(inner))
     state_a, state_b = pl.pallas_call(
         far_kernel,
         out_shape=[first_state, second_state],

time: 96.4 us -> 84.1 us (0.87)
  local copies, waits for them, and re-layouts: 23.7 us -> 5 us
  Pallas kernels: 38.4 us -> 41.7 us
  starting transfers between devices: 16.4 us -> 19 us
    unnamed x23 -> x15, local copies, waits for them, and re-layouts: 23.7 us -> 4.99 us
    ppermute x3, starting transfers between devices: 5.54 us -> 8.16 us  [on_device(): lax.ppermute(own, 'sub', [(i, (i + shift) % subs) for i in range(subs)])]
    pallas_call x1, Pallas kernels: 10.6 us -> 12.5 us  [relax(): pl.pallas_call(near_kernel, out_shape=[first_state, second_state, *rows,...]
    ppermute x6, waiting for transfers between devices: 0.02 us -> 1.67 us  [swap(): return lax.ppermute(array, 'sub', pairs + [(j, i) for i, j in pairs])]
    pallas_call x1, Pallas kernels: 4.51 us -> 5.86 us  [relax(): pl.pallas_call(own_kernel, out_shape=[pltpu.HBM((planes,) + first_state.s...]
    ppermute x3, waiting for transfers between devices: 5.33 us -> 4.32 us  [on_device(): lax.ppermute(own, 'sub', [(i, (i + shift) % subs) for i in range(subs)])]
  transfers between devices with their start and end apart: 9 -> 9, of which waited for: 3 -> 3; matrix products, arithmetic and copies ran while one was open for 0% -> 0% of each run, Pallas kernels for 21% -> 28%
where the time goes in v9:
time: 84.1 us; the launch traced here: 83.7 us
  Pallas kernels  41.7 us (50%)
  starting transfers between devices  19 us (23%)
  blocking collectives  11.9 us (14%)
  waiting for transfers between devices  5.98 us (7%)
  local copies, waits for them, and re-layouts  5 us (6%)
    pallas_call x1, Pallas kernels, relax(): pl.pallas_call(near_kernel, out_shape=[first_state, second_state, *rows,...  12.5 us
    all_to_all x1, blocking collectives, on_device(): lax.all_to_all(pieces, 'nbhd', split_axis=0, concat_axis=0, tiled=True)  11.9 us
    pallas_call x1, Pallas kernels, on_device(): pl.pallas_call(functools.partial(modes_kernel, float(subs * cells), rows_...  11 us
    ppermute x6, starting transfers between devices, swap(): return lax.ppermute(array, 'sub', pairs + [(j, i) for i, j in pairs])  10.9 us
    ppermute x3, starting transfers between devices, on_device(): lax.ppermute(own, 'sub', [(i, (i + shift) % subs) for i in range(subs)])  8.16 us
    pallas_call x1, Pallas kernels, relax(): pl.pallas_call(own_kernel, out_shape=[pltpu.HBM((planes,) + first_state.s...  5.86 us
    unnamed x15, local copies, waits for them, and re-layouts  4.99 us
    pallas_call x1, Pallas kernels, relax(): pl.pallas_call(far_kernel, out_shape=[first_state, second_state], in_spec...  4.73 us
  transfers between devices with their start and end apart: 9, of which 3 were waited for; matrix products, arithmetic and copies ran while one was open for 0% of the time, Pallas kernels for 28%

profile of v9, /device:TPU:0, one launch (start us, length us, event | category | flops | bytes accessed | tf_op | source)
XLA Modules:
  0.0 83.7 jit_solution(12063600280208032323)
XLA Ops:
  0.1 3.2 %shard_map.74 = (bf16[33,96,128]{2,1,0:T(8,128)(2,1)S(1)}, bf16[33,96,128]{2,1,0:T(8,128)(2,1)}, bf16[16,96,128]{2,1,0:T(8,128)(2,1)}, bf16[16,96,128]{2,1,0:T(8,128)(2,1)S(1)}) custom-call(s32[4]{0:T(128)S(1)} %pad_add_fusion.flags, s32[64,96]{1,0:T(8,128)} %bitcast.15, bf16[64,96,128]{2,1,0:T(8,128)(2,1)} %bitcast.13), custom_call_target="tpu_custom_call" | custom-call | tf_op jit(solution)/shard_map/pallas_call | solution.py:446
  3.3 3.1 %collective-permute-start.2 = (bf16[33,96,128]{2,1,0:T(8,128)(2,1)S(1)}, bf16[33,96,128]{2,1,0:T(8,128)(2,1)S(1)}, u32[]{:S(2)}, u32[]{:S(2)}) collective-permute-start(bf16[33,96,128]{2,1,0:T(8,128)(2,1)S(1)} %get-tuple-element.27), channel_id=1, source_target_pairs={{0,1},{2,3},{1,0},{3,2},{4,5},{6,7},{5,4},{7,6},{8,9},{10,11},{9,8... | collective-permute-start | bytes 2433032 | tf_op jit(solution)/shard_map/ppermute | solution.py:410
  6.4 0.7 collective-permute-start.3
  7.1 4.4 %collective-permute-start.4 = (bf16[16,96,128]{2,1,0:T(8,128)(2,1)}, bf16[16,96,128]{2,1,0:T(8,128)(2,1)S(1)}, u32[]{:S(2)}, u32[]{:S(2)}) collective-permute-start(bf16[16,96,128]{2,1,0:T(8,128)(2,1)} %get-tuple-element.36), channel_id=1, source_target_pairs={{0,1},{2,3},{1,0},{3,2},{4,5},{6,7},{5,4},{7,6},{8,9},{10,11},{9,8... | collective-permute-start | bytes 1179656 | tf_op jit(solution)/shard_map/ppermute | solution.py:410
  11.5 0.7 collective-permute-start.5
  12.2 1.4 %copy-done.1 = bf16[1,4,16,96,128]{4,3,2,1,0:T(8,128)(2,1)S(1)} copy-done((bf16[1,4,16,96,128]{4,3,2,1,0:T(8,128)(2,1)S(1)}, bf16[1,4,16,96,128]{4,3,2,1,0:T(8,128)(2,1)}, u32[]{:S(2)}) %copy-start.1) | copy-done | bytes 1572888
  13.6 0.8 copy-done.2
  14.4 0.7 copy-done.3
  15.1 0.7 copy-done.5
  16.4 5.9 %shard_map.73 = (f32[4,18,128,128]{3,2,1,0:T(8,128)}, f32[2,18,128,128]{3,2,1,0:T(8,128)}, bf16[16,32,128]{2,1,0:T(8,128)(2,1)S(1)}, bf16[8,96,128]{2,1,0:T(8,12...) custom-call(s32[4]{0:T(128)S(1)} %pad_add_fusion.flags, bf16[64,96,128]{2,1,0:T(8,128)(2,1)S(1)} %bitcast.14, ...), custom_call_target="tpu_custom_call" | custom-call | tf_op jit(solution)/shard_map/pallas_call | solution.py:461
  22.3 1.3 %collective-permute-start = (bf16[8,96,128]{2,1,0:T(8,128)(2,1)}, bf16[8,96,128]{2,1,0:T(8,128)(2,1)S(1)}, u32[]{:S(2)}, u32[]{:S(2)}) collective-permute-start(bf16[8,96,128]{2,1,0:T(8,128)(2,1)} %get-tuple-element.25), channel_id=1, source_target_pairs={{0,1},{2,3},{1,0},{3,2},{4,5},{6,7},{5,4},{7,6},{8,9},{10,11},{9,8... | collective-permute-start | bytes 589832 | tf_op jit(solution)/shard_map/ppermute | solution.py:410
  23.6 1.7 %collective-permute-done.2.near_a = bf16[33,96,128]{2,1,0:T(8,128)(2,1)S(1)} collective-permute-done((bf16[33,96,128]{2,1,0:T(8,128)(2,1)S(1)}, bf16[33,96,128]{2,1,0:T(8,128)(2,1)S(1)}, u32[]{:S(2)}, u32[]{:S(2)}) %collective-permute-start.2) | collective-permute-done | bytes 811040 | tf_op jit(solution)/shard_map/ppermute | solution.py:410
  25.3 0.7 collective-permute-start.1
  26.0 12.5 %shard_map.75 = (f32[12,18,128,128]{3,2,1,0:T(8,128)S(1)}, f32[10,18,128,128]{3,2,1,0:T(8,128)S(1)}, f32[6,192,128]{2,1,0:T(8,128)S(1)}, f32[8,64,128]{2,1,0:T(8...) custom-call(s32[4]{0:T(128)S(1)} %pad_add_fusion.flags, ...), custom_call_target="tpu_custom_call" | custom-call | tf_op jit(solution)/shard_map/pallas_call | solution.py:480
  38.5 4.7 %shard_map.76 = (f32[12,18,128,128]{3,2,1,0:T(8,128)S(1)}, f32[10,18,128,128]{3,2,1,0:T(8,128)S(1)}) custom-call(s32[4]{0:T(128)S(1)} %pad_add_fusion.flags, bf16[16,96,128]{2,1,0:T(8,128)(2,1)S(1)} %collective-permute-done.4.far_a, bf16[16,96,128]{2,1,0:T(8,128)(2,1)S(1)} %collective-permute-done.5.far_b, ...), custom_call_target="tpu_custom_call", output_to_operand_aliasing={{0}: (5, {}), {1}: (6, {})} | custom-call | tf_op jit(solution)/shard_map/pallas_call | solution.py:494
  43.2 4.4 %shard_map.77 = (f32[12,18,128,128]{3,2,1,0:T(8,128)S(1)}, f32[10,18,128,128]{3,2,1,0:T(8,128)S(1)}, bf16[2,128,2048]{2,1,0:T(8,128)(2,1)S(1)}, f32[136,128]{1,0:T(8,128)S(1)}) custom-call(s32[4]{0:T(128)S(1)} %pad_add_fusion.flags, bf16[8,96,128]{2,1,0:T(8,128)(2,1)S(1)} %collective-permute-done.last_a, ...), custom_call_target="tpu_custom_call", output_to_operand_aliasing={{0}: (7, {}), {1}: (8, {})} | custom-call | tf_op jit(solution)/shard_map/pallas_call | solution.py:502
  47.7 4.1 %collective-permute-start.8 = (f32[136,128]{1,0:T(8,128)S(1)}, f32[136,128]{1,0:T(8,128)S(1)}, u32[]{:S(2)}, u32[]{:S(2)}) collective-permute-start(f32[136,128]{1,0:T(8,128)S(1)} %get-tuple-element.42.refs_1_), channel_id=1, source_target_pairs={{0,3},{1,0},{2,1},{3,2},{4,7},{5,4},{6,5},{7,6},{8,11},{9,8},{10,9... | collective-permute-start | bytes 208904 | tf_op jit(solution)/shard_map/ppermute | solution.py:671
  51.8 2.2 %collective-permute-start.7 = (f32[136,128]{1,0:T(8,128)S(1)}, f32[136,128]{1,0:T(8,128)S(1)}, u32[]{:S(2)}, u32[]{:S(2)}) collective-permute-start(f32[136,128]{1,0:T(8,128)S(1)} %get-tuple-element.42.refs_1_), channel_id=1, source_target_pairs={{0,2},{1,3},{2,0},{3,1},{4,6},{5,7},{6,4},{7,5},{8,10},{9,11},{10,... | collective-permute-start | bytes 208904 | tf_op jit(solution)/shard_map/ppermute | solution.py:671
  54.0 1.8 %collective-permute-start.6 = (f32[136,128]{1,0:T(8,128)S(1)}, f32[136,128]{1,0:T(8,128)S(1)}, u32[]{:S(2)}, u32[]{:S(2)}) collective-permute-start(f32[136,128]{1,0:T(8,128)S(1)} %get-tuple-element.42.refs_1_), channel_id=1, source_target_pairs={{0,1},{1,2},{2,3},{3,0},{4,5},{5,6},{6,7},{7,4},{8,9},{9,10},{10,1... | collective-permute-start | bytes 208904 | tf_op jit(solution)/shard_map/ppermute | solution.py:671
  55.8 2.6 %collective-permute-done.7.refs_3_ = f32[136,128]{1,0:T(8,128)S(1)} collective-permute-done((f32[136,128]{1,0:T(8,128)S(1)}, f32[136,128]{1,0:T(8,128)S(1)}, u32[]{:S(2)}, u32[]{:S(2)}) %collective-permute-start.7) | collective-permute-done | bytes 69664 | tf_op jit(solution)/shard_map/ppermute | solution.py:671
  58.4 1.7 %collective-permute-done.6.refs_2_ = f32[136,128]{1,0:T(8,128)S(1)} collective-permute-done((f32[136,128]{1,0:T(8,128)S(1)}, f32[136,128]{1,0:T(8,128)S(1)}, u32[]{:S(2)}, u32[]{:S(2)}) %collective-permute-start.6) | collective-permute-done | bytes 69664 | tf_op jit(solution)/shard_map/ppermute | solution.py:671
  60.2 11.0 %shard_map.78 = bf16[8,32,768]{2,1,0:T(8,128)(2,1)S(1)} custom-call(s32[8]{0:T(128)S(1)} %dynamic-slice_bitcast_fusion.refs_0_, f32[136,128]{1,0:T(8,128)S(1)} %get-tuple-element.42.refs_1_, f32[136,128]{1,0:T(8,128)S(1)} %collective-permute-done.6.refs_2_, f32[136,128]{1,0:T(8,128)S(1)} %collective-permute-done.7.refs_3_, ...), custom_call_target="tpu_custom_call" | custom-call | tf_op jit(solution)/shard_map/pallas_call | solution.py:677
  71.1 11.9 %all_to_all.5 = bf16[8,32,768]{2,1,0:T(8,128)(2,1)S(1)} all-to-all(bf16[8,32,768]{2,1,0:T(8,128)(2,1)S(1)} %shard_map.78), channel_id=1, replica_groups=mesh['nbhd'=8,'sub'=4] {'nbhd'}, dimensions={0} | all-to-all | bytes 786432 | tf_op jit(solution)/shard_map/all_to_all | solution.py:689
  83.0 0.7 copy.17
  (18 shorter events, 0.8 us)
Async XLA Ops:
  0.0 55.8 %copy-start = (s32[8,8]{1,0:T(8,128)S(1)}, s32[8,8]{1,0:T(8,128)}, u32[]{:S(2)}) copy-start(s32[8,8]{1,0:T(8,128)} %param.13) | copy-start | bytes 772
  3.3 22.0 %collective-permute-start.2 = (bf16[33,96,128]{2,1,0:T(8,128)(2,1)S(1)}, bf16[33,96,128]{2,1,0:T(8,128)(2,1)S(1)}, u32[]{:S(2)}, u32[]{:S(2)}) collective-permute-start(bf16[33,96,128]{2,1,0:T(8,128)(2,1)S(1)} %get-tuple-element.27), channel_id=1, source_target_pairs={{0,1},{2,3},{1,0},{3,2},{4,5},{6,7},{5,4},{7,6},{8,9},{10,11},{9,8... | collective-permute-start | bytes 2433032 | tf_op jit(solution)/shard_map/ppermute | solution.py:410
  6.4 19.6 %collective-permute-start.3 = (bf16[33,96,128]{2,1,0:T(8,128)(2,1)}, bf16[33,96,128]{2,1,0:T(8,128)(2,1)S(1)}, u32[]{:S(2)}, u32[]{:S(2)}) collective-permute-start(bf16[33,96,128]{2,1,0:T(8,128)(2,1)} %get-tuple-element.28), channel_id=1, source_target_pairs={{1,2},{2,1},{5,6},{6,5},{9,10},{10,9},{13,14},{14,13},{17,18},{18,... | collective-permute-start | bytes 2433032 | tf_op jit(solution)/shard_map/ppermute | solution.py:410
  7.1 31.4 %collective-permute-start.4 = (bf16[16,96,128]{2,1,0:T(8,128)(2,1)}, bf16[16,96,128]{2,1,0:T(8,128)(2,1)S(1)}, u32[]{:S(2)}, u32[]{:S(2)}) collective-permute-start(bf16[16,96,128]{2,1,0:T(8,128)(2,1)} %get-tuple-element.36), channel_id=1, source_target_pairs={{0,1},{2,3},{1,0},{3,2},{4,5},{6,7},{5,4},{7,6},{8,9},{10,11},{9,8... | collective-permute-start | bytes 1179656 | tf_op jit(solution)/shard_map/ppermute | solution.py:410
  11.5 27.0 %collective-permute-start.5 = (bf16[16,96,128]{2,1,0:T(8,128)(2,1)S(1)}, bf16[16,96,128]{2,1,0:T(8,128)(2,1)S(1)}, u32[]{:S(2)}, u32[]{:S(2)}) collective-permute-start(bf16[16,96,128]{2,1,0:T(8,128)(2,1)S(1)} %get-tuple-element.37), channel_id=1, source_target_pairs={{1,2},{2,1},{5,6},{6,5},{9,10},{10,9},{13,14},{14,13},{17,18},{18,... | collective-permute-start | bytes 1179656 | tf_op jit(solution)/shard_map/ppermute | solution.py:410
  12.2 1.4 %copy-start.1 = (bf16[1,4,16,96,128]{4,3,2,1,0:T(8,128)(2,1)S(1)}, bf16[1,4,16,96,128]{4,3,2,1,0:T(8,128)(2,1)}, u32[]{:S(2)}) copy-start(bf16[1,4,16,96,128]{4,3,2,1,0:T(8,128)(2,1)} %param.7) | copy-start | bytes 4718596
  13.6 0.8 copy-start.2
  14.4 0.7 copy-start.3
  15.1 0.7 copy-start.5
  15.8 0.7 copy-start.6
  22.3 20.9 %collective-permute-start = (bf16[8,96,128]{2,1,0:T(8,128)(2,1)}, bf16[8,96,128]{2,1,0:T(8,128)(2,1)S(1)}, u32[]{:S(2)}, u32[]{:S(2)}) collective-permute-start(bf16[8,96,128]{2,1,0:T(8,128)(2,1)} %get-tuple-element.25), channel_id=1, source_target_pairs={{0,1},{2,3},{1,0},{3,2},{4,5},{6,7},{5,4},{7,6},{8,9},{10,11},{9,8... | collective-permute-start | bytes 589832 | tf_op jit(solution)/shard_map/ppermute | solution.py:410
  25.3 17.9 %collective-permute-start.1 = (bf16[8,96,128]{2,1,0:T(8,128)(2,1)}, bf16[8,96,128]{2,1,0:T(8,128)(2,1)S(1)}, u32[]{:S(2)}, u32[]{:S(2)}) collective-permute-start(bf16[8,96,128]{2,1,0:T(8,128)(2,1)} %get-tuple-element.26), channel_id=1, source_target_pairs={{1,2},{2,1},{5,6},{6,5},{9,10},{10,9},{13,14},{14,13},{17,18},{18,... | collective-permute-start | bytes 589832 | tf_op jit(solution)/shard_map/ppermute | solution.py:410
  43.2 16.9 %copy-start.4 = (f32[1,128,32]{1,2,0:T(8,128)S(1)}, f32[1,128,32]{1,2,0:T(8,128)}, u32[]{:S(2)}) copy-start(f32[1,128,32]{1,2,0:T(8,128)} %param.12) | copy-start | bytes 49156
  47.7 8.2 %collective-permute-start.8 = (f32[136,128]{1,0:T(8,128)S(1)}, f32[136,128]{1,0:T(8,128)S(1)}, u32[]{:S(2)}, u32[]{:S(2)}) collective-permute-start(f32[136,128]{1,0:T(8,128)S(1)} %get-tuple-element.42.refs_1_), channel_id=1, source_target_pairs={{0,3},{1,0},{2,1},{3,2},{4,7},{5,4},{6,5},{7,6},{8,11},{9,8},{10,9... | collective-permute-start | bytes 208904 | tf_op jit(solution)/shard_map/ppermute | solution.py:671
  51.8 6.6 %collective-permute-start.7 = (f32[136,128]{1,0:T(8,128)S(1)}, f32[136,128]{1,0:T(8,128)S(1)}, u32[]{:S(2)}, u32[]{:S(2)}) collective-permute-start(f32[136,128]{1,0:T(8,128)S(1)} %get-tuple-element.42.refs_1_), channel_id=1, source_target_pairs={{0,2},{1,3},{2,0},{3,1},{4,6},{5,7},{6,4},{7,5},{8,10},{9,11},{10,... | collective-permute-start | bytes 208904 | tf_op jit(solution)/shard_map/ppermute | solution.py:671
  54.0 6.1 %collective-permute-start.6 = (f32[136,128]{1,0:T(8,128)S(1)}, f32[136,128]{1,0:T(8,128)S(1)}, u32[]{:S(2)}, u32[]{:S(2)}) collective-permute-start(f32[136,128]{1,0:T(8,128)S(1)} %get-tuple-element.42.refs_1_), channel_id=1, source_target_pairs={{0,1},{1,2},{2,3},{3,0},{4,5},{5,6},{6,7},{7,4},{8,9},{9,10},{10,1... | collective-permute-start | bytes 208904 | tf_op jit(solution)/shard_map/ppermute | solution.py:671

commit v10 on v9

--- a/solution.py
+++ b/solution.py
@@ -185,23 +185,20 @@
     return jnp.left_shift(jnp.int32(1), 2 * marks).astype(jnp.float32)
 
 
-def pack_kernel(flags, class_map, lines, near_a, near_b, far_a, far_b, classes, sems):
+def pack_kernel(flags, class_map, lines, near_a, near_b, classes, sems):
     count, rows_z = classes.shape
-    far = far_a.shape[0]
     near = near_a.shape[0] - 1
     upward = flags[0]
-    fetch = pltpu.make_async_copy(class_map, classes, sems.at[4])
+    fetch = pltpu.make_async_copy(class_map, classes, sems.at[2])
     fetch.start()
     copies = []
-    for out, skip, size, start in (
-        (near_a, 1, near, upward * (count - near)),
-        (near_b, 1, near, (1 - upward) * (count - near)),
-        (far_a, 0, far, near - upward * far),
-        (far_b, 0, far, near - (1 - upward) * far),
+    for out, start in (
+        (near_a, upward * (count - near)),
+        (near_b, (1 - upward) * (count - near)),
     ):
         copies.append(
             pltpu.make_async_copy(
-                lines.at[pl.ds(start, size)], out.at[pl.ds(skip, size)], sems.at[len(copies)]
+                lines.at[pl.ds(start, near)], out.at[pl.ds(1, near)], sems.at[len(copies)]
             )
         )
         copies[-1].start()
@@ -226,8 +223,8 @@
     hand,
     inner,
     pad_rows,
-    last_a,
-    last_b,
+    far_a,
+    far_b,
     own_kappa,
     state_a,
     state_b,
@@ -276,8 +273,9 @@
     relax_lines(state_a, state_b, weights, (lines + rows_y,), inside, rows_y, rows_z, True)
     sends[1].start()
     half = rows_y // 2
-    for out, upward in ((last_a, flags[0]), (last_b, 1 - flags[0])):
-        out[...] = own[pl.ds(upward * half + (1 - upward) * (lines - rows_y), half)]
+    far = far_a.shape[0]
+    for out, upward in ((far_a, flags[0]), (far_b, 1 - flags[0])):
+        out[...] = own[pl.ds(upward * half + (1 - upward) * (lines - half - far), far)]
     for copy in sends:
         copy.wait()
 
@@ -352,22 +350,10 @@
         relax_lines(src, dst, weights, ends, count, rows_y, rows_z, sweep < SWEEPS)
 
 
-def far_kernel(flags, far_a, far_b, weights, pad_rows, old_a, old_b, state_a, state_b):
-    del old_a, old_b
-    rows_y = pad_rows.shape[0]
-    count, rows_z = far_a.shape[:2]
-    total = weights.shape[1]
-    even = flags[0]
-    shift = even * (total - 2 * rows_y - count)
-    fill(state_a, far_a, 0, count, rows_y + shift, pad_rows)
-    fill(state_a, far_b, 0, count, total - rows_y - count - shift, pad_rows)
-    advance((state_a, state_b), weights, rows_y, count, total, rows_y, rows_z)
-
-
-def last_kernel(
+def far_kernel(
     flags,
-    last_a,
-    last_b,
+    far_a,
+    far_b,
     weights,
     stiff_rows,
     pad_rows,
@@ -383,14 +369,15 @@
     del old_a, old_b
     width = snap.shape[1]
     rows_y = pad_rows.shape[0]
-    count, rows_z = last_a.shape[:2]
+    count, rows_z = far_a.shape[:2]
     planes = stiff_rows.shape[1] // rows_y
     lines = weights.shape[1]
-    shift = flags[0] * (lines - 3 * count)
-    fill(state_a, last_a, 0, count, count + shift, pad_rows)
-    fill(state_a, last_b, 0, count, lines - 2 * count - shift, pad_rows)
+    half = rows_y // 2
+    shift = flags[0] * (lines - 2 * half - count)
+    fill(state_a, far_a, 0, count, half + shift, pad_rows)
+    fill(state_a, far_b, 0, count, lines - half - count - shift, pad_rows)
     buffers = (state_a, state_b)
-    advance(buffers, weights, count, count, lines, rows_y, rows_z)
+    advance(buffers, weights, half, count, lines, rows_y, rows_z)
     final = buffers[SWEEPS % 2]
     outer = (planes, 2 * planes - 1)
     total = gram_terms(final, outer, planes, stiff_rows, snap, both, near_gram[...])
@@ -443,29 +430,27 @@
         jax.ShapeDtypeStruct((6, 3 * count, LANES), jnp.float32),
         jax.ShapeDtypeStruct((8, count, LANES), jnp.float32),
     ]
-    near_a, near_b, far_a, far_b = pl.pallas_call(
+    near_a, near_b = pl.pallas_call(
         pack_kernel,
-        out_shape=[part((near + 1, rows_z, width))] * 2 + [part((rows_y, rows_z, width))] * 2,
+        out_shape=[part((near + 1, rows_z, width))] * 2,
         in_specs=[smem] + [hbm] * 2,
-        out_specs=[vmem] * 4,
+        out_specs=[vmem] * 2,
         scratch_shapes=[
             pltpu.VMEM((count, rows_z), jnp.int32),
-            pltpu.SemaphoreType.DMA((5,)),
+            pltpu.SemaphoreType.DMA((3,)),
         ],
         compiler_params=params,
     )(flags, in_hbm(flat_classes), in_hbm(lines))
     near_a = swap(near_a, 0)
     near_b = swap(near_b, 1)
-    far_a = swap(far_a, 0)
-    far_b = swap(far_b, 1)
-    hand, inner, pad_rows, last_a, last_b, own_kappa = pl.pallas_call(
+    hand, inner, pad_rows, far_a, far_b, own_kappa = pl.pallas_call(
         own_kernel,
         out_shape=[
             pltpu.HBM((planes,) + first_state.shape[1:], jnp.float32),
             pltpu.HBM((planes - 2,) + first_state.shape[1:], jnp.float32),
             part((rows_y, LANES - rows_z, width)),
-            part((half, rows_z, width)),
-            part((half, rows_z, width)),
+            part((rows_y + half, rows_z, width)),
+            part((rows_y + half, rows_z, width)),
             jax.ShapeDtypeStruct((count, LANES), jnp.float32),
         ],
         in_specs=[smem] + [vmem] * 5,
@@ -475,8 +460,8 @@
         + [pltpu.SemaphoreType.DMA((2,))],
         compiler_params=pltpu.CompilerParams(vmem_limit_bytes=40 * 2**20),
     )(flags, lines, flat_classes, y_vals, z_vals, face_ids[None])
-    last_a = swap(last_a, 0)
-    last_b = swap(last_b, 1)
+    far_a = swap(far_a, 0)
+    far_b = swap(far_b, 1)
     state_a, state_b, weights, stiff_rows, snap_near, gram_near = pl.pallas_call(
         near_kernel,
         out_shape=[
@@ -491,16 +476,8 @@
         scratch_shapes=[kappa, both, pltpu.SemaphoreType.DMA((2,))],
         compiler_params=params,
     )(flags, near_a, near_b, own_kappa, pad_rows, in_hbm(hand), in_hbm(inner))
-    state_a, state_b = pl.pallas_call(
+    _, _, snap_far, gram = pl.pallas_call(
         far_kernel,
-        out_shape=[first_state, second_state],
-        in_specs=[smem] + [vmem] * 6,
-        out_specs=[vmem] * 2,
-        input_output_aliases={5: 0, 6: 1},
-        compiler_params=params,
-    )(flags, far_a, far_b, weights, pad_rows, held(state_a), held(state_b))
-    _, _, snap_far, gram = pl.pallas_call(
-        last_kernel,
         out_shape=[
             first_state,
             second_state,
@@ -514,8 +491,8 @@
         compiler_params=params,
     )(
         flags,
-        last_a,
-        last_b,
+        far_a,
+        far_b,
         weights,
         stiff_rows,
         pad_rows,
@@ -534,32 +511,48 @@
     return jnp.broadcast_to(tile[row : row + 1, :], (8, tile.shape[1]))
 
 
+def pivot_block(left, right, first_lane):
+    sub = lax.broadcasted_iota(jnp.int32, (8, 128), 0)
+    cols = [lane_copy(left, first_lane + j) for j in range(8)]
+    for j in range(8):
+        recip = pl.reciprocal(row_copy(cols[j], j), approx=True)
+        here = sub == j
+        mult = jnp.where(here, recip, -cols[j] * recip)
+        for l in range(j + 1, 8):
+            cols[l] = jnp.where(here, 0.0, cols[l]) + mult * row_copy(cols[l], j)
+        left = jnp.where(here, 0.0, left) + mult * row_copy(left, j)
+        right = jnp.where(here, 0.0, right) + mult * row_copy(right, j)
+        yield left, right
+
+
 def solve_spd(left, right):
     size = left.shape[0]
     count = size // 8
-    sub = lax.broadcasted_iota(jnp.int32, (8, 128), 0)
     lhs = [left[8 * t : 8 * t + 8] for t in range(count)]
     rhs = [right[8 * t : 8 * t + 8] for t in range(count)]
+    for panel in pivot_block(lhs[0], rhs[0], 0):
+        lhs[0], rhs[0] = panel
     for k in range(count):
-        cols = [lane_copy(lhs[k], 8 * k + j) for j in range(8)]
-        panel_l, panel_r = lhs[k], rhs[k]
-        for j in range(8):
-            recip = pl.reciprocal(row_copy(cols[j], j), approx=True)
-            here = sub == j
-            mult = jnp.where(here, recip, -cols[j] * recip)
-            for l in range(j + 1, 8):
-                cols[l] = jnp.where(here, 0.0, cols[l]) + mult * row_copy(cols[l], j)
-            panel_l = jnp.where(here, 0.0, panel_l) + mult * row_copy(panel_l, j)
-            panel_r = jnp.where(here, 0.0, panel_r) + mult * row_copy(panel_r, j)
-        rows_l = [row_copy(panel_l, j) for j in range(8)]
-        rows_r = [row_copy(panel_r, j) for j in range(8)]
-        order = list(range(k + 1, count)) + list(range(k))
-        for t in order:
+        rows_l = [row_copy(lhs[k], j) for j in range(8)]
+        rows_r = [row_copy(rhs[k], j) for j in range(8)]
+
+        def update(t, k=k, rows_l=rows_l, rows_r=rows_r):
             tile_cols = [lane_copy(lhs[t], 8 * k + j) for j in range(8)]
             if k + 1 < count:
                 lhs[t] = lhs[t] - tree([tile_cols[j] * rows_l[j] for j in range(8)])
             rhs[t] = rhs[t] - tree([tile_cols[j] * rows_r[j] for j in range(8)])
-        lhs[k], rhs[k] = panel_l, panel_r
+
+        others = [t for t in range(count) if t not in (k, k + 1)]
+        if k + 1 < count:
+            update(k + 1)
+            panel = None
+            for panel in pivot_block(lhs[k + 1], rhs[k + 1], 8 * (k + 1)):
+                for t in others[:2]:
+                    update(t)
+                others = others[2:]
+            lhs[k + 1], rhs[k + 1] = panel
+        for t in others:
+            update(t)
     return jnp.concatenate(rhs, axis=0)
 
 

time: 84.1 us -> 84.3 us (level)
  starting transfers between devices: 19 us -> 17.5 us
  waiting for transfers between devices: 5.98 us -> 7.08 us
    ppermute x6 -> x4, starting transfers between devices: 10.9 us -> 8.89 us  [swap(): return lax.ppermute(array, 'sub', pairs + [(j, i) for i, j in pairs])]
    ppermute x6 -> x4, waiting for transfers between devices: 1.67 us -> 2.94 us  [swap(): return lax.ppermute(array, 'sub', pairs + [(j, i) for i, j in pairs])]
    pallas_call x2 -> x1, Pallas kernels: 9.14 us -> 9.55 us  [relax(): pl.pallas_call(far_kernel, out_shape=[first_state, second_state, kept(2),...]
  transfers between devices with their start and end apart: 9 -> 7, of which waited for: 3 -> 3; matrix products, arithmetic and copies ran while one was open for 0% -> 0% of each run, Pallas kernels for 28% -> 22%
where the time goes in v10:
time: 84.3 us; the launch traced here: 83.9 us
  Pallas kernels  42.3 us (50%)
  starting transfers between devices  17.5 us (21%)
  blocking collectives  11.9 us (14%)
  waiting for transfers between devices  7.08 us (8%)
  local copies, waits for them, and re-layouts  5 us (6%)
    pallas_call x1, Pallas kernels, relax(): pl.pallas_call(near_kernel, out_shape=[first_state, second_state, *rows,...  12.5 us
    all_to_all x1, blocking collectives, on_device(): lax.all_to_all(pieces, 'nbhd', split_axis=0, concat_axis=0, tiled=True)  11.9 us
    pallas_call x1, Pallas kernels, on_device(): pl.pallas_call(functools.partial(modes_kernel, float(subs * cells), rows_...  10.9 us
    pallas_call x1, Pallas kernels, relax(): pl.pallas_call(far_kernel, out_shape=[first_state, second_state, kept(2),...  9.55 us
    ppermute x4, starting transfers between devices, swap(): return lax.ppermute(array, 'sub', pairs + [(j, i) for i, j in pairs])  8.89 us
    ppermute x3, starting transfers between devices, on_device(): lax.ppermute(own, 'sub', [(i, (i + shift) % subs) for i in range(subs)])  8.64 us
    pallas_call x1, Pallas kernels, relax(): pl.pallas_call(own_kernel, out_shape=[pltpu.HBM((planes,) + first_state.s...  6.1 us
    unnamed x15, local copies, waits for them, and re-layouts  4.99 us
  transfers between devices with their start and end apart: 7, of which 3 were waited for; matrix products, arithmetic and copies ran while one was open for 0% of the time, Pallas kernels for 22%

profile of v10, /device:TPU:0, one launch (start us, length us, event | category | flops | bytes accessed | tf_op | source)
XLA Modules:
  0.0 83.9 jit_solution(373703455450596104)
XLA Ops:
  0.0 0.1 pad_add_fusion.flags
  0.1 3.2 %shard_map.74 = (bf16[33,96,128]{2,1,0:T(8,128)(2,1)}, bf16[33,96,128]{2,1,0:T(8,128)(2,1)}) custom-call(s32[4]{0:T(128)S(1)} %pad_add_fusion.flags, s32[64,96]{1,0:T(8,128)} %bitcast.15, bf16[64,96,128]{2,1,0:T(8,128)(2,1)} %bitcast.13), custom_call_target="tpu_custom_call" | custom-call | tf_op jit(solution)/shard_map/pallas_call | solution.py:433
  3.3 3.1 %collective-permute-start.2 = (bf16[33,96,128]{2,1,0:T(8,128)(2,1)}, bf16[33,96,128]{2,1,0:T(8,128)(2,1)S(1)}, u32[]{:S(2)}, u32[]{:S(2)}) collective-permute-start(bf16[33,96,128]{2,1,0:T(8,128)(2,1)} %get-tuple-element.23), channel_id=1, source_target_pairs={{0,1},{2,3},{1,0},{3,2},{4,5},{6,7},{5,4},{7,6},{8,9},{10,11},{9,8... | collective-permute-start | bytes 2433032 | tf_op jit(solution)/shard_map/ppermute | solution.py:397
  6.4 0.7 collective-permute-start.3
  7.1 1.4 %copy-done.1 = bf16[1,4,16,96,128]{4,3,2,1,0:T(8,128)(2,1)S(1)} copy-done((bf16[1,4,16,96,128]{4,3,2,1,0:T(8,128)(2,1)S(1)}, bf16[1,4,16,96,128]{4,3,2,1,0:T(8,128)(2,1)}, u32[]{:S(2)}) %copy-start.1) | copy-done | bytes 1572888
  8.5 0.8 copy-done.2
  9.3 0.7 copy-done.3
  10.0 0.7 copy-done.5
  10.7 0.7 copy-done.6
  11.3 6.1 %shard_map.73 = (f32[4,18,128,128]{3,2,1,0:T(8,128)}, f32[2,18,128,128]{3,2,1,0:T(8,128)}, bf16[16,32,128]{2,1,0:T(8,128)(2,1)S(1)}, bf16[24,96,128]{2,1,0:T(8,1...) custom-call(s32[4]{0:T(128)S(1)} %pad_add_fusion.flags, bf16[64,96,128]{2,1,0:T(8,128)(2,1)S(1)} %bitcast.14, ...), custom_call_target="tpu_custom_call" | custom-call | tf_op jit(solution)/shard_map/pallas_call | solution.py:446
  17.4 4.4 %collective-permute-start = (bf16[24,96,128]{2,1,0:T(8,128)(2,1)}, bf16[24,96,128]{2,1,0:T(8,128)(2,1)S(1)}, u32[]{:S(2)}, u32[]{:S(2)}) collective-permute-start(bf16[24,96,128]{2,1,0:T(8,128)(2,1)} %get-tuple-element.21), channel_id=1, source_target_pairs={{0,1},{2,3},{1,0},{3,2},{4,5},{6,7},{5,4},{7,6},{8,9},{10,11},{9,8... | collective-permute-start | bytes 1769480 | tf_op jit(solution)/shard_map/ppermute | solution.py:397
  21.9 0.7 collective-permute-start.1
  22.6 2.9 %collective-permute-done.2.near_a = bf16[33,96,128]{2,1,0:T(8,128)(2,1)S(1)} collective-permute-done((bf16[33,96,128]{2,1,0:T(8,128)(2,1)}, bf16[33,96,128]{2,1,0:T(8,128)(2,1)S(1)}, u32[]{:S(2)}, u32[]{:S(2)}) %collective-permute-start.2) | collective-permute-done | bytes 811040 | tf_op jit(solution)/shard_map/ppermute | solution.py:397
  25.5 12.5 %shard_map.75 = (f32[12,18,128,128]{3,2,1,0:T(8,128)S(1)}, f32[10,18,128,128]{3,2,1,0:T(8,128)S(1)}, f32[6,192,128]{2,1,0:T(8,128)S(1)}, f32[8,64,128]{2,1,0:T(8...) custom-call(s32[4]{0:T(128)S(1)} %pad_add_fusion.flags, ...), custom_call_target="tpu_custom_call" | custom-call | tf_op jit(solution)/shard_map/pallas_call | solution.py:465
  38.0 0.0 copy-start.4
  38.1 9.6 %shard_map.76 = (f32[12,18,128,128]{3,2,1,0:T(8,128)S(1)}, f32[10,18,128,128]{3,2,1,0:T(8,128)S(1)}, bf16[2,128,2048]{2,1,0:T(8,128)(2,1)S(1)}, f32[136,128]{1,0:T(8,128)S(1)}) custom-call(s32[4]{0:T(128)S(1)} %pad_add_fusion.flags, bf16[24,96,128]{2,1,0:T(8,128)(2,1)S(1)} %collective-permute-done.far_a, ...), custom_call_target="tpu_custom_call", output_to_operand_aliasing={{0}: (7, {}), {1}: (8, {})} | custom-call | tf_op jit(solution)/shard_map/pallas_call | solution.py:479
  47.6 4.1 %collective-permute-start.6 = (f32[136,128]{1,0:T(8,128)S(1)}, f32[136,128]{1,0:T(8,128)S(1)}, u32[]{:S(2)}, u32[]{:S(2)}) collective-permute-start(f32[136,128]{1,0:T(8,128)S(1)} %get-tuple-element.34.refs_1_), channel_id=1, source_target_pairs={{0,3},{1,0},{2,1},{3,2},{4,7},{5,4},{6,5},{7,6},{8,11},{9,8},{10,9... | collective-permute-start | bytes 208904 | tf_op jit(solution)/shard_map/ppermute | solution.py:664
  51.8 2.6 %collective-permute-start.5 = (f32[136,128]{1,0:T(8,128)S(1)}, f32[136,128]{1,0:T(8,128)S(1)}, u32[]{:S(2)}, u32[]{:S(2)}) collective-permute-start(f32[136,128]{1,0:T(8,128)S(1)} %get-tuple-element.34.refs_1_), channel_id=1, source_target_pairs={{0,2},{1,3},{2,0},{3,1},{4,6},{5,7},{6,4},{7,5},{8,10},{9,11},{10,... | collective-permute-start | bytes 208904 | tf_op jit(solution)/shard_map/ppermute | solution.py:664
  54.3 1.9 %collective-permute-start.4 = (f32[136,128]{1,0:T(8,128)S(1)}, f32[136,128]{1,0:T(8,128)S(1)}, u32[]{:S(2)}, u32[]{:S(2)}) collective-permute-start(f32[136,128]{1,0:T(8,128)S(1)} %get-tuple-element.34.refs_1_), channel_id=1, source_target_pairs={{0,1},{1,2},{2,3},{3,0},{4,5},{5,6},{6,7},{7,4},{8,9},{9,10},{10,1... | collective-permute-start | bytes 208904 | tf_op jit(solution)/shard_map/ppermute | solution.py:664
  56.3 1.8 %collective-permute-done.5.refs_3_ = f32[136,128]{1,0:T(8,128)S(1)} collective-permute-done((f32[136,128]{1,0:T(8,128)S(1)}, f32[136,128]{1,0:T(8,128)S(1)}, u32[]{:S(2)}, u32[]{:S(2)}) %collective-permute-start.5) | collective-permute-done | bytes 69664 | tf_op jit(solution)/shard_map/ppermute | solution.py:664
  58.0 2.4 %collective-permute-done.4.refs_2_ = f32[136,128]{1,0:T(8,128)S(1)} collective-permute-done((f32[136,128]{1,0:T(8,128)S(1)}, f32[136,128]{1,0:T(8,128)S(1)}, u32[]{:S(2)}, u32[]{:S(2)}) %collective-permute-start.4) | collective-permute-done | bytes 69664 | tf_op jit(solution)/shard_map/ppermute | solution.py:664
  60.4 10.9 %shard_map.77 = bf16[8,32,768]{2,1,0:T(8,128)(2,1)S(1)} custom-call(s32[8]{0:T(128)S(1)} %dynamic-slice_bitcast_fusion.refs_0_, f32[136,128]{1,0:T(8,128)S(1)} %get-tuple-element.34.refs_1_, f32[136,128]{1,0:T(8,128)S(1)} %collective-permute-done.4.refs_2_, f32[136,128]{1,0:T(8,128)S(1)} %collective-permute-done.5.refs_3_, ...), custom_call_target="tpu_custom_call" | custom-call | tf_op jit(solution)/shard_map/pallas_call | solution.py:670
  71.3 11.9 %all_to_all.5 = bf16[8,32,768]{2,1,0:T(8,128)(2,1)S(1)} all-to-all(bf16[8,32,768]{2,1,0:T(8,128)(2,1)S(1)} %shard_map.77), channel_id=1, replica_groups=mesh['nbhd'=8,'sub'=4] {'nbhd'}, dimensions={0} | all-to-all | bytes 786432 | tf_op jit(solution)/shard_map/all_to_all | solution.py:682
  83.2 0.7 copy.13
  (13 shorter events, 0.0 us)
Async XLA Ops:
  0.0 56.3 %copy-start = (s32[8,8]{1,0:T(8,128)S(1)}, s32[8,8]{1,0:T(8,128)}, u32[]{:S(2)}) copy-start(s32[8,8]{1,0:T(8,128)} %param.13) | copy-start | bytes 772
  3.3 22.2 %collective-permute-start.2 = (bf16[33,96,128]{2,1,0:T(8,128)(2,1)}, bf16[33,96,128]{2,1,0:T(8,128)(2,1)S(1)}, u32[]{:S(2)}, u32[]{:S(2)}) collective-permute-start(bf16[33,96,128]{2,1,0:T(8,128)(2,1)} %get-tuple-element.23), channel_id=1, source_target_pairs={{0,1},{2,3},{1,0},{3,2},{4,5},{6,7},{5,4},{7,6},{8,9},{10,11},{9,8... | collective-permute-start | bytes 2433032 | tf_op jit(solution)/shard_map/ppermute | solution.py:397
  6.4 19.1 %collective-permute-start.3 = (bf16[33,96,128]{2,1,0:T(8,128)(2,1)}, bf16[33,96,128]{2,1,0:T(8,128)(2,1)S(1)}, u32[]{:S(2)}, u32[]{:S(2)}) collective-permute-start(bf16[33,96,128]{2,1,0:T(8,128)(2,1)} %get-tuple-element.24), channel_id=1, source_target_pairs={{1,2},{2,1},{5,6},{6,5},{9,10},{10,9},{13,14},{14,13},{17,18},{18,... | collective-permute-start | bytes 2433032 | tf_op jit(solution)/shard_map/ppermute | solution.py:397
  7.1 1.4 %copy-start.1 = (bf16[1,4,16,96,128]{4,3,2,1,0:T(8,128)(2,1)S(1)}, bf16[1,4,16,96,128]{4,3,2,1,0:T(8,128)(2,1)}, u32[]{:S(2)}) copy-start(bf16[1,4,16,96,128]{4,3,2,1,0:T(8,128)(2,1)} %param.7) | copy-start | bytes 4718596
  8.5 0.8 copy-start.2
  9.3 0.7 copy-start.3
  10.0 0.7 copy-start.5
  10.7 0.7 copy-start.6
  17.4 20.6 %collective-permute-start = (bf16[24,96,128]{2,1,0:T(8,128)(2,1)}, bf16[24,96,128]{2,1,0:T(8,128)(2,1)S(1)}, u32[]{:S(2)}, u32[]{:S(2)}) collective-permute-start(bf16[24,96,128]{2,1,0:T(8,128)(2,1)} %get-tuple-element.21), channel_id=1, source_target_pairs={{0,1},{2,3},{1,0},{3,2},{4,5},{6,7},{5,4},{7,6},{8,9},{10,11},{9,8... | collective-permute-start | bytes 1769480 | tf_op jit(solution)/shard_map/ppermute | solution.py:397
  21.9 16.2 %collective-permute-start.1 = (bf16[24,96,128]{2,1,0:T(8,128)(2,1)}, bf16[24,96,128]{2,1,0:T(8,128)(2,1)S(1)}, u32[]{:S(2)}, u32[]{:S(2)}) collective-permute-start(bf16[24,96,128]{2,1,0:T(8,128)(2,1)} %get-tuple-element.22), channel_id=1, source_target_pairs={{1,2},{2,1},{5,6},{6,5},{9,10},{10,9},{13,14},{14,13},{17,18},{18,... | collective-permute-start | bytes 1769480 | tf_op jit(solution)/shard_map/ppermute | solution.py:397
  38.0 22.4 %copy-start.4 = (f32[1,128,32]{1,2,0:T(8,128)S(1)}, f32[1,128,32]{1,2,0:T(8,128)}, u32[]{:S(2)}) copy-start(f32[1,128,32]{1,2,0:T(8,128)} %param.12) | copy-start | bytes 49156
  47.6 8.7 %collective-permute-start.6 = (f32[136,128]{1,0:T(8,128)S(1)}, f32[136,128]{1,0:T(8,128)S(1)}, u32[]{:S(2)}, u32[]{:S(2)}) collective-permute-start(f32[136,128]{1,0:T(8,128)S(1)} %get-tuple-element.34.refs_1_), channel_id=1, source_target_pairs={{0,3},{1,0},{2,1},{3,2},{4,7},{5,4},{6,5},{7,6},{8,11},{9,8},{10,9... | collective-permute-start | bytes 208904 | tf_op jit(solution)/shard_map/ppermute | solution.py:664
  51.8 6.3 %collective-permute-start.5 = (f32[136,128]{1,0:T(8,128)S(1)}, f32[136,128]{1,0:T(8,128)S(1)}, u32[]{:S(2)}, u32[]{:S(2)}) collective-permute-start(f32[136,128]{1,0:T(8,128)S(1)} %get-tuple-element.34.refs_1_), channel_id=1, source_target_pairs={{0,2},{1,3},{2,0},{3,1},{4,6},{5,7},{6,4},{7,5},{8,10},{9,11},{10,... | collective-permute-start | bytes 208904 | tf_op jit(solution)/shard_map/ppermute | solution.py:664
  54.3 6.1 %collective-permute-start.4 = (f32[136,128]{1,0:T(8,128)S(1)}, f32[136,128]{1,0:T(8,128)S(1)}, u32[]{:S(2)}, u32[]{:S(2)}) collective-permute-start(f32[136,128]{1,0:T(8,128)S(1)} %get-tuple-element.34.refs_1_), channel_id=1, source_target_pairs={{0,1},{1,2},{2,3},{3,0},{4,5},{5,6},{6,7},{7,4},{8,9},{9,10},{10,1... | collective-permute-start | bytes 208904 | tf_op jit(solution)/shard_map/ppermute | solution.py:664

commit v11 on v10

--- a/solution.py
+++ b/solution.py
@@ -189,19 +189,23 @@
     count, rows_z = classes.shape
     near = near_a.shape[0] - 1
     upward = flags[0]
-    fetch = pltpu.make_async_copy(class_map, classes, sems.at[2])
+    fetch = pltpu.make_async_copy(class_map, classes, sems.at[16])
     fetch.start()
     copies = []
+    chunk = near // 8
     for out, start in (
         (near_a, upward * (count - near)),
         (near_b, (1 - upward) * (count - near)),
     ):
-        copies.append(
-            pltpu.make_async_copy(
-                lines.at[pl.ds(start, near)], out.at[pl.ds(1, near)], sems.at[len(copies)]
+        for at in range(0, near, chunk):
+            copies.append(
+                pltpu.make_async_copy(
+                    lines.at[pl.ds(start + at, chunk)],
+                    out.at[pl.ds(1 + at, chunk)],
+                    sems.at[len(copies)],
+                )
             )
-        )
-        copies[-1].start()
+            copies[-1].start()
     fetch.wait()
     marks = classes[...].astype(jnp.float32).astype(jnp.bfloat16)
     width = near_a.shape[2]
@@ -261,17 +265,22 @@
     lax.fori_loop(planes, 2 * planes, edges, 0)
     fill(state_a, own, 0, lines, lines, pad_rows)
     sends = [
-        pltpu.make_async_copy(state_a.at[pl.ds(planes, planes)], hand, sems.at[0]),
-        pltpu.make_async_copy(state_b.at[pl.ds(planes, planes - 2)], inner, sems.at[1]),
+        pltpu.make_async_copy(state_a.at[planes + p], hand.at[p], sems.at[p])
+        for p in range(planes)
     ]
-    sends[0].start()
+    for copy in sends:
+        copy.start()
     kappa[...] = jnp.ones(kappa.shape, jnp.float32)
     kappa[pl.ds(lines, lines), pl.ds(0, rows_z)] = powers(classes[...])
     own_kappa[...] = kappa[pl.ds(lines, lines)]
     weight_rows(kappa, weights, stiff_rows, lines, flags[1], flags[2], rows_y, rows_z)
     inside = lines - 2 * rows_y
     relax_lines(state_a, state_b, weights, (lines + rows_y,), inside, rows_y, rows_z, True)
-    sends[1].start()
+    for p in range(planes - 2):
+        sends.append(
+            pltpu.make_async_copy(state_b.at[planes + p], inner.at[p], sems.at[planes + p])
+        )
+        sends[-1].start()
     half = rows_y // 2
     far = far_a.shape[0]
     for out, upward in ((far_a, flags[0]), (far_b, 1 - flags[0])):
@@ -303,12 +312,18 @@
     rows_y = pad_rows.shape[0]
     near = lines // 2
     planes = lines // rows_y
-    taken = [
-        pltpu.make_async_copy(hand, state_a.at[pl.ds(planes, planes)], sems.at[0]),
-        pltpu.make_async_copy(inner, state_b.at[pl.ds(planes, planes - 2)], sems.at[1]),
-    ]
-    for copy in taken:
-        copy.start()
+    taken = []
+    cut = (rows_y + 2) // 2
+    for source, state, count in ((hand, state_a, planes), (inner, state_b, planes - 2)):
+        for p in range(count):
+            for start in (0, cut):
+                some = pl.ds(start, cut)
+                taken.append(
+                    pltpu.make_async_copy(
+                        source.at[p, some], state.at[planes + p, some], sems.at[len(taken)]
+                    )
+                )
+                taken[-1].start()
     even, first, last = flags[0], flags[1], flags[2]
     base_a = pl.multiple_of(even * (2 * lines), 8)
     base_b = pl.multiple_of((1 - even) * (2 * lines), 8)
@@ -437,7 +452,7 @@
         out_specs=[vmem] * 2,
         scratch_shapes=[
             pltpu.VMEM((count, rows_z), jnp.int32),
-            pltpu.SemaphoreType.DMA((3,)),
+            pltpu.SemaphoreType.DMA((17,)),
         ],
         compiler_params=params,
     )(flags, in_hbm(flat_classes), in_hbm(lines))
@@ -457,7 +472,7 @@
         out_specs=[hbm] * 2 + [vmem] * 4,
         scratch_shapes=[first_state, second_state, kappa]
         + [pltpu.VMEM(item.shape, item.dtype) for item in rows]
-        + [pltpu.SemaphoreType.DMA((2,))],
+        + [pltpu.SemaphoreType.DMA((2 * planes - 2,))],
         compiler_params=pltpu.CompilerParams(vmem_limit_bytes=40 * 2**20),
     )(flags, lines, flat_classes, y_vals, z_vals, face_ids[None])
     far_a = swap(far_a, 0)
@@ -473,7 +488,7 @@
         ],
         in_specs=[smem] + [vmem] * 4 + [hbm] * 2,
         out_specs=[vmem] * 6,
-        scratch_shapes=[kappa, both, pltpu.SemaphoreType.DMA((2,))],
+        scratch_shapes=[kappa, both, pltpu.SemaphoreType.DMA((4 * planes - 4,))],
         compiler_params=params,
     )(flags, near_a, near_b, own_kappa, pad_rows, in_hbm(hand), in_hbm(inner))
     _, _, snap_far, gram = pl.pallas_call(
@@ -608,16 +623,24 @@
     )
 
 
-def modes_kernel(cell_count, rows_z, *refs):
-    mask_ref, *part_refs, start_ref, near_hbm, far_hbm, out_ref, snap_ref, sems = refs
-    planes, _, columns = snap_ref.shape
-    places = [(far_hbm, 0, 0, 1), (near_hbm, 0, 1, planes - 2), (far_hbm, 1, planes - 1, 1)]
-    fetches = [
-        pltpu.make_async_copy(src.at[pl.ds(at, n)], snap_ref.at[pl.ds(to, n)], sems.at[k])
-        for k, (src, at, to, n) in enumerate(places)
-    ]
-    for fetch in fetches:
-        fetch.start()
+def order_kernel(rows_z, near_ref, far_ref, out_ref):
+    planes = near_ref.shape[0] + 2
+    rows_y = near_ref.shape[2] // LANES
+    piece_rows = planes * rows_y // out_ref.shape[0]
+    for p in range(planes):
+        inside = 0 < p < planes - 1
+        source, at = (near_ref, p - 1) if inside else (far_ref, min(p, 1))
+        for y in range(rows_y):
+            piece, spot = divmod(p * rows_y + y, piece_rows)
+            out_ref[piece, :, pl.ds(spot * rows_z, rows_z)] = source[
+                at, :, pl.ds(y * LANES, rows_z)
+            ]
+
+
+def modes_kernel(cell_count, *refs):
+    mask_ref, *part_refs, start_ref, snap_hbm, out_ref, snap_ref, sem = refs
+    fetch = pltpu.make_async_copy(snap_hbm, snap_ref, sem)
+    fetch.start()
     total = part_refs[0][...]
     for part in part_refs[1:]:
         total = total + part[...]
@@ -639,18 +662,11 @@
         inner = dot_rows(products[:, :width], block)
         block = whiten(inner, products[:, width:])
     modes = block.astype(jnp.bfloat16)
-    for fetch in fetches:
-        fetch.wait()
-    lanes = LANES
-    rows_y = columns // lanes
-    piece_rows = planes * rows_y // out_ref.shape[0]
-    for p in range(planes):
-        basis = jnp.dot(modes, snap_ref[p], preferred_element_type=jnp.float32)
-        for y in range(rows_y):
-            piece, spot = divmod(p * rows_y + y, piece_rows)
-            values = basis[:, y * lanes : y * lanes + rows_z].astype(jnp.bfloat16)
-            wanted = mask_ref[piece] != 0
-            out_ref[piece, :, pl.ds(spot * rows_z, rows_z)] = jnp.where(wanted, values, 0.0)
+    fetch.wait()
+    for piece in range(out_ref.shape[0]):
+        basis = jnp.dot(modes, snap_ref[piece], preferred_element_type=jnp.float32)
+        wanted = mask_ref[piece] != 0
+        out_ref[piece] = jnp.where(wanted, basis.astype(jnp.bfloat16), 0.0)
 
 
 def on_device(snap_init, channel_map, yface_vals, zface_vals, face_of, start_block, correlation):
@@ -665,20 +681,25 @@
         for shift in range(1, subs)
     ]
     cells = planes * rows_y * rows_z
+    ordered = pl.pallas_call(
+        functools.partial(order_kernel, rows_z),
+        out_shape=jax.ShapeDtypeStruct((owner_count, width, cells // owner_count), jnp.bfloat16),
+        compiler_params=pltpu.CompilerParams(vmem_limit_bytes=8 * 2**20),
+    )(snap_near, snap_far)
     modes = start_block.shape[-1]
     mask = lax.dynamic_slice_in_dim(correlation, lax.axis_index("nbhd"), 1, axis=0)[0]
     pieces = pl.pallas_call(
-        functools.partial(modes_kernel, float(subs * cells), rows_z),
+        functools.partial(modes_kernel, float(subs * cells)),
         out_shape=jax.ShapeDtypeStruct((owner_count, modes, cells // owner_count), jnp.bfloat16),
         in_specs=[pl.BlockSpec(memory_space=pltpu.SMEM)]
         + [pl.BlockSpec(memory_space=pltpu.VMEM)] * (subs + 1)
-        + [pl.BlockSpec(memory_space=pltpu.HBM)] * 2,
+        + [pl.BlockSpec(memory_space=pltpu.HBM)],
         scratch_shapes=[
-            pltpu.VMEM((planes, width, rows_y * LANES), jnp.bfloat16),
-            pltpu.SemaphoreType.DMA((3,)),
+            pltpu.VMEM(ordered.shape, ordered.dtype),
+            pltpu.SemaphoreType.DMA,
         ],
         compiler_params=pltpu.CompilerParams(vmem_limit_bytes=24 * 2**20),
-    )(mask, *parts, start_block[0].T, snap_near, snap_far)
+    )(mask, *parts, start_block[0].T, ordered)
     received = lax.all_to_all(pieces, "nbhd", split_axis=0, concat_axis=0, tiled=True)
     return received[None, None]
 

time: 84.3 us -> 84.3 us (level)
  waiting for transfers between devices: 7.08 us -> 6.17 us
    ppermute x3, waiting for transfers between devices: 4.15 us -> 3.27 us  [on_device(): lax.ppermute(own, 'sub', [(i, (i + shift) % subs) for i in range(subs)])]
    pallas_call x1 -> x2, Pallas kernels: 10.9 us -> 11.5 us  [the longest x1 10.7 us: on_device(): pl.pallas_call(functools.partial(modes_kernel, float(subs * cells)), out_...]
  transfers between devices with their start and end apart: 7 -> 7, of which waited for: 3 -> 3; matrix products, arithmetic and copies ran while one was open for 0% -> 0% of each run, Pallas kernels for 22% -> 23%
where the time goes in v11:
time: 84.3 us; the launch traced here: 83.8 us
  Pallas kernels  43.1 us (51%)
  starting transfers between devices  17.5 us (21%)
  blocking collectives  11.9 us (14%)
  waiting for transfers between devices  6.17 us (7%)
  local copies, waits for them, and re-layouts  5 us (6%)
    pallas_call x1, Pallas kernels, relax(): pl.pallas_call(near_kernel, out_shape=[first_state, second_state, *rows,...  12.5 us
    all_to_all x1, blocking collectives, on_device(): lax.all_to_all(pieces, 'nbhd', split_axis=0, concat_axis=0, tiled=True)  11.9 us
    pallas_call x1, Pallas kernels, on_device(): pl.pallas_call(functools.partial(modes_kernel, float(subs * cells)), out_...  10.7 us
    pallas_call x1, Pallas kernels, relax(): pl.pallas_call(far_kernel, out_shape=[first_state, second_state, kept(2),...  9.54 us
    ppermute x4, starting transfers between devices, swap(): return lax.ppermute(array, 'sub', pairs + [(j, i) for i, j in pairs])  8.89 us
    ppermute x3, starting transfers between devices, on_device(): lax.ppermute(own, 'sub', [(i, (i + shift) % subs) for i in range(subs)])  8.64 us
    pallas_call x1, Pallas kernels, relax(): pl.pallas_call(own_kernel, out_shape=[pltpu.HBM((planes,) + first_state.s...  6.13 us
    unnamed x15, local copies, waits for them, and re-layouts  4.99 us
  transfers between devices with their start and end apart: 7, of which 3 were waited for; matrix products, arithmetic and copies ran while one was open for 0% of the time, Pallas kernels for 23%

profile of v11, /device:TPU:0, one launch (start us, length us, event | category | flops | bytes accessed | tf_op | source)
XLA Modules:
  0.0 83.8 jit_solution(17689164750413258275)
XLA Ops:
  0.0 0.1 pad_add_fusion.flags
  0.1 3.4 %shard_map.74 = (bf16[33,96,128]{2,1,0:T(8,128)(2,1)}, bf16[33,96,128]{2,1,0:T(8,128)(2,1)}) custom-call(s32[4]{0:T(128)S(1)} %pad_add_fusion.flags, s32[64,96]{1,0:T(8,128)} %bitcast.15, bf16[64,96,128]{2,1,0:T(8,128)(2,1)} %bitcast.13), custom_call_target="tpu_custom_call" | custom-call | tf_op jit(solution)/shard_map/pallas_call | solution.py:448
  3.5 3.1 %collective-permute-start.2 = (bf16[33,96,128]{2,1,0:T(8,128)(2,1)}, bf16[33,96,128]{2,1,0:T(8,128)(2,1)S(1)}, u32[]{:S(2)}, u32[]{:S(2)}) collective-permute-start(bf16[33,96,128]{2,1,0:T(8,128)(2,1)} %get-tuple-element.23), channel_id=1, source_target_pairs={{0,1},{2,3},{1,0},{3,2},{4,5},{6,7},{5,4},{7,6},{8,9},{10,11},{9,8... | collective-permute-start | bytes 2433032 | tf_op jit(solution)/shard_map/ppermute | solution.py:412
  6.6 0.7 collective-permute-start.3
  7.3 1.4 %copy-done.1 = bf16[1,4,16,96,128]{4,3,2,1,0:T(8,128)(2,1)S(1)} copy-done((bf16[1,4,16,96,128]{4,3,2,1,0:T(8,128)(2,1)S(1)}, bf16[1,4,16,96,128]{4,3,2,1,0:T(8,128)(2,1)}, u32[]{:S(2)}) %copy-start.1) | copy-done | bytes 1572888
  8.7 0.8 copy-done.2
  9.4 0.7 copy-done.3
  10.2 0.7 copy-done.5
  10.9 0.7 copy-done.6
  11.5 6.1 %shard_map.73 = (f32[4,18,128,128]{3,2,1,0:T(8,128)}, f32[2,18,128,128]{3,2,1,0:T(8,128)}, bf16[16,32,128]{2,1,0:T(8,128)(2,1)S(1)}, bf16[24,96,128]{2,1,0:T(8,1...) custom-call(s32[4]{0:T(128)S(1)} %pad_add_fusion.flags, bf16[64,96,128]{2,1,0:T(8,128)(2,1)S(1)} %bitcast.14, ...), custom_call_target="tpu_custom_call" | custom-call | tf_op jit(solution)/shard_map/pallas_call | solution.py:461
  17.7 4.4 %collective-permute-start = (bf16[24,96,128]{2,1,0:T(8,128)(2,1)}, bf16[24,96,128]{2,1,0:T(8,128)(2,1)S(1)}, u32[]{:S(2)}, u32[]{:S(2)}) collective-permute-start(bf16[24,96,128]{2,1,0:T(8,128)(2,1)} %get-tuple-element.21), channel_id=1, source_target_pairs={{0,1},{2,3},{1,0},{3,2},{4,5},{6,7},{5,4},{7,6},{8,9},{10,11},{9,8... | collective-permute-start | bytes 1769480 | tf_op jit(solution)/shard_map/ppermute | solution.py:412
  22.1 0.7 collective-permute-start.1
  22.8 2.9 %collective-permute-done.2.near_a = bf16[33,96,128]{2,1,0:T(8,128)(2,1)S(1)} collective-permute-done((bf16[33,96,128]{2,1,0:T(8,128)(2,1)}, bf16[33,96,128]{2,1,0:T(8,128)(2,1)S(1)}, u32[]{:S(2)}, u32[]{:S(2)}) %collective-permute-start.2) | collective-permute-done | bytes 811040 | tf_op jit(solution)/shard_map/ppermute | solution.py:412
  25.7 12.5 %shard_map.75 = (f32[12,18,128,128]{3,2,1,0:T(8,128)S(1)}, f32[10,18,128,128]{3,2,1,0:T(8,128)S(1)}, f32[6,192,128]{2,1,0:T(8,128)S(1)}, f32[8,64,128]{2,1,0:T(8...) custom-call(s32[4]{0:T(128)S(1)} %pad_add_fusion.flags, ...), custom_call_target="tpu_custom_call" | custom-call | tf_op jit(solution)/shard_map/pallas_call | solution.py:480
  38.2 9.5 %shard_map.76 = (f32[12,18,128,128]{3,2,1,0:T(8,128)S(1)}, f32[10,18,128,128]{3,2,1,0:T(8,128)S(1)}, bf16[2,128,2048]{2,1,0:T(8,128)(2,1)S(1)}, f32[136,128]{1,0:T(8,128)S(1)}) custom-call(s32[4]{0:T(128)S(1)} %pad_add_fusion.flags, bf16[24,96,128]{2,1,0:T(8,128)(2,1)S(1)} %collective-permute-done.far_a, ...), custom_call_target="tpu_custom_call", output_to_operand_aliasing={{0}: (7, {}), {1}: (8, {})} | custom-call | tf_op jit(solution)/shard_map/pallas_call | solution.py:494
  47.8 4.1 %collective-permute-start.6 = (f32[136,128]{1,0:T(8,128)S(1)}, f32[136,128]{1,0:T(8,128)S(1)}, u32[]{:S(2)}, u32[]{:S(2)}) collective-permute-start(f32[136,128]{1,0:T(8,128)S(1)} %get-tuple-element.34.refs_1_), channel_id=1, source_target_pairs={{0,3},{1,0},{2,1},{3,2},{4,7},{5,4},{6,5},{7,6},{8,11},{9,8},{10,9... | collective-permute-start | bytes 208904 | tf_op jit(solution)/shard_map/ppermute | solution.py:680
  51.9 2.6 %collective-permute-start.5 = (f32[136,128]{1,0:T(8,128)S(1)}, f32[136,128]{1,0:T(8,128)S(1)}, u32[]{:S(2)}, u32[]{:S(2)}) collective-permute-start(f32[136,128]{1,0:T(8,128)S(1)} %get-tuple-element.34.refs_1_), channel_id=1, source_target_pairs={{0,2},{1,3},{2,0},{3,1},{4,6},{5,7},{6,4},{7,5},{8,10},{9,11},{10,... | collective-permute-start | bytes 208904 | tf_op jit(solution)/shard_map/ppermute | solution.py:680
  54.4 1.9 %collective-permute-start.4 = (f32[136,128]{1,0:T(8,128)S(1)}, f32[136,128]{1,0:T(8,128)S(1)}, u32[]{:S(2)}, u32[]{:S(2)}) collective-permute-start(f32[136,128]{1,0:T(8,128)S(1)} %get-tuple-element.34.refs_1_), channel_id=1, source_target_pairs={{0,1},{1,2},{2,3},{3,0},{4,5},{5,6},{6,7},{7,4},{8,9},{9,10},{10,1... | collective-permute-start | bytes 208904 | tf_op jit(solution)/shard_map/ppermute | solution.py:680
  56.4 0.9 %shard_map.77.refs_6_ = bf16[8,128,768]{2,1,0:T(8,128)(2,1)S(1)} custom-call(bf16[2,128,2048]{2,1,0:T(8,128)(2,1)S(1)} %get-tuple-element.35.near_ref, bf16[2,128,2048]{2,1,0:T(8,128)(2,1)S(1)} %get-tuple-element.36.far_ref), custom_call_target="tpu_custom_call" | custom-call | tf_op jit(solution)/shard_map/pallas_call | solution.py:684
  57.3 0.9 %collective-permute-done.5.refs_3_ = f32[136,128]{1,0:T(8,128)S(1)} collective-permute-done((f32[136,128]{1,0:T(8,128)S(1)}, f32[136,128]{1,0:T(8,128)S(1)}, u32[]{:S(2)}, u32[]{:S(2)}) %collective-permute-start.5) | collective-permute-done | bytes 69664 | tf_op jit(solution)/shard_map/ppermute | solution.py:680
  58.2 2.4 %collective-permute-done.4.refs_2_ = f32[136,128]{1,0:T(8,128)S(1)} collective-permute-done((f32[136,128]{1,0:T(8,128)S(1)}, f32[136,128]{1,0:T(8,128)S(1)}, u32[]{:S(2)}, u32[]{:S(2)}) %collective-permute-start.4) | collective-permute-done | bytes 69664 | tf_op jit(solution)/shard_map/ppermute | solution.py:680
  60.6 10.7 %shard_map.78 = bf16[8,32,768]{2,1,0:T(8,128)(2,1)S(1)} custom-call(s32[8]{0:T(128)S(1)} %dynamic-slice_bitcast_fusion.refs_0_, f32[136,128]{1,0:T(8,128)S(1)} %get-tuple-element.34.refs_1_, f32[136,128]{1,0:T(8,128)S(1)} %collective-permute-done.4.refs_2_, f32[136,128]{1,0:T(8,128)S(1)} %collective-permute-done.5.refs_3_, ...), custom_call_target="tpu_custom_call" | custom-call | tf_op jit(solution)/shard_map/pallas_call | solution.py:691
  71.2 11.9 %all_to_all.5 = bf16[8,32,768]{2,1,0:T(8,128)(2,1)S(1)} all-to-all(bf16[8,32,768]{2,1,0:T(8,128)(2,1)S(1)} %shard_map.78), channel_id=1, replica_groups=mesh['nbhd'=8,'sub'=4] {'nbhd'}, dimensions={0} | all-to-all | bytes 786432 | tf_op jit(solution)/shard_map/all_to_all | solution.py:703
  83.1 0.7 copy.13
  (14 shorter events, 0.0 us)
Async XLA Ops:
  0.0 56.4 %copy-start = (s32[8,8]{1,0:T(8,128)S(1)}, s32[8,8]{1,0:T(8,128)}, u32[]{:S(2)}) copy-start(s32[8,8]{1,0:T(8,128)} %param.13) | copy-start | bytes 772
  3.5 22.2 %collective-permute-start.2 = (bf16[33,96,128]{2,1,0:T(8,128)(2,1)}, bf16[33,96,128]{2,1,0:T(8,128)(2,1)S(1)}, u32[]{:S(2)}, u32[]{:S(2)}) collective-permute-start(bf16[33,96,128]{2,1,0:T(8,128)(2,1)} %get-tuple-element.23), channel_id=1, source_target_pairs={{0,1},{2,3},{1,0},{3,2},{4,5},{6,7},{5,4},{7,6},{8,9},{10,11},{9,8... | collective-permute-start | bytes 2433032 | tf_op jit(solution)/shard_map/ppermute | solution.py:412
  6.6 19.1 %collective-permute-start.3 = (bf16[33,96,128]{2,1,0:T(8,128)(2,1)}, bf16[33,96,128]{2,1,0:T(8,128)(2,1)S(1)}, u32[]{:S(2)}, u32[]{:S(2)}) collective-permute-start(bf16[33,96,128]{2,1,0:T(8,128)(2,1)} %get-tuple-element.24), channel_id=1, source_target_pairs={{1,2},{2,1},{5,6},{6,5},{9,10},{10,9},{13,14},{14,13},{17,18},{18,... | collective-permute-start | bytes 2433032 | tf_op jit(solution)/shard_map/ppermute | solution.py:412
  7.3 1.4 %copy-start.1 = (bf16[1,4,16,96,128]{4,3,2,1,0:T(8,128)(2,1)S(1)}, bf16[1,4,16,96,128]{4,3,2,1,0:T(8,128)(2,1)}, u32[]{:S(2)}) copy-start(bf16[1,4,16,96,128]{4,3,2,1,0:T(8,128)(2,1)} %param.7) | copy-start | bytes 4718596
  8.7 0.8 copy-start.2
  9.4 0.7 copy-start.3
  10.2 0.7 copy-start.5
  10.9 0.7 copy-start.6
  17.7 20.5 %collective-permute-start = (bf16[24,96,128]{2,1,0:T(8,128)(2,1)}, bf16[24,96,128]{2,1,0:T(8,128)(2,1)S(1)}, u32[]{:S(2)}, u32[]{:S(2)}) collective-permute-start(bf16[24,96,128]{2,1,0:T(8,128)(2,1)} %get-tuple-element.21), channel_id=1, source_target_pairs={{0,1},{2,3},{1,0},{3,2},{4,5},{6,7},{5,4},{7,6},{8,9},{10,11},{9,8... | collective-permute-start | bytes 1769480 | tf_op jit(solution)/shard_map/ppermute | solution.py:412
  22.1 16.1 %collective-permute-start.1 = (bf16[24,96,128]{2,1,0:T(8,128)(2,1)}, bf16[24,96,128]{2,1,0:T(8,128)(2,1)S(1)}, u32[]{:S(2)}, u32[]{:S(2)}) collective-permute-start(bf16[24,96,128]{2,1,0:T(8,128)(2,1)} %get-tuple-element.22), channel_id=1, source_target_pairs={{1,2},{2,1},{5,6},{6,5},{9,10},{10,9},{13,14},{14,13},{17,18},{18,... | collective-permute-start | bytes 1769480 | tf_op jit(solution)/shard_map/ppermute | solution.py:412
  38.2 22.4 %copy-start.4 = (f32[1,128,32]{1,2,0:T(8,128)S(1)}, f32[1,128,32]{1,2,0:T(8,128)}, u32[]{:S(2)}) copy-start(f32[1,128,32]{1,2,0:T(8,128)} %param.12) | copy-start | bytes 49156
  47.8 9.5 %collective-permute-start.6 = (f32[136,128]{1,0:T(8,128)S(1)}, f32[136,128]{1,0:T(8,128)S(1)}, u32[]{:S(2)}, u32[]{:S(2)}) collective-permute-start(f32[136,128]{1,0:T(8,128)S(1)} %get-tuple-element.34.refs_1_), channel_id=1, source_target_pairs={{0,3},{1,0},{2,1},{3,2},{4,7},{5,4},{6,5},{7,6},{8,11},{9,8},{10,9... | collective-permute-start | bytes 208904 | tf_op jit(solution)/shard_map/ppermute | solution.py:680
  51.9 6.3 %collective-permute-start.5 = (f32[136,128]{1,0:T(8,128)S(1)}, f32[136,128]{1,0:T(8,128)S(1)}, u32[]{:S(2)}, u32[]{:S(2)}) collective-permute-start(f32[136,128]{1,0:T(8,128)S(1)} %get-tuple-element.34.refs_1_), channel_id=1, source_target_pairs={{0,2},{1,3},{2,0},{3,1},{4,6},{5,7},{6,4},{7,5},{8,10},{9,11},{10,... | collective-permute-start | bytes 208904 | tf_op jit(solution)/shard_map/ppermute | solution.py:680
  54.4 6.1 %collective-permute-start.4 = (f32[136,128]{1,0:T(8,128)S(1)}, f32[136,128]{1,0:T(8,128)S(1)}, u32[]{:S(2)}, u32[]{:S(2)}) collective-permute-start(f32[136,128]{1,0:T(8,128)S(1)} %get-tuple-element.34.refs_1_), channel_id=1, source_target_pairs={{0,1},{1,2},{2,3},{3,0},{4,5},{5,6},{6,7},{7,4},{8,9},{9,10},{10,1... | collective-permute-start | bytes 208904 | tf_op jit(solution)/shard_map/ppermute | solution.py:680

commit v12 on v11

--- a/solution.py
+++ b/solution.py
@@ -185,27 +185,25 @@
     return jnp.left_shift(jnp.int32(1), 2 * marks).astype(jnp.float32)
 
 
-def pack_kernel(flags, class_map, lines, near_a, near_b, classes, sems):
+def pack_kernel(flags, class_map, lines, near_a, near_b, mid_a, mid_b, classes, sems):
     count, rows_z = classes.shape
-    near = near_a.shape[0] - 1
+    size = mid_a.shape[0]
     upward = flags[0]
-    fetch = pltpu.make_async_copy(class_map, classes, sems.at[16])
+    fetch = pltpu.make_async_copy(class_map, classes, sems.at[4])
     fetch.start()
     copies = []
-    chunk = near // 8
-    for out, start in (
-        (near_a, upward * (count - near)),
-        (near_b, (1 - upward) * (count - near)),
+    for out, skip, start in (
+        (near_a, 1, upward * (count - size)),
+        (near_b, 1, (1 - upward) * (count - size)),
+        (mid_a, 0, size + upward * (count - 3 * size)),
+        (mid_b, 0, size + (1 - upward) * (count - 3 * size)),
     ):
-        for at in range(0, near, chunk):
-            copies.append(
-                pltpu.make_async_copy(
-                    lines.at[pl.ds(start + at, chunk)],
-                    out.at[pl.ds(1 + at, chunk)],
-                    sems.at[len(copies)],
-                )
+        copies.append(
+            pltpu.make_async_copy(
+                lines.at[pl.ds(start, size)], out.at[pl.ds(skip, size)], sems.at[len(copies)]
             )
-            copies[-1].start()
+        )
+        copies[-1].start()
     fetch.wait()
     marks = classes[...].astype(jnp.float32).astype(jnp.bfloat16)
     width = near_a.shape[2]
@@ -301,16 +299,13 @@
     state_b,
     weights,
     stiff_rows,
-    snap,
-    gram,
     kappa,
-    both,
     sems,
 ):
     lines = own_kappa.shape[0]
     rows_z = near_a.shape[1]
     rows_y = pad_rows.shape[0]
-    near = lines // 2
+    gap = lines + rows_y
     planes = lines // rows_y
     taken = []
     cut = (rows_y + 2) // 2
@@ -333,8 +328,9 @@
         marks = part[0][:lines].astype(jnp.float32).astype(jnp.int32)
         kappa[pl.ds(base, lines)] = powers(marks)
     weight_rows(kappa, weights, stiff_rows, lines, first, last, rows_y, rows_z)
-    fill(state_a, near_a, 1, near, near + even * (lines + near), pad_rows)
-    fill(state_a, near_b, 1, near, near + (1 - even) * (lines + near), pad_rows)
+    low = lines - rows_y
+    fill(state_a, near_a, 1, rows_y, low + even * gap, pad_rows)
+    fill(state_a, near_b, 1, rows_y, low + (1 - even) * gap, pad_rows)
     for copy in taken:
         copy.wait()
     ghost_low = state_a[planes, 0]
@@ -347,9 +343,39 @@
             state_b[e - 1, 0] = ghost_low
             state_b[e - 1, rows_y + 1] = ghost_high
     step = functools.partial(relax_lines, weights=weights, rows_y=rows_y, rows_z=rows_z)
-    ends = (lines - rows_y, 2 * lines - rows_y)
-    step(state_a, state_b, first_lines=ends, count=2 * rows_y, keep=True)
-    step(state_b, state_a, first_lines=(lines,), count=lines, keep=True)
+    step(state_a, state_b, first_lines=(lines, 2 * lines - rows_y), count=rows_y, keep=True)
+    inner = (lines + rows_y,)
+    step(state_b, state_a, first_lines=inner, count=lines - 2 * rows_y, keep=True)
+
+
+def mid_kernel(
+    flags,
+    mid_a,
+    mid_b,
+    weights,
+    stiff_rows,
+    pad_rows,
+    old_a,
+    old_b,
+    state_a,
+    state_b,
+    snap,
+    gram,
+    both,
+):
+    del old_a, old_b
+    rows_y = pad_rows.shape[0]
+    rows_z = mid_a.shape[1]
+    lines = stiff_rows.shape[1]
+    planes = lines // rows_y
+    even = flags[0]
+    low = lines - 2 * rows_y
+    gap = lines + 3 * rows_y
+    fill(state_a, mid_a, 0, rows_y, low + even * gap, pad_rows)
+    fill(state_a, mid_b, 0, rows_y, low + (1 - even) * gap, pad_rows)
+    step = functools.partial(relax_lines, weights=weights, rows_y=rows_y, rows_z=rows_z)
+    step(state_a, state_b, first_lines=(lines - rows_y, 2 * lines), count=rows_y, keep=True)
+    step(state_b, state_a, first_lines=(lines, 2 * lines - rows_y), count=rows_y, keep=True)
     inner = (lines + rows_y,)
     step(state_a, state_b, first_lines=inner, count=lines - 2 * rows_y, keep=False)
     inside = range(planes + 1, 2 * planes - 1)
@@ -420,7 +446,7 @@
     flags = jnp.stack([even, index == 0, index == subs - 1, 0]).astype(jnp.int32)
     lines = initial.reshape(planes * rows_y, rows_z, width)
     count = planes * rows_y
-    near, half = 2 * rows_y, rows_y // 2
+    half = rows_y // 2
     flat_classes = classes.reshape(count, rows_z)
     part = functools.partial(jax.ShapeDtypeStruct, dtype=initial.dtype)
     vmem = pl.BlockSpec(memory_space=pltpu.VMEM)
@@ -445,19 +471,21 @@
         jax.ShapeDtypeStruct((6, 3 * count, LANES), jnp.float32),
         jax.ShapeDtypeStruct((8, count, LANES), jnp.float32),
     ]
-    near_a, near_b = pl.pallas_call(
+    near_a, near_b, mid_a, mid_b = pl.pallas_call(
         pack_kernel,
-        out_shape=[part((near + 1, rows_z, width))] * 2,
+        out_shape=[part((rows_y + 1, rows_z, width))] * 2 + [part((rows_y, rows_z, width))] * 2,
         in_specs=[smem] + [hbm] * 2,
-        out_specs=[vmem] * 2,
+        out_specs=[vmem] * 4,
         scratch_shapes=[
             pltpu.VMEM((count, rows_z), jnp.int32),
-            pltpu.SemaphoreType.DMA((17,)),
+            pltpu.SemaphoreType.DMA((5,)),
         ],
         compiler_params=params,
     )(flags, in_hbm(flat_classes), in_hbm(lines))
     near_a = swap(near_a, 0)
     near_b = swap(near_b, 1)
+    mid_a = swap(mid_a, 0)
+    mid_b = swap(mid_b, 1)
     hand, inner, pad_rows, far_a, far_b, own_kappa = pl.pallas_call(
         own_kernel,
         out_shape=[
@@ -477,20 +505,28 @@
     )(flags, lines, flat_classes, y_vals, z_vals, face_ids[None])
     far_a = swap(far_a, 0)
     far_b = swap(far_b, 1)
-    state_a, state_b, weights, stiff_rows, snap_near, gram_near = pl.pallas_call(
+    state_a, state_b, weights, stiff_rows = pl.pallas_call(
         near_kernel,
+        out_shape=[first_state, second_state, *rows],
+        in_specs=[smem] + [vmem] * 4 + [hbm] * 2,
+        out_specs=[vmem] * 4,
+        scratch_shapes=[kappa, pltpu.SemaphoreType.DMA((4 * planes - 4,))],
+        compiler_params=params,
+    )(flags, near_a, near_b, own_kappa, pad_rows, in_hbm(hand), in_hbm(inner))
+    state_a, state_b, snap_near, gram_near = pl.pallas_call(
+        mid_kernel,
         out_shape=[
             first_state,
             second_state,
-            *rows,
             kept(planes - 2),
             jax.ShapeDtypeStruct((width, 2 * width), jnp.float32),
         ],
-        in_specs=[smem] + [vmem] * 4 + [hbm] * 2,
-        out_specs=[vmem] * 6,
-        scratch_shapes=[kappa, both, pltpu.SemaphoreType.DMA((4 * planes - 4,))],
+        in_specs=[smem] + [vmem] * 7,
+        out_specs=[vmem] * 4,
+        scratch_shapes=[both],
+        input_output_aliases={6: 0, 7: 1},
         compiler_params=params,
-    )(flags, near_a, near_b, own_kappa, pad_rows, in_hbm(hand), in_hbm(inner))
+    )(flags, mid_a, mid_b, weights, stiff_rows, pad_rows, held(state_a), held(state_b))
     _, _, snap_far, gram = pl.pallas_call(
         far_kernel,
         out_shape=[

time: 84.3 us -> 100 us (1.19)
  starting transfers between devices: 17.5 us -> 27.4 us
  waiting for transfers between devices: 6.17 us -> 11.8 us
    ppermute x3, starting transfers between devices: 8.64 us -> 15.7 us  [on_device(): lax.ppermute(own, 'sub', [(i, (i + shift) % subs) for i in range(subs)])]
    ppermute x4 -> x6, waiting for transfers between devices: 2.91 us -> 8.2 us  [swap(): return lax.ppermute(array, 'sub', pairs + [(j, i) for i, j in pairs])]
    ppermute x4 -> x6, starting transfers between devices: 8.89 us -> 11.7 us  [swap(): return lax.ppermute(array, 'sub', pairs + [(j, i) for i, j in pairs])]
    pallas_call x2 -> x3, Pallas kernels: 15.9 us -> 16.2 us  [the longest x1 6.74 us: relax(): pl.pallas_call(mid_kernel, out_shape=[first_state, second_state, kept(pla...]
  transfers between devices with their start and end apart: 7 -> 9, of which waited for: 3 -> 3; matrix products, arithmetic and copies ran while one was open for 0% -> 0% of each run, Pallas kernels for 23% -> 20%
where the time goes in v12:
time: 100 us; the launch traced here: 99.8 us
  Pallas kernels  43.4 us (43%)
  starting transfers between devices  27.4 us (27%)
  blocking collectives  11.9 us (12%)
  waiting for transfers between devices  11.8 us (12%)
  local copies, waits for them, and re-layouts  5 us (5%)
    ppermute x3, starting transfers between devices, on_device(): lax.ppermute(own, 'sub', [(i, (i + shift) % subs) for i in range(subs)])  15.7 us
    all_to_all x1, blocking collectives, on_device(): lax.all_to_all(pieces, 'nbhd', split_axis=0, concat_axis=0, tiled=True)  11.9 us
    ppermute x6, starting transfers between devices, swap(): return lax.ppermute(array, 'sub', pairs + [(j, i) for i, j in pairs])  11.7 us
    pallas_call x1, Pallas kernels, on_device(): pl.pallas_call(functools.partial(modes_kernel, float(subs * cells)), out_...  10.7 us
    pallas_call x1, Pallas kernels, relax(): pl.pallas_call(far_kernel, out_shape=[first_state, second_state, kept(2),...  9.56 us
    ppermute x6, waiting for transfers between devices, swap(): return lax.ppermute(array, 'sub', pairs + [(j, i) for i, j in pairs])  8.2 us
    pallas_call x1, Pallas kernels, relax(): pl.pallas_call(mid_kernel, out_shape=[first_state, second_state, kept(pla...  6.74 us
    pallas_call x1, Pallas kernels, relax(): pl.pallas_call(near_kernel, out_shape=[first_state, second_state, *rows],...  6.58 us
  transfers between devices with their start and end apart: 9, of which 3 were waited for; matrix products, arithmetic and copies ran while one was open for 0% of the time, Pallas kernels for 20%

profile of v12, /device:TPU:0, one launch (start us, length us, event | category | flops | bytes accessed | tf_op | source)
XLA Modules:
  0.0 99.8 jit_solution(17848542172719626831)
XLA Ops:
  0.1 2.9 %shard_map.74 = (bf16[17,96,128]{2,1,0:T(8,128)(2,1)S(1)}, bf16[17,96,128]{2,1,0:T(8,128)(2,1)S(1)}, bf16[16,96,128]{2,1,0:T(8,128)(2,1)}, bf16[16,96,128]{2,1,0:T(8,128)(2,1)}) custom-call(s32[4]{0:T(128)S(1)} %pad_add_fusion.flags, s32[64,96]{1,0:T(8,128)} %bitcast.15, bf16[64,96,128]{2,1,0:T(8,128)(2,1)} %bitcast.13), custom_call_target="tpu_custom_call" | custom-call | tf_op jit(solution)/shard_map/pallas_call | solution.py:474
  2.9 3.1 %collective-permute-start.2 = (bf16[17,96,128]{2,1,0:T(8,128)(2,1)S(1)}, bf16[17,96,128]{2,1,0:T(8,128)(2,1)S(1)}, u32[]{:S(2)}, u32[]{:S(2)}) collective-permute-start(bf16[17,96,128]{2,1,0:T(8,128)(2,1)S(1)} %get-tuple-element.27), channel_id=1, source_target_pairs={{0,1},{2,3},{1,0},{3,2},{4,5},{6,7},{5,4},{7,6},{8,9},{10,11},{9,8... | collective-permute-start | bytes 1253384 | tf_op jit(solution)/shard_map/ppermute | solution.py:438
  6.0 1.4 %copy-done.1 = bf16[1,4,16,96,128]{4,3,2,1,0:T(8,128)(2,1)S(1)} copy-done((bf16[1,4,16,96,128]{4,3,2,1,0:T(8,128)(2,1)S(1)}, bf16[1,4,16,96,128]{4,3,2,1,0:T(8,128)(2,1)}, u32[]{:S(2)}) %copy-start.1) | copy-done | bytes 1572888
  7.4 0.8 copy-done.2
  8.2 0.7 copy-done.3
  8.9 0.7 copy-done.5
  10.3 6.2 %shard_map.73 = (f32[4,18,128,128]{3,2,1,0:T(8,128)}, f32[2,18,128,128]{3,2,1,0:T(8,128)}, bf16[16,32,128]{2,1,0:T(8,128)(2,1)S(1)}, bf16[24,96,128]{2,1,0:T(8,1...) custom-call(s32[4]{0:T(128)S(1)} %pad_add_fusion.flags, bf16[64,96,128]{2,1,0:T(8,128)(2,1)S(1)} %bitcast.14, ...), custom_call_target="tpu_custom_call" | custom-call | tf_op jit(solution)/shard_map/pallas_call | solution.py:489
  16.5 0.7 collective-permute-start.1
  17.2 0.7 collective-permute-start.3
  17.9 6.5 %collective-permute-start.4 = (bf16[16,96,128]{2,1,0:T(8,128)(2,1)}, bf16[16,96,128]{2,1,0:T(8,128)(2,1)S(1)}, u32[]{:S(2)}, u32[]{:S(2)}) collective-permute-start(bf16[16,96,128]{2,1,0:T(8,128)(2,1)} %get-tuple-element.35), channel_id=1, source_target_pairs={{0,1},{2,3},{1,0},{3,2},{4,5},{6,7},{5,4},{7,6},{8,9},{10,11},{9,8... | collective-permute-start | bytes 1179656 | tf_op jit(solution)/shard_map/ppermute | solution.py:438
  24.5 0.7 collective-permute-start.5
  25.2 6.6 %shard_map.75 = (f32[12,18,128,128]{3,2,1,0:T(8,128)S(1)}, f32[10,18,128,128]{3,2,1,0:T(8,128)S(1)}, f32[6,192,128]{2,1,0:T(8,128)S(1)}, f32[8,64,128]{2,1,0:T(8,128)S(1)}) custom-call(s32[4]{0:T(128)S(1)} %pad_add_fusion.flags, bf16[17,96,128]{2,1,0:T(8,128)(2,1)S(1)} %collective-permute-done.2.near_a, ...), custom_call_target="tpu_custom_call" | custom-call | tf_op jit(solution)/shard_map/pallas_call | solution.py:508
  31.7 8.2 %collective-permute-done.4.mid_a = bf16[16,96,128]{2,1,0:T(8,128)(2,1)S(1)} collective-permute-done((bf16[16,96,128]{2,1,0:T(8,128)(2,1)}, bf16[16,96,128]{2,1,0:T(8,128)(2,1)S(1)}, u32[]{:S(2)}, u32[]{:S(2)}) %collective-permute-start.4) | collective-permute-done | bytes 393248 | tf_op jit(solution)/shard_map/ppermute | solution.py:438
  39.9 6.7 %shard_map.76 = (f32[12,18,128,128]{3,2,1,0:T(8,128)S(1)}, f32[10,18,128,128]{3,2,1,0:T(8,128)S(1)}, bf16[2,128,2048]{2,1,0:T(8,128)(2,1)S(1)}, f32[128,256]{1,0:T(8,128)S(1)}) custom-call(s32[4]{0:T(128)S(1)} %pad_add_fusion.flags, bf16[16,96,128]{2,1,0:T(8,128)(2,1)S(1)} %collective-permute-done.4.mid_a, ...), custom_call_target="tpu_custom_call", output_to_operand_aliasing={{0}: (6, {}), {1}: (7, {})} | custom-call | tf_op jit(solution)/shard_map/pallas_call | solution.py:516
  46.7 9.6 %shard_map.77 = (f32[12,18,128,128]{3,2,1,0:T(8,128)S(1)}, f32[10,18,128,128]{3,2,1,0:T(8,128)S(1)}, bf16[2,128,2048]{2,1,0:T(8,128)(2,1)S(1)}, f32[136,128]{1,0:T(8,128)S(1)}) custom-call(s32[4]{0:T(128)S(1)} %pad_add_fusion.flags, bf16[24,96,128]{2,1,0:T(8,128)(2,1)S(1)} %collective-permute-done.far_a, ...), custom_call_target="tpu_custom_call", output_to_operand_aliasing={{0}: (7, {}), {1}: (8, {})} | custom-call | tf_op jit(solution)/shard_map/pallas_call | solution.py:530
  56.3 2.5 %collective-permute-start.8 = (f32[136,128]{1,0:T(8,128)S(1)}, f32[136,128]{1,0:T(8,128)S(1)}, u32[]{:S(2)}, u32[]{:S(2)}) collective-permute-start(f32[136,128]{1,0:T(8,128)S(1)} %get-tuple-element.42.refs_1_), channel_id=1, source_target_pairs={{0,3},{1,0},{2,1},{3,2},{4,7},{5,4},{6,5},{7,6},{8,11},{9,8},{10,9... | collective-permute-start | bytes 208904 | tf_op jit(solution)/shard_map/ppermute | solution.py:716
  58.8 11.6 %collective-permute-start.7 = (f32[136,128]{1,0:T(8,128)S(1)}, f32[136,128]{1,0:T(8,128)S(1)}, u32[]{:S(2)}, u32[]{:S(2)}) collective-permute-start(f32[136,128]{1,0:T(8,128)S(1)} %get-tuple-element.42.refs_1_), channel_id=1, source_target_pairs={{0,2},{1,3},{2,0},{3,1},{4,6},{5,7},{6,4},{7,5},{8,10},{9,11},{10,... | collective-permute-start | bytes 208904 | tf_op jit(solution)/shard_map/ppermute | solution.py:716
  70.4 1.6 %collective-permute-start.6 = (f32[136,128]{1,0:T(8,128)S(1)}, f32[136,128]{1,0:T(8,128)S(1)}, u32[]{:S(2)}, u32[]{:S(2)}) collective-permute-start(f32[136,128]{1,0:T(8,128)S(1)} %get-tuple-element.42.refs_1_), channel_id=1, source_target_pairs={{0,1},{1,2},{2,3},{3,0},{4,5},{5,6},{6,7},{7,4},{8,9},{9,10},{10,1... | collective-permute-start | bytes 208904 | tf_op jit(solution)/shard_map/ppermute | solution.py:716
  72.0 0.9 shard_map.78.refs_6_
  72.8 2.0 %collective-permute-done.7.refs_3_ = f32[136,128]{1,0:T(8,128)S(1)} collective-permute-done((f32[136,128]{1,0:T(8,128)S(1)}, f32[136,128]{1,0:T(8,128)S(1)}, u32[]{:S(2)}, u32[]{:S(2)}) %collective-permute-start.7) | collective-permute-done | bytes 69664 | tf_op jit(solution)/shard_map/ppermute | solution.py:716
  74.9 1.6 %collective-permute-done.6.refs_2_ = f32[136,128]{1,0:T(8,128)S(1)} collective-permute-done((f32[136,128]{1,0:T(8,128)S(1)}, f32[136,128]{1,0:T(8,128)S(1)}, u32[]{:S(2)}, u32[]{:S(2)}) %collective-permute-start.6) | collective-permute-done | bytes 69664 | tf_op jit(solution)/shard_map/ppermute | solution.py:716
  76.5 10.7 %shard_map.79 = bf16[8,32,768]{2,1,0:T(8,128)(2,1)S(1)} custom-call(s32[8]{0:T(128)S(1)} %dynamic-slice_bitcast_fusion.refs_0_, f32[136,128]{1,0:T(8,128)S(1)} %get-tuple-element.42.refs_1_, f32[136,128]{1,0:T(8,128)S(1)} %collective-permute-done.6.refs_2_, f32[136,128]{1,0:T(8,128)S(1)} %collective-permute-done.7.refs_3_, ...), custom_call_target="tpu_custom_call" | custom-call | tf_op jit(solution)/shard_map/pallas_call | solution.py:727
  87.2 11.9 %all_to_all.5 = bf16[8,32,768]{2,1,0:T(8,128)(2,1)S(1)} all-to-all(bf16[8,32,768]{2,1,0:T(8,128)(2,1)S(1)} %shard_map.79), channel_id=1, replica_groups=mesh['nbhd'=8,'sub'=4] {'nbhd'}, dimensions={0} | all-to-all | bytes 786432 | tf_op jit(solution)/shard_map/all_to_all | solution.py:739
  99.0 0.7 copy.17
  (19 shorter events, 0.8 us)
Async XLA Ops:
  0.0 71.9 %copy-start = (s32[8,8]{1,0:T(8,128)S(1)}, s32[8,8]{1,0:T(8,128)}, u32[]{:S(2)}) copy-start(s32[8,8]{1,0:T(8,128)} %param.13) | copy-start | bytes 772
  2.9 21.5 %collective-permute-start.2 = (bf16[17,96,128]{2,1,0:T(8,128)(2,1)S(1)}, bf16[17,96,128]{2,1,0:T(8,128)(2,1)S(1)}, u32[]{:S(2)}, u32[]{:S(2)}) collective-permute-start(bf16[17,96,128]{2,1,0:T(8,128)(2,1)S(1)} %get-tuple-element.27), channel_id=1, source_target_pairs={{0,1},{2,3},{1,0},{3,2},{4,5},{6,7},{5,4},{7,6},{8,9},{10,11},{9,8... | collective-permute-start | bytes 1253384 | tf_op jit(solution)/shard_map/ppermute | solution.py:438
  6.0 1.4 %copy-start.1 = (bf16[1,4,16,96,128]{4,3,2,1,0:T(8,128)(2,1)S(1)}, bf16[1,4,16,96,128]{4,3,2,1,0:T(8,128)(2,1)}, u32[]{:S(2)}) copy-start(bf16[1,4,16,96,128]{4,3,2,1,0:T(8,128)(2,1)} %param.7) | copy-start | bytes 4718596
  7.4 0.8 copy-start.2
  8.2 0.7 copy-start.3
  8.9 0.7 copy-start.5
  9.6 0.7 copy-start.6
  16.4 30.2 %collective-permute-start = (bf16[24,96,128]{2,1,0:T(8,128)(2,1)}, bf16[24,96,128]{2,1,0:T(8,128)(2,1)S(1)}, u32[]{:S(2)}, u32[]{:S(2)}) collective-permute-start(bf16[24,96,128]{2,1,0:T(8,128)(2,1)} %get-tuple-element.25), channel_id=1, source_target_pairs={{0,1},{2,3},{1,0},{3,2},{4,5},{6,7},{5,4},{7,6},{8,9},{10,11},{9,8... | collective-permute-start | bytes 1769480 | tf_op jit(solution)/shard_map/ppermute | solution.py:438
  16.5 30.2 %collective-permute-start.1 = (bf16[24,96,128]{2,1,0:T(8,128)(2,1)}, bf16[24,96,128]{2,1,0:T(8,128)(2,1)S(1)}, u32[]{:S(2)}, u32[]{:S(2)}) collective-permute-start(bf16[24,96,128]{2,1,0:T(8,128)(2,1)} %get-tuple-element.26), channel_id=1, source_target_pairs={{1,2},{2,1},{5,6},{6,5},{9,10},{10,9},{13,14},{14,13},{17,18},{18,... | collective-permute-start | bytes 1769480 | tf_op jit(solution)/shard_map/ppermute | solution.py:438
  17.2 7.9 %collective-permute-start.3 = (bf16[17,96,128]{2,1,0:T(8,128)(2,1)S(1)}, bf16[17,96,128]{2,1,0:T(8,128)(2,1)S(1)}, u32[]{:S(2)}, u32[]{:S(2)}) collective-permute-start(bf16[17,96,128]{2,1,0:T(8,128)(2,1)S(1)} %get-tuple-element.28), channel_id=1, source_target_pairs={{1,2},{2,1},{5,6},{6,5},{9,10},{10,9},{13,14},{14,13},{17,18},{18,... | collective-permute-start | bytes 1253384 | tf_op jit(solution)/shard_map/ppermute | solution.py:438
  17.9 22.0 %collective-permute-start.4 = (bf16[16,96,128]{2,1,0:T(8,128)(2,1)}, bf16[16,96,128]{2,1,0:T(8,128)(2,1)S(1)}, u32[]{:S(2)}, u32[]{:S(2)}) collective-permute-start(bf16[16,96,128]{2,1,0:T(8,128)(2,1)} %get-tuple-element.35), channel_id=1, source_target_pairs={{0,1},{2,3},{1,0},{3,2},{4,5},{6,7},{5,4},{7,6},{8,9},{10,11},{9,8... | collective-permute-start | bytes 1179656 | tf_op jit(solution)/shard_map/ppermute | solution.py:438
  24.5 15.5 %collective-permute-start.5 = (bf16[16,96,128]{2,1,0:T(8,128)(2,1)}, bf16[16,96,128]{2,1,0:T(8,128)(2,1)S(1)}, u32[]{:S(2)}, u32[]{:S(2)}) collective-permute-start(bf16[16,96,128]{2,1,0:T(8,128)(2,1)} %get-tuple-element.36), channel_id=1, source_target_pairs={{1,2},{2,1},{5,6},{6,5},{9,10},{10,9},{13,14},{14,13},{17,18},{18,... | collective-permute-start | bytes 1179656 | tf_op jit(solution)/shard_map/ppermute | solution.py:438
  46.7 29.8 %copy-start.4 = (f32[1,128,32]{1,2,0:T(8,128)S(1)}, f32[1,128,32]{1,2,0:T(8,128)}, u32[]{:S(2)}) copy-start(f32[1,128,32]{1,2,0:T(8,128)} %param.12) | copy-start | bytes 49156
  56.3 16.6 %collective-permute-start.8 = (f32[136,128]{1,0:T(8,128)S(1)}, f32[136,128]{1,0:T(8,128)S(1)}, u32[]{:S(2)}, u32[]{:S(2)}) collective-permute-start(f32[136,128]{1,0:T(8,128)S(1)} %get-tuple-element.42.refs_1_), channel_id=1, source_target_pairs={{0,3},{1,0},{2,1},{3,2},{4,7},{5,4},{6,5},{7,6},{8,11},{9,8},{10,9... | collective-permute-start | bytes 208904 | tf_op jit(solution)/shard_map/ppermute | solution.py:716
  58.8 16.1 %collective-permute-start.7 = (f32[136,128]{1,0:T(8,128)S(1)}, f32[136,128]{1,0:T(8,128)S(1)}, u32[]{:S(2)}, u32[]{:S(2)}) collective-permute-start(f32[136,128]{1,0:T(8,128)S(1)} %get-tuple-element.42.refs_1_), channel_id=1, source_target_pairs={{0,2},{1,3},{2,0},{3,1},{4,6},{5,7},{6,4},{7,5},{8,10},{9,11},{10,... | collective-permute-start | bytes 208904 | tf_op jit(solution)/shard_map/ppermute | solution.py:716
  70.4 6.1 %collective-permute-start.6 = (f32[136,128]{1,0:T(8,128)S(1)}, f32[136,128]{1,0:T(8,128)S(1)}, u32[]{:S(2)}, u32[]{:S(2)}) collective-permute-start(f32[136,128]{1,0:T(8,128)S(1)} %get-tuple-element.42.refs_1_), channel_id=1, source_target_pairs={{0,1},{1,2},{2,3},{3,0},{4,5},{5,6},{6,7},{7,4},{8,9},{9,10},{10,1... | collective-permute-start | bytes 208904 | tf_op jit(solution)/shard_map/ppermute | solution.py:716

commit v13 on v11

--- a/solution.py
+++ b/solution.py
@@ -526,26 +526,62 @@
     return jnp.broadcast_to(tile[row : row + 1, :], (8, tile.shape[1]))
 
 
-def pivot_block(left, right, first_lane):
+def pivot_pairs(left, right, first_lane, heads):
     sub = lax.broadcasted_iota(jnp.int32, (8, 128), 0)
     cols = [lane_copy(left, first_lane + j) for j in range(8)]
-    for j in range(8):
-        recip = pl.reciprocal(row_copy(cols[j], j), approx=True)
-        here = sub == j
-        mult = jnp.where(here, recip, -cols[j] * recip)
-        for l in range(j + 1, 8):
-            cols[l] = jnp.where(here, 0.0, cols[l]) + mult * row_copy(cols[l], j)
-        left = jnp.where(here, 0.0, left) + mult * row_copy(left, j)
-        right = jnp.where(here, 0.0, right) + mult * row_copy(right, j)
+    for j in range(0, 8, 2):
+        first, second = cols[j], cols[j + 1]
+        p, q, s = row_copy(first, j), row_copy(second, j), row_copy(second, j + 1)
+        det = p * s - q * q
+        recip = pl.reciprocal(det, approx=True)
+        a, b, c = s * recip, q * recip, p * recip
+        first = first - jnp.where(sub == j, 1.0, 0.0)
+        second = second - jnp.where(sub == j + 1, 1.0, 0.0)
+
+        def reduce(tile, j=j, a=a, b=b, c=c, first=first, second=second):
+            w = tile.shape[1]
+            r0, r1 = row_copy(tile, j), row_copy(tile, j + 1)
+            x0 = a[:, :w] * r0 - b[:, :w] * r1
+            x1 = c[:, :w] * r1 - b[:, :w] * r0
+            return tile - (first[:, :w] * x0 + second[:, :w] * x1)
+
+        if heads is not None:
+            r0, r1 = row_copy(right, j), row_copy(right, j + 1)
+            inverse = pl.reciprocal(p, approx=True)
+            heads.append(r0 * lax.rsqrt(p))
+            heads.append((r1 - (q * inverse) * r0) * lax.rsqrt(det * inverse))
+        for l in range(j + 2, 8):
+            cols[l] = reduce(cols[l])
+        left, right = reduce(left), reduce(right)
         yield left, right
+
+
+def gather_rows(rows):
+    sub = lax.broadcasted_iota(jnp.int32, rows[0].shape, 0)
+    out = rows[0]
+    for i in range(1, 8):
+        out = jnp.where(sub == i, rows[i], out)
+    return out
+
+
+def unit_diagonal(matrix):
+    row = lax.broadcasted_iota(jnp.int32, matrix.shape, 0)
+    col = lax.broadcasted_iota(jnp.int32, matrix.shape, 1)
+    diagonal = jnp.where(row == col, matrix, 0.0)
+    across = lax.rsqrt(jnp.sum(diagonal, axis=0, keepdims=True))
+    down = lax.rsqrt(jnp.sum(diagonal, axis=1, keepdims=True))
+    return across, down
 
 
 def solve_spd(left, right):
     size = left.shape[0]
     count = size // 8
+    across, down = unit_diagonal(left)
+    left = left * across * down
+    right = right * down
     lhs = [left[8 * t : 8 * t + 8] for t in range(count)]
     rhs = [right[8 * t : 8 * t + 8] for t in range(count)]
-    for panel in pivot_block(lhs[0], rhs[0], 0):
+    for panel in pivot_pairs(lhs[0], rhs[0], 0, None):
         lhs[0], rhs[0] = panel
     for k in range(count):
         rows_l = [row_copy(lhs[k], j) for j in range(8)]
@@ -561,14 +597,14 @@
         if k + 1 < count:
             update(k + 1)
             panel = None
-            for panel in pivot_block(lhs[k + 1], rhs[k + 1], 8 * (k + 1)):
-                for t in others[:2]:
+            for panel in pivot_pairs(lhs[k + 1], rhs[k + 1], 8 * (k + 1), None):
+                for t in others[:4]:
                     update(t)
-                others = others[2:]
+                others = others[4:]
             lhs[k + 1], rhs[k + 1] = panel
         for t in others:
             update(t)
-    return jnp.concatenate(rhs, axis=0)
+    return jnp.concatenate(rhs, axis=0) * down
 
 
 def tree(terms):
@@ -580,30 +616,24 @@
 def whiten(inner, block):
     size = inner.shape[0]
     count = size // 8
-    sub = lax.broadcasted_iota(jnp.int32, (8, 128), 0)
+    across, down = unit_diagonal(inner)
+    inner = inner * across * down
+    block = block * down
     lhs = [inner[8 * t : 8 * t + 8] for t in range(count)]
     rhs = [block[8 * t : 8 * t + 8] for t in range(count)]
     done = []
     for k in range(count):
-        live = range(k, count)
-        cols = {t: [lane_copy(lhs[t], 8 * k + j) for j in range(8)] for t in live}
-        scale = None
-        for j in range(8):
-            pivot = row_copy(cols[k][j], j)
-            recip = pl.reciprocal(pivot, approx=True)
-            root = lax.rsqrt(pivot)
-            scale = root if scale is None else jnp.where(sub >= j, root, scale)
-            head = {l: row_copy(cols[k][l], j) for l in range(j + 1, 8)}
-            row_l, row_r = row_copy(lhs[k], j), row_copy(rhs[k], j)
-            for t in live:
-                mult = cols[t][j] * recip
-                if t == k:
-                    mult = jnp.where(sub > j, mult, 0.0)
-                for l in range(j + 1, 8):
-                    cols[t][l] = cols[t][l] - mult * head[l]
-                lhs[t] = lhs[t] - mult[:, : row_l.shape[1]] * row_l
-                rhs[t] = rhs[t] - mult * row_r
-        done.append(rhs[k] * scale)
+        heads = []
+        panel = None
+        for panel in pivot_pairs(lhs[k], rhs[k], 8 * k, heads):
+            pass
+        done.append(gather_rows(heads))
+        rows_l = [row_copy(panel[0], j) for j in range(8)]
+        rows_r = [row_copy(panel[1], j) for j in range(8)]
+        for t in range(k + 1, count):
+            tile_cols = [lane_copy(lhs[t], 8 * k + j) for j in range(8)]
+            lhs[t] = lhs[t] - tree([tile_cols[j][:, :size] * rows_l[j] for j in range(8)])
+            rhs[t] = rhs[t] - tree([tile_cols[j] * rows_r[j] for j in range(8)])
     return jnp.concatenate(done, axis=0)
 
 

time: 84.3 us -> 85.6 us (1.015)
  Pallas kernels: 43.1 us -> 44.4 us
    pallas_call x1, Pallas kernels: 10.7 us -> 12 us  [on_device(): pl.pallas_call(functools.partial(modes_kernel, float(subs * cells)), out_...]
where the time goes in v13:
time: 85.6 us; the launch traced here: 85.2 us
  Pallas kernels  44.4 us (52%)
  starting transfers between devices  17.5 us (20%)
  blocking collectives  11.9 us (14%)
  waiting for transfers between devices  6.17 us (7%)
  local copies, waits for them, and re-layouts  5 us (6%)
    pallas_call x1, Pallas kernels, relax(): pl.pallas_call(near_kernel, out_shape=[first_state, second_state, *rows,...  12.5 us
    pallas_call x1, Pallas kernels, on_device(): pl.pallas_call(functools.partial(modes_kernel, float(subs * cells)), out_...  12 us
    all_to_all x1, blocking collectives, on_device(): lax.all_to_all(pieces, 'nbhd', split_axis=0, concat_axis=0, tiled=True)  11.9 us
    pallas_call x1, Pallas kernels, relax(): pl.pallas_call(far_kernel, out_shape=[first_state, second_state, kept(2),...  9.54 us
    ppermute x4, starting transfers between devices, swap(): return lax.ppermute(array, 'sub', pairs + [(j, i) for i, j in pairs])  8.89 us
    ppermute x3, starting transfers between devices, on_device(): lax.ppermute(own, 'sub', [(i, (i + shift) % subs) for i in range(subs)])  8.64 us
    pallas_call x1, Pallas kernels, relax(): pl.pallas_call(own_kernel, out_shape=[pltpu.HBM((planes,) + first_state.s...  6.13 us
    unnamed x15, local copies, waits for them, and re-layouts  4.99 us
  transfers between devices with their start and end apart: 7, of which 3 were waited for; matrix products, arithmetic and copies ran while one was open for 0% of the time, Pallas kernels for 23%

profile of v13, /device:TPU:0, one launch (start us, length us, event | category | flops | bytes accessed | tf_op | source)
XLA Modules:
  0.0 85.2 jit_solution(11818242333565510126)
XLA Ops:
  0.0 0.1 pad_add_fusion.flags
  0.1 3.4 %shard_map.74 = (bf16[33,96,128]{2,1,0:T(8,128)(2,1)}, bf16[33,96,128]{2,1,0:T(8,128)(2,1)}) custom-call(s32[4]{0:T(128)S(1)} %pad_add_fusion.flags, s32[64,96]{1,0:T(8,128)} %bitcast.15, bf16[64,96,128]{2,1,0:T(8,128)(2,1)} %bitcast.13), custom_call_target="tpu_custom_call" | custom-call | tf_op jit(solution)/shard_map/pallas_call | solution.py:448
  3.5 3.1 %collective-permute-start.2 = (bf16[33,96,128]{2,1,0:T(8,128)(2,1)}, bf16[33,96,128]{2,1,0:T(8,128)(2,1)S(1)}, u32[]{:S(2)}, u32[]{:S(2)}) collective-permute-start(bf16[33,96,128]{2,1,0:T(8,128)(2,1)} %get-tuple-element.23), channel_id=1, source_target_pairs={{0,1},{2,3},{1,0},{3,2},{4,5},{6,7},{5,4},{7,6},{8,9},{10,11},{9,8... | collective-permute-start | bytes 2433032 | tf_op jit(solution)/shard_map/ppermute | solution.py:412
  6.6 0.7 collective-permute-start.3
  7.3 1.4 %copy-done.1 = bf16[1,4,16,96,128]{4,3,2,1,0:T(8,128)(2,1)S(1)} copy-done((bf16[1,4,16,96,128]{4,3,2,1,0:T(8,128)(2,1)S(1)}, bf16[1,4,16,96,128]{4,3,2,1,0:T(8,128)(2,1)}, u32[]{:S(2)}) %copy-start.1) | copy-done | bytes 1572888
  8.7 0.8 copy-done.2
  9.4 0.7 copy-done.3
  10.2 0.7 copy-done.5
  10.9 0.7 copy-done.6
  11.5 6.1 %shard_map.73 = (f32[4,18,128,128]{3,2,1,0:T(8,128)}, f32[2,18,128,128]{3,2,1,0:T(8,128)}, bf16[16,32,128]{2,1,0:T(8,128)(2,1)S(1)}, bf16[24,96,128]{2,1,0:T(8,1...) custom-call(s32[4]{0:T(128)S(1)} %pad_add_fusion.flags, bf16[64,96,128]{2,1,0:T(8,128)(2,1)S(1)} %bitcast.14, ...), custom_call_target="tpu_custom_call" | custom-call | tf_op jit(solution)/shard_map/pallas_call | solution.py:461
  17.7 4.4 %collective-permute-start = (bf16[24,96,128]{2,1,0:T(8,128)(2,1)}, bf16[24,96,128]{2,1,0:T(8,128)(2,1)S(1)}, u32[]{:S(2)}, u32[]{:S(2)}) collective-permute-start(bf16[24,96,128]{2,1,0:T(8,128)(2,1)} %get-tuple-element.21), channel_id=1, source_target_pairs={{0,1},{2,3},{1,0},{3,2},{4,5},{6,7},{5,4},{7,6},{8,9},{10,11},{9,8... | collective-permute-start | bytes 1769480 | tf_op jit(solution)/shard_map/ppermute | solution.py:412
  22.1 0.7 collective-permute-start.1
  22.8 2.9 %collective-permute-done.2.near_a = bf16[33,96,128]{2,1,0:T(8,128)(2,1)S(1)} collective-permute-done((bf16[33,96,128]{2,1,0:T(8,128)(2,1)}, bf16[33,96,128]{2,1,0:T(8,128)(2,1)S(1)}, u32[]{:S(2)}, u32[]{:S(2)}) %collective-permute-start.2) | collective-permute-done | bytes 811040 | tf_op jit(solution)/shard_map/ppermute | solution.py:412
  25.7 12.5 %shard_map.75 = (f32[12,18,128,128]{3,2,1,0:T(8,128)S(1)}, f32[10,18,128,128]{3,2,1,0:T(8,128)S(1)}, f32[6,192,128]{2,1,0:T(8,128)S(1)}, f32[8,64,128]{2,1,0:T(8...) custom-call(s32[4]{0:T(128)S(1)} %pad_add_fusion.flags, ...), custom_call_target="tpu_custom_call" | custom-call | tf_op jit(solution)/shard_map/pallas_call | solution.py:480
  38.2 9.5 %shard_map.76 = (f32[12,18,128,128]{3,2,1,0:T(8,128)S(1)}, f32[10,18,128,128]{3,2,1,0:T(8,128)S(1)}, bf16[2,128,2048]{2,1,0:T(8,128)(2,1)S(1)}, f32[136,128]{1,0:T(8,128)S(1)}) custom-call(s32[4]{0:T(128)S(1)} %pad_add_fusion.flags, bf16[24,96,128]{2,1,0:T(8,128)(2,1)S(1)} %collective-permute-done.far_a, ...), custom_call_target="tpu_custom_call", output_to_operand_aliasing={{0}: (7, {}), {1}: (8, {})} | custom-call | tf_op jit(solution)/shard_map/pallas_call | solution.py:494
  47.8 4.1 %collective-permute-start.6 = (f32[136,128]{1,0:T(8,128)S(1)}, f32[136,128]{1,0:T(8,128)S(1)}, u32[]{:S(2)}, u32[]{:S(2)}) collective-permute-start(f32[136,128]{1,0:T(8,128)S(1)} %get-tuple-element.34.refs_1_), channel_id=1, source_target_pairs={{0,3},{1,0},{2,1},{3,2},{4,7},{5,4},{6,5},{7,6},{8,11},{9,8},{10,9... | collective-permute-start | bytes 208904 | tf_op jit(solution)/shard_map/ppermute | solution.py:710
  51.9 2.6 %collective-permute-start.5 = (f32[136,128]{1,0:T(8,128)S(1)}, f32[136,128]{1,0:T(8,128)S(1)}, u32[]{:S(2)}, u32[]{:S(2)}) collective-permute-start(f32[136,128]{1,0:T(8,128)S(1)} %get-tuple-element.34.refs_1_), channel_id=1, source_target_pairs={{0,2},{1,3},{2,0},{3,1},{4,6},{5,7},{6,4},{7,5},{8,10},{9,11},{10,... | collective-permute-start | bytes 208904 | tf_op jit(solution)/shard_map/ppermute | solution.py:710
  54.4 1.9 %collective-permute-start.4 = (f32[136,128]{1,0:T(8,128)S(1)}, f32[136,128]{1,0:T(8,128)S(1)}, u32[]{:S(2)}, u32[]{:S(2)}) collective-permute-start(f32[136,128]{1,0:T(8,128)S(1)} %get-tuple-element.34.refs_1_), channel_id=1, source_target_pairs={{0,1},{1,2},{2,3},{3,0},{4,5},{5,6},{6,7},{7,4},{8,9},{9,10},{10,1... | collective-permute-start | bytes 208904 | tf_op jit(solution)/shard_map/ppermute | solution.py:710
  56.4 0.9 %shard_map.77.refs_6_ = bf16[8,128,768]{2,1,0:T(8,128)(2,1)S(1)} custom-call(bf16[2,128,2048]{2,1,0:T(8,128)(2,1)S(1)} %get-tuple-element.35.near_ref, bf16[2,128,2048]{2,1,0:T(8,128)(2,1)S(1)} %get-tuple-element.36.far_ref), custom_call_target="tpu_custom_call" | custom-call | tf_op jit(solution)/shard_map/pallas_call | solution.py:714
  57.3 0.9 %collective-permute-done.5.refs_3_ = f32[136,128]{1,0:T(8,128)S(1)} collective-permute-done((f32[136,128]{1,0:T(8,128)S(1)}, f32[136,128]{1,0:T(8,128)S(1)}, u32[]{:S(2)}, u32[]{:S(2)}) %collective-permute-start.5) | collective-permute-done | bytes 69664 | tf_op jit(solution)/shard_map/ppermute | solution.py:710
  58.2 2.4 %collective-permute-done.4.refs_2_ = f32[136,128]{1,0:T(8,128)S(1)} collective-permute-done((f32[136,128]{1,0:T(8,128)S(1)}, f32[136,128]{1,0:T(8,128)S(1)}, u32[]{:S(2)}, u32[]{:S(2)}) %collective-permute-start.4) | collective-permute-done | bytes 69664 | tf_op jit(solution)/shard_map/ppermute | solution.py:710
  60.6 12.0 %shard_map.78 = bf16[8,32,768]{2,1,0:T(8,128)(2,1)S(1)} custom-call(s32[8]{0:T(128)S(1)} %dynamic-slice_bitcast_fusion.refs_0_, f32[136,128]{1,0:T(8,128)S(1)} %get-tuple-element.34.refs_1_, f32[136,128]{1,0:T(8,128)S(1)} %collective-permute-done.4.refs_2_, f32[136,128]{1,0:T(8,128)S(1)} %collective-permute-done.5.refs_3_, ...), custom_call_target="tpu_custom_call" | custom-call | tf_op jit(solution)/shard_map/pallas_call | solution.py:721
  72.6 11.9 %all_to_all.5 = bf16[8,32,768]{2,1,0:T(8,128)(2,1)S(1)} all-to-all(bf16[8,32,768]{2,1,0:T(8,128)(2,1)S(1)} %shard_map.78), channel_id=1, replica_groups=mesh['nbhd'=8,'sub'=4] {'nbhd'}, dimensions={0} | all-to-all | bytes 786432 | tf_op jit(solution)/shard_map/all_to_all | solution.py:733
  84.4 0.7 copy.13
  (14 shorter events, 0.0 us)
Async XLA Ops:
  0.0 56.4 %copy-start = (s32[8,8]{1,0:T(8,128)S(1)}, s32[8,8]{1,0:T(8,128)}, u32[]{:S(2)}) copy-start(s32[8,8]{1,0:T(8,128)} %param.13) | copy-start | bytes 772
  3.5 22.2 %collective-permute-start.2 = (bf16[33,96,128]{2,1,0:T(8,128)(2,1)}, bf16[33,96,128]{2,1,0:T(8,128)(2,1)S(1)}, u32[]{:S(2)}, u32[]{:S(2)}) collective-permute-start(bf16[33,96,128]{2,1,0:T(8,128)(2,1)} %get-tuple-element.23), channel_id=1, source_target_pairs={{0,1},{2,3},{1,0},{3,2},{4,5},{6,7},{5,4},{7,6},{8,9},{10,11},{9,8... | collective-permute-start | bytes 2433032 | tf_op jit(solution)/shard_map/ppermute | solution.py:412
  6.6 19.1 %collective-permute-start.3 = (bf16[33,96,128]{2,1,0:T(8,128)(2,1)}, bf16[33,96,128]{2,1,0:T(8,128)(2,1)S(1)}, u32[]{:S(2)}, u32[]{:S(2)}) collective-permute-start(bf16[33,96,128]{2,1,0:T(8,128)(2,1)} %get-tuple-element.24), channel_id=1, source_target_pairs={{1,2},{2,1},{5,6},{6,5},{9,10},{10,9},{13,14},{14,13},{17,18},{18,... | collective-permute-start | bytes 2433032 | tf_op jit(solution)/shard_map/ppermute | solution.py:412
  7.3 1.4 %copy-start.1 = (bf16[1,4,16,96,128]{4,3,2,1,0:T(8,128)(2,1)S(1)}, bf16[1,4,16,96,128]{4,3,2,1,0:T(8,128)(2,1)}, u32[]{:S(2)}) copy-start(bf16[1,4,16,96,128]{4,3,2,1,0:T(8,128)(2,1)} %param.7) | copy-start | bytes 4718596
  8.7 0.8 copy-start.2
  9.4 0.7 copy-start.3
  10.2 0.7 copy-start.5
  10.9 0.7 copy-start.6
  17.7 20.5 %collective-permute-start = (bf16[24,96,128]{2,1,0:T(8,128)(2,1)}, bf16[24,96,128]{2,1,0:T(8,128)(2,1)S(1)}, u32[]{:S(2)}, u32[]{:S(2)}) collective-permute-start(bf16[24,96,128]{2,1,0:T(8,128)(2,1)} %get-tuple-element.21), channel_id=1, source_target_pairs={{0,1},{2,3},{1,0},{3,2},{4,5},{6,7},{5,4},{7,6},{8,9},{10,11},{9,8... | collective-permute-start | bytes 1769480 | tf_op jit(solution)/shard_map/ppermute | solution.py:412
  22.1 16.1 %collective-permute-start.1 = (bf16[24,96,128]{2,1,0:T(8,128)(2,1)}, bf16[24,96,128]{2,1,0:T(8,128)(2,1)S(1)}, u32[]{:S(2)}, u32[]{:S(2)}) collective-permute-start(bf16[24,96,128]{2,1,0:T(8,128)(2,1)} %get-tuple-element.22), channel_id=1, source_target_pairs={{1,2},{2,1},{5,6},{6,5},{9,10},{10,9},{13,14},{14,13},{17,18},{18,... | collective-permute-start | bytes 1769480 | tf_op jit(solution)/shard_map/ppermute | solution.py:412
  38.2 22.4 %copy-start.4 = (f32[1,128,32]{1,2,0:T(8,128)S(1)}, f32[1,128,32]{1,2,0:T(8,128)}, u32[]{:S(2)}) copy-start(f32[1,128,32]{1,2,0:T(8,128)} %param.12) | copy-start | bytes 49156
  47.8 9.5 %collective-permute-start.6 = (f32[136,128]{1,0:T(8,128)S(1)}, f32[136,128]{1,0:T(8,128)S(1)}, u32[]{:S(2)}, u32[]{:S(2)}) collective-permute-start(f32[136,128]{1,0:T(8,128)S(1)} %get-tuple-element.34.refs_1_), channel_id=1, source_target_pairs={{0,3},{1,0},{2,1},{3,2},{4,7},{5,4},{6,5},{7,6},{8,11},{9,8},{10,9... | collective-permute-start | bytes 208904 | tf_op jit(solution)/shard_map/ppermute | solution.py:710
  51.9 6.3 %collective-permute-start.5 = (f32[136,128]{1,0:T(8,128)S(1)}, f32[136,128]{1,0:T(8,128)S(1)}, u32[]{:S(2)}, u32[]{:S(2)}) collective-permute-start(f32[136,128]{1,0:T(8,128)S(1)} %get-tuple-element.34.refs_1_), channel_id=1, source_target_pairs={{0,2},{1,3},{2,0},{3,1},{4,6},{5,7},{6,4},{7,5},{8,10},{9,11},{10,... | collective-permute-start | bytes 208904 | tf_op jit(solution)/shard_map/ppermute | solution.py:710
  54.4 6.1 %collective-permute-start.4 = (f32[136,128]{1,0:T(8,128)S(1)}, f32[136,128]{1,0:T(8,128)S(1)}, u32[]{:S(2)}, u32[]{:S(2)}) collective-permute-start(f32[136,128]{1,0:T(8,128)S(1)} %get-tuple-element.34.refs_1_), channel_id=1, source_target_pairs={{0,1},{1,2},{2,3},{3,0},{4,5},{5,6},{6,7},{7,4},{8,9},{9,10},{10,1... | collective-permute-start | bytes 208904 | tf_op jit(solution)/shard_map/ppermute | solution.py:710
